TPU v7x, 32 devices: a whole 2x2x4 slice. The times are simulated.
32 devices in a mesh: fsdp: 8 (over z, x), tp: 4 (over y, core).
Axes of the slice: x: 2, y: 2, z: 4, core: 2. Of those that a mesh axis runs over, the one named last changes fastest.
Arguments:
- master: float32 [14336, 4096], P(('fsdp', 'tp')), may hold values from -0.046875 to 0.046875
- moment_one: float32 [14336, 4096], P(('fsdp', 'tp')), may hold values from -6 to 6
- moment_two: float32 [14336, 4096], P(('fsdp', 'tp')), may hold values from 0.1 to 10
- gradient: bfloat16 [14336, 4096], P(('fsdp', 'tp')), may hold values from -6 to 6
- hidden_act: bfloat16 [4096, 14336], P('fsdp', 'tp'), may hold values from -6 to 6
Outputs:
- new_master: float32 [14336, 4096], P(('fsdp', 'tp'))
- new_one: float32 [14336, 4096], P(('fsdp', 'tp'))
- new_two: float32 [14336, 4096], P(('fsdp', 'tp'))
- decoded: bfloat16 [4096, 4096], P('fsdp', 'tp')
All inputs are finite; a program needn't handle non-finite values.
Results may differ from a plain program's by a relative error of at most 0.0049.
Values may be sent and summed in bfloat16 or wider, within the bound.
No kernel may reach another device: no remote copies, remote signals or barrier semaphores. Data moves between devices by JAX's collectives and lax.ppermute only.
A program may use at most 192 MiB of HBM per device.

v0:
```python
import jax
import jax.numpy as jnp
from jax import lax
from jax.sharding import PartitionSpec as P


def local(master, moment_one, moment_two, gradient, hidden_act):
    grad_float = gradient.astype(jnp.float32)
    new_one = 0.9 * moment_one + 0.1 * grad_float
    new_two = 0.95 * moment_two + 0.05 * grad_float * grad_float
    new_master = master - 0.001 * new_one / (jnp.sqrt(new_two) + 1e-08)
    rollout_weight = new_master.astype(jnp.bfloat16)
    groups = lax.axis_size("tp")
    block_rows = rollout_weight.shape[0]
    row_count = hidden_act.shape[0]
    shards = hidden_act.shape[1] // block_rows
    arranged = hidden_act.reshape(row_count, shards // groups, groups, block_rows)
    received = lax.all_to_all(arranged, "tp", split_axis=2, concat_axis=1, tiled=True)
    act_cols = received.reshape(row_count, shards * block_rows)
    partial_out = jnp.dot(
        act_cols,
        lax.all_gather(rollout_weight, "fsdp", axis=0, tiled=True),
        preferred_element_type=jnp.float32,
    )
    decoded = lax.psum_scatter(partial_out, "tp", scatter_dimension=1, tiled=True).astype(
        jnp.bfloat16
    )
    return (new_master, new_one, new_two, decoded)


def solution(mesh):
    placed = (
        P(("fsdp", "tp"), None),
        P(("fsdp", "tp"), None),
        P(("fsdp", "tp"), None),
        P(("fsdp", "tp"), None),
        P("fsdp", "tp"),
    )
    return jax.shard_map(
        local,
        mesh=mesh,
        in_specs=placed,
        out_specs=(
            P(("fsdp", "tp"), None),
            P(("fsdp", "tp"), None),
            P(("fsdp", "tp"), None),
            P("fsdp", "tp"),
        ),
        check_vma=False,
    )
```

profile of v0, /device:TPU:0, one launch (start us, length us, event | category | flops | bytes accessed | tf_op | source)
XLA Modules:
  0.0 692.8 jit_solution(6568333531687837767)
XLA Ops:
  7.2 0.0 all-gather.2.cloned.1.call-start
  7.2 19.1 %fusion.2 = (bf16[448,4096]{1,0:T(8,128)(2,1)}, f32[448,4096]{1,0:T(8,128)}, f32[448,4096]{1,0:T(8,128)}, f32[448,4096]{1,0:T(8,128)}) fusion(f32[448,4096]{1,0:T(8,128)} %param.5, bf16[448,4096]{1,0:T(8,128)(2,1)} %param.8, f32[448,4096]{1,0:T(8,128)} %param.6, f32[448,4096]{1,0:T(8,128)} %param.7), kind=kLoop, calls=%fused_computation.6 | loop fusion | flops 23855104 | bytes 51380224 | tf_op jit(solution)/shard_map/convert_element_type | solution.py:12
  26.3 0.0 all-gather.2.cloned.1.call-update
  26.3 0.0 reduce-scatter.2.cloned.1.call-start
  26.4 6.0 copy.13
  32.3 2.3 copy.14
  34.6 46.8 %all_to_all.15 = bf16[512,2,4,448]{0,3,1,2:T(8,128)(2,1)} all-to-all(bf16[512,2,4,448]{0,3,1,2:T(8,128)(2,1)S(1)} %copy.14), channel_id=1, replica_groups=mesh['fsdp'=8,'tp'=4] {'tp'}, dimensions={2} | all-to-all | bytes 7340032 | tf_op jit(solution)/shard_map/all_to_all | solution.py:18
  81.4 506.8 %all-gather.2.cloned.1.call-done = bf16[3584,4096]{1,0:T(8,128)(2,1)} async-done(((bf16[448,4096]{1,0:T(8,128)(2,1)}), bf16[3584,4096]{1,0:T(8,128)(2,1)}) %all-gather.2.cloned.1.call-update) | async-done | bytes 29360144 | tf_op jit(solution)/shard_map/all_gather | solution.py:22
  588.3 22.8 %convolution_bitcast_fusion = f32[512,4096]{0,1:T(8,128)} fusion(bf16[3584,4096]{1,0:T(8,128)(2,1)} %all-gather.2.cloned.1.call-done, bf16[512,3584]{0,1:T(8,128)(2,1)} %bitcast.11), kind=kOutput, calls=%fused_computation.5 | convolution fusion | flops 15032385536 | bytes 41418752 | tf_op jit(solution)/shard_map/dot_general | solution.py:20
  611.0 0.0 reduce-scatter.2.cloned.1.call-update
  611.0 71.8 %reduce-scatter.2.cloned.1.call-done = f32[512,1024]{0,1:T(8,128)} async-done(((f32[512,4096]{0,1:T(8,128)}), f32[512,1024]{0,1:T(8,128)}) %reduce-scatter.2.cloned.1.call-update) | async-done | bytes 2097168 | tf_op jit(solution)/shard_map/reduce_scatter | solution.py:25
  682.9 1.7 convert_element_type.11
  684.6 1.3 copy.15
Async XLA Ops:
  7.2 581.1 %all-gather.2.cloned.1.call-start = ((), (), s32[]{:S(2)}) async-start(), calls=%async_computation.2 | async-start | bytes 33030144 | tf_op jit(solution)/shard_map/all_gather | solution.py:22
  26.3 656.6 %reduce-scatter.2.cloned.1.call-start = ((), (), s32[]{:S(2)}) async-start(), calls=%async_computation.3 | async-start | bytes 10485760 | tf_op jit(solution)/shard_map/reduce_scatter | solution.py:25
Sparse Core Ops, SparseCore 0:
  26.4 561.7 all-gather.1
  611.1 71.6 reduce-scatter.1
where the time goes:
time: 693 us
  waiting for transfers between devices  579 us (84%)
  blocking collectives  46.8 us (7%)
  matrix products  22.8 us (3%)
  other arithmetic  20.8 us (3%)
  between operations  14 us (2%)
  local copies, waits for them, and re-layouts  9.56 us (1%)
    all_gather x1, waiting for transfers between devices, local(): lax.all_gather(rollout_weight, 'fsdp', axis=0, tiled=True)  507 us
    reduce_scatter x1, waiting for transfers between devices, local(): lax.psum_scatter(partial_out, 'tp', scatter_dimension=1, tiled=True)  71.8 us
    all_to_all x1, blocking collectives, local(): lax.all_to_all(arranged, 'tp', split_axis=2, concat_axis=1, tiled=True)  46.8 us
    dot_general x1, matrix products, local(): jnp.dot(act_cols, lax.all_gather(rollout_weight, 'fsdp', axis=0, tiled=Tr...  22.8 us
    convert_element_type x1, other arithmetic, local(): rollout_weight = new_master.astype(jnp.bfloat16)  19.1 us
  transfers between devices with their start and end apart: 2, of which 2 were waited for; matrix products, arithmetic and copies ran while one was open for 1% of the time, Pallas kernels for 0%

commit v1 on v0

v1 whole, which is shorter than its diff:
```python
import jax
import jax.numpy as jnp
from jax import lax
from jax.experimental import pallas as pl
from jax.experimental.pallas import tpu as pltpu
from jax.sharding import PartitionSpec as P

AXES = ("fsdp", "tp")
ROW_CHUNKS = 2
COL_CHUNKS = 4


def adam_kernel(y_ref, master_ref, one_ref, two_ref, grad_ref, new_master_ref, new_one_ref, new_two_ref, *weight_refs):
    grad = grad_ref[...].astype(jnp.float32)
    new_one = 0.9 * one_ref[...] + 0.1 * grad
    new_two = 0.95 * two_ref[...] + 0.05 * grad * grad
    new_master = master_ref[...] - 0.001 * new_one / (jnp.sqrt(new_two) + 1e-08)
    new_one_ref[...] = new_one
    new_two_ref[...] = new_two
    new_master_ref[...] = new_master
    weight = new_master.astype(jnp.bfloat16)
    quarter = weight.shape[1] // 4
    part = quarter // len(weight_refs)

    def put(first):
        for q, ref in enumerate(weight_refs):
            for i, half in enumerate((first, 1 - first)):
                for core in range(2):
                    at = (2 * half + core) * quarter + q * part
                    ref[:, (2 * i + core) * part : (2 * i + core + 1) * part] = weight[:, at : at + part]

    @pl.when(y_ref[0] == 0)
    def _():
        put(0)

    @pl.when(y_ref[0] != 0)
    def _():
        put(1)


def adam(y, master, moment_one, moment_two, gradient):
    rows, cols = master.shape
    step = max(s for s in range(16, 65, 16) if rows % s == 0)
    block = pl.BlockSpec((step, cols), lambda i: (i, 0))
    piece = pl.BlockSpec((step, cols // COL_CHUNKS), lambda i: (i, 0))
    full = jax.ShapeDtypeStruct((rows, cols), jnp.float32)
    out = pl.pallas_call(
        adam_kernel,
        grid=(rows // step,),
        in_specs=[pl.BlockSpec(memory_space=pltpu.SMEM), block, block, block, block],
        out_specs=[block, block, block] + [piece] * COL_CHUNKS,
        out_shape=[full, full, full]
        + [jax.ShapeDtypeStruct((rows, cols // COL_CHUNKS), jnp.bfloat16)] * COL_CHUNKS,
        compiler_params=pltpu.CompilerParams(vmem_limit_bytes=40 * 1024 * 1024),
        cost_estimate=pl.CostEstimate(flops=12 * rows * cols, bytes_accessed=28 * rows * cols, transcendentals=rows * cols),
        name="adam",
    )(y.reshape(1), master, moment_one, moment_two, gradient)
    return out[0], out[1], out[2], out[3:]


def swap_if(flag, low, high):
    return jnp.where(flag, high, low), jnp.where(flag, low, high)


def in_order(parts, index):
    count = len(parts)
    if count == 1:
        return parts
    half = count // 2
    flag = (index & half) != 0
    pairs = [swap_if(flag, a, b) for a, b in zip(parts[:half], parts[half:])]
    return in_order([p[0] for p in pairs], index) + in_order([p[1] for p in pairs], index)


def local(master, moment_one, moment_two, gradient, hidden_act):
    fsdp, tp = lax.axis_size("fsdp"), lax.axis_size("tp")
    xs = fsdp // tp
    f, t = lax.axis_index("fsdp"), lax.axis_index("tp")
    z, x, y, c = f // xs, f % xs, t // 2, t % 2

    def permute(value, to):
        pairs = []
        for zi in range(tp):
            for xi in range(xs):
                for yi in range(2):
                    for ci in range(2):
                        zo, xo, yo, co = to(zi, xi, yi, ci)
                        pairs.append(((zi * xs + xi) * tp + 2 * yi + ci, (zo * xs + xo) * tp + 2 * yo + co))
        return lax.ppermute(value, AXES, pairs)

    new_master, new_one, new_two, weights = adam(y, master, moment_one, moment_two, gradient)

    rows = hidden_act.shape[0]
    depth = hidden_act.shape[1] // 2
    span = depth // xs
    columns = [
        jnp.concatenate([hidden_act[:, (2 * k + s) * span : (2 * k + s + 1) * span] for k in range(xs)], axis=1)
        for s in range(2)
    ]
    own, other = swap_if(y != 0, *columns)
    part_rows = rows // 2 // ROW_CHUNKS
    own = own.reshape(2, ROW_CHUNKS, part_rows, depth)
    other = other.reshape(2, ROW_CHUNKS, part_rows, depth)
    acts = []
    for m in range(ROW_CHUNKS):
        mine = own[:, m]
        theirs = permute(other[:, m], lambda z, x, y, c: (z, x, 1 - y, c))
        got = []
        for a in range(2):
            data = jnp.where(((z // 2) ^ a ^ y) == 0, mine, theirs)
            first, second = swap_if((z % 2) != 0, data[0], data[1])
            for b, piece in enumerate((first, second)):
                got.append(permute(piece, lambda z, x, y, c: (2 * ((z // 2) ^ a) + c, x, y, (z % 2) ^ b)))
        acts.append(jnp.concatenate(got, axis=0))

    tables = []
    for piece in weights:
        parts = [piece] + [permute(piece, lambda z, x, y, c: (z, x ^ d, y, c)) for d in range(1, xs)]
        here = jnp.stack(in_order(parts, x))
        there = permute(here, lambda z, x, y, c: (z, x, y, 1 - c))
        zero, one = swap_if(c != 0, here, there)
        tables.append(jnp.stack([zero, one], axis=1).reshape(depth, piece.shape[1]))

    blocks = [[], []]
    for m in range(ROW_CHUNKS):
        line = [[], []]
        for table in tables:
            total = jnp.dot(acts[m], table, preferred_element_type=jnp.float32)
            half = table.shape[1] // 2
            back = permute(total[:, half:].astype(jnp.bfloat16), lambda z, x, y, c: (z, x, 1 - y, c))
            total = (total[:, :half] + back).reshape(2, 2, part_rows, half)
            keep, send = swap_if((c ^ (z % 2)) != 0, total[:, 0], total[:, 1])
            back = permute(send.astype(jnp.bfloat16), lambda z, x, y, c: (z ^ 1, x, y, c))
            total = keep + back
            back = permute(total[1].astype(jnp.bfloat16), lambda z, x, y, c: (z ^ 2, x, y, c))
            total = (total[0] + back).astype(jnp.bfloat16)
            keep, send = swap_if(c != 0, total[:, : half // 2], total[:, half // 2 :])
            back = permute(send, lambda z, x, y, c: (z, x, y, 1 - c))
            top, bottom = swap_if(c != 0, keep, back)
            line[0].append(top)
            line[1].append(bottom)
        for s in range(2):
            blocks[s].append(jnp.concatenate(line[s], axis=1))
    decoded = jnp.concatenate(blocks[0] + blocks[1], axis=0)
    return (new_master, new_one, new_two, decoded)


def solution(mesh):
    placed = (
        P(("fsdp", "tp"), None),
        P(("fsdp", "tp"), None),
        P(("fsdp", "tp"), None),
        P(("fsdp", "tp"), None),
        P("fsdp", "tp"),
    )
    return jax.shard_map(
        local,
        mesh=mesh,
        in_specs=placed,
        out_specs=(
            P(("fsdp", "tp"), None),
            P(("fsdp", "tp"), None),
            P(("fsdp", "tp"), None),
            P("fsdp", "tp"),
        ),
        check_vma=False,
    )
```

time: 693 us -> 333 us (0.48)
  waiting for transfers between devices: 579 us -> 149 us
  starting transfers between devices: 0.08 us -> 106 us
  blocking collectives: 46.8 us -> 0 us
  Pallas kernels: 0 us -> 19.4 us
  between operations: 14 us -> 1.64 us
    all_gather x1 -> x0, waiting for transfers between devices: 507 us -> none  [local(): lax.all_gather(rollout_weight, 'fsdp', axis=0, tiled=True)]
    ppermute x0 -> x50, waiting for transfers between devices: none -> 149 us  [permute(): return lax.ppermute(value, AXES, pairs)]
    ppermute x0 -> x50, starting transfers between devices: none -> 106 us  [permute(): return lax.ppermute(value, AXES, pairs)]
    reduce_scatter x1 -> x0, waiting for transfers between devices: 71.8 us -> none  [local(): lax.psum_scatter(partial_out, 'tp', scatter_dimension=1, tiled=True)]
    all_to_all x1 -> x0, blocking collectives: 46.8 us -> none  [local(): lax.all_to_all(arranged, 'tp', split_axis=2, concat_axis=1, tiled=True)]
    convert_element_type x2 -> x16, other arithmetic: 20.8 us -> 0.62 us  [the longest x8 0.4 us: local(): send.astype(jnp.bfloat16)]
    pallas_call x0 -> x1, Pallas kernels: none -> 19.4 us  [adam(): pl.pallas_call(adam_kernel, grid=(rows // step,), in_specs=[pl.BlockSpec(...]
    concatenate x0 -> x2, other arithmetic: none -> 12.6 us  [the longest x1 9.94 us: local(): decoded = jnp.concatenate(blocks[0] + blocks[1], axis=0)]
  transfers between devices with their start and end apart: 2 -> 50, of which waited for: 2 -> 21; matrix products, arithmetic and copies ran while one was open for 1% -> 11% of each run, Pallas kernels for 0% -> 6%
where the time goes in v1:
time: 333 us; the launch traced here: 331 us
  waiting for transfers between devices  149 us (45%)
  starting transfers between devices  106 us (32%)
  other arithmetic  27.5 us (8%)
  Pallas kernels  19.4 us (6%)
  matrix products  16.5 us (5%)
  local copies, waits for them, and re-layouts  10.9 us (3%)
    ppermute x50, waiting for transfers between devices, permute(): return lax.ppermute(value, AXES, pairs)  149 us
    ppermute x50, starting transfers between devices, permute(): return lax.ppermute(value, AXES, pairs)  106 us
    pallas_call x1, Pallas kernels, adam(): pl.pallas_call(adam_kernel, grid=(rows // step,), in_specs=[pl.BlockSpec(...  19.4 us
    dot_general x8, matrix products, local(): total = jnp.dot(acts[m], table, preferred_element_type=jnp.float32)  16.5 us
    concatenate x1, other arithmetic, local(): decoded = jnp.concatenate(blocks[0] + blocks[1], axis=0)  9.94 us
  transfers between devices with their start and end apart: 50, of which 21 were waited for; matrix products, arithmetic and copies ran while one was open for 11% of the time, Pallas kernels for 6%

profile of v1, /device:TPU:0, one launch (start us, length us, event | category | flops | bytes accessed | tf_op | source)
XLA Modules:
  0.0 331.4 jit_solution(18237116201913241719)
XLA Ops:
  3.0 2.6 pad_maximum_fusion.4
  7.0 3.0 collective-permute-start
  10.0 19.4 %adam.1 = (f32[448,4096]{1,0:T(8,128)}, f32[448,4096]{1,0:T(8,128)}, f32[448,4096]{1,0:T(8,128)}, bf16[448,1024]{1,0:T(8,128)(2,1)}, bf16[448,1024]{1,0:T(8,128)...) custom-call(s32[1]{0:T(128)} %bitcast.y_ref, f32[448,4096]{1,0:T(8,128)} %master_ref.1, ...), custom_call_target="tpu_custom_call" | custom-call | flops 22020096 | bytes 51380224 | tf_op jit(solution)/shard_map/adam/pallas_call | solution.py:47
  35.9 14.5 %collective-permute-done.29 = bf16[2,128,1792]{2,1,0:T(8,128)(2,1)} collective-permute-done((bf16[2,128,1792]{2,1,0:T(8,128)(2,1)}, bf16[2,128,1792]{2,1,0:T(8,128)(2,1)}, u32[]{:S(2)}, u32[]{:S(2)}) %collective-permute-start.29) | collective-permute-done | bytes 917536 | tf_op jit(solution)/shard_map/ppermute | solution.py:89
  53.1 2.9 collective-permute-start.2
  57.8 14.9 %collective-permute-done.11 = bf16[448,1024]{1,0:T(8,128)(2,1)} collective-permute-done((bf16[448,1024]{1,0:T(8,128)(2,1)S(1)}, bf16[448,1024]{1,0:T(8,128)(2,1)}, u32[]{:S(2)}, u32[]{:S(2)}) %collective-permute-start.11) | collective-permute-done | bytes 917536 | tf_op jit(solution)/shard_map/ppermute | solution.py:89
  72.7 3.1 collective-permute-start.3
  77.1 15.3 %collective-permute-done.17 = bf16[448,1024]{1,0:T(8,128)(2,1)} collective-permute-done((bf16[448,1024]{1,0:T(8,128)(2,1)S(1)}, bf16[448,1024]{1,0:T(8,128)(2,1)}, u32[]{:S(2)}, u32[]{:S(2)}) %collective-permute-start.17) | collective-permute-done | bytes 917536 | tf_op jit(solution)/shard_map/ppermute | solution.py:89
  93.8 16.6 %collective-permute-done.23 = bf16[448,1024]{1,0:T(8,128)(2,1)S(1)} collective-permute-done((bf16[448,1024]{1,0:T(8,128)(2,1)S(1)}, bf16[448,1024]{1,0:T(8,128)(2,1)S(1)}, u32[]{:S(2)}, u32[]{:S(2)}) %collective-permute-start.23) | collective-permute-done | bytes 917536 | tf_op jit(solution)/shard_map/ppermute | solution.py:89
  112.0 3.2 collective-permute-start.6
  115.2 5.3 %collective-permute-start.12 = (bf16[2,448,1024]{2,1,0:T(8,128)(2,1)S(1)}, bf16[2,448,1024]{2,1,0:T(8,128)(2,1)S(1)}, u32[]{:S(2)}, u32[]{:S(2)}) collective-permute-start(bf16[2,448,1024]{2,1,0:T(8,128)(2,1)S(1)} %pad_maximum_fusion.7), channel_id=1, source_target_pairs={{0,1},{1,0},{2,3},{3,2},{4,5},{5,4},{6,7},{7,6},{8,9},{9,8},{10,11... | collective-permute-start | bytes 5505032 | tf_op jit(solution)/shard_map/ppermute | solution.py:89
  121.2 2.7 collective-permute-start.32
  123.9 6.9 %collective-permute-done.31 = bf16[128,1792]{1,0:T(8,128)(2,1)S(1)} collective-permute-done((bf16[128,1792]{1,0:T(8,128)(2,1)S(1)}, bf16[128,1792]{1,0:T(8,128)(2,1)S(1)}, u32[]{:S(2)}, u32[]{:S(2)}) %collective-permute-start.31) | collective-permute-done | bytes 458784 | tf_op jit(solution)/shard_map/ppermute | solution.py:89
  131.6 23.3 %collective-permute-done.32 = bf16[128,1792]{1,0:T(8,128)(2,1)S(1)} collective-permute-done((bf16[128,1792]{1,0:T(8,128)(2,1)S(1)}, bf16[128,1792]{1,0:T(8,128)(2,1)S(1)}, u32[]{:S(2)}, u32[]{:S(2)}) %collective-permute-start.32) | collective-permute-done | bytes 458784 | tf_op jit(solution)/shard_map/ppermute | solution.py:89
  190.0 8.9 %collective-permute-done.25 = bf16[512,512]{1,0:T(8,128)(2,1)S(1)} collective-permute-done((bf16[512,512]{1,0:T(8,128)(2,1)S(1)}, bf16[512,512]{1,0:T(8,128)(2,1)S(1)}, u32[]{:S(2)}, u32[]{:S(2)}) %collective-permute-start.25) | collective-permute-done | bytes 524320 | tf_op jit(solution)/shard_map/ppermute | solution.py:89
  199.0 19.2 %collective-permute-start.8 = (bf16[2,128,512]{2,1,0:T(8,128)(2,1)S(1)}, bf16[2,128,512]{2,1,0:T(8,128)(2,1)S(1)}, u32[]{:S(2)}, u32[]{:S(2)}) collective-permute-start(bf16[2,128,512]{2,1,0:T(8,128)(2,1)S(1)} %fusion), channel_id=1, source_target_pairs={{0,8},{1,9},{2,10},{3,11},{4,12},{5,13},{6,14},{7,15},{8,0},{9,1},... | collective-permute-start | bytes 786440 | tf_op jit(solution)/shard_map/ppermute | solution.py:89
  218.4 11.0 %collective-permute-start.14 = (bf16[2,128,512]{2,1,0:T(8,128)(2,1)S(1)}, bf16[2,128,512]{2,1,0:T(8,128)(2,1)S(1)}, u32[]{:S(2)}, u32[]{:S(2)}) collective-permute-start(bf16[2,128,512]{2,1,0:T(8,128)(2,1)S(1)} %fusion.1), channel_id=1, source_target_pairs={{0,8},{1,9},{2,10},{3,11},{4,12},{5,13},{6,14},{7,15},{8,0},{9,1},... | collective-permute-start | bytes 786440 | tf_op jit(solution)/shard_map/ppermute | solution.py:89
  229.6 11.0 %collective-permute-start.20 = (bf16[2,128,512]{2,1,0:T(8,128)(2,1)S(1)}, bf16[2,128,512]{2,1,0:T(8,128)(2,1)S(1)}, u32[]{:S(2)}, u32[]{:S(2)}) collective-permute-start(bf16[2,128,512]{2,1,0:T(8,128)(2,1)S(1)} %fusion.2), channel_id=1, source_target_pairs={{0,8},{1,9},{2,10},{3,11},{4,12},{5,13},{6,14},{7,15},{8,0},{9,1},... | collective-permute-start | bytes 786440 | tf_op jit(solution)/shard_map/ppermute | solution.py:89
  240.9 11.0 %collective-permute-start.26 = (bf16[2,128,512]{2,1,0:T(8,128)(2,1)S(1)}, bf16[2,128,512]{2,1,0:T(8,128)(2,1)S(1)}, u32[]{:S(2)}, u32[]{:S(2)}) collective-permute-start(bf16[2,128,512]{2,1,0:T(8,128)(2,1)S(1)} %fusion.3), channel_id=1, source_target_pairs={{0,8},{1,9},{2,10},{3,11},{4,12},{5,13},{6,14},{7,15},{8,0},{9,1},... | collective-permute-start | bytes 786440 | tf_op jit(solution)/shard_map/ppermute | solution.py:89
  252.0 10.1 %collective-permute-start.35 = (bf16[2,128,512]{2,1,0:T(8,128)(2,1)S(1)}, bf16[2,128,512]{2,1,0:T(8,128)(2,1)S(1)}, u32[]{:S(2)}, u32[]{:S(2)}) collective-permute-start(bf16[2,128,512]{2,1,0:T(8,128)(2,1)S(1)} %fusion.4), channel_id=1, source_target_pairs={{0,8},{1,9},{2,10},{3,11},{4,12},{5,13},{6,14},{7,15},{8,0},{9,1},... | collective-permute-start | bytes 786440 | tf_op jit(solution)/shard_map/ppermute | solution.py:89
  266.7 6.9 %collective-permute-done.35 = bf16[2,128,512]{2,1,0:T(8,128)(2,1)S(1)} collective-permute-done((bf16[2,128,512]{2,1,0:T(8,128)(2,1)S(1)}, bf16[2,128,512]{2,1,0:T(8,128)(2,1)S(1)}, u32[]{:S(2)}, u32[]{:S(2)}) %collective-permute-start.35) | collective-permute-done | bytes 262176 | tf_op jit(solution)/shard_map/ppermute | solution.py:89
  273.8 6.6 %collective-permute-done.39 = bf16[2,128,512]{2,1,0:T(8,128)(2,1)S(1)} collective-permute-done((bf16[2,128,512]{2,1,0:T(8,128)(2,1)S(1)}, bf16[2,128,512]{2,1,0:T(8,128)(2,1)S(1)}, u32[]{:S(2)}, u32[]{:S(2)}) %collective-permute-start.39) | collective-permute-done | bytes 262176 | tf_op jit(solution)/shard_map/ppermute | solution.py:89
  281.0 7.8 %collective-permute-done.43 = bf16[2,128,512]{2,1,0:T(8,128)(2,1)S(1)} collective-permute-done((bf16[2,128,512]{2,1,0:T(8,128)(2,1)S(1)}, bf16[2,128,512]{2,1,0:T(8,128)(2,1)S(1)}, u32[]{:S(2)}, u32[]{:S(2)}) %collective-permute-start.43) | collective-permute-done | bytes 262176 | tf_op jit(solution)/shard_map/ppermute | solution.py:89
  289.0 3.8 %collective-permute-done.47 = bf16[2,128,512]{2,1,0:T(8,128)(2,1)S(1)} collective-permute-done((bf16[2,128,512]{2,1,0:T(8,128)(2,1)S(1)}, bf16[2,128,512]{2,1,0:T(8,128)(2,1)S(1)}, u32[]{:S(2)}, u32[]{:S(2)}) %collective-permute-start.47) | collective-permute-done | bytes 262176 | tf_op jit(solution)/shard_map/ppermute | solution.py:89
  293.0 3.0 collective-permute-start.40
  296.2 7.7 %collective-permute-done.21 = bf16[128,512]{1,0:T(8,128)(2,1)S(1)} collective-permute-done((bf16[128,512]{1,0:T(8,128)(2,1)S(1)}, bf16[128,512]{1,0:T(8,128)(2,1)S(1)}, u32[]{:S(2)}, u32[]{:S(2)}) %collective-permute-start.21) | collective-permute-done | bytes 131104 | tf_op jit(solution)/shard_map/ppermute | solution.py:89
  304.0 2.8 collective-permute-done.27
  306.8 2.8 collective-permute-done.36
  309.6 2.8 collective-permute-done.40
  312.4 4.2 %collective-permute-done.44 = bf16[128,512]{1,0:T(8,128)(2,1)S(1)} collective-permute-done((bf16[128,512]{1,0:T(8,128)(2,1)S(1)}, bf16[128,512]{1,0:T(8,128)(2,1)S(1)}, u32[]{:S(2)}, u32[]{:S(2)}) %collective-permute-start.44) | collective-permute-done | bytes 131104 | tf_op jit(solution)/shard_map/ppermute | solution.py:89
  316.6 2.6 collective-permute-done.48
  321.5 9.9 %maximum_maximum_fusion = bf16[512,1024]{1,0:T(8,128)(2,1)} fusion(bf16[128,256]{1,0:T(8,128)(2,1)S(1)} %get-tuple-element.72, bf16[128,256]{1,0:T(8,128)(2,1)S(1)} %get-tuple-element.70, bf16[128,256]{1,0:T(8,128)(2,1)S(1)} %get-tuple-element.68, bf16[128,256]{1,0:T(8,128)(2,1)S(1)} %get-tuple-element.66, bf16[128,256]{1,0:T(8,128)(2,1)S(1)} %get-tuple-element.64, ...), kind=kLoop, calls=%fused_computation.36 | loop fusion | flops 16777216 | bytes 2097152 | tf_op jit(solution)/shard_map/concatenate | solution.py:144
  (197 shorter events, 64.2 us)
Async XLA Ops:
  7.0 28.7 %collective-permute-start = (bf16[2,128,1792]{2,1,0:T(8,128)(2,1)}, bf16[2,128,1792]{2,1,0:T(8,128)(2,1)}, u32[]{:S(2)}, u32[]{:S(2)}) collective-permute-start(bf16[2,128,1792]{2,1,0:T(8,128)(2,1)} %get-tuple-element.36), channel_id=1, source_target_pairs={{0,2},{1,3},{2,0},{3,1},{4,6},{5,7},{6,4},{7,5},{8,10},{9,11},{10,... | collective-permute-start | bytes 2752520 | tf_op jit(solution)/shard_map/ppermute | solution.py:89
  10.0 40.3 %collective-permute-start.29 = (bf16[2,128,1792]{2,1,0:T(8,128)(2,1)}, bf16[2,128,1792]{2,1,0:T(8,128)(2,1)}, u32[]{:S(2)}, u32[]{:S(2)}) collective-permute-start(bf16[2,128,1792]{2,1,0:T(8,128)(2,1)} %get-tuple-element.37), channel_id=1, source_target_pairs={{0,2},{1,3},{2,0},{3,1},{4,6},{5,7},{6,4},{7,5},{8,10},{9,11},{10,... | collective-permute-start | bytes 2752520 | tf_op jit(solution)/shard_map/ppermute | solution.py:89
  29.5 23.6 %collective-permute-start.5 = (bf16[448,1024]{1,0:T(8,128)(2,1)}, bf16[448,1024]{1,0:T(8,128)(2,1)}, u32[]{:S(2)}, u32[]{:S(2)}) collective-permute-start(bf16[448,1024]{1,0:T(8,128)(2,1)} %get-tuple-element.14), channel_id=1, source_target_pairs={{0,4},{1,5},{2,6},{3,7},{4,0},{5,1},{6,2},{7,3},{8,12},{9,13},{10,... | collective-permute-start | bytes 2752520 | tf_op jit(solution)/shard_map/ppermute | solution.py:89
  31.4 41.3 %collective-permute-start.11 = (bf16[448,1024]{1,0:T(8,128)(2,1)S(1)}, bf16[448,1024]{1,0:T(8,128)(2,1)}, u32[]{:S(2)}, u32[]{:S(2)}) collective-permute-start(bf16[448,1024]{1,0:T(8,128)(2,1)S(1)} %get-tuple-element.15), channel_id=1, source_target_pairs={{0,4},{1,5},{2,6},{3,7},{4,0},{5,1},{6,2},{7,3},{8,12},{9,13},{10,... | collective-permute-start | bytes 2752520 | tf_op jit(solution)/shard_map/ppermute | solution.py:89
  31.5 60.9 %collective-permute-start.17 = (bf16[448,1024]{1,0:T(8,128)(2,1)S(1)}, bf16[448,1024]{1,0:T(8,128)(2,1)}, u32[]{:S(2)}, u32[]{:S(2)}) collective-permute-start(bf16[448,1024]{1,0:T(8,128)(2,1)S(1)} %get-tuple-element.16), channel_id=1, source_target_pairs={{0,4},{1,5},{2,6},{3,7},{4,0},{5,1},{6,2},{7,3},{8,12},{9,13},{10,... | collective-permute-start | bytes 2752520 | tf_op jit(solution)/shard_map/ppermute | solution.py:89
  35.7 74.8 %collective-permute-start.23 = (bf16[448,1024]{1,0:T(8,128)(2,1)S(1)}, bf16[448,1024]{1,0:T(8,128)(2,1)S(1)}, u32[]{:S(2)}, u32[]{:S(2)}) collective-permute-start(bf16[448,1024]{1,0:T(8,128)(2,1)S(1)} %get-tuple-element.17), channel_id=1, source_target_pairs={{0,4},{1,5},{2,6},{3,7},{4,0},{5,1},{6,2},{7,3},{8,12},{9,13},{10,... | collective-permute-start | bytes 2752520 | tf_op jit(solution)/shard_map/ppermute | solution.py:89
  52.1 59.9 %collective-permute-start.1 = (bf16[128,1792]{1,0:T(8,128)(2,1)S(1)}, bf16[128,1792]{1,0:T(8,128)(2,1)S(1)}, u32[]{:S(2)}, u32[]{:S(2)}) collective-permute-start(bf16[128,1792]{1,0:T(8,128)(2,1)S(1)} %get-tuple-element.52), channel_id=1, source_target_pairs={{0,0},{1,8},{2,2},{3,10},{4,4},{5,12},{6,6},{7,14},{8,1},{9,9},{10... | collective-permute-start | bytes 1376264 | tf_op jit(solution)/shard_map/ppermute | solution.py:89
  53.1 67.4 %collective-permute-start.2 = (bf16[128,1792]{1,0:T(8,128)(2,1)S(1)}, bf16[128,1792]{1,0:T(8,128)(2,1)S(1)}, u32[]{:S(2)}, u32[]{:S(2)}) collective-permute-start(bf16[128,1792]{1,0:T(8,128)(2,1)S(1)} %get-tuple-element.51), channel_id=1, source_target_pairs={{0,1},{1,9},{2,3},{3,11},{4,5},{5,13},{6,7},{7,15},{8,0},{9,8},{10... | collective-permute-start | bytes 1376264 | tf_op jit(solution)/shard_map/ppermute | solution.py:89
  72.7 47.9 %collective-permute-start.3 = (bf16[128,1792]{1,0:T(8,128)(2,1)S(1)}, bf16[128,1792]{1,0:T(8,128)(2,1)S(1)}, u32[]{:S(2)}, u32[]{:S(2)}) collective-permute-start(bf16[128,1792]{1,0:T(8,128)(2,1)S(1)} %get-tuple-element.50), channel_id=1, source_target_pairs={{0,16},{1,24},{2,18},{3,26},{4,20},{5,28},{6,22},{7,30},{8,17},{9,... | collective-permute-start | bytes 1376264 | tf_op jit(solution)/shard_map/ppermute | solution.py:89
  92.4 28.8 %collective-permute-start.4 = (bf16[128,1792]{1,0:T(8,128)(2,1)S(1)}, bf16[128,1792]{1,0:T(8,128)(2,1)S(1)}, u32[]{:S(2)}, u32[]{:S(2)}) collective-permute-start(bf16[128,1792]{1,0:T(8,128)(2,1)S(1)} %get-tuple-element.49), channel_id=1, source_target_pairs={{0,17},{1,25},{2,19},{3,27},{4,21},{5,29},{6,23},{7,31},{8,16},{9,... | collective-permute-start | bytes 1376264 | tf_op jit(solution)/shard_map/ppermute | solution.py:89
  112.0 43.0 %collective-permute-start.6 = (bf16[2,448,1024]{2,1,0:T(8,128)(2,1)S(1)}, bf16[2,448,1024]{2,1,0:T(8,128)(2,1)S(1)}, u32[]{:S(2)}, u32[]{:S(2)}) collective-permute-start(bf16[2,448,1024]{2,1,0:T(8,128)(2,1)S(1)} %pad_maximum_fusion.6), channel_id=1, source_target_pairs={{0,1},{1,0},{2,3},{3,2},{4,5},{5,4},{6,7},{7,6},{8,9},{9,8},{10,11... | collective-permute-start | bytes 5505032 | tf_op jit(solution)/shard_map/ppermute | solution.py:89
  115.2 45.5 %collective-permute-start.12 = (bf16[2,448,1024]{2,1,0:T(8,128)(2,1)S(1)}, bf16[2,448,1024]{2,1,0:T(8,128)(2,1)S(1)}, u32[]{:S(2)}, u32[]{:S(2)}) collective-permute-start(bf16[2,448,1024]{2,1,0:T(8,128)(2,1)S(1)} %pad_maximum_fusion.7), channel_id=1, source_target_pairs={{0,1},{1,0},{2,3},{3,2},{4,5},{5,4},{6,7},{7,6},{8,9},{9,8},{10,11... | collective-permute-start | bytes 5505032 | tf_op jit(solution)/shard_map/ppermute | solution.py:89
  120.5 43.9 %collective-permute-start.18 = (bf16[2,448,1024]{2,1,0:T(8,128)(2,1)S(1)}, bf16[2,448,1024]{2,1,0:T(8,128)(2,1)S(1)}, u32[]{:S(2)}, u32[]{:S(2)}) collective-permute-start(bf16[2,448,1024]{2,1,0:T(8,128)(2,1)S(1)} %pad_maximum_fusion.8), channel_id=1, source_target_pairs={{0,1},{1,0},{2,3},{3,2},{4,5},{5,4},{6,7},{7,6},{8,9},{9,8},{10,11... | collective-permute-start | bytes 5505032 | tf_op jit(solution)/shard_map/ppermute | solution.py:89
  121.2 33.7 %collective-permute-start.32 = (bf16[128,1792]{1,0:T(8,128)(2,1)S(1)}, bf16[128,1792]{1,0:T(8,128)(2,1)S(1)}, u32[]{:S(2)}, u32[]{:S(2)}) collective-permute-start(bf16[128,1792]{1,0:T(8,128)(2,1)S(1)} %get-tuple-element.54), channel_id=1, source_target_pairs={{0,16},{1,24},{2,18},{3,26},{4,20},{5,28},{6,22},{7,30},{8,17},{9,... | collective-permute-start | bytes 1376264 | tf_op jit(solution)/shard_map/ppermute | solution.py:89
  130.8 24.1 %collective-permute-start.33 = (bf16[128,1792]{1,0:T(8,128)(2,1)S(1)}, bf16[128,1792]{1,0:T(8,128)(2,1)S(1)}, u32[]{:S(2)}, u32[]{:S(2)}) collective-permute-start(bf16[128,1792]{1,0:T(8,128)(2,1)S(1)} %get-tuple-element.53), channel_id=1, source_target_pairs={{0,17},{1,25},{2,19},{3,27},{4,21},{5,29},{6,23},{7,31},{8,16},{9,... | collective-permute-start | bytes 1376264 | tf_op jit(solution)/shard_map/ppermute | solution.py:89
  154.9 22.9 %collective-permute-start.24 = (bf16[2,448,1024]{2,1,0:T(8,128)(2,1)S(1)}, bf16[2,448,1024]{2,1,0:T(8,128)(2,1)S(1)}, u32[]{:S(2)}, u32[]{:S(2)}) collective-permute-start(bf16[2,448,1024]{2,1,0:T(8,128)(2,1)S(1)} %pad_maximum_fusion.9), channel_id=1, source_target_pairs={{0,1},{1,0},{2,3},{3,2},{4,5},{5,4},{6,7},{7,6},{8,9},{9,8},{10,11... | collective-permute-start | bytes 5505032 | tf_op jit(solution)/shard_map/ppermute | solution.py:89
  159.1 27.5 %collective-permute-start.7 = (bf16[512,512]{1,0:T(8,128)(2,1)S(1)}, bf16[512,512]{1,0:T(8,128)(2,1)S(1)}, u32[]{:S(2)}, u32[]{:S(2)}) collective-permute-start(bf16[512,512]{1,0:T(8,128)(2,1)S(1)} %slice.735), channel_id=1, source_target_pairs={{0,2},{1,3},{2,0},{3,1},{4,6},{5,7},{6,4},{7,5},{8,10},{9,11},{10,... | collective-permute-start | bytes 1572872 | tf_op jit(solution)/shard_map/ppermute | solution.py:89
  163.8 23.6 %collective-permute-start.13 = (bf16[512,512]{1,0:T(8,128)(2,1)S(1)}, bf16[512,512]{1,0:T(8,128)(2,1)S(1)}, u32[]{:S(2)}, u32[]{:S(2)}) collective-permute-start(bf16[512,512]{1,0:T(8,128)(2,1)S(1)} %slice.734), channel_id=1, source_target_pairs={{0,2},{1,3},{2,0},{3,1},{4,6},{5,7},{6,4},{7,5},{8,10},{9,11},{10,... | collective-permute-start | bytes 1572872 | tf_op jit(solution)/shard_map/ppermute | solution.py:89
  182.7 35.7 %collective-permute-start.34 = (bf16[512,512]{1,0:T(8,128)(2,1)S(1)}, bf16[512,512]{1,0:T(8,128)(2,1)S(1)}, u32[]{:S(2)}, u32[]{:S(2)}) collective-permute-start(bf16[512,512]{1,0:T(8,128)(2,1)S(1)} %slice.731), channel_id=1, source_target_pairs={{0,2},{1,3},{2,0},{3,1},{4,6},{5,7},{6,4},{7,5},{8,10},{9,11},{10,... | collective-permute-start | bytes 1572872 | tf_op jit(solution)/shard_map/ppermute | solution.py:89
  186.6 43.1 %collective-permute-start.38 = (bf16[512,512]{1,0:T(8,128)(2,1)S(1)}, bf16[512,512]{1,0:T(8,128)(2,1)S(1)}, u32[]{:S(2)}, u32[]{:S(2)}) collective-permute-start(bf16[512,512]{1,0:T(8,128)(2,1)S(1)} %slice.730), channel_id=1, source_target_pairs={{0,2},{1,3},{2,0},{3,1},{4,6},{5,7},{6,4},{7,5},{8,10},{9,11},{10,... | collective-permute-start | bytes 1572872 | tf_op jit(solution)/shard_map/ppermute | solution.py:89
  187.4 53.5 %collective-permute-start.42 = (bf16[512,512]{1,0:T(8,128)(2,1)S(1)}, bf16[512,512]{1,0:T(8,128)(2,1)S(1)}, u32[]{:S(2)}, u32[]{:S(2)}) collective-permute-start(bf16[512,512]{1,0:T(8,128)(2,1)S(1)} %slice.729), channel_id=1, source_target_pairs={{0,2},{1,3},{2,0},{3,1},{4,6},{5,7},{6,4},{7,5},{8,10},{9,11},{10,... | collective-permute-start | bytes 1572872 | tf_op jit(solution)/shard_map/ppermute | solution.py:89
  189.2 62.8 %collective-permute-start.46 = (bf16[512,512]{1,0:T(8,128)(2,1)S(1)}, bf16[512,512]{1,0:T(8,128)(2,1)S(1)}, u32[]{:S(2)}, u32[]{:S(2)}) collective-permute-start(bf16[512,512]{1,0:T(8,128)(2,1)S(1)} %slice.728), channel_id=1, source_target_pairs={{0,2},{1,3},{2,0},{3,1},{4,6},{5,7},{6,4},{7,5},{8,10},{9,11},{10,... | collective-permute-start | bytes 1572872 | tf_op jit(solution)/shard_map/ppermute | solution.py:89
  199.0 63.5 %collective-permute-start.8 = (bf16[2,128,512]{2,1,0:T(8,128)(2,1)S(1)}, bf16[2,128,512]{2,1,0:T(8,128)(2,1)S(1)}, u32[]{:S(2)}, u32[]{:S(2)}) collective-permute-start(bf16[2,128,512]{2,1,0:T(8,128)(2,1)S(1)} %fusion), channel_id=1, source_target_pairs={{0,8},{1,9},{2,10},{3,11},{4,12},{5,13},{6,14},{7,15},{8,0},{9,1},... | collective-permute-start | bytes 786440 | tf_op jit(solution)/shard_map/ppermute | solution.py:89
  218.4 44.3 %collective-permute-start.14 = (bf16[2,128,512]{2,1,0:T(8,128)(2,1)S(1)}, bf16[2,128,512]{2,1,0:T(8,128)(2,1)S(1)}, u32[]{:S(2)}, u32[]{:S(2)}) collective-permute-start(bf16[2,128,512]{2,1,0:T(8,128)(2,1)S(1)} %fusion.1), channel_id=1, source_target_pairs={{0,8},{1,9},{2,10},{3,11},{4,12},{5,13},{6,14},{7,15},{8,0},{9,1},... | collective-permute-start | bytes 786440 | tf_op jit(solution)/shard_map/ppermute | solution.py:89
  229.6 35.3 %collective-permute-start.20 = (bf16[2,128,512]{2,1,0:T(8,128)(2,1)S(1)}, bf16[2,128,512]{2,1,0:T(8,128)(2,1)S(1)}, u32[]{:S(2)}, u32[]{:S(2)}) collective-permute-start(bf16[2,128,512]{2,1,0:T(8,128)(2,1)S(1)} %fusion.2), channel_id=1, source_target_pairs={{0,8},{1,9},{2,10},{3,11},{4,12},{5,13},{6,14},{7,15},{8,0},{9,1},... | collective-permute-start | bytes 786440 | tf_op jit(solution)/shard_map/ppermute | solution.py:89
  240.9 24.3 %collective-permute-start.26 = (bf16[2,128,512]{2,1,0:T(8,128)(2,1)S(1)}, bf16[2,128,512]{2,1,0:T(8,128)(2,1)S(1)}, u32[]{:S(2)}, u32[]{:S(2)}) collective-permute-start(bf16[2,128,512]{2,1,0:T(8,128)(2,1)S(1)} %fusion.3), channel_id=1, source_target_pairs={{0,8},{1,9},{2,10},{3,11},{4,12},{5,13},{6,14},{7,15},{8,0},{9,1},... | collective-permute-start | bytes 786440 | tf_op jit(solution)/shard_map/ppermute | solution.py:89
  252.0 21.5 %collective-permute-start.35 = (bf16[2,128,512]{2,1,0:T(8,128)(2,1)S(1)}, bf16[2,128,512]{2,1,0:T(8,128)(2,1)S(1)}, u32[]{:S(2)}, u32[]{:S(2)}) collective-permute-start(bf16[2,128,512]{2,1,0:T(8,128)(2,1)S(1)} %fusion.4), channel_id=1, source_target_pairs={{0,8},{1,9},{2,10},{3,11},{4,12},{5,13},{6,14},{7,15},{8,0},{9,1},... | collective-permute-start | bytes 786440 | tf_op jit(solution)/shard_map/ppermute | solution.py:89
  262.7 26.1 %collective-permute-start.43 = (bf16[2,128,512]{2,1,0:T(8,128)(2,1)S(1)}, bf16[2,128,512]{2,1,0:T(8,128)(2,1)S(1)}, u32[]{:S(2)}, u32[]{:S(2)}) collective-permute-start(bf16[2,128,512]{2,1,0:T(8,128)(2,1)S(1)} %fusion.6), channel_id=1, source_target_pairs={{0,8},{1,9},{2,10},{3,11},{4,12},{5,13},{6,14},{7,15},{8,0},{9,1},... | collective-permute-start | bytes 786440 | tf_op jit(solution)/shard_map/ppermute | solution.py:89
  264.9 27.9 %collective-permute-start.47 = (bf16[2,128,512]{2,1,0:T(8,128)(2,1)S(1)}, bf16[2,128,512]{2,1,0:T(8,128)(2,1)S(1)}, u32[]{:S(2)}, u32[]{:S(2)}) collective-permute-start(bf16[2,128,512]{2,1,0:T(8,128)(2,1)S(1)} %fusion.7), channel_id=1, source_target_pairs={{0,8},{1,9},{2,10},{3,11},{4,12},{5,13},{6,14},{7,15},{8,0},{9,1},... | collective-permute-start | bytes 786440 | tf_op jit(solution)/shard_map/ppermute | solution.py:89
  265.2 27.8 %collective-permute-start.9 = (bf16[128,512]{1,0:T(8,128)(2,1)S(1)}, bf16[128,512]{1,0:T(8,128)(2,1)S(1)}, u32[]{:S(2)}, u32[]{:S(2)}) collective-permute-start(bf16[128,512]{1,0:T(8,128)(2,1)S(1)} %fusion.24), channel_id=1, source_target_pairs={{0,16},{1,17},{2,18},{3,19},{4,20},{5,21},{6,22},{7,23},{8,24},{9,... | collective-permute-start | bytes 393224 | tf_op jit(solution)/shard_map/ppermute | solution.py:89
  273.6 22.5 %collective-permute-start.15 = (bf16[128,512]{1,0:T(8,128)(2,1)S(1)}, bf16[128,512]{1,0:T(8,128)(2,1)S(1)}, u32[]{:S(2)}, u32[]{:S(2)}) collective-permute-start(bf16[128,512]{1,0:T(8,128)(2,1)S(1)} %fusion.25), channel_id=1, source_target_pairs={{0,16},{1,17},{2,18},{3,19},{4,20},{5,21},{6,22},{7,23},{8,24},{9,... | collective-permute-start | bytes 393224 | tf_op jit(solution)/shard_map/ppermute | solution.py:89
  280.3 23.6 %collective-permute-start.21 = (bf16[128,512]{1,0:T(8,128)(2,1)S(1)}, bf16[128,512]{1,0:T(8,128)(2,1)S(1)}, u32[]{:S(2)}, u32[]{:S(2)}) collective-permute-start(bf16[128,512]{1,0:T(8,128)(2,1)S(1)} %fusion.26), channel_id=1, source_target_pairs={{0,16},{1,17},{2,18},{3,19},{4,20},{5,21},{6,22},{7,23},{8,24},{9,... | collective-permute-start | bytes 393224 | tf_op jit(solution)/shard_map/ppermute | solution.py:89
  (27 other events, 256.7 us)

commit v2 on v1

v2 whole, which is shorter than its diff:
```python
import jax
import jax.numpy as jnp
from jax import lax
from jax.experimental import pallas as pl
from jax.experimental.pallas import tpu as pltpu
from jax.sharding import PartitionSpec as P

AXES = ("fsdp", "tp")
ROW_CHUNKS = 2
COL_CHUNKS = 2


def adam_kernel(where_ref, master_ref, one_ref, two_ref, grad_ref, *refs):
    new_master_ref, new_one_ref, new_two_ref, weight_ref = refs[-4:]
    grad = grad_ref[...].astype(jnp.float32)
    new_one = 0.9 * one_ref[...] + 0.1 * grad
    new_two = 0.95 * two_ref[...] + 0.05 * grad * grad
    new_master = master_ref[...] - 0.001 * new_one / (jnp.sqrt(new_two) + 1e-08)
    new_one_ref[...] = new_one
    new_two_ref[...] = new_two
    new_master_ref[...] = new_master
    weight_ref[...] = new_master.astype(jnp.bfloat16)


def adam(where, q, args, previous):
    rows, cols = args[0].shape
    width = cols // 4 // COL_CHUNKS
    step = max(s for s in range(16, 225, 16) if rows % s == 0)
    block = pl.BlockSpec((step, width), lambda i, j, w: (i, j * COL_CHUNKS + q))
    piece = pl.BlockSpec((step, width), lambda i, j, w: (i, 2 * ((j % 2) ^ w[1]) + ((j // 2) ^ w[0])))
    full = jax.ShapeDtypeStruct((rows, cols), jnp.float32)
    size = rows * cols // COL_CHUNKS
    return pl.pallas_call(
        adam_kernel,
        grid_spec=pltpu.PrefetchScalarGridSpec(
            num_scalar_prefetch=1,
            grid=(rows // step, 4),
            in_specs=[block] * 4 + [pl.BlockSpec(memory_space=pl.ANY)] * len(previous),
            out_specs=[block, block, block, piece],
        ),
        out_shape=[full, full, full, jax.ShapeDtypeStruct((rows, cols // COL_CHUNKS), jnp.bfloat16)],
        input_output_aliases={5 + i: i for i in range(len(previous))},
        compiler_params=pltpu.CompilerParams(vmem_limit_bytes=32 * 1024 * 1024),
        cost_estimate=pl.CostEstimate(flops=size, bytes_accessed=size, transcendentals=0),
        name="adam",
    )(where, *args, *previous)


def swap_if(flag, low, high):
    return jnp.where(flag, high, low), jnp.where(flag, low, high)


def by_distance(parts, index):
    count = len(parts)
    if count == 1:
        return parts
    half = count // 2
    flag = (index & half) != 0
    pairs = [swap_if(flag, a, b) for a, b in zip(parts[:half], parts[half:])]
    return by_distance([p[0] for p in pairs], index) + by_distance([p[1] for p in pairs], index)


def local(master, moment_one, moment_two, gradient, hidden_act):
    fsdp, tp = lax.axis_size("fsdp"), lax.axis_size("tp")
    xs = fsdp // tp
    f, t = lax.axis_index("fsdp"), lax.axis_index("tp")
    z, x, y, c = f // xs, f % xs, t // 2, t % 2

    def permute(value, to):
        pairs = []
        for zi in range(tp):
            for xi in range(xs):
                for yi in range(2):
                    for ci in range(2):
                        zo, xo, yo, co = to(zi, xi, yi, ci)
                        pairs.append(((zi * xs + xi) * tp + 2 * yi + ci, (zo * xs + xo) * tp + 2 * yo + co))
        return lax.ppermute(value, AXES, pairs)

    rows = hidden_act.shape[0]
    depth = hidden_act.shape[1] // 2
    span = depth // xs // 2
    columns = []
    for s in range(2):
        cores = []
        for k in range(2):
            at = [(4 * i + 2 * s + k) * span for i in range(xs)]
            cores += by_distance([hidden_act[:, a : a + span] for a in at], x)
        columns.append(jnp.concatenate(cores, axis=1))
    own, other = swap_if(y != 0, *columns)
    part_rows = rows // ROW_CHUNKS
    acts = []
    for m in range(ROW_CHUNKS):
        mine = own[m * part_rows : (m + 1) * part_rows]
        theirs = permute(other[m * part_rows : (m + 1) * part_rows], lambda z, x, y, c: (z, x, 1 - y, c))
        first, second = swap_if(((z // 2) ^ y) != 0, mine, theirs)
        got = [
            permute(data, lambda z, x, y, c: (2 * ((z // 2) ^ a) + c, x, y, z % 2))
            for a, data in enumerate((first, second))
        ]
        got = jnp.stack(got)
        also = permute(got, lambda z, x, y, c: (z, x, y, 1 - c))
        near, far = swap_if((c ^ (z % 2)) != 0, got, also)
        acts.append(jnp.stack([near, far], axis=1).reshape(4 * part_rows, depth))

    where = jnp.stack([y, c]).astype(jnp.int32)
    updated = []
    tables = []
    for q in range(COL_CHUNKS):
        *updated, piece = adam(where, q, (master, moment_one, moment_two, gradient), updated)
        parts = [piece] + [permute(piece, lambda z, x, y, c: (z, x ^ d, y, c)) for d in range(1, xs)]
        half = piece.shape[1] // 2
        here = jnp.concatenate([p[:, :half] for p in parts], axis=0)
        there = jnp.concatenate([p[:, half:] for p in parts], axis=0)
        there = permute(there, lambda z, x, y, c: (z, x, y, 1 - c))
        zero, one = swap_if(c != 0, here, there)
        tables.append(jnp.concatenate([zero, one], axis=0))

    blocks = []
    for m in range(ROW_CHUNKS):
        line = []
        for table in tables:
            total = jnp.dot(acts[m], table, preferred_element_type=jnp.float32)
            half = table.shape[1] // 2
            back = permute(total[:, half:].astype(jnp.bfloat16), lambda z, x, y, c: (z, x, 1 - y, c))
            total = (total[:, :half] + back).reshape(2, 2, part_rows, half)
            back = permute(total[:, 1].astype(jnp.bfloat16), lambda z, x, y, c: (z ^ 1, x, y, c))
            total = total[:, 0] + back
            back = permute(total[1].astype(jnp.bfloat16), lambda z, x, y, c: (z ^ 2, x, y, c))
            line.append((total[0] + back).astype(jnp.bfloat16))
        blocks.append(jnp.concatenate(line, axis=1))
    decoded = jnp.concatenate(blocks, axis=0)
    return (*updated, decoded)


def solution(mesh):
    placed = (
        P(("fsdp", "tp"), None),
        P(("fsdp", "tp"), None),
        P(("fsdp", "tp"), None),
        P(("fsdp", "tp"), None),
        P("fsdp", "tp"),
    )
    return jax.shard_map(
        local,
        mesh=mesh,
        in_specs=placed,
        out_specs=(
            P(("fsdp", "tp"), None),
            P(("fsdp", "tp"), None),
            P(("fsdp", "tp"), None),
            P("fsdp", "tp"),
        ),
        check_vma=False,
    )
```

time: 333 us -> 329 us (0.988)
  starting transfers between devices: 106 us -> 32.5 us
  waiting for transfers between devices: 149 us -> 208 us
  local copies, waits for them, and re-layouts: 10.9 us -> 24.1 us
    ppermute x50 -> x24, starting transfers between devices: 106 us -> 32.5 us  [permute(): return lax.ppermute(value, AXES, pairs)]
    ppermute x50 -> x24, waiting for transfers between devices: 149 us -> 208 us  [permute(): return lax.ppermute(value, AXES, pairs)]
    select_n x21 -> x4, other arithmetic: 2.72 us -> 14.5 us  [swap_if(): return (jnp.where(flag, high, low), jnp.where(flag, low, high))]
    concatenate x2 -> x3, other arithmetic: 12.6 us -> 3.97 us  [the longest x2 2.84 us: local(): there = jnp.concatenate([p[:, half:] for p in parts], axis=0)]
    concatenate x2, local copies, waits for them, and re-layouts: 0.06 us -> 6.65 us  [local(): columns.append(jnp.concatenate(cores, axis=1))]
    slice x1 -> x5, local copies, waits for them, and re-layouts: 2.32 us -> 7.89 us  [the longest x4 6.85 us: local(): here = jnp.concatenate([p[:, :half] for p in parts], axis=0)]
    unnamed x24 -> x18, local copies, waits for them, and re-layouts: 3.69 us -> 8.25 us
    pallas_call x1 -> x2, Pallas kernels: 19.4 us -> 17.9 us  [adam(): pl.pallas_call(adam_kernel, grid_spec=pltpu.PrefetchScalarGridSpec(num_sc...]
  transfers between devices with their start and end apart: 50 -> 24, of which waited for: 21 -> 12; matrix products, arithmetic and copies ran while one was open for 11% -> 13% of each run, Pallas kernels for 6% -> 5%
where the time goes in v2:
time: 329 us; the launch traced here: 328 us
  waiting for transfers between devices  208 us (63%)
  starting transfers between devices  32.5 us (10%)
  other arithmetic  28.5 us (9%)
  local copies, waits for them, and re-layouts  24.1 us (7%)
  Pallas kernels  17.9 us (5%)
  matrix products  15.8 us (5%)
    ppermute x24, waiting for transfers between devices, permute(): return lax.ppermute(value, AXES, pairs)  208 us
    ppermute x24, starting transfers between devices, permute(): return lax.ppermute(value, AXES, pairs)  32.5 us
    pallas_call x2, Pallas kernels, adam(): pl.pallas_call(adam_kernel, grid_spec=pltpu.PrefetchScalarGridSpec(num_sc...  17.9 us
    dot_general x4, matrix products, local(): total = jnp.dot(acts[m], table, preferred_element_type=jnp.float32)  15.8 us
    select_n x4, other arithmetic, swap_if(): return (jnp.where(flag, high, low), jnp.where(flag, low, high))  14.5 us
    unnamed x18, local copies, waits for them, and re-layouts  8.25 us
    slice x4, local copies, waits for them, and re-layouts, local(): here = jnp.concatenate([p[:, :half] for p in parts], axis=0)  6.85 us
    concatenate x2, local copies, waits for them, and re-layouts, local(): columns.append(jnp.concatenate(cores, axis=1))  6.65 us
  transfers between devices with their start and end apart: 24, of which 12 were waited for; matrix products, arithmetic and copies ran while one was open for 13% of the time, Pallas kernels for 5%

profile of v2, /device:TPU:0, one launch (start us, length us, event | category | flops | bytes accessed | tf_op | source)
XLA Modules:
  0.0 327.9 jit_solution(2416412471193525132)
XLA Ops:
  0.7 4.5 %broadcast_select_fusion.10 = (bf16[512,448]{1,0:T(8,128)(2,1)}, bf16[512,448]{1,0:T(8,128)(2,1)S(1)}, bf16[512,448]{1,0:T(8,128)(2,1)S(1)}, bf16[512,448]{1,0:T...) fusion(pred[]{:T(512)S(6)} %ne.62, ...), kind=kLoop, calls=%fused_computation.69 | loop fusion | flops 1835008 | bytes 7340033 | tf_op jit(solution)/shard_map/jit(_where)/select_n | solution.py:50
  5.1 2.9 concatenate.34
  8.0 3.8 %concatenate.33 = bf16[512,1792]{1,0:T(8,128)(2,1)} concatenate(bf16[512,448]{1,0:T(8,128)(2,1)} %get-tuple-element.37, bf16[512,448]{1,0:T(8,128)(2,1)S(1)} %get-tuple-element.31, bf16[512,448]{1,0:T(8,128)(2,1)S(1)} %get-tuple-element.32, bf16[512,448]{1,0:T(8,128)(2,1)S(1)} %get-tuple-element.33), dimensions={1} | concatenate | bytes 3670016 | tf_op jit(solution)/shard_map/concatenate | solution.py:88
  11.8 3.0 broadcast_select_fusion.4
  15.8 3.0 collective-permute-start
  18.9 3.1 copy-done
  22.0 3.1 copy-done.1
  27.1 8.8 %adam.2 = (f32[448,4096]{1,0:T(8,128)}, f32[448,4096]{1,0:T(8,128)}, f32[448,4096]{1,0:T(8,128)}, bf16[448,2048]{1,0:T(8,128)(2,1)S(1)}) custom-call(s32[2]{0:T(128)S(1)} %pad_add_fusion.where_ref, f32[448,4096]{1,0:T(8,128)S(1)} %copy-done, f32[448,4096]{1,0:T(8,128)S(1)} %copy-done.1, f32[448,4096]{1,0:T(8,128)} %two_ref.3, bf16[448,4096]{1,0:T(8,128)(2,1)S(1)} %copy-done.2), custom_call_target="tpu_custom_call" | custom-call | flops 917504 | bytes 917504 | tf_op jit(solution)/shard_map/adam/pallas_call | solution.py:33
  36.0 9.1 %adam.3 = (f32[448,4096]{1,0:T(8,128)}, f32[448,4096]{1,0:T(8,128)}, f32[448,4096]{1,0:T(8,128)}, bf16[448,2048]{1,0:T(8,128)(2,1)}) custom-call(s32[2]{0:T(128)S(1)} %pad_add_fusion.where_ref, f32[448,4096]{1,0:T(8,128)S(1)} %copy-done, f32[448,4096]{1,0:T(8,128)S(1)} %copy-done.1, ...), custom_call_target="tpu_custom_call", output_to_operand_aliasing={{0}: (5, {}), {1}: (6, {}), {2}: (7, {})} | custom-call | flops 917504 | bytes 917504 | tf_op jit(solution)/shard_map/adam/pallas_call | solution.py:33
  47.1 12.0 %collective-permute-done.14 = bf16[256,1792]{1,0:T(8,128)(2,1)} collective-permute-done((bf16[256,1792]{1,0:T(8,128)(2,1)S(1)}, bf16[256,1792]{1,0:T(8,128)(2,1)}, u32[]{:S(2)}, u32[]{:S(2)}) %collective-permute-start.14) | collective-permute-done | bytes 917536 | tf_op jit(solution)/shard_map/ppermute | solution.py:77
  59.1 3.5 %broadcast_select_fusion.9 = (bf16[256,1792]{1,0:T(8,128)(2,1)}, bf16[256,1792]{1,0:T(8,128)(2,1)}, bf16[256,1792]{1,0:T(8,128)(2,1)S(1)}, bf16[256,1792]{1,0:T(8,128)(2,1)S(1)}) fusion(bf16[256,1792]{1,0:T(8,128)(2,1)} %collective-permute-done, pred[]{:T(512)S(6)} %ne.60, bf16[512,1792]{1,0:T(8,128)(2,1)} %get-tuple-element.28, ...), kind=kLoop, calls=%fused_computation.48 | loop fusion | flops 1835008 | bytes 7340033 | tf_op jit(solution)/shard_map/jit(_where)/select_n | solution.py:50
  62.7 2.8 collective-permute-start.16
  68.9 36.8 %collective-permute-done.16 = bf16[256,1792]{1,0:T(8,128)(2,1)S(1)} collective-permute-done((bf16[256,1792]{1,0:T(8,128)(2,1)S(1)}, bf16[256,1792]{1,0:T(8,128)(2,1)S(1)}, u32[]{:S(2)}, u32[]{:S(2)}) %collective-permute-start.16) | collective-permute-done | bytes 917536 | tf_op jit(solution)/shard_map/ppermute | solution.py:77
  111.7 14.4 %collective-permute-done.4 = bf16[448,2048]{1,0:T(8,128)(2,1)} collective-permute-done((bf16[448,2048]{1,0:T(8,128)(2,1)S(1)}, bf16[448,2048]{1,0:T(8,128)(2,1)}, u32[]{:S(2)}, u32[]{:S(2)}) %collective-permute-start.4) | collective-permute-done | bytes 1835040 | tf_op jit(solution)/shard_map/ppermute | solution.py:77
  129.1 2.8 collective-permute-start.2
  131.9 8.3 %collective-permute-start.1 = (bf16[256,1792]{1,0:T(8,128)(2,1)}, bf16[256,1792]{1,0:T(8,128)(2,1)}, u32[]{:S(2)}, u32[]{:S(2)}) collective-permute-start(bf16[256,1792]{1,0:T(8,128)(2,1)} %get-tuple-element.38), channel_id=1, source_target_pairs={{0,0},{1,8},{2,2},{3,10},{4,4},{5,12},{6,6},{7,14},{8,1},{9,9},{10... | collective-permute-start | bytes 2752520 | tf_op jit(solution)/shard_map/ppermute | solution.py:77
  140.2 32.8 %collective-permute-done.2 = bf16[256,1792]{1,0:T(8,128)(2,1)} collective-permute-done((bf16[256,1792]{1,0:T(8,128)(2,1)}, bf16[256,1792]{1,0:T(8,128)(2,1)}, u32[]{:S(2)}, u32[]{:S(2)}) %collective-permute-start.2) | collective-permute-done | bytes 917536 | tf_op jit(solution)/shard_map/ppermute | solution.py:77
  176.6 3.5 %broadcast_select_fusion.1 = (bf16[896,1024]{1,0:T(8,128)(2,1)S(1)}, bf16[896,1024]{1,0:T(8,128)(2,1)S(1)}, bf16[896,1024]{1,0:T(8,128)(2,1)S(1)}, bf16[896,1024]{1,0:T(8,128)(2,1)S(1)}) fusion(bf16[896,1024]{1,0:T(8,128)(2,1)} %collective-permute-done.10, pred[]{:T(512)S(6)} %ne.63, bf16[448,1024]{1,0:T(8,128)(2,1)S(1)} %copy-done.4, ...), kind=kLoop, calls=%fused_computation.27 | loop fusion | flops 11010048 | bytes 14680065 | tf_op jit(solution)/shard_map/jit(_where)/select_n | solution.py:50
  180.7 3.9 %fusion = f32[1024,1024]{1,0:T(8,128)S(1)} fusion(bf16[1024,1792]{1,0:T(8,128)(2,1)S(1)} %bitcast.90, bf16[896,1024]{1,0:T(8,128)(2,1)S(1)} %get-tuple-element.25, bf16[896,1024]{1,0:T(8,128)(2,1)S(1)} %get-tuple-element.24), kind=kOutput, calls=%fused_computation.4 | convolution fusion | flops 3765436416 | bytes 11534336 | tf_op jit(solution)/shard_map/dot_general | solution.py:122
  186.5 3.9 %fusion.2 = f32[1024,1024]{1,0:T(8,128)S(1)} fusion(bf16[1024,1792]{1,0:T(8,128)(2,1)S(1)} %bitcast.91, bf16[896,1024]{1,0:T(8,128)(2,1)S(1)} %get-tuple-element.54, bf16[896,1024]{1,0:T(8,128)(2,1)S(1)} %get-tuple-element.55), kind=kOutput, calls=%fused_computation.6 | convolution fusion | flops 3765436416 | bytes 11534336 | tf_op jit(solution)/shard_map/dot_general | solution.py:122
  193.2 3.9 %fusion.1 = f32[1024,1024]{1,0:T(8,128)S(1)} fusion(bf16[1024,1792]{1,0:T(8,128)(2,1)S(1)} %bitcast.92, bf16[896,1024]{1,0:T(8,128)(2,1)S(1)} %get-tuple-element.25, bf16[896,1024]{1,0:T(8,128)(2,1)S(1)} %get-tuple-element.24), kind=kOutput, calls=%fused_computation.5 | convolution fusion | flops 3765436416 | bytes 11534336 | tf_op jit(solution)/shard_map/dot_general | solution.py:122
  197.1 3.9 %fusion.3 = f32[1024,1024]{1,0:T(8,128)S(1)} fusion(bf16[1024,1792]{1,0:T(8,128)(2,1)S(1)} %bitcast.93, bf16[896,1024]{1,0:T(8,128)(2,1)S(1)} %get-tuple-element.54, bf16[896,1024]{1,0:T(8,128)(2,1)S(1)} %get-tuple-element.55), kind=kOutput, calls=%fused_computation.7 | convolution fusion | flops 3765436416 | bytes 11534336 | tf_op jit(solution)/shard_map/dot_general | solution.py:122
  203.6 7.3 %collective-permute-done.21 = bf16[1024,512]{1,0:T(8,128)(2,1)S(1)} collective-permute-done((bf16[1024,512]{1,0:T(8,128)(2,1)S(1)}, bf16[1024,512]{1,0:T(8,128)(2,1)S(1)}, u32[]{:S(2)}, u32[]{:S(2)}) %collective-permute-start.21) | collective-permute-done | bytes 1048608 | tf_op jit(solution)/shard_map/ppermute | solution.py:77
  211.9 21.5 %collective-permute-done.18 = bf16[1024,512]{1,0:T(8,128)(2,1)S(1)} collective-permute-done((bf16[1024,512]{1,0:T(8,128)(2,1)S(1)}, bf16[1024,512]{1,0:T(8,128)(2,1)S(1)}, u32[]{:S(2)}, u32[]{:S(2)}) %collective-permute-start.18) | collective-permute-done | bytes 1048608 | tf_op jit(solution)/shard_map/ppermute | solution.py:77
  234.5 21.3 %collective-permute-done.11 = bf16[1024,512]{1,0:T(8,128)(2,1)S(1)} collective-permute-done((bf16[1024,512]{1,0:T(8,128)(2,1)S(1)}, bf16[1024,512]{1,0:T(8,128)(2,1)S(1)}, u32[]{:S(2)}, u32[]{:S(2)}) %collective-permute-start.11) | collective-permute-done | bytes 1048608 | tf_op jit(solution)/shard_map/ppermute | solution.py:77
  256.8 20.9 %collective-permute-done.6 = bf16[1024,512]{1,0:T(8,128)(2,1)S(1)} collective-permute-done((bf16[1024,512]{1,0:T(8,128)(2,1)S(1)}, bf16[1024,512]{1,0:T(8,128)(2,1)S(1)}, u32[]{:S(2)}, u32[]{:S(2)}) %collective-permute-start.6) | collective-permute-done | bytes 1048608 | tf_op jit(solution)/shard_map/ppermute | solution.py:77
  278.9 2.8 collective-permute-start.23
  282.4 2.8 collective-permute-start.13
  285.2 17.1 %collective-permute-done.7 = bf16[2,256,512]{2,1,0:T(8,128)(2,1)S(1)} collective-permute-done((bf16[2,256,512]{2,1,0:T(8,128)(2,1)S(1)}, bf16[2,256,512]{2,1,0:T(8,128)(2,1)S(1)}, u32[]{:S(2)}, u32[]{:S(2)}) %collective-permute-start.7) | collective-permute-done | bytes 524320 | tf_op jit(solution)/shard_map/ppermute | solution.py:77
  302.7 14.5 %collective-permute-done.20 = bf16[256,512]{1,0:T(8,128)(2,1)S(1)} collective-permute-done((bf16[256,512]{1,0:T(8,128)(2,1)S(1)}, bf16[256,512]{1,0:T(8,128)(2,1)S(1)}, u32[]{:S(2)}, u32[]{:S(2)}) %collective-permute-start.20) | collective-permute-done | bytes 262176 | tf_op jit(solution)/shard_map/ppermute | solution.py:77
  317.3 5.5 %collective-permute-done.13 = bf16[256,512]{1,0:T(8,128)(2,1)S(1)} collective-permute-done((bf16[256,512]{1,0:T(8,128)(2,1)S(1)}, bf16[256,512]{1,0:T(8,128)(2,1)S(1)}, u32[]{:S(2)}, u32[]{:S(2)}) %collective-permute-start.13) | collective-permute-done | bytes 262176 | tf_op jit(solution)/shard_map/ppermute | solution.py:77
  322.9 3.8 %collective-permute-done.8 = bf16[256,512]{1,0:T(8,128)(2,1)S(1)} collective-permute-done((bf16[256,512]{1,0:T(8,128)(2,1)S(1)}, bf16[256,512]{1,0:T(8,128)(2,1)S(1)}, u32[]{:S(2)}, u32[]{:S(2)}) %collective-permute-start.8) | collective-permute-done | bytes 262176 | tf_op jit(solution)/shard_map/ppermute | solution.py:77
  (86 shorter events, 35.2 us)
Async XLA Ops:
  15.8 31.3 %collective-permute-start = (bf16[256,1792]{1,0:T(8,128)(2,1)}, bf16[256,1792]{1,0:T(8,128)(2,1)}, u32[]{:S(2)}, u32[]{:S(2)}) collective-permute-start(bf16[256,1792]{1,0:T(8,128)(2,1)} %get-tuple-element.44), channel_id=1, source_target_pairs={{0,2},{1,3},{2,0},{3,1},{4,6},{5,7},{6,4},{7,5},{8,10},{9,11},{10,... | collective-permute-start | bytes 2752520 | tf_op jit(solution)/shard_map/ppermute | solution.py:77
  18.8 40.3 %collective-permute-start.14 = (bf16[256,1792]{1,0:T(8,128)(2,1)S(1)}, bf16[256,1792]{1,0:T(8,128)(2,1)}, u32[]{:S(2)}, u32[]{:S(2)}) collective-permute-start(bf16[256,1792]{1,0:T(8,128)(2,1)S(1)} %get-tuple-element.45), channel_id=1, source_target_pairs={{0,2},{1,3},{2,0},{3,1},{4,6},{5,7},{6,4},{7,5},{8,10},{9,11},{10,... | collective-permute-start | bytes 2752520 | tf_op jit(solution)/shard_map/ppermute | solution.py:77
  18.9 3.1 copy-start
  22.0 3.1 copy-start.1
  25.1 2.0 copy-start.2
  45.1 62.2 %collective-permute-start.9 = (bf16[448,2048]{1,0:T(8,128)(2,1)}, bf16[448,2048]{1,0:T(8,128)(2,1)}, u32[]{:S(2)}, u32[]{:S(2)}) collective-permute-start(bf16[448,2048]{1,0:T(8,128)(2,1)} %get-tuple-element.19), channel_id=1, source_target_pairs={{0,4},{1,5},{2,6},{3,7},{4,0},{5,1},{6,2},{7,3},{8,12},{9,13},{10,... | collective-permute-start | bytes 5505032 | tf_op jit(solution)/shard_map/ppermute | solution.py:77
  47.0 79.1 %collective-permute-start.4 = (bf16[448,2048]{1,0:T(8,128)(2,1)S(1)}, bf16[448,2048]{1,0:T(8,128)(2,1)}, u32[]{:S(2)}, u32[]{:S(2)}) collective-permute-start(bf16[448,2048]{1,0:T(8,128)(2,1)S(1)} %get-tuple-element.18), channel_id=1, source_target_pairs={{0,4},{1,5},{2,6},{3,7},{4,0},{5,1},{6,2},{7,3},{8,12},{9,13},{10,... | collective-permute-start | bytes 5505032 | tf_op jit(solution)/shard_map/ppermute | solution.py:77
  62.7 43.1 %collective-permute-start.16 = (bf16[256,1792]{1,0:T(8,128)(2,1)S(1)}, bf16[256,1792]{1,0:T(8,128)(2,1)S(1)}, u32[]{:S(2)}, u32[]{:S(2)}) collective-permute-start(bf16[256,1792]{1,0:T(8,128)(2,1)S(1)} %get-tuple-element.42), channel_id=1, source_target_pairs={{0,16},{1,24},{2,18},{3,26},{4,20},{5,28},{6,22},{7,30},{8,17},{9,... | collective-permute-start | bytes 2752520 | tf_op jit(solution)/shard_map/ppermute | solution.py:77
  65.5 40.3 %collective-permute-start.15 = (bf16[256,1792]{1,0:T(8,128)(2,1)S(1)}, bf16[256,1792]{1,0:T(8,128)(2,1)S(1)}, u32[]{:S(2)}, u32[]{:S(2)}) collective-permute-start(bf16[256,1792]{1,0:T(8,128)(2,1)S(1)} %get-tuple-element.43), channel_id=1, source_target_pairs={{0,0},{1,8},{2,2},{3,10},{4,4},{5,12},{6,6},{7,14},{8,1},{9,9},{10... | collective-permute-start | bytes 2752520 | tf_op jit(solution)/shard_map/ppermute | solution.py:77
  105.7 4.0 %copy-start.5 = (bf16[256,1792]{1,0:T(8,128)(2,1)}, bf16[256,1792]{1,0:T(8,128)(2,1)S(1)}, u32[]{:S(2)}) copy-start(bf16[256,1792]{1,0:T(8,128)(2,1)S(1)} %collective-permute-done.16) | copy-start | bytes 2752516
  105.7 4.0 %copy-start.7 = (bf16[256,1792]{1,0:T(8,128)(2,1)}, bf16[256,1792]{1,0:T(8,128)(2,1)S(1)}, u32[]{:S(2)}) copy-start(bf16[256,1792]{1,0:T(8,128)(2,1)S(1)} %collective-permute-done.15) | copy-start | bytes 2752516
  107.2 67.5 %collective-permute-start.17 = (bf16[2,256,1792]{2,1,0:T(8,128)(2,1)}, bf16[2,256,1792]{2,1,0:T(8,128)(2,1)}, u32[]{:S(2)}, u32[]{:S(2)}) collective-permute-start(bf16[2,256,1792]{2,1,0:T(8,128)(2,1)} %pad_maximum_fusion.13), channel_id=1, source_target_pairs={{0,1},{1,0},{2,3},{3,2},{4,5},{5,4},{6,7},{7,6},{8,9},{9,8},{10,11... | collective-permute-start | bytes 5505032 | tf_op jit(solution)/shard_map/ppermute | solution.py:77
  111.2 65.3 %collective-permute-start.10 = (bf16[896,1024]{1,0:T(8,128)(2,1)}, bf16[896,1024]{1,0:T(8,128)(2,1)}, u32[]{:S(2)}, u32[]{:S(2)}) collective-permute-start(bf16[896,1024]{1,0:T(8,128)(2,1)} %pad_maximum_fusion.11), channel_id=1, source_target_pairs={{0,1},{1,0},{2,3},{3,2},{4,5},{5,4},{6,7},{7,6},{8,9},{9,8},{10,11... | collective-permute-start | bytes 5505032 | tf_op jit(solution)/shard_map/ppermute | solution.py:77
  129.1 45.6 %copy-start.6 = (bf16[256,1792]{1,0:T(8,128)(2,1)S(1)}, bf16[256,1792]{1,0:T(8,128)(2,1)}, u32[]{:S(2)}) copy-start(bf16[256,1792]{1,0:T(8,128)(2,1)} %copy-done.5) | copy-start | bytes 2752516
  129.1 47.5 %collective-permute-start.5 = (bf16[896,1024]{1,0:T(8,128)(2,1)}, bf16[896,1024]{1,0:T(8,128)(2,1)}, u32[]{:S(2)}, u32[]{:S(2)}) collective-permute-start(bf16[896,1024]{1,0:T(8,128)(2,1)} %pad_maximum_fusion.9), channel_id=1, source_target_pairs={{0,1},{1,0},{2,3},{3,2},{4,5},{5,4},{6,7},{7,6},{8,9},{9,8},{10,11... | collective-permute-start | bytes 5505032 | tf_op jit(solution)/shard_map/ppermute | solution.py:77
  129.1 43.8 %collective-permute-start.2 = (bf16[256,1792]{1,0:T(8,128)(2,1)}, bf16[256,1792]{1,0:T(8,128)(2,1)}, u32[]{:S(2)}, u32[]{:S(2)}) collective-permute-start(bf16[256,1792]{1,0:T(8,128)(2,1)} %get-tuple-element.39), channel_id=1, source_target_pairs={{0,16},{1,24},{2,18},{3,26},{4,20},{5,28},{6,22},{7,30},{8,17},{9,... | collective-permute-start | bytes 2752520 | tf_op jit(solution)/shard_map/ppermute | solution.py:77
  131.9 41.1 %collective-permute-start.1 = (bf16[256,1792]{1,0:T(8,128)(2,1)}, bf16[256,1792]{1,0:T(8,128)(2,1)}, u32[]{:S(2)}, u32[]{:S(2)}) collective-permute-start(bf16[256,1792]{1,0:T(8,128)(2,1)} %get-tuple-element.38), channel_id=1, source_target_pairs={{0,0},{1,8},{2,2},{3,10},{4,4},{5,12},{6,6},{7,14},{8,1},{9,9},{10... | collective-permute-start | bytes 2752520 | tf_op jit(solution)/shard_map/ppermute | solution.py:77
  140.2 34.5 %copy-start.8 = (bf16[256,1792]{1,0:T(8,128)(2,1)S(1)}, bf16[256,1792]{1,0:T(8,128)(2,1)}, u32[]{:S(2)}) copy-start(bf16[256,1792]{1,0:T(8,128)(2,1)} %copy-done.7) | copy-start | bytes 2752516
  174.6 2.0 copy-start.3
  174.6 16.5 %collective-permute-start.3 = (bf16[2,256,1792]{2,1,0:T(8,128)(2,1)S(1)}, bf16[2,256,1792]{2,1,0:T(8,128)(2,1)S(1)}, u32[]{:S(2)}, u32[]{:S(2)}) collective-permute-start(bf16[2,256,1792]{2,1,0:T(8,128)(2,1)S(1)} %pad_maximum_fusion.8), channel_id=1, source_target_pairs={{0,1},{1,0},{2,3},{3,2},{4,5},{5,4},{6,7},{7,6},{8,9},{9,8},{10,11... | collective-permute-start | bytes 5505032 | tf_op jit(solution)/shard_map/ppermute | solution.py:77
  184.9 26.1 %collective-permute-start.21 = (bf16[1024,512]{1,0:T(8,128)(2,1)S(1)}, bf16[1024,512]{1,0:T(8,128)(2,1)S(1)}, u32[]{:S(2)}, u32[]{:S(2)}) collective-permute-start(bf16[1024,512]{1,0:T(8,128)(2,1)S(1)} %slice.280), channel_id=1, source_target_pairs={{0,2},{1,3},{2,0},{3,1},{4,6},{5,7},{6,4},{7,5},{8,10},{9,11},{10,... | collective-permute-start | bytes 3145736 | tf_op jit(solution)/shard_map/ppermute | solution.py:77
  190.6 42.8 %collective-permute-start.18 = (bf16[1024,512]{1,0:T(8,128)(2,1)S(1)}, bf16[1024,512]{1,0:T(8,128)(2,1)S(1)}, u32[]{:S(2)}, u32[]{:S(2)}) collective-permute-start(bf16[1024,512]{1,0:T(8,128)(2,1)S(1)} %slice.281), channel_id=1, source_target_pairs={{0,2},{1,3},{2,0},{3,1},{4,6},{5,7},{6,4},{7,5},{8,10},{9,11},{10,... | collective-permute-start | bytes 3145736 | tf_op jit(solution)/shard_map/ppermute | solution.py:77
  201.3 54.6 %collective-permute-start.11 = (bf16[1024,512]{1,0:T(8,128)(2,1)S(1)}, bf16[1024,512]{1,0:T(8,128)(2,1)S(1)}, u32[]{:S(2)}, u32[]{:S(2)}) collective-permute-start(bf16[1024,512]{1,0:T(8,128)(2,1)S(1)} %slice.282), channel_id=1, source_target_pairs={{0,2},{1,3},{2,0},{3,1},{4,6},{5,7},{6,4},{7,5},{8,10},{9,11},{10,... | collective-permute-start | bytes 3145736 | tf_op jit(solution)/shard_map/ppermute | solution.py:77
  203.0 74.7 %collective-permute-start.6 = (bf16[1024,512]{1,0:T(8,128)(2,1)S(1)}, bf16[1024,512]{1,0:T(8,128)(2,1)S(1)}, u32[]{:S(2)}, u32[]{:S(2)}) collective-permute-start(bf16[1024,512]{1,0:T(8,128)(2,1)S(1)} %slice.283), channel_id=1, source_target_pairs={{0,2},{1,3},{2,0},{3,1},{4,6},{5,7},{6,4},{7,5},{8,10},{9,11},{10,... | collective-permute-start | bytes 3145736 | tf_op jit(solution)/shard_map/ppermute | solution.py:77
  211.3 67.4 %collective-permute-start.22 = (bf16[2,256,512]{2,1,0:T(8,128)(2,1)S(1)}, bf16[2,256,512]{2,1,0:T(8,128)(2,1)S(1)}, u32[]{:S(2)}, u32[]{:S(2)}) collective-permute-start(bf16[2,256,512]{2,1,0:T(8,128)(2,1)S(1)} %fusion.11), channel_id=1, source_target_pairs={{0,8},{1,9},{2,10},{3,11},{4,12},{5,13},{6,14},{7,15},{8,0},{9,1},... | collective-permute-start | bytes 1572872 | tf_op jit(solution)/shard_map/ppermute | solution.py:77
  234.0 47.7 %collective-permute-start.19 = (bf16[2,256,512]{2,1,0:T(8,128)(2,1)S(1)}, bf16[2,256,512]{2,1,0:T(8,128)(2,1)S(1)}, u32[]{:S(2)}, u32[]{:S(2)}) collective-permute-start(bf16[2,256,512]{2,1,0:T(8,128)(2,1)S(1)} %fusion.10), channel_id=1, source_target_pairs={{0,8},{1,9},{2,10},{3,11},{4,12},{5,13},{6,14},{7,15},{8,0},{9,1},... | collective-permute-start | bytes 1572872 | tf_op jit(solution)/shard_map/ppermute | solution.py:77
  256.3 25.9 %collective-permute-start.12 = (bf16[2,256,512]{2,1,0:T(8,128)(2,1)S(1)}, bf16[2,256,512]{2,1,0:T(8,128)(2,1)S(1)}, u32[]{:S(2)}, u32[]{:S(2)}) collective-permute-start(bf16[2,256,512]{2,1,0:T(8,128)(2,1)S(1)} %fusion.9), channel_id=1, source_target_pairs={{0,8},{1,9},{2,10},{3,11},{4,12},{5,13},{6,14},{7,15},{8,0},{9,1},... | collective-permute-start | bytes 1572872 | tf_op jit(solution)/shard_map/ppermute | solution.py:77
  278.2 24.1 %collective-permute-start.7 = (bf16[2,256,512]{2,1,0:T(8,128)(2,1)S(1)}, bf16[2,256,512]{2,1,0:T(8,128)(2,1)S(1)}, u32[]{:S(2)}, u32[]{:S(2)}) collective-permute-start(bf16[2,256,512]{2,1,0:T(8,128)(2,1)S(1)} %fusion.8), channel_id=1, source_target_pairs={{0,8},{1,9},{2,10},{3,11},{4,12},{5,13},{6,14},{7,15},{8,0},{9,1},... | collective-permute-start | bytes 1572872 | tf_op jit(solution)/shard_map/ppermute | solution.py:77
  278.9 23.7 %collective-permute-start.23 = (bf16[256,512]{1,0:T(8,128)(2,1)S(1)}, bf16[256,512]{1,0:T(8,128)(2,1)S(1)}, u32[]{:S(2)}, u32[]{:S(2)}) collective-permute-start(bf16[256,512]{1,0:T(8,128)(2,1)S(1)} %fusion.23), channel_id=1, source_target_pairs={{0,16},{1,17},{2,18},{3,19},{4,20},{5,21},{6,22},{7,23},{8,24},{9,... | collective-permute-start | bytes 786440 | tf_op jit(solution)/shard_map/ppermute | solution.py:77
  282.0 35.2 %collective-permute-start.20 = (bf16[256,512]{1,0:T(8,128)(2,1)S(1)}, bf16[256,512]{1,0:T(8,128)(2,1)S(1)}, u32[]{:S(2)}, u32[]{:S(2)}) collective-permute-start(bf16[256,512]{1,0:T(8,128)(2,1)S(1)} %fusion.22), channel_id=1, source_target_pairs={{0,16},{1,17},{2,18},{3,19},{4,20},{5,21},{6,22},{7,23},{8,24},{9,... | collective-permute-start | bytes 786440 | tf_op jit(solution)/shard_map/ppermute | solution.py:77
  282.4 40.4 %collective-permute-start.13 = (bf16[256,512]{1,0:T(8,128)(2,1)S(1)}, bf16[256,512]{1,0:T(8,128)(2,1)S(1)}, u32[]{:S(2)}, u32[]{:S(2)}) collective-permute-start(bf16[256,512]{1,0:T(8,128)(2,1)S(1)} %fusion.21), channel_id=1, source_target_pairs={{0,16},{1,17},{2,18},{3,19},{4,20},{5,21},{6,22},{7,23},{8,24},{9,... | collective-permute-start | bytes 786440 | tf_op jit(solution)/shard_map/ppermute | solution.py:77
  302.5 24.1 %collective-permute-start.8 = (bf16[256,512]{1,0:T(8,128)(2,1)S(1)}, bf16[256,512]{1,0:T(8,128)(2,1)S(1)}, u32[]{:S(2)}, u32[]{:S(2)}) collective-permute-start(bf16[256,512]{1,0:T(8,128)(2,1)S(1)} %fusion.20), channel_id=1, source_target_pairs={{0,16},{1,17},{2,18},{3,19},{4,20},{5,21},{6,22},{7,23},{8,24},{9,... | collective-permute-start | bytes 786440 | tf_op jit(solution)/shard_map/ppermute | solution.py:77
  (1 other events, 2.0 us)

commit v3 on v0

v3 whole, which is shorter than its diff:
```python
import jax
import jax.numpy as jnp
from jax import lax
from jax.experimental import pallas as pl
from jax.experimental.pallas import tpu as pltpu
from jax.sharding import PartitionSpec as P

AXES = ("fsdp", "tp")
ROW_CHUNKS = 2
COL_CHUNKS = 4


def adam_step(master_ref, one_ref, two_ref, grad_ref, new_master_ref, new_one_ref, new_two_ref, weight_ref):
    grad = grad_ref[...].astype(jnp.float32)
    new_one = 0.9 * one_ref[...] + 0.1 * grad
    new_two = 0.95 * two_ref[...] + 0.05 * grad * grad
    new_master = master_ref[...] - 0.001 * new_one / (jnp.sqrt(new_two) + 1e-08)
    new_one_ref[...] = new_one
    new_two_ref[...] = new_two
    new_master_ref[...] = new_master
    weight_ref[...] = new_master.astype(jnp.bfloat16)


def adam(where, chunks, args, previous):
    rows, cols = args[0].shape
    width = cols // 4 // COL_CHUNKS
    step = max(s for s in range(16, 225, 16) if rows % s == 0)
    count = len(chunks)

    def kernel(where_ref, *refs):
        sources = refs[:4]
        targets = refs[-3 - count : -count]
        y, c = where_ref[0], where_ref[1]
        for q, weight_ref in zip(chunks, refs[-count:]):
            block = pl.BlockSpec((step, width), lambda j, i: (i, j * COL_CHUNKS + q))
            piece = pl.BlockSpec((step, width), lambda j, i: (i, 2 * ((j % 2) ^ c) + ((j // 2) ^ y)))
            pltpu.emit_pipeline(
                adam_step,
                grid=(4, rows // step),
                in_specs=[block] * 4,
                out_specs=[block] * 3 + [piece],
            )(*sources, *targets, weight_ref)

    hbm = pl.BlockSpec(memory_space=pltpu.HBM)
    full = jax.ShapeDtypeStruct((rows, cols), jnp.float32)
    size = rows * cols * count // COL_CHUNKS
    out = pl.pallas_call(
        kernel,
        in_specs=[pl.BlockSpec(memory_space=pltpu.SMEM)] + [hbm] * (4 + len(previous)),
        out_specs=[hbm] * (3 + count),
        out_shape=[full] * 3 + [jax.ShapeDtypeStruct((rows, cols // COL_CHUNKS), jnp.bfloat16)] * count,
        input_output_aliases={5 + i: i for i in range(len(previous))},
        compiler_params=pltpu.CompilerParams(vmem_limit_bytes=60 * 1024 * 1024),
        cost_estimate=pl.CostEstimate(flops=12 * size, bytes_accessed=28 * size, transcendentals=size),
        name="adam",
    )(where, *args, *previous)
    return out[:3], out[3:]


def pack(where, act, xs):
    rows, cols = act.shape
    run = cols // xs // 2
    part = rows // ROW_CHUNKS

    def kernel(where_ref, act_ref, *out_refs):
        for y in range(2):
            for x in range(xs):

                @pl.when((where_ref[0] == y) & (where_ref[2] == x))
                def _():
                    for m in range(ROW_CHUNKS):
                        for s in range(2):
                            for d in range(xs):
                                at = (2 * (x ^ d) + (y ^ s)) * run
                                out_refs[2 * m + s][:, d * run : (d + 1) * run] = act_ref[
                                    m * part : (m + 1) * part, at : at + run
                                ]

    out = pl.pallas_call(
        kernel,
        in_specs=[pl.BlockSpec(memory_space=pltpu.SMEM), pl.BlockSpec(memory_space=pltpu.VMEM)],
        out_specs=[pl.BlockSpec(memory_space=pltpu.VMEM)] * (2 * ROW_CHUNKS),
        out_shape=[jax.ShapeDtypeStruct((part, cols // 2), act.dtype)] * (2 * ROW_CHUNKS),
        compiler_params=pltpu.CompilerParams(vmem_limit_bytes=32 * 1024 * 1024),
        cost_estimate=pl.CostEstimate(flops=0, bytes_accessed=4 * rows * cols, transcendentals=0),
        name="pack",
    )(where, act)
    return out[0::2], out[1::2]


def swap_if(flag, low, high):
    return jnp.where(flag, high, low), jnp.where(flag, low, high)


def after(value, *done):
    return lax.optimization_barrier((value, *done))[0]


def local(master, moment_one, moment_two, gradient, hidden_act):
    fsdp, tp = lax.axis_size("fsdp"), lax.axis_size("tp")
    xs = fsdp // tp
    f, t = lax.axis_index("fsdp"), lax.axis_index("tp")
    z, x, y, c = f // xs, f % xs, t // 2, t % 2
    where = jnp.stack([y, c, x]).astype(jnp.int32)

    def permute(value, to):
        pairs = []
        for zi in range(tp):
            for xi in range(xs):
                for yi in range(2):
                    for ci in range(2):
                        zo, xo, yo, co = to(zi, xi, yi, ci)
                        pairs.append(((zi * xs + xi) * tp + 2 * yi + ci, (zo * xs + xo) * tp + 2 * yo + co))
        return lax.ppermute(value, AXES, pairs)

    rows = hidden_act.shape[0]
    part = rows // ROW_CHUNKS
    own, other = pack(where, hidden_act, xs)

    args = (master, moment_one, moment_two, gradient)
    updated, pieces = adam(where, [0], args, [])
    updated, rest = adam(where, list(range(1, COL_CHUNKS)), args, updated)
    tables, crossed = [], []
    for piece in [*pieces, *rest]:
        if crossed:
            piece = after(piece, crossed[-1])
        parts = [piece] + [permute(piece, lambda z, x, y, c: (z, x ^ d, y, c)) for d in range(1, xs)]
        crossed.append(parts[-1])
        half = piece.shape[1] // 2
        here = jnp.stack([p[:, :half] for p in parts])
        there = jnp.stack([p[:, half:] for p in parts])
        there = permute(there, lambda z, x, y, c: (z, x, y, 1 - c))
        tables.append(jnp.stack(swap_if(c != 0, here, there), axis=1).reshape(-1, half))

    acts, theirs, moved = [], [], []
    for m in range(ROW_CHUNKS):
        send = other[m] if m == 0 else after(other[m], theirs[-1])
        theirs.append(permute(send, lambda z, x, y, c: (z, x, 1 - y, c)))
        pair = swap_if(((z // 2) ^ y) != 0, own[m], theirs[m])
        if m:
            pair = after(pair, moved[-1], crossed[2 * m - 1])
        got = [
            permute(data, lambda z, x, y, c: (2 * ((z // 2) ^ a) + c, x, y, z % 2)) for a, data in enumerate(pair)
        ]
        got = jnp.concatenate(got, axis=0)
        moved.append(got)
        acts.append((got, permute(got, lambda z, x, y, c: (z, x, y, 1 - c))))

    flip = (c ^ (z % 2)) != 0
    backs, leaving, result = [], [], []
    for m in range(ROW_CHUNKS):
        line = []
        for table in tables:
            j = len(backs)
            totals = [jnp.dot(a, table, preferred_element_type=jnp.float32) for a in acts[m]]
            half = table.shape[1] // 2
            send = jnp.stack([total[:, half:].astype(jnp.bfloat16) for total in totals])
            if j >= 2:
                send = after(send, backs[j - 2])
            back = permute(send, lambda z, x, y, c: (z, x, 1 - y, c))
            backs.append(back)
            if j >= 1:
                back = after(back, leaving[-1])
            near, far = swap_if(flip, *[total[:, :half] + b for total, b in zip(totals, back)])
            back = permute(far.astype(jnp.bfloat16), lambda z, x, y, c: (z ^ 1, x, y, c))
            near = near + back
            send = near[part:].astype(jnp.bfloat16)
            leaving.append(send)
            back = permute(send, lambda z, x, y, c: (z ^ 2, x, y, c))
            line.append((near[:part] + back).astype(jnp.bfloat16))
        result.append(jnp.concatenate(line, axis=1))
    decoded = jnp.concatenate(result, axis=0)
    return (*updated, decoded)


def solution(mesh):
    placed = (
        P(("fsdp", "tp"), None),
        P(("fsdp", "tp"), None),
        P(("fsdp", "tp"), None),
        P(("fsdp", "tp"), None),
        P("fsdp", "tp"),
    )
    return jax.shard_map(
        local,
        mesh=mesh,
        in_specs=placed,
        out_specs=(
            P(("fsdp", "tp"), None),
            P(("fsdp", "tp"), None),
            P(("fsdp", "tp"), None),
            P("fsdp", "tp"),
        ),
        check_vma=False,
    )
```

time: 693 us -> 275 us (0.40)
  waiting for transfers between devices: 579 us -> 147 us
  starting transfers between devices: 0.08 us -> 53.7 us
  blocking collectives: 46.8 us -> 0 us
  Pallas kernels: 0 us -> 35.2 us
  other arithmetic: 20.8 us -> 8.04 us
  between operations: 14 us -> 1.52 us
    all_gather x1 -> x0, waiting for transfers between devices: 507 us -> none  [local(): lax.all_gather(rollout_weight, 'fsdp', axis=0, tiled=True)]
    ppermute x0 -> x40, waiting for transfers between devices: none -> 147 us  [permute(): return lax.ppermute(value, AXES, pairs)]
    reduce_scatter x1 -> x0, waiting for transfers between devices: 71.8 us -> none  [local(): lax.psum_scatter(partial_out, 'tp', scatter_dimension=1, tiled=True)]
    ppermute x0 -> x40, starting transfers between devices: none -> 53.7 us  [permute(): return lax.ppermute(value, AXES, pairs)]
    all_to_all x1 -> x0, blocking collectives: 46.8 us -> none  [local(): lax.all_to_all(arranged, 'tp', split_axis=2, concat_axis=1, tiled=True)]
    pallas_call x0 -> x3, Pallas kernels: none -> 35.2 us  [the longest x2 33.4 us: adam(): pl.pallas_call(kernel, in_specs=[pl.BlockSpec(memory_space=pltpu.SMEM)] +...]
    convert_element_type x2 -> x16, other arithmetic: 20.8 us -> 1.58 us  [the longest x8 1.24 us: local(): far.astype(jnp.bfloat16)]
    dot_general x1 -> x16, matrix products: 22.8 us -> 18.8 us  [local(): jnp.dot(a, table, preferred_element_type=jnp.float32)]
  transfers between devices with their start and end apart: 2 -> 40, of which waited for: 2 -> 21; matrix products, arithmetic and copies ran while one was open for 1% -> 12% of each run, Pallas kernels for 0% -> 12%
where the time goes in v3:
time: 275 us; the launch traced here: 273 us
  waiting for transfers between devices  147 us (53%)
  starting transfers between devices  53.7 us (20%)
  Pallas kernels  35.2 us (13%)
  matrix products  18.8 us (7%)
  local copies, waits for them, and re-layouts  8.81 us (3%)
  other arithmetic  8.04 us (3%)
    ppermute x40, waiting for transfers between devices, permute(): return lax.ppermute(value, AXES, pairs)  147 us
    ppermute x40, starting transfers between devices, permute(): return lax.ppermute(value, AXES, pairs)  53.7 us
    pallas_call x2, Pallas kernels, adam(): pl.pallas_call(kernel, in_specs=[pl.BlockSpec(memory_space=pltpu.SMEM)] +...  33.4 us
    dot_general x16, matrix products, local(): jnp.dot(a, table, preferred_element_type=jnp.float32)  18.8 us
  transfers between devices with their start and end apart: 40, of which 21 were waited for; matrix products, arithmetic and copies ran while one was open for 12% of the time, Pallas kernels for 12%

profile of v3, /device:TPU:0, one launch (start us, length us, event | category | flops | bytes accessed | tf_op | source)
XLA Modules:
  0.0 273.5 jit_solution(15872173802548877626)
XLA Ops:
  0.7 2.0 copy-done
  2.8 1.8 pack.1
  4.6 3.0 %collective-permute-start = (bf16[256,1792]{1,0:T(8,128)(2,1)}, bf16[256,1792]{1,0:T(8,128)(2,1)}, u32[]{:S(2)}, u32[]{:S(2)}) collective-permute-start(bf16[256,1792]{1,0:T(8,128)(2,1)} %get-tuple-element.43), channel_id=1, source_target_pairs={{0,2},{1,3},{2,0},{3,1},{4,6},{5,7},{6,4},{7,5},{8,10},{9,11},{10,... | collective-permute-start | bytes 2752520 | tf_op jit(solution)/shard_map/ppermute | solution.py:114
  7.5 8.7 %adam.2 = (f32[448,4096]{1,0:T(8,128)}, f32[448,4096]{1,0:T(8,128)}, f32[448,4096]{1,0:T(8,128)}, bf16[448,1024]{1,0:T(8,128)(2,1)}) custom-call(s32[3]{0:T(128)} %copy-done.1, f32[448,4096]{1,0:T(8,128)} %refs_0_.3, f32[448,4096]{1,0:T(8,128)} %refs_1_.3, f32[448,4096]{1,0:T(8,128)} %refs_2_.3, bf16[448,4096]{1,0:T(8,128)(2,1)} %refs_3_.3), custom_call_target="tpu_custom_call" | custom-call | flops 5505024 | bytes 12845056 | tf_op jit(solution)/shard_map/adam/pallas_call | solution.py:47
  17.7 10.5 %collective-permute-done = bf16[256,1792]{1,0:T(8,128)(2,1)} collective-permute-done((bf16[256,1792]{1,0:T(8,128)(2,1)}, bf16[256,1792]{1,0:T(8,128)(2,1)}, u32[]{:S(2)}, u32[]{:S(2)}) %collective-permute-start) | collective-permute-done | bytes 917536 | tf_op jit(solution)/shard_map/ppermute | solution.py:114
  28.2 2.6 broadcast_select_fusion.2
  30.8 8.3 %collective-permute-start.1 = (bf16[256,1792]{1,0:T(8,128)(2,1)}, bf16[256,1792]{1,0:T(8,128)(2,1)}, u32[]{:S(2)}, u32[]{:S(2)}) collective-permute-start(bf16[256,1792]{1,0:T(8,128)(2,1)} %get-tuple-element.87), channel_id=1, source_target_pairs={{0,0},{1,8},{2,2},{3,10},{4,4},{5,12},{6,6},{7,14},{8,1},{9,9},{10... | collective-permute-start | bytes 2752520 | tf_op jit(solution)/shard_map/ppermute | solution.py:114
  39.2 2.8 %collective-permute-start.2 = (bf16[256,1792]{1,0:T(8,128)(2,1)}, bf16[256,1792]{1,0:T(8,128)(2,1)}, u32[]{:S(2)}, u32[]{:S(2)}) collective-permute-start(bf16[256,1792]{1,0:T(8,128)(2,1)} %get-tuple-element.86), channel_id=1, source_target_pairs={{0,16},{1,24},{2,18},{3,26},{4,20},{5,28},{6,22},{7,30},{8,17},{9,... | collective-permute-start | bytes 2752520 | tf_op jit(solution)/shard_map/ppermute | solution.py:114
  42.1 24.7 %adam.3 = (f32[448,4096]{1,0:T(8,128)}, f32[448,4096]{1,0:T(8,128)}, f32[448,4096]{1,0:T(8,128)}, bf16[448,1024]{1,0:T(8,128)(2,1)}, bf16[448,1024]{1,0:T(8,128)(2,1)}, /*index=5*/bf16[448,1024]{1,0:T(8,128)(2,1)}) custom-call(s32[3]{0:T(128)} %copy-done.1, f32[448,4096]{1,0:T(8,128)} %refs_0_.3, ...), custom_call_target="tpu_custom_call", output_to_operand_aliasing={{0}: (5, {}), {1}: (6, {}), {2}: (7, {})} | custom-call | flops 16515072 | bytes 38535168 | tf_op jit(solution)/shard_map/adam/pallas_call | solution.py:47
  72.5 5.3 %collective-permute-done.2 = bf16[256,1792]{1,0:T(8,128)(2,1)} collective-permute-done((bf16[256,1792]{1,0:T(8,128)(2,1)}, bf16[256,1792]{1,0:T(8,128)(2,1)}, u32[]{:S(2)}, u32[]{:S(2)}) %collective-permute-start.2) | collective-permute-done | bytes 917536 | tf_op jit(solution)/shard_map/ppermute | solution.py:114
  79.1 4.7 %collective-permute-done.24 = bf16[256,1792]{1,0:T(8,128)(2,1)S(1)} collective-permute-done((bf16[256,1792]{1,0:T(8,128)(2,1)S(1)}, bf16[256,1792]{1,0:T(8,128)(2,1)S(1)}, u32[]{:S(2)}, u32[]{:S(2)}) %collective-permute-start.24) | collective-permute-done | bytes 917536 | tf_op jit(solution)/shard_map/ppermute | solution.py:114
  90.7 37.5 %collective-permute-done.26 = bf16[256,1792]{1,0:T(8,128)(2,1)S(1)} collective-permute-done((bf16[256,1792]{1,0:T(8,128)(2,1)S(1)}, bf16[256,1792]{1,0:T(8,128)(2,1)S(1)}, u32[]{:S(2)}, u32[]{:S(2)}) %collective-permute-start.26) | collective-permute-done | bytes 917536 | tf_op jit(solution)/shard_map/ppermute | solution.py:114
  131.1 1.6 collective-permute-start.19
  134.4 19.5 %collective-permute-done.19 = bf16[448,1024]{1,0:T(8,128)(2,1)S(1)} collective-permute-done((bf16[448,1024]{1,0:T(8,128)(2,1)S(1)}, bf16[448,1024]{1,0:T(8,128)(2,1)S(1)}, u32[]{:S(2)}, u32[]{:S(2)}) %collective-permute-start.19) | collective-permute-done | bytes 917536 | tf_op jit(solution)/shard_map/ppermute | solution.py:114
  163.1 17.9 %collective-permute-done.6 = bf16[2,512,256]{1,2,0:T(8,128)(2,1)S(1)} collective-permute-done((bf16[2,512,256]{1,2,0:T(8,128)(2,1)S(1)}, bf16[2,512,256]{1,2,0:T(8,128)(2,1)S(1)}, u32[]{:S(2)}, u32[]{:S(2)}) %collective-permute-start.6) | collective-permute-done | bytes 524320 | tf_op jit(solution)/shard_map/ppermute | solution.py:114
  182.3 6.9 %collective-permute-done.7 = bf16[512,256]{0,1:T(8,128)(2,1)S(1)} collective-permute-done((bf16[512,256]{0,1:T(8,128)(2,1)S(1)}, bf16[512,256]{0,1:T(8,128)(2,1)S(1)}, u32[]{:S(2)}, u32[]{:S(2)}) %collective-permute-start.7) | collective-permute-done | bytes 262176 | tf_op jit(solution)/shard_map/ppermute | solution.py:114
  189.4 1.6 collective-permute-start.8
  191.2 1.6 collective-permute-start.12
  204.9 4.3 %collective-permute-done.17 = bf16[512,256]{0,1:T(8,128)(2,1)S(1)} collective-permute-done((bf16[512,256]{0,1:T(8,128)(2,1)S(1)}, bf16[512,256]{0,1:T(8,128)(2,1)S(1)}, u32[]{:S(2)}, u32[]{:S(2)}) %collective-permute-start.17) | collective-permute-done | bytes 262176 | tf_op jit(solution)/shard_map/ppermute | solution.py:114
  211.7 5.6 %collective-permute-done.22 = bf16[512,256]{0,1:T(8,128)(2,1)S(1)} collective-permute-done((bf16[512,256]{0,1:T(8,128)(2,1)S(1)}, bf16[512,256]{0,1:T(8,128)(2,1)S(1)}, u32[]{:S(2)}, u32[]{:S(2)}) %collective-permute-start.22) | collective-permute-done | bytes 262176 | tf_op jit(solution)/shard_map/ppermute | solution.py:114
  217.4 4.4 %collective-permute-done.28 = bf16[2,512,256]{1,2,0:T(8,128)(2,1)S(1)} collective-permute-done((bf16[2,512,256]{1,2,0:T(8,128)(2,1)S(1)}, bf16[2,512,256]{1,2,0:T(8,128)(2,1)S(1)}, u32[]{:S(2)}, u32[]{:S(2)}) %collective-permute-start.28) | collective-permute-done | bytes 524320 | tf_op jit(solution)/shard_map/ppermute | solution.py:114
  224.7 4.9 %collective-permute-done.29 = bf16[512,256]{0,1:T(8,128)(2,1)S(1)} collective-permute-done((bf16[512,256]{0,1:T(8,128)(2,1)S(1)}, bf16[512,256]{0,1:T(8,128)(2,1)S(1)}, u32[]{:S(2)}, u32[]{:S(2)}) %collective-permute-start.29) | collective-permute-done | bytes 262176 | tf_op jit(solution)/shard_map/ppermute | solution.py:114
  230.0 3.1 %collective-permute-done.31 = bf16[2,512,256]{1,2,0:T(8,128)(2,1)S(1)} collective-permute-done((bf16[2,512,256]{1,2,0:T(8,128)(2,1)S(1)}, bf16[2,512,256]{1,2,0:T(8,128)(2,1)S(1)}, u32[]{:S(2)}, u32[]{:S(2)}) %collective-permute-start.31) | collective-permute-done | bytes 524320 | tf_op jit(solution)/shard_map/ppermute | solution.py:114
  235.3 1.6 collective-permute-start.23
  237.0 4.6 %collective-permute-done.32 = bf16[512,256]{0,1:T(8,128)(2,1)S(1)} collective-permute-done((bf16[512,256]{0,1:T(8,128)(2,1)S(1)}, bf16[512,256]{0,1:T(8,128)(2,1)S(1)}, u32[]{:S(2)}, u32[]{:S(2)}) %collective-permute-start.32) | collective-permute-done | bytes 262176 | tf_op jit(solution)/shard_map/ppermute | solution.py:114
  241.8 2.5 collective-permute-done.34
  245.4 4.0 %collective-permute-start.30 = (bf16[256,256]{0,1:T(8,128)(2,1)S(1)}, bf16[256,256]{0,1:T(8,128)(2,1)S(1)}, u32[]{:S(2)}, u32[]{:S(2)}) collective-permute-start(bf16[256,256]{0,1:T(8,128)(2,1)S(1)} %slice.515), channel_id=1, source_target_pairs={{0,16},{1,17},{2,18},{3,19},{4,20},{5,21},{6,22},{7,23},{8,24},{9,... | collective-permute-start | bytes 393224 | tf_op jit(solution)/shard_map/ppermute | solution.py:114
  249.4 4.1 %collective-permute-done.35 = bf16[512,256]{0,1:T(8,128)(2,1)S(1)} collective-permute-done((bf16[512,256]{0,1:T(8,128)(2,1)S(1)}, bf16[512,256]{0,1:T(8,128)(2,1)S(1)}, u32[]{:S(2)}, u32[]{:S(2)}) %collective-permute-start.35) | collective-permute-done | bytes 262176 | tf_op jit(solution)/shard_map/ppermute | solution.py:114
  254.0 4.7 %collective-permute-done.33 = bf16[256,256]{0,1:T(8,128)(2,1)S(1)} collective-permute-done((bf16[256,256]{0,1:T(8,128)(2,1)S(1)}, bf16[256,256]{0,1:T(8,128)(2,1)S(1)}, u32[]{:S(2)}, u32[]{:S(2)}) %collective-permute-start.33) | collective-permute-done | bytes 131104 | tf_op jit(solution)/shard_map/ppermute | solution.py:114
  258.7 3.2 %collective-permute-start.36 = (bf16[256,256]{0,1:T(8,128)(2,1)S(1)}, bf16[256,256]{0,1:T(8,128)(2,1)S(1)}, u32[]{:S(2)}, u32[]{:S(2)}) collective-permute-start(bf16[256,256]{0,1:T(8,128)(2,1)S(1)} %slice.513), channel_id=1, source_target_pairs={{0,16},{1,17},{2,18},{3,19},{4,20},{5,21},{6,22},{7,23},{8,24},{9,... | collective-permute-start | bytes 393224 | tf_op jit(solution)/shard_map/ppermute | solution.py:114
  262.0 5.6 %collective-permute-start.39 = (bf16[256,256]{0,1:T(8,128)(2,1)S(1)}, bf16[256,256]{0,1:T(8,128)(2,1)S(1)}, u32[]{:S(2)}, u32[]{:S(2)}) collective-permute-start(bf16[256,256]{0,1:T(8,128)(2,1)S(1)} %slice.512), channel_id=1, source_target_pairs={{0,16},{1,17},{2,18},{3,19},{4,20},{5,21},{6,22},{7,23},{8,24},{9,... | collective-permute-start | bytes 393224 | tf_op jit(solution)/shard_map/ppermute | solution.py:114
  268.5 3.5 %collective-permute-done.39 = bf16[256,256]{0,1:T(8,128)(2,1)S(1)} collective-permute-done((bf16[256,256]{0,1:T(8,128)(2,1)S(1)}, bf16[256,256]{0,1:T(8,128)(2,1)S(1)}, u32[]{:S(2)}, u32[]{:S(2)}) %collective-permute-start.39) | collective-permute-done | bytes 131104 | tf_op jit(solution)/shard_map/ppermute | solution.py:114
  (168 shorter events, 55.0 us)
Async XLA Ops:
  4.6 23.6 %collective-permute-start = (bf16[256,1792]{1,0:T(8,128)(2,1)}, bf16[256,1792]{1,0:T(8,128)(2,1)}, u32[]{:S(2)}, u32[]{:S(2)}) collective-permute-start(bf16[256,1792]{1,0:T(8,128)(2,1)} %get-tuple-element.43), channel_id=1, source_target_pairs={{0,2},{1,3},{2,0},{3,1},{4,6},{5,7},{6,4},{7,5},{8,10},{9,11},{10,... | collective-permute-start | bytes 2752520 | tf_op jit(solution)/shard_map/ppermute | solution.py:114
  16.2 52.0 %collective-permute-start.4 = (bf16[448,1024]{1,0:T(8,128)(2,1)}, bf16[448,1024]{1,0:T(8,128)(2,1)}, u32[]{:S(2)}, u32[]{:S(2)}) collective-permute-start(bf16[448,1024]{1,0:T(8,128)(2,1)} %get-tuple-element.45), channel_id=1, source_target_pairs={{0,4},{1,5},{2,6},{3,7},{4,0},{5,1},{6,2},{7,3},{8,12},{9,13},{10,... | collective-permute-start | bytes 2752520 | tf_op jit(solution)/shard_map/ppermute | solution.py:114
  30.8 40.4 %collective-permute-start.1 = (bf16[256,1792]{1,0:T(8,128)(2,1)}, bf16[256,1792]{1,0:T(8,128)(2,1)}, u32[]{:S(2)}, u32[]{:S(2)}) collective-permute-start(bf16[256,1792]{1,0:T(8,128)(2,1)} %get-tuple-element.87), channel_id=1, source_target_pairs={{0,0},{1,8},{2,2},{3,10},{4,4},{5,12},{6,6},{7,14},{8,1},{9,9},{10... | collective-permute-start | bytes 2752520 | tf_op jit(solution)/shard_map/ppermute | solution.py:114
  39.2 38.6 %collective-permute-start.2 = (bf16[256,1792]{1,0:T(8,128)(2,1)}, bf16[256,1792]{1,0:T(8,128)(2,1)}, u32[]{:S(2)}, u32[]{:S(2)}) collective-permute-start(bf16[256,1792]{1,0:T(8,128)(2,1)} %get-tuple-element.86), channel_id=1, source_target_pairs={{0,16},{1,24},{2,18},{3,26},{4,20},{5,28},{6,22},{7,30},{8,17},{9,... | collective-permute-start | bytes 2752520 | tf_op jit(solution)/shard_map/ppermute | solution.py:114
  66.8 17.0 %collective-permute-start.24 = (bf16[256,1792]{1,0:T(8,128)(2,1)S(1)}, bf16[256,1792]{1,0:T(8,128)(2,1)S(1)}, u32[]{:S(2)}, u32[]{:S(2)}) collective-permute-start(bf16[256,1792]{1,0:T(8,128)(2,1)S(1)} %get-tuple-element.58), channel_id=1, source_target_pairs={{0,2},{1,3},{2,0},{3,1},{4,6},{5,7},{6,4},{7,5},{8,10},{9,11},{10,... | collective-permute-start | bytes 2752520 | tf_op jit(solution)/shard_map/ppermute | solution.py:114
  68.3 17.0 %collective-permute-start.9 = (bf16[448,1024]{1,0:T(8,128)(2,1)}, bf16[448,1024]{1,0:T(8,128)(2,1)S(1)}, u32[]{:S(2)}, u32[]{:S(2)}) collective-permute-start(bf16[448,1024]{1,0:T(8,128)(2,1)} %get-tuple-element.47), channel_id=1, source_target_pairs={{0,4},{1,5},{2,6},{3,7},{4,0},{5,1},{6,2},{7,3},{8,12},{9,13},{10,... | collective-permute-start | bytes 2752520 | tf_op jit(solution)/shard_map/ppermute | solution.py:114
  71.1 17.3 %collective-permute-start.5 = (bf16[2,448,512]{2,1,0:T(8,128)(2,1)S(1)}, bf16[2,448,512]{2,1,0:T(8,128)(2,1)S(1)}, u32[]{:S(2)}, u32[]{:S(2)}) collective-permute-start(bf16[2,448,512]{2,1,0:T(8,128)(2,1)S(1)} %pad_maximum_fusion.4), channel_id=1, source_target_pairs={{0,1},{1,0},{2,3},{3,2},{4,5},{5,4},{6,7},{7,6},{8,9},{9,8},{10,11... | collective-permute-start | bytes 2752520 | tf_op jit(solution)/shard_map/ppermute | solution.py:114
  79.0 75.1 %collective-permute-start.3 = (bf16[512,1792]{1,0:T(8,128)(2,1)S(1)}, bf16[512,1792]{1,0:T(8,128)(2,1)S(1)}, u32[]{:S(2)}, u32[]{:S(2)}) collective-permute-start(bf16[512,1792]{1,0:T(8,128)(2,1)S(1)} %constant_dynamic-update-slice_fusion), channel_id=1, source_target_pairs={{0,1},{1,0},{2,3},{3,2},{4,5},{5,4},{6,7},{7,6},{8,9},{9,8},{10,11... | collective-permute-start | bytes 5505032 | tf_op jit(solution)/shard_map/ppermute | solution.py:114
  86.1 42.0 %collective-permute-start.26 = (bf16[256,1792]{1,0:T(8,128)(2,1)S(1)}, bf16[256,1792]{1,0:T(8,128)(2,1)S(1)}, u32[]{:S(2)}, u32[]{:S(2)}) collective-permute-start(bf16[256,1792]{1,0:T(8,128)(2,1)S(1)} %get-tuple-element.61), channel_id=1, source_target_pairs={{0,16},{1,24},{2,18},{3,26},{4,20},{5,28},{6,22},{7,30},{8,17},{9,... | collective-permute-start | bytes 2752520 | tf_op jit(solution)/shard_map/ppermute | solution.py:114
  86.8 44.3 %collective-permute-start.14 = (bf16[448,1024]{1,0:T(8,128)(2,1)S(1)}, bf16[448,1024]{1,0:T(8,128)(2,1)S(1)}, u32[]{:S(2)}, u32[]{:S(2)}) collective-permute-start(bf16[448,1024]{1,0:T(8,128)(2,1)S(1)} %copy-done.3), channel_id=1, source_target_pairs={{0,4},{1,5},{2,6},{3,7},{4,0},{5,1},{6,2},{7,3},{8,12},{9,13},{10,... | collective-permute-start | bytes 2752520 | tf_op jit(solution)/shard_map/ppermute | solution.py:114
  88.4 39.9 %collective-permute-start.10 = (bf16[2,448,512]{2,1,0:T(8,128)(2,1)S(1)}, bf16[2,448,512]{2,1,0:T(8,128)(2,1)S(1)}, u32[]{:S(2)}, u32[]{:S(2)}) collective-permute-start(bf16[2,448,512]{2,1,0:T(8,128)(2,1)S(1)} %pad_maximum_fusion.6), channel_id=1, source_target_pairs={{0,1},{1,0},{2,3},{3,2},{4,5},{5,4},{6,7},{7,6},{8,9},{9,8},{10,11... | collective-permute-start | bytes 2752520 | tf_op jit(solution)/shard_map/ppermute | solution.py:114
  128.2 69.3 %collective-permute-start.27 = (bf16[512,1792]{1,0:T(8,128)(2,1)S(1)}, bf16[512,1792]{1,0:T(8,128)(2,1)S(1)}, u32[]{:S(2)}, u32[]{:S(2)}) collective-permute-start(bf16[512,1792]{1,0:T(8,128)(2,1)S(1)} %constant_dynamic-update-slice_fusion.2), channel_id=1, source_target_pairs={{0,1},{1,0},{2,3},{3,2},{4,5},{5,4},{6,7},{7,6},{8,9},{9,8},{10,11... | collective-permute-start | bytes 5505032 | tf_op jit(solution)/shard_map/ppermute | solution.py:114
  131.1 22.8 %collective-permute-start.19 = (bf16[448,1024]{1,0:T(8,128)(2,1)S(1)}, bf16[448,1024]{1,0:T(8,128)(2,1)S(1)}, u32[]{:S(2)}, u32[]{:S(2)}) collective-permute-start(bf16[448,1024]{1,0:T(8,128)(2,1)S(1)} %copy-done.2), channel_id=1, source_target_pairs={{0,4},{1,5},{2,6},{3,7},{4,0},{5,1},{6,2},{7,3},{8,12},{9,13},{10,... | collective-permute-start | bytes 2752520 | tf_op jit(solution)/shard_map/ppermute | solution.py:114
  132.9 23.2 %collective-permute-start.15 = (bf16[2,448,512]{2,1,0:T(8,128)(2,1)S(1)}, bf16[2,448,512]{2,1,0:T(8,128)(2,1)S(1)}, u32[]{:S(2)}, u32[]{:S(2)}) collective-permute-start(bf16[2,448,512]{2,1,0:T(8,128)(2,1)S(1)} %pad_maximum_fusion.8), channel_id=1, source_target_pairs={{0,1},{1,0},{2,3},{3,2},{4,5},{5,4},{6,7},{7,6},{8,9},{9,8},{10,11... | collective-permute-start | bytes 2752520 | tf_op jit(solution)/shard_map/ppermute | solution.py:114
  154.1 38.7 %collective-permute-start.20 = (bf16[2,448,512]{2,1,0:T(8,128)(2,1)S(1)}, bf16[2,448,512]{2,1,0:T(8,128)(2,1)S(1)}, u32[]{:S(2)}, u32[]{:S(2)}) collective-permute-start(bf16[2,448,512]{2,1,0:T(8,128)(2,1)S(1)} %pad_maximum_fusion.10), channel_id=1, source_target_pairs={{0,1},{1,0},{2,3},{3,2},{4,5},{5,4},{6,7},{7,6},{8,9},{9,8},{10,11... | collective-permute-start | bytes 2752520 | tf_op jit(solution)/shard_map/ppermute | solution.py:114
  155.4 35.6 %collective-permute-start.11 = (bf16[2,512,256]{1,2,0:T(8,128)(2,1)S(1)}, bf16[2,512,256]{1,2,0:T(8,128)(2,1)S(1)}, u32[]{:S(2)}, u32[]{:S(2)}) collective-permute-start(bf16[2,512,256]{1,2,0:T(8,128)(2,1)S(1)} %pad_maximum_fusion.13), channel_id=1, source_target_pairs={{0,2},{1,3},{2,0},{3,1},{4,6},{5,7},{6,4},{7,5},{8,10},{9,11},{10,... | collective-permute-start | bytes 1572872 | tf_op jit(solution)/shard_map/ppermute | solution.py:114
  160.1 20.9 %collective-permute-start.6 = (bf16[2,512,256]{1,2,0:T(8,128)(2,1)S(1)}, bf16[2,512,256]{1,2,0:T(8,128)(2,1)S(1)}, u32[]{:S(2)}, u32[]{:S(2)}) collective-permute-start(bf16[2,512,256]{1,2,0:T(8,128)(2,1)S(1)} %pad_maximum_fusion.12), channel_id=1, source_target_pairs={{0,2},{1,3},{2,0},{3,1},{4,6},{5,7},{6,4},{7,5},{8,10},{9,11},{10,... | collective-permute-start | bytes 1572872 | tf_op jit(solution)/shard_map/ppermute | solution.py:114
  181.7 20.9 %collective-permute-start.16 = (bf16[2,512,256]{1,2,0:T(8,128)(2,1)S(1)}, bf16[2,512,256]{1,2,0:T(8,128)(2,1)S(1)}, u32[]{:S(2)}, u32[]{:S(2)}) collective-permute-start(bf16[2,512,256]{1,2,0:T(8,128)(2,1)S(1)} %pad_maximum_fusion.14), channel_id=1, source_target_pairs={{0,2},{1,3},{2,0},{3,1},{4,6},{5,7},{6,4},{7,5},{8,10},{9,11},{10,... | collective-permute-start | bytes 1572872 | tf_op jit(solution)/shard_map/ppermute | solution.py:114
  189.4 12.8 %collective-permute-start.8 = (bf16[256,256]{0,1:T(8,128)(2,1)S(1)}, bf16[256,256]{0,1:T(8,128)(2,1)S(1)}, u32[]{:S(2)}, u32[]{:S(2)}) collective-permute-start(bf16[256,256]{0,1:T(8,128)(2,1)S(1)} %slice.519), channel_id=1, source_target_pairs={{0,16},{1,17},{2,18},{3,19},{4,20},{5,21},{6,22},{7,23},{8,24},{9,... | collective-permute-start | bytes 393224 | tf_op jit(solution)/shard_map/ppermute | solution.py:114
  191.2 11.2 %collective-permute-start.12 = (bf16[512,256]{0,1:T(8,128)(2,1)S(1)}, bf16[512,256]{0,1:T(8,128)(2,1)S(1)}, u32[]{:S(2)}, u32[]{:S(2)}) collective-permute-start(bf16[512,256]{0,1:T(8,128)(2,1)S(1)} %select_convert_fusion.6), channel_id=1, source_target_pairs={{0,8},{1,9},{2,10},{3,11},{4,12},{5,13},{6,14},{7,15},{8,0},{9,1},... | collective-permute-start | bytes 786440 | tf_op jit(solution)/shard_map/ppermute | solution.py:114
  195.7 14.9 %collective-permute-start.21 = (bf16[2,512,256]{1,2,0:T(8,128)(2,1)S(1)}, bf16[2,512,256]{1,2,0:T(8,128)(2,1)S(1)}, u32[]{:S(2)}, u32[]{:S(2)}) collective-permute-start(bf16[2,512,256]{1,2,0:T(8,128)(2,1)S(1)} %pad_maximum_fusion.15), channel_id=1, source_target_pairs={{0,2},{1,3},{2,0},{3,1},{4,6},{5,7},{6,4},{7,5},{8,10},{9,11},{10,... | collective-permute-start | bytes 1572872 | tf_op jit(solution)/shard_map/ppermute | solution.py:114
  203.4 18.5 %collective-permute-start.28 = (bf16[2,512,256]{1,2,0:T(8,128)(2,1)S(1)}, bf16[2,512,256]{1,2,0:T(8,128)(2,1)S(1)}, u32[]{:S(2)}, u32[]{:S(2)}) collective-permute-start(bf16[2,512,256]{1,2,0:T(8,128)(2,1)S(1)} %pad_maximum_fusion.16), channel_id=1, source_target_pairs={{0,2},{1,3},{2,0},{3,1},{4,6},{5,7},{6,4},{7,5},{8,10},{9,11},{10,... | collective-permute-start | bytes 1572872 | tf_op jit(solution)/shard_map/ppermute | solution.py:114
  211.4 21.7 %collective-permute-start.31 = (bf16[2,512,256]{1,2,0:T(8,128)(2,1)S(1)}, bf16[2,512,256]{1,2,0:T(8,128)(2,1)S(1)}, u32[]{:S(2)}, u32[]{:S(2)}) collective-permute-start(bf16[2,512,256]{1,2,0:T(8,128)(2,1)S(1)} %pad_maximum_fusion.17), channel_id=1, source_target_pairs={{0,2},{1,3},{2,0},{3,1},{4,6},{5,7},{6,4},{7,5},{8,10},{9,11},{10,... | collective-permute-start | bytes 1572872 | tf_op jit(solution)/shard_map/ppermute | solution.py:114
  222.6 11.2 %collective-permute-start.13 = (bf16[256,256]{0,1:T(8,128)(2,1)S(1)}, bf16[256,256]{0,1:T(8,128)(2,1)S(1)}, u32[]{:S(2)}, u32[]{:S(2)}) collective-permute-start(bf16[256,256]{0,1:T(8,128)(2,1)S(1)} %slice.518), channel_id=1, source_target_pairs={{0,16},{1,17},{2,18},{3,19},{4,20},{5,21},{6,22},{7,23},{8,24},{9,... | collective-permute-start | bytes 393224 | tf_op jit(solution)/shard_map/ppermute | solution.py:114
  224.1 20.3 %collective-permute-start.34 = (bf16[2,512,256]{1,2,0:T(8,128)(2,1)S(1)}, bf16[2,512,256]{1,2,0:T(8,128)(2,1)S(1)}, u32[]{:S(2)}, u32[]{:S(2)}) collective-permute-start(bf16[2,512,256]{1,2,0:T(8,128)(2,1)S(1)} %pad_maximum_fusion.18), channel_id=1, source_target_pairs={{0,2},{1,3},{2,0},{3,1},{4,6},{5,7},{6,4},{7,5},{8,10},{9,11},{10,... | collective-permute-start | bytes 1572872 | tf_op jit(solution)/shard_map/ppermute | solution.py:114
  233.9 11.1 %collective-permute-start.18 = (bf16[256,256]{0,1:T(8,128)(2,1)S(1)}, bf16[256,256]{0,1:T(8,128)(2,1)S(1)}, u32[]{:S(2)}, u32[]{:S(2)}) collective-permute-start(bf16[256,256]{0,1:T(8,128)(2,1)S(1)} %slice.517), channel_id=1, source_target_pairs={{0,16},{1,17},{2,18},{3,19},{4,20},{5,21},{6,22},{7,23},{8,24},{9,... | collective-permute-start | bytes 393224 | tf_op jit(solution)/shard_map/ppermute | solution.py:114
  235.3 10.0 %collective-permute-start.23 = (bf16[256,256]{0,1:T(8,128)(2,1)S(1)}, bf16[256,256]{0,1:T(8,128)(2,1)S(1)}, u32[]{:S(2)}, u32[]{:S(2)}) collective-permute-start(bf16[256,256]{0,1:T(8,128)(2,1)S(1)} %slice.516), channel_id=1, source_target_pairs={{0,16},{1,17},{2,18},{3,19},{4,20},{5,21},{6,22},{7,23},{8,24},{9,... | collective-permute-start | bytes 393224 | tf_op jit(solution)/shard_map/ppermute | solution.py:114
  236.9 16.8 %collective-permute-start.37 = (bf16[2,512,256]{1,2,0:T(8,128)(2,1)S(1)}, bf16[2,512,256]{1,2,0:T(8,128)(2,1)S(1)}, u32[]{:S(2)}, u32[]{:S(2)}) collective-permute-start(bf16[2,512,256]{1,2,0:T(8,128)(2,1)S(1)} %pad_maximum_fusion.19), channel_id=1, source_target_pairs={{0,2},{1,3},{2,0},{3,1},{4,6},{5,7},{6,4},{7,5},{8,10},{9,11},{10,... | collective-permute-start | bytes 1572872 | tf_op jit(solution)/shard_map/ppermute | solution.py:114
  244.5 8.9 %collective-permute-start.35 = (bf16[512,256]{0,1:T(8,128)(2,1)S(1)}, bf16[512,256]{0,1:T(8,128)(2,1)S(1)}, u32[]{:S(2)}, u32[]{:S(2)}) collective-permute-start(bf16[512,256]{0,1:T(8,128)(2,1)S(1)} %select_convert_fusion.1), channel_id=1, source_target_pairs={{0,8},{1,9},{2,10},{3,11},{4,12},{5,13},{6,14},{7,15},{8,0},{9,1},... | collective-permute-start | bytes 786440 | tf_op jit(solution)/shard_map/ppermute | solution.py:114
  249.3 9.3 %collective-permute-start.33 = (bf16[256,256]{0,1:T(8,128)(2,1)S(1)}, bf16[256,256]{0,1:T(8,128)(2,1)S(1)}, u32[]{:S(2)}, u32[]{:S(2)}) collective-permute-start(bf16[256,256]{0,1:T(8,128)(2,1)S(1)} %slice.514), channel_id=1, source_target_pairs={{0,16},{1,17},{2,18},{3,19},{4,20},{5,21},{6,22},{7,23},{8,24},{9,... | collective-permute-start | bytes 393224 | tf_op jit(solution)/shard_map/ppermute | solution.py:114
  258.7 9.8 %collective-permute-start.36 = (bf16[256,256]{0,1:T(8,128)(2,1)S(1)}, bf16[256,256]{0,1:T(8,128)(2,1)S(1)}, u32[]{:S(2)}, u32[]{:S(2)}) collective-permute-start(bf16[256,256]{0,1:T(8,128)(2,1)S(1)} %slice.513), channel_id=1, source_target_pairs={{0,16},{1,17},{2,18},{3,19},{4,20},{5,21},{6,22},{7,23},{8,24},{9,... | collective-permute-start | bytes 393224 | tf_op jit(solution)/shard_map/ppermute | solution.py:114
  262.0 10.0 %collective-permute-start.39 = (bf16[256,256]{0,1:T(8,128)(2,1)S(1)}, bf16[256,256]{0,1:T(8,128)(2,1)S(1)}, u32[]{:S(2)}, u32[]{:S(2)}) collective-permute-start(bf16[256,256]{0,1:T(8,128)(2,1)S(1)} %slice.512), channel_id=1, source_target_pairs={{0,16},{1,17},{2,18},{3,19},{4,20},{5,21},{6,22},{7,23},{8,24},{9,... | collective-permute-start | bytes 393224 | tf_op jit(solution)/shard_map/ppermute | solution.py:114
  (14 other events, 83.2 us)

commit v4 on v3

v4 whole, which is shorter than its diff:
```python
import jax
import jax.numpy as jnp
from jax import lax
from jax.experimental import pallas as pl
from jax.experimental.pallas import tpu as pltpu
from jax.sharding import PartitionSpec as P

AXES = ("fsdp", "tp")
ROW_CHUNKS = 2
COL_CHUNKS = 4


def adam(where, chunks, args, previous):
    rows, cols = args[0].shape
    width = cols // 4 // COL_CHUNKS
    step = max(s for s in range(16, 449, 16) if rows % s == 0)
    tiles = rows // step
    count = len(chunks)
    each = 4 * tiles

    def kernel(where_ref, master_ref, one_ref, two_ref, grad_ref, *refs):
        new_master_ref, new_one_ref, new_two_ref = refs[-3 - count : -count]
        grad = grad_ref[...].astype(jnp.float32)
        new_one = 0.9 * one_ref[...] + 0.1 * grad
        new_two = 0.95 * two_ref[...] + 0.05 * grad * grad
        new_master = master_ref[...] - 0.001 * new_one / (jnp.sqrt(new_two) + 1e-08)
        new_one_ref[...] = new_one
        new_two_ref[...] = new_two
        new_master_ref[...] = new_master
        weight = new_master.astype(jnp.bfloat16)
        for k, weight_ref in enumerate(refs[-count:]):

            @pl.when(pl.program_id(0) // each == k)
            def _():
                weight_ref[...] = weight

    def at(i, w):
        j = i % each // tiles
        return i % tiles, j * COL_CHUNKS + chunks[0] + i // each

    def piece_at(k):
        def index(i, w):
            i = jnp.clip(i - k * each, 0, each - 1)
            j = i // tiles
            return i % tiles, 2 * ((j % 2) ^ w[1]) + ((j // 2) ^ w[0])

        return index

    source = pl.BlockSpec((step, width), at)
    target = pl.BlockSpec((step, width), at)
    pieces = [pl.BlockSpec((step, width), piece_at(k)) for k in range(count)]
    full = jax.ShapeDtypeStruct((rows, cols), jnp.float32)
    size = rows * cols * count // COL_CHUNKS
    out = pl.pallas_call(
        kernel,
        grid_spec=pltpu.PrefetchScalarGridSpec(
            num_scalar_prefetch=1,
            grid=(count * each,),
            in_specs=[source] * 4 + [pl.BlockSpec(memory_space=pl.ANY)] * len(previous),
            out_specs=[target] * 3 + pieces,
        ),
        out_shape=[full] * 3 + [jax.ShapeDtypeStruct((rows, cols // COL_CHUNKS), jnp.bfloat16)] * count,
        input_output_aliases={5 + i: i for i in range(len(previous))},
        compiler_params=pltpu.CompilerParams(vmem_limit_bytes=60 * 1024 * 1024),
        cost_estimate=pl.CostEstimate(flops=size, bytes_accessed=size, transcendentals=0),
        name="adam",
    )(where, *args, *previous)
    return out[:3], out[3:]


def pack(where, act, xs):
    rows, cols = act.shape
    run = cols // xs // 2
    part = rows // ROW_CHUNKS

    def kernel(where_ref, act_ref, *out_refs):
        for y in range(2):
            for x in range(xs):

                @pl.when((where_ref[0] == y) & (where_ref[2] == x))
                def _():
                    for m in range(ROW_CHUNKS):
                        for s in range(2):
                            for d in range(xs):
                                at = (2 * (x ^ d) + (y ^ s)) * run
                                out_refs[2 * m + s][:, d * run : (d + 1) * run] = act_ref[
                                    m * part : (m + 1) * part, at : at + run
                                ]

    out = pl.pallas_call(
        kernel,
        in_specs=[pl.BlockSpec(memory_space=pltpu.SMEM), pl.BlockSpec(memory_space=pltpu.VMEM)],
        out_specs=[pl.BlockSpec(memory_space=pltpu.VMEM)] * (2 * ROW_CHUNKS),
        out_shape=[jax.ShapeDtypeStruct((part, cols // 2), act.dtype)] * (2 * ROW_CHUNKS),
        compiler_params=pltpu.CompilerParams(vmem_limit_bytes=32 * 1024 * 1024),
        cost_estimate=pl.CostEstimate(flops=0, bytes_accessed=4 * rows * cols, transcendentals=0),
        name="pack",
    )(where, act)
    return out[0::2], out[1::2]


def swap_if(flag, low, high):
    return jnp.where(flag, high, low), jnp.where(flag, low, high)


def after(value, *done):
    return lax.optimization_barrier((value, *done))[0] if done else value


def local(master, moment_one, moment_two, gradient, hidden_act):
    fsdp, tp = lax.axis_size("fsdp"), lax.axis_size("tp")
    xs = fsdp // tp
    f, t = lax.axis_index("fsdp"), lax.axis_index("tp")
    z, x, y, c = f // xs, f % xs, t // 2, t % 2
    where = jnp.stack([y, c, x]).astype(jnp.int32)

    def permute(value, to):
        pairs = []
        for zi in range(tp):
            for xi in range(xs):
                for yi in range(2):
                    for ci in range(2):
                        zo, xo, yo, co = to(zi, xi, yi, ci)
                        pairs.append(((zi * xs + xi) * tp + 2 * yi + ci, (zo * xs + xo) * tp + 2 * yo + co))
        return lax.ppermute(value, AXES, pairs)

    rows = hidden_act.shape[0]
    part = rows // ROW_CHUNKS
    own, other = pack(where, hidden_act, xs)

    args = (master, moment_one, moment_two, gradient)
    updated, first = adam(where, [0], args, [])
    updated, rest = adam(where, list(range(1, COL_CHUNKS)), args, updated)
    pieces = [*first, *rest]
    flip = (c ^ (z % 2)) != 0
    crossed, tables = [], []
    theirs, moved, acts = [], [], []
    sends, backs, leaving, result = [], [], [], []

    def to_plane(m):
        send = other[m] if m == 0 else after(other[m], theirs[-1])
        theirs.append(permute(send, lambda z, x, y, c: (z, x, 1 - y, c)))
        pair = swap_if(((z // 2) ^ y) != 0, own[m], theirs[m])
        if m:
            pair = after(pair, moved[-1], crossed[1])
        got = [
            permute(data, lambda z, x, y, c: (2 * ((z // 2) ^ a) + c, x, y, z % 2)) for a, data in enumerate(pair)
        ]
        moved.append(got)

    def to_cores(m, *done):
        got = jnp.concatenate(after(moved[m], *done), axis=0)
        moved[m] = got
        acts.append((got, permute(got, lambda z, x, y, c: (z, x, y, 1 - c))))

    def gather(q, *done):
        piece = after(pieces[q], crossed[-1]) if q else pieces[q]
        parts = [piece] + [permute(piece, lambda z, x, y, c: (z, x ^ d, y, c)) for d in range(1, xs)]
        crossed.append(parts[-1])
        half = piece.shape[1] // 2
        parts = after(parts, *done)
        here = jnp.stack([p[:, :half] for p in parts])
        there = jnp.stack([p[:, half:] for p in parts])
        there = permute(there, lambda z, x, y, c: (z, x, y, 1 - c))
        tables.append(jnp.stack(swap_if(c != 0, here, there), axis=1).reshape(-1, half))

    def multiply(m, q):
        table = tables[q]
        half = table.shape[1] // 2
        totals = [jnp.dot(a, table, preferred_element_type=jnp.float32) for a in acts[m]]
        send = jnp.stack([total[:, half:].astype(jnp.bfloat16) for total in totals])
        if len(backs) >= 2:
            send = after(send, backs[-2])
        sends.append(send)
        backs.append(permute(send, lambda z, x, y, c: (z, x, 1 - y, c)))
        return [total[:, :half] for total in totals], len(backs) - 1

    def reduce(totals, j):
        back = after(backs[j], leaving[-1]) if leaving else backs[j]
        near, far = swap_if(flip, *[total + b for total, b in zip(totals, back)])
        back = permute(far.astype(jnp.bfloat16), lambda z, x, y, c: (z ^ 1, x, y, c))
        near = near + back
        send = near[part:].astype(jnp.bfloat16)
        leaving.append(send)
        back = permute(send, lambda z, x, y, c: (z ^ 2, x, y, c))
        result.append((near[:part] + back).astype(jnp.bfloat16))

    gather(0)
    gather(1)
    to_plane(0)
    to_plane(1)
    to_cores(0)
    jobs = [multiply(0, 0), multiply(0, 1)]
    gather(2, sends[0], sends[1])
    gather(3, backs[0])
    jobs.append(multiply(0, 2))
    to_cores(1, backs[1])
    jobs.append(multiply(0, 3))
    jobs += [multiply(1, q) for q in range(COL_CHUNKS)]
    for job in jobs:
        reduce(*job)
    result = [jnp.concatenate(result[i : i + COL_CHUNKS], axis=1) for i in range(0, len(result), COL_CHUNKS)]
    decoded = jnp.concatenate(result, axis=0)
    return (*updated, decoded)


def solution(mesh):
    placed = (
        P(("fsdp", "tp"), None),
        P(("fsdp", "tp"), None),
        P(("fsdp", "tp"), None),
        P(("fsdp", "tp"), None),
        P("fsdp", "tp"),
    )
    return jax.shard_map(
        local,
        mesh=mesh,
        in_specs=placed,
        out_specs=(
            P(("fsdp", "tp"), None),
            P(("fsdp", "tp"), None),
            P(("fsdp", "tp"), None),
            P("fsdp", "tp"),
        ),
        check_vma=False,
    )
```

time: 275 us -> 256 us (0.931)
  Pallas kernels: 35.2 us -> 27.4 us
  waiting for transfers between devices: 147 us -> 142 us
    pallas_call x2, Pallas kernels: 33.4 us -> 25.6 us  [adam(): pl.pallas_call(kernel, grid_spec=pltpu.PrefetchScalarGridSpec(num_scalar_...]
    ppermute x40, waiting for transfers between devices: 147 us -> 142 us  [permute(): return lax.ppermute(value, AXES, pairs)]
  transfers between devices with their start and end apart: 40 -> 40, of which waited for: 21 -> 22; matrix products, arithmetic and copies ran while one was open for 12% -> 12% of each run, Pallas kernels for 12% -> 10%
where the time goes in v4:
time: 256 us; the launch traced here: 255 us
  waiting for transfers between devices  142 us (55%)
  starting transfers between devices  51 us (20%)
  Pallas kernels  27.4 us (11%)
  matrix products  18.7 us (7%)
  local copies, waits for them, and re-layouts  7.68 us (3%)
  other arithmetic  6.82 us (3%)
    ppermute x40, waiting for transfers between devices, permute(): return lax.ppermute(value, AXES, pairs)  142 us
    ppermute x40, starting transfers between devices, permute(): return lax.ppermute(value, AXES, pairs)  51 us
    pallas_call x2, Pallas kernels, adam(): pl.pallas_call(kernel, grid_spec=pltpu.PrefetchScalarGridSpec(num_scalar_...  25.6 us
    dot_general x16, matrix products, multiply(): jnp.dot(a, table, preferred_element_type=jnp.float32)  18.7 us
  transfers between devices with their start and end apart: 40, of which 22 were waited for; matrix products, arithmetic and copies ran while one was open for 12% of the time, Pallas kernels for 10%

profile of v4, /device:TPU:0, one launch (start us, length us, event | category | flops | bytes accessed | tf_op | source)
XLA Modules:
  0.0 255.4 jit_solution(10241115145438602860)
XLA Ops:
  0.7 2.0 copy-done
  4.6 3.0 %collective-permute-start = (bf16[256,1792]{1,0:T(8,128)(2,1)}, bf16[256,1792]{1,0:T(8,128)(2,1)}, u32[]{:S(2)}, u32[]{:S(2)}) collective-permute-start(bf16[256,1792]{1,0:T(8,128)(2,1)} %get-tuple-element.49), channel_id=1, source_target_pairs={{0,2},{1,3},{2,0},{3,1},{4,6},{5,7},{6,4},{7,5},{8,10},{9,11},{10,... | collective-permute-start | bytes 2752520 | tf_op jit(solution)/shard_map/ppermute | solution.py:125
  7.5 7.0 %adam.2 = (f32[448,4096]{1,0:T(8,128)}, f32[448,4096]{1,0:T(8,128)}, f32[448,4096]{1,0:T(8,128)}, bf16[448,1024]{1,0:T(8,128)(2,1)}) custom-call(s32[3]{0:T(128)} %copy-done.1, f32[448,4096]{1,0:T(8,128)} %master_ref.3, f32[448,4096]{1,0:T(8,128)} %one_ref.3, f32[448,4096]{1,0:T(8,128)} %two_ref.3, bf16[448,4096]{1,0:T(8,128)(2,1)} %grad_ref.3), custom_call_target="tpu_custom_call" | custom-call | flops 458752 | bytes 458752 | tf_op jit(solution)/shard_map/adam/pallas_call | solution.py:54
  16.0 18.6 %adam.3 = (f32[448,4096]{1,0:T(8,128)}, f32[448,4096]{1,0:T(8,128)}, f32[448,4096]{1,0:T(8,128)}, bf16[448,1024]{1,0:T(8,128)(2,1)}, bf16[448,1024]{1,0:T(8,128)(2,1)}, /*index=5*/bf16[448,1024]{1,0:T(8,128)(2,1)}) custom-call(s32[3]{0:T(128)} %copy-done.1, f32[448,4096]{1,0:T(8,128)} %master_ref.3, ...), custom_call_target="tpu_custom_call", output_to_operand_aliasing={{0}: (5, {}), {1}: (6, {}), {2}: (7, {})} | custom-call | flops 1376256 | bytes 1376256 | tf_op jit(solution)/shard_map/adam/pallas_call | solution.py:54
  38.5 2.7 %collective-permute-start.2 = (bf16[256,1792]{1,0:T(8,128)(2,1)S(1)}, bf16[256,1792]{1,0:T(8,128)(2,1)S(1)}, u32[]{:S(2)}, u32[]{:S(2)}) collective-permute-start(bf16[256,1792]{1,0:T(8,128)(2,1)S(1)} %get-tuple-element.98), channel_id=1, source_target_pairs={{0,16},{1,24},{2,18},{3,26},{4,20},{5,28},{6,22},{7,30},{8,17},{9,... | collective-permute-start | bytes 2752520 | tf_op jit(solution)/shard_map/ppermute | solution.py:125
  43.0 2.1 collective-permute-start.5
  45.2 12.2 %collective-permute-done.24 = bf16[256,1792]{1,0:T(8,128)(2,1)S(1)} collective-permute-done((bf16[256,1792]{1,0:T(8,128)(2,1)S(1)}, bf16[256,1792]{1,0:T(8,128)(2,1)S(1)}, u32[]{:S(2)}, u32[]{:S(2)}) %collective-permute-start.24) | collective-permute-done | bytes 917536 | tf_op jit(solution)/shard_map/ppermute | solution.py:125
  57.6 23.7 %collective-permute-done.2 = bf16[256,1792]{1,0:T(8,128)(2,1)S(1)} collective-permute-done((bf16[256,1792]{1,0:T(8,128)(2,1)S(1)}, bf16[256,1792]{1,0:T(8,128)(2,1)S(1)}, u32[]{:S(2)}, u32[]{:S(2)}) %collective-permute-start.2) | collective-permute-done | bytes 917536 | tf_op jit(solution)/shard_map/ppermute | solution.py:125
  82.5 4.0 %collective-permute-start.3 = (bf16[512,1792]{1,0:T(8,128)(2,1)S(1)}, bf16[512,1792]{1,0:T(8,128)(2,1)S(1)}, u32[]{:S(2)}, u32[]{:S(2)}) collective-permute-start(bf16[512,1792]{1,0:T(8,128)(2,1)S(1)} %constant_dynamic-update-slice_fusion), channel_id=1, source_target_pairs={{0,1},{1,0},{2,3},{3,2},{4,5},{5,4},{6,7},{7,6},{8,9},{9,8},{10,11... | collective-permute-start | bytes 5505032 | tf_op jit(solution)/shard_map/ppermute | solution.py:125
  89.0 2.2 collective-permute-done.10
  91.7 18.2 %collective-permute-done.14 = bf16[448,1024]{1,0:T(8,128)(2,1)S(1)} collective-permute-done((bf16[448,1024]{1,0:T(8,128)(2,1)S(1)}, bf16[448,1024]{1,0:T(8,128)(2,1)S(1)}, u32[]{:S(2)}, u32[]{:S(2)}) %collective-permute-start.14) | collective-permute-done | bytes 917536 | tf_op jit(solution)/shard_map/ppermute | solution.py:125
  116.6 5.7 %collective-permute-done.26 = bf16[256,1792]{1,0:T(8,128)(2,1)S(1)} collective-permute-done((bf16[256,1792]{1,0:T(8,128)(2,1)S(1)}, bf16[256,1792]{1,0:T(8,128)(2,1)S(1)}, u32[]{:S(2)}, u32[]{:S(2)}) %collective-permute-start.26) | collective-permute-done | bytes 917536 | tf_op jit(solution)/shard_map/ppermute | solution.py:125
  122.3 5.5 %collective-permute-done.11 = bf16[2,512,256]{1,2,0:T(8,128)(2,1)S(1)} collective-permute-done((bf16[2,512,256]{1,2,0:T(8,128)(2,1)S(1)}, bf16[2,512,256]{1,2,0:T(8,128)(2,1)S(1)}, u32[]{:S(2)}, u32[]{:S(2)}) %collective-permute-start.11) | collective-permute-done | bytes 524320 | tf_op jit(solution)/shard_map/ppermute | solution.py:125
  132.0 5.6 %collective-permute-done.6 = bf16[2,512,256]{1,2,0:T(8,128)(2,1)S(1)} collective-permute-done((bf16[2,512,256]{1,2,0:T(8,128)(2,1)S(1)}, bf16[2,512,256]{1,2,0:T(8,128)(2,1)S(1)}, u32[]{:S(2)}, u32[]{:S(2)}) %collective-permute-start.6) | collective-permute-done | bytes 524320 | tf_op jit(solution)/shard_map/ppermute | solution.py:125
  138.3 8.6 %collective-permute-done.7 = bf16[512,256]{0,1:T(8,128)(2,1)S(1)} collective-permute-done((bf16[512,256]{0,1:T(8,128)(2,1)S(1)}, bf16[512,256]{0,1:T(8,128)(2,1)S(1)}, u32[]{:S(2)}, u32[]{:S(2)}) %collective-permute-start.7) | collective-permute-done | bytes 262176 | tf_op jit(solution)/shard_map/ppermute | solution.py:125
  154.0 4.2 %collective-permute-done.12 = bf16[512,256]{0,1:T(8,128)(2,1)S(1)} collective-permute-done((bf16[512,256]{0,1:T(8,128)(2,1)S(1)}, bf16[512,256]{0,1:T(8,128)(2,1)S(1)}, u32[]{:S(2)}, u32[]{:S(2)}) %collective-permute-start.12) | collective-permute-done | bytes 262176 | tf_op jit(solution)/shard_map/ppermute | solution.py:125
  164.1 3.0 %collective-permute-done.16 = bf16[2,512,256]{1,2,0:T(8,128)(2,1)S(1)} collective-permute-done((bf16[2,512,256]{1,2,0:T(8,128)(2,1)S(1)}, bf16[2,512,256]{1,2,0:T(8,128)(2,1)S(1)}, u32[]{:S(2)}, u32[]{:S(2)}) %collective-permute-start.16) | collective-permute-done | bytes 524320 | tf_op jit(solution)/shard_map/ppermute | solution.py:125
  169.0 4.7 %collective-permute-done.17 = bf16[512,256]{0,1:T(8,128)(2,1)S(1)} collective-permute-done((bf16[512,256]{0,1:T(8,128)(2,1)S(1)}, bf16[512,256]{0,1:T(8,128)(2,1)S(1)}, u32[]{:S(2)}, u32[]{:S(2)}) %collective-permute-start.17) | collective-permute-done | bytes 262176 | tf_op jit(solution)/shard_map/ppermute | solution.py:125
  173.9 2.9 %collective-permute-done.21 = bf16[2,512,256]{1,2,0:T(8,128)(2,1)S(1)} collective-permute-done((bf16[2,512,256]{1,2,0:T(8,128)(2,1)S(1)}, bf16[2,512,256]{1,2,0:T(8,128)(2,1)S(1)}, u32[]{:S(2)}, u32[]{:S(2)}) %collective-permute-start.21) | collective-permute-done | bytes 524320 | tf_op jit(solution)/shard_map/ppermute | solution.py:125
  179.8 2.7 %collective-permute-start.18 = (bf16[256,256]{0,1:T(8,128)(2,1)S(1)}, bf16[256,256]{0,1:T(8,128)(2,1)S(1)}, u32[]{:S(2)}, u32[]{:S(2)}) collective-permute-start(bf16[256,256]{0,1:T(8,128)(2,1)S(1)} %slice.513), channel_id=1, source_target_pairs={{0,16},{1,17},{2,18},{3,19},{4,20},{5,21},{6,22},{7,23},{8,24},{9,... | collective-permute-start | bytes 393224 | tf_op jit(solution)/shard_map/ppermute | solution.py:125
  182.4 3.6 %collective-permute-done.22 = bf16[512,256]{0,1:T(8,128)(2,1)S(1)} collective-permute-done((bf16[512,256]{0,1:T(8,128)(2,1)S(1)}, bf16[512,256]{0,1:T(8,128)(2,1)S(1)}, u32[]{:S(2)}, u32[]{:S(2)}) %collective-permute-start.22) | collective-permute-done | bytes 262176 | tf_op jit(solution)/shard_map/ppermute | solution.py:125
  186.2 2.2 collective-permute-start.23
  195.4 15.0 %collective-permute-done.28 = bf16[2,512,256]{1,2,0:T(8,128)(2,1)S(1)} collective-permute-done((bf16[2,512,256]{1,2,0:T(8,128)(2,1)S(1)}, bf16[2,512,256]{1,2,0:T(8,128)(2,1)S(1)}, u32[]{:S(2)}, u32[]{:S(2)}) %collective-permute-start.28) | collective-permute-done | bytes 524320 | tf_op jit(solution)/shard_map/ppermute | solution.py:125
  210.8 4.3 %collective-permute-start.29 = (bf16[512,256]{0,1:T(8,128)(2,1)S(1)}, bf16[512,256]{0,1:T(8,128)(2,1)S(1)}, u32[]{:S(2)}, u32[]{:S(2)}) collective-permute-start(bf16[512,256]{0,1:T(8,128)(2,1)S(1)} %select_convert_fusion.3), channel_id=1, source_target_pairs={{0,8},{1,9},{2,10},{3,11},{4,12},{5,13},{6,14},{7,15},{8,0},{9,1},... | collective-permute-start | bytes 786440 | tf_op jit(solution)/shard_map/ppermute | solution.py:125
  216.8 3.0 %collective-permute-done.29 = bf16[512,256]{0,1:T(8,128)(2,1)S(1)} collective-permute-done((bf16[512,256]{0,1:T(8,128)(2,1)S(1)}, bf16[512,256]{0,1:T(8,128)(2,1)S(1)}, u32[]{:S(2)}, u32[]{:S(2)}) %collective-permute-start.29) | collective-permute-done | bytes 262176 | tf_op jit(solution)/shard_map/ppermute | solution.py:125
  220.2 1.8 collective-permute-start.32
  223.7 5.1 %collective-permute-done.32 = bf16[512,256]{0,1:T(8,128)(2,1)S(1)} collective-permute-done((bf16[512,256]{0,1:T(8,128)(2,1)S(1)}, bf16[512,256]{0,1:T(8,128)(2,1)S(1)}, u32[]{:S(2)}, u32[]{:S(2)}) %collective-permute-start.32) | collective-permute-done | bytes 262176 | tf_op jit(solution)/shard_map/ppermute | solution.py:125
  233.6 5.2 %collective-permute-done.35 = bf16[512,256]{0,1:T(8,128)(2,1)S(1)} collective-permute-done((bf16[512,256]{0,1:T(8,128)(2,1)S(1)}, bf16[512,256]{0,1:T(8,128)(2,1)S(1)}, u32[]{:S(2)}, u32[]{:S(2)}) %collective-permute-start.35) | collective-permute-done | bytes 262176 | tf_op jit(solution)/shard_map/ppermute | solution.py:125
  239.4 4.2 %collective-permute-done.33 = bf16[256,256]{0,1:T(8,128)(2,1)S(1)} collective-permute-done((bf16[256,256]{0,1:T(8,128)(2,1)S(1)}, bf16[256,256]{0,1:T(8,128)(2,1)S(1)}, u32[]{:S(2)}, u32[]{:S(2)}) %collective-permute-start.33) | collective-permute-done | bytes 131104 | tf_op jit(solution)/shard_map/ppermute | solution.py:125
  243.7 2.7 %collective-permute-done.38 = bf16[512,256]{0,1:T(8,128)(2,1)S(1)} collective-permute-done((bf16[512,256]{0,1:T(8,128)(2,1)S(1)}, bf16[512,256]{0,1:T(8,128)(2,1)S(1)}, u32[]{:S(2)}, u32[]{:S(2)}) %collective-permute-start.38) | collective-permute-done | bytes 262176 | tf_op jit(solution)/shard_map/ppermute | solution.py:125
  246.6 2.2 collective-permute-start.39
  249.7 4.2 %collective-permute-done.39 = bf16[256,256]{0,1:T(8,128)(2,1)S(1)} collective-permute-done((bf16[256,256]{0,1:T(8,128)(2,1)S(1)}, bf16[256,256]{0,1:T(8,128)(2,1)S(1)}, u32[]{:S(2)}, u32[]{:S(2)}) %collective-permute-start.39) | collective-permute-done | bytes 131104 | tf_op jit(solution)/shard_map/ppermute | solution.py:125
  (164 shorter events, 61.8 us)
Async XLA Ops:
  4.6 31.3 %collective-permute-start = (bf16[256,1792]{1,0:T(8,128)(2,1)}, bf16[256,1792]{1,0:T(8,128)(2,1)}, u32[]{:S(2)}, u32[]{:S(2)}) collective-permute-start(bf16[256,1792]{1,0:T(8,128)(2,1)} %get-tuple-element.49), channel_id=1, source_target_pairs={{0,2},{1,3},{2,0},{3,1},{4,6},{5,7},{6,4},{7,5},{8,10},{9,11},{10,... | collective-permute-start | bytes 2752520 | tf_op jit(solution)/shard_map/ppermute | solution.py:125
  14.5 26.7 %collective-permute-start.4 = (bf16[448,1024]{1,0:T(8,128)(2,1)}, bf16[448,1024]{1,0:T(8,128)(2,1)}, u32[]{:S(2)}, u32[]{:S(2)}) collective-permute-start(bf16[448,1024]{1,0:T(8,128)(2,1)} %get-tuple-element.51), channel_id=1, source_target_pairs={{0,4},{1,5},{2,6},{3,7},{4,0},{5,1},{6,2},{7,3},{8,12},{9,13},{10,... | collective-permute-start | bytes 2752520 | tf_op jit(solution)/shard_map/ppermute | solution.py:125
  35.8 21.6 %collective-permute-start.24 = (bf16[256,1792]{1,0:T(8,128)(2,1)S(1)}, bf16[256,1792]{1,0:T(8,128)(2,1)S(1)}, u32[]{:S(2)}, u32[]{:S(2)}) collective-permute-start(bf16[256,1792]{1,0:T(8,128)(2,1)S(1)} %get-tuple-element.68), channel_id=1, source_target_pairs={{0,2},{1,3},{2,0},{3,1},{4,6},{5,7},{6,4},{7,5},{8,10},{9,11},{10,... | collective-permute-start | bytes 2752520 | tf_op jit(solution)/shard_map/ppermute | solution.py:125
  37.8 19.8 %collective-permute-start.1 = (bf16[256,1792]{1,0:T(8,128)(2,1)S(1)}, bf16[256,1792]{1,0:T(8,128)(2,1)S(1)}, u32[]{:S(2)}, u32[]{:S(2)}) collective-permute-start(bf16[256,1792]{1,0:T(8,128)(2,1)S(1)} %get-tuple-element.99), channel_id=1, source_target_pairs={{0,0},{1,8},{2,2},{3,10},{4,4},{5,12},{6,6},{7,14},{8,1},{9,9},{10... | collective-permute-start | bytes 2752520 | tf_op jit(solution)/shard_map/ppermute | solution.py:125
  38.5 42.8 %collective-permute-start.2 = (bf16[256,1792]{1,0:T(8,128)(2,1)S(1)}, bf16[256,1792]{1,0:T(8,128)(2,1)S(1)}, u32[]{:S(2)}, u32[]{:S(2)}) collective-permute-start(bf16[256,1792]{1,0:T(8,128)(2,1)S(1)} %get-tuple-element.98), channel_id=1, source_target_pairs={{0,16},{1,24},{2,18},{3,26},{4,20},{5,28},{6,22},{7,30},{8,17},{9,... | collective-permute-start | bytes 2752520 | tf_op jit(solution)/shard_map/ppermute | solution.py:125
  41.2 40.1 %collective-permute-start.9 = (bf16[448,1024]{1,0:T(8,128)(2,1)S(1)}, bf16[448,1024]{1,0:T(8,128)(2,1)S(1)}, u32[]{:S(2)}, u32[]{:S(2)}) collective-permute-start(bf16[448,1024]{1,0:T(8,128)(2,1)S(1)} %copy-done.4), channel_id=1, source_target_pairs={{0,4},{1,5},{2,6},{3,7},{4,0},{5,1},{6,2},{7,3},{8,12},{9,13},{10,... | collective-permute-start | bytes 2752520 | tf_op jit(solution)/shard_map/ppermute | solution.py:125
  43.0 43.7 %collective-permute-start.5 = (bf16[2,448,512]{2,1,0:T(8,128)(2,1)S(1)}, bf16[2,448,512]{2,1,0:T(8,128)(2,1)S(1)}, u32[]{:S(2)}, u32[]{:S(2)}) collective-permute-start(bf16[2,448,512]{2,1,0:T(8,128)(2,1)S(1)} %pad_maximum_fusion.4), channel_id=1, source_target_pairs={{0,1},{1,0},{2,3},{3,2},{4,5},{5,4},{6,7},{7,6},{8,9},{9,8},{10,11... | collective-permute-start | bytes 2752520 | tf_op jit(solution)/shard_map/ppermute | solution.py:125
  81.3 35.2 %collective-permute-start.25 = (bf16[256,1792]{1,0:T(8,128)(2,1)S(1)}, bf16[256,1792]{1,0:T(8,128)(2,1)S(1)}, u32[]{:S(2)}, u32[]{:S(2)}) collective-permute-start(bf16[256,1792]{1,0:T(8,128)(2,1)S(1)} %get-tuple-element.70), channel_id=1, source_target_pairs={{0,0},{1,8},{2,2},{3,10},{4,4},{5,12},{6,6},{7,14},{8,1},{9,9},{10... | collective-permute-start | bytes 2752520 | tf_op jit(solution)/shard_map/ppermute | solution.py:125
  82.2 40.1 %collective-permute-start.26 = (bf16[256,1792]{1,0:T(8,128)(2,1)S(1)}, bf16[256,1792]{1,0:T(8,128)(2,1)S(1)}, u32[]{:S(2)}, u32[]{:S(2)}) collective-permute-start(bf16[256,1792]{1,0:T(8,128)(2,1)S(1)} %get-tuple-element.71), channel_id=1, source_target_pairs={{0,16},{1,24},{2,18},{3,26},{4,20},{5,28},{6,22},{7,30},{8,17},{9,... | collective-permute-start | bytes 2752520 | tf_op jit(solution)/shard_map/ppermute | solution.py:125
  82.5 29.1 %collective-permute-start.3 = (bf16[512,1792]{1,0:T(8,128)(2,1)S(1)}, bf16[512,1792]{1,0:T(8,128)(2,1)S(1)}, u32[]{:S(2)}, u32[]{:S(2)}) collective-permute-start(bf16[512,1792]{1,0:T(8,128)(2,1)S(1)} %constant_dynamic-update-slice_fusion), channel_id=1, source_target_pairs={{0,1},{1,0},{2,3},{3,2},{4,5},{5,4},{6,7},{7,6},{8,9},{9,8},{10,11... | collective-permute-start | bytes 5505032 | tf_op jit(solution)/shard_map/ppermute | solution.py:125
  86.7 23.1 %collective-permute-start.14 = (bf16[448,1024]{1,0:T(8,128)(2,1)S(1)}, bf16[448,1024]{1,0:T(8,128)(2,1)S(1)}, u32[]{:S(2)}, u32[]{:S(2)}) collective-permute-start(bf16[448,1024]{1,0:T(8,128)(2,1)S(1)} %copy-done.3), channel_id=1, source_target_pairs={{0,4},{1,5},{2,6},{3,7},{4,0},{5,1},{6,2},{7,3},{8,12},{9,13},{10,... | collective-permute-start | bytes 2752520 | tf_op jit(solution)/shard_map/ppermute | solution.py:125
  109.8 22.2 %collective-permute-start.19 = (bf16[448,1024]{1,0:T(8,128)(2,1)S(1)}, bf16[448,1024]{1,0:T(8,128)(2,1)S(1)}, u32[]{:S(2)}, u32[]{:S(2)}) collective-permute-start(bf16[448,1024]{1,0:T(8,128)(2,1)S(1)} %copy-done.2), channel_id=1, source_target_pairs={{0,4},{1,5},{2,6},{3,7},{4,0},{5,1},{6,2},{7,3},{8,12},{9,13},{10,... | collective-permute-start | bytes 2752520 | tf_op jit(solution)/shard_map/ppermute | solution.py:125
  112.9 14.9 %collective-permute-start.11 = (bf16[2,512,256]{1,2,0:T(8,128)(2,1)S(1)}, bf16[2,512,256]{1,2,0:T(8,128)(2,1)S(1)}, u32[]{:S(2)}, u32[]{:S(2)}) collective-permute-start(bf16[2,512,256]{1,2,0:T(8,128)(2,1)S(1)} %pad_maximum_fusion.13), channel_id=1, source_target_pairs={{0,2},{1,3},{2,0},{3,1},{4,6},{5,7},{6,4},{7,5},{8,10},{9,11},{10,... | collective-permute-start | bytes 1572872 | tf_op jit(solution)/shard_map/ppermute | solution.py:125
  115.7 21.9 %collective-permute-start.6 = (bf16[2,512,256]{1,2,0:T(8,128)(2,1)S(1)}, bf16[2,512,256]{1,2,0:T(8,128)(2,1)S(1)}, u32[]{:S(2)}, u32[]{:S(2)}) collective-permute-start(bf16[2,512,256]{1,2,0:T(8,128)(2,1)S(1)} %pad_maximum_fusion.12), channel_id=1, source_target_pairs={{0,2},{1,3},{2,0},{3,1},{4,6},{5,7},{6,4},{7,5},{8,10},{9,11},{10,... | collective-permute-start | bytes 1572872 | tf_op jit(solution)/shard_map/ppermute | solution.py:125
  116.6 31.5 %collective-permute-start.15 = (bf16[2,448,512]{2,1,0:T(8,128)(2,1)S(1)}, bf16[2,448,512]{2,1,0:T(8,128)(2,1)S(1)}, u32[]{:S(2)}, u32[]{:S(2)}) collective-permute-start(bf16[2,448,512]{2,1,0:T(8,128)(2,1)S(1)} %pad_maximum_fusion.8), channel_id=1, source_target_pairs={{0,1},{1,0},{2,3},{3,2},{4,5},{5,4},{6,7},{7,6},{8,9},{9,8},{10,11... | collective-permute-start | bytes 2752520 | tf_op jit(solution)/shard_map/ppermute | solution.py:125
  127.9 60.5 %collective-permute-start.27 = (bf16[512,1792]{1,0:T(8,128)(2,1)S(1)}, bf16[512,1792]{1,0:T(8,128)(2,1)S(1)}, u32[]{:S(2)}, u32[]{:S(2)}) collective-permute-start(bf16[512,1792]{1,0:T(8,128)(2,1)S(1)} %constant_dynamic-update-slice_fusion.2), channel_id=1, source_target_pairs={{0,1},{1,0},{2,3},{3,2},{4,5},{5,4},{6,7},{7,6},{8,9},{9,8},{10,11... | collective-permute-start | bytes 5505032 | tf_op jit(solution)/shard_map/ppermute | solution.py:125
  137.9 21.7 %collective-permute-start.20 = (bf16[2,448,512]{2,1,0:T(8,128)(2,1)S(1)}, bf16[2,448,512]{2,1,0:T(8,128)(2,1)S(1)}, u32[]{:S(2)}, u32[]{:S(2)}) collective-permute-start(bf16[2,448,512]{2,1,0:T(8,128)(2,1)S(1)} %pad_maximum_fusion.10), channel_id=1, source_target_pairs={{0,1},{1,0},{2,3},{3,2},{4,5},{5,4},{6,7},{7,6},{8,9},{9,8},{10,11... | collective-permute-start | bytes 2752520 | tf_op jit(solution)/shard_map/ppermute | solution.py:125
  147.1 21.8 %collective-permute-start.8 = (bf16[256,256]{0,1:T(8,128)(2,1)S(1)}, bf16[256,256]{0,1:T(8,128)(2,1)S(1)}, u32[]{:S(2)}, u32[]{:S(2)}) collective-permute-start(bf16[256,256]{0,1:T(8,128)(2,1)S(1)} %slice.515), channel_id=1, source_target_pairs={{0,16},{1,17},{2,18},{3,19},{4,20},{5,21},{6,22},{7,23},{8,24},{9,... | collective-permute-start | bytes 393224 | tf_op jit(solution)/shard_map/ppermute | solution.py:125
  147.4 10.8 %collective-permute-start.12 = (bf16[512,256]{0,1:T(8,128)(2,1)S(1)}, bf16[512,256]{0,1:T(8,128)(2,1)S(1)}, u32[]{:S(2)}, u32[]{:S(2)}) collective-permute-start(bf16[512,256]{0,1:T(8,128)(2,1)S(1)} %select_convert_fusion.6), channel_id=1, source_target_pairs={{0,8},{1,9},{2,10},{3,11},{4,12},{5,13},{6,14},{7,15},{8,0},{9,1},... | collective-permute-start | bytes 786440 | tf_op jit(solution)/shard_map/ppermute | solution.py:125
  152.3 14.8 %collective-permute-start.16 = (bf16[2,512,256]{1,2,0:T(8,128)(2,1)S(1)}, bf16[2,512,256]{1,2,0:T(8,128)(2,1)S(1)}, u32[]{:S(2)}, u32[]{:S(2)}) collective-permute-start(bf16[2,512,256]{1,2,0:T(8,128)(2,1)S(1)} %pad_maximum_fusion.14), channel_id=1, source_target_pairs={{0,2},{1,3},{2,0},{3,1},{4,6},{5,7},{6,4},{7,5},{8,10},{9,11},{10,... | collective-permute-start | bytes 1572872 | tf_op jit(solution)/shard_map/ppermute | solution.py:125
  158.4 10.6 %collective-permute-start.13 = (bf16[256,256]{0,1:T(8,128)(2,1)S(1)}, bf16[256,256]{0,1:T(8,128)(2,1)S(1)}, u32[]{:S(2)}, u32[]{:S(2)}) collective-permute-start(bf16[256,256]{0,1:T(8,128)(2,1)S(1)} %slice.514), channel_id=1, source_target_pairs={{0,16},{1,17},{2,18},{3,19},{4,20},{5,21},{6,22},{7,23},{8,24},{9,... | collective-permute-start | bytes 393224 | tf_op jit(solution)/shard_map/ppermute | solution.py:125
  162.5 14.3 %collective-permute-start.21 = (bf16[2,512,256]{1,2,0:T(8,128)(2,1)S(1)}, bf16[2,512,256]{1,2,0:T(8,128)(2,1)S(1)}, u32[]{:S(2)}, u32[]{:S(2)}) collective-permute-start(bf16[2,512,256]{1,2,0:T(8,128)(2,1)S(1)} %pad_maximum_fusion.15), channel_id=1, source_target_pairs={{0,2},{1,3},{2,0},{3,1},{4,6},{5,7},{6,4},{7,5},{8,10},{9,11},{10,... | collective-permute-start | bytes 1572872 | tf_op jit(solution)/shard_map/ppermute | solution.py:125
  177.0 9.1 %collective-permute-start.22 = (bf16[512,256]{0,1:T(8,128)(2,1)S(1)}, bf16[512,256]{0,1:T(8,128)(2,1)S(1)}, u32[]{:S(2)}, u32[]{:S(2)}) collective-permute-start(bf16[512,256]{0,1:T(8,128)(2,1)S(1)} %select_convert_fusion.4), channel_id=1, source_target_pairs={{0,8},{1,9},{2,10},{3,11},{4,12},{5,13},{6,14},{7,15},{8,0},{9,1},... | collective-permute-start | bytes 786440 | tf_op jit(solution)/shard_map/ppermute | solution.py:125
  179.8 50.8 %collective-permute-start.18 = (bf16[256,256]{0,1:T(8,128)(2,1)S(1)}, bf16[256,256]{0,1:T(8,128)(2,1)S(1)}, u32[]{:S(2)}, u32[]{:S(2)}) collective-permute-start(bf16[256,256]{0,1:T(8,128)(2,1)S(1)} %slice.513), channel_id=1, source_target_pairs={{0,16},{1,17},{2,18},{3,19},{4,20},{5,21},{6,22},{7,23},{8,24},{9,... | collective-permute-start | bytes 393224 | tf_op jit(solution)/shard_map/ppermute | solution.py:125
  186.2 44.4 %collective-permute-start.23 = (bf16[256,256]{0,1:T(8,128)(2,1)S(1)}, bf16[256,256]{0,1:T(8,128)(2,1)S(1)}, u32[]{:S(2)}, u32[]{:S(2)}) collective-permute-start(bf16[256,256]{0,1:T(8,128)(2,1)S(1)} %slice.512), channel_id=1, source_target_pairs={{0,16},{1,17},{2,18},{3,19},{4,20},{5,21},{6,22},{7,23},{8,24},{9,... | collective-permute-start | bytes 393224 | tf_op jit(solution)/shard_map/ppermute | solution.py:125
  189.6 30.4 %collective-permute-start.31 = (bf16[2,512,256]{1,2,0:T(8,128)(2,1)S(1)}, bf16[2,512,256]{1,2,0:T(8,128)(2,1)S(1)}, u32[]{:S(2)}, u32[]{:S(2)}) collective-permute-start(bf16[2,512,256]{1,2,0:T(8,128)(2,1)S(1)} %pad_maximum_fusion.17), channel_id=1, source_target_pairs={{0,2},{1,3},{2,0},{3,1},{4,6},{5,7},{6,4},{7,5},{8,10},{9,11},{10,... | collective-permute-start | bytes 1572872 | tf_op jit(solution)/shard_map/ppermute | solution.py:125
  192.5 17.9 %collective-permute-start.28 = (bf16[2,512,256]{1,2,0:T(8,128)(2,1)S(1)}, bf16[2,512,256]{1,2,0:T(8,128)(2,1)S(1)}, u32[]{:S(2)}, u32[]{:S(2)}) collective-permute-start(bf16[2,512,256]{1,2,0:T(8,128)(2,1)S(1)} %pad_maximum_fusion.16), channel_id=1, source_target_pairs={{0,2},{1,3},{2,0},{3,1},{4,6},{5,7},{6,4},{7,5},{8,10},{9,11},{10,... | collective-permute-start | bytes 1572872 | tf_op jit(solution)/shard_map/ppermute | solution.py:125
  210.8 9.0 %collective-permute-start.29 = (bf16[512,256]{0,1:T(8,128)(2,1)S(1)}, bf16[512,256]{0,1:T(8,128)(2,1)S(1)}, u32[]{:S(2)}, u32[]{:S(2)}) collective-permute-start(bf16[512,256]{0,1:T(8,128)(2,1)S(1)} %select_convert_fusion.3), channel_id=1, source_target_pairs={{0,8},{1,9},{2,10},{3,11},{4,12},{5,13},{6,14},{7,15},{8,0},{9,1},... | collective-permute-start | bytes 786440 | tf_op jit(solution)/shard_map/ppermute | solution.py:125
  215.2 13.8 %collective-permute-start.34 = (bf16[2,512,256]{1,2,0:T(8,128)(2,1)S(1)}, bf16[2,512,256]{1,2,0:T(8,128)(2,1)S(1)}, u32[]{:S(2)}, u32[]{:S(2)}) collective-permute-start(bf16[2,512,256]{1,2,0:T(8,128)(2,1)S(1)} %pad_maximum_fusion.18), channel_id=1, source_target_pairs={{0,2},{1,3},{2,0},{3,1},{4,6},{5,7},{6,4},{7,5},{8,10},{9,11},{10,... | collective-permute-start | bytes 1572872 | tf_op jit(solution)/shard_map/ppermute | solution.py:125
  222.1 17.0 %collective-permute-start.37 = (bf16[2,512,256]{1,2,0:T(8,128)(2,1)S(1)}, bf16[2,512,256]{1,2,0:T(8,128)(2,1)S(1)}, u32[]{:S(2)}, u32[]{:S(2)}) collective-permute-start(bf16[2,512,256]{1,2,0:T(8,128)(2,1)S(1)} %pad_maximum_fusion.19), channel_id=1, source_target_pairs={{0,2},{1,3},{2,0},{3,1},{4,6},{5,7},{6,4},{7,5},{8,10},{9,11},{10,... | collective-permute-start | bytes 1572872 | tf_op jit(solution)/shard_map/ppermute | solution.py:125
  229.2 9.6 %collective-permute-start.35 = (bf16[512,256]{0,1:T(8,128)(2,1)S(1)}, bf16[512,256]{0,1:T(8,128)(2,1)S(1)}, u32[]{:S(2)}, u32[]{:S(2)}) collective-permute-start(bf16[512,256]{0,1:T(8,128)(2,1)S(1)} %select_convert_fusion.1), channel_id=1, source_target_pairs={{0,8},{1,9},{2,10},{3,11},{4,12},{5,13},{6,14},{7,15},{8,0},{9,1},... | collective-permute-start | bytes 786440 | tf_op jit(solution)/shard_map/ppermute | solution.py:125
  232.1 11.5 %collective-permute-start.33 = (bf16[256,256]{0,1:T(8,128)(2,1)S(1)}, bf16[256,256]{0,1:T(8,128)(2,1)S(1)}, u32[]{:S(2)}, u32[]{:S(2)}) collective-permute-start(bf16[256,256]{0,1:T(8,128)(2,1)S(1)} %slice.510), channel_id=1, source_target_pairs={{0,16},{1,17},{2,18},{3,19},{4,20},{5,21},{6,22},{7,23},{8,24},{9,... | collective-permute-start | bytes 393224 | tf_op jit(solution)/shard_map/ppermute | solution.py:125
  (13 other events, 88.9 us)

commit v5 on v4

--- a/solution.py
+++ b/solution.py
@@ -129,28 +129,29 @@
     own, other = pack(where, hidden_act, xs)
 
     args = (master, moment_one, moment_two, gradient)
-    updated, first = adam(where, [0], args, [])
-    updated, rest = adam(where, list(range(1, COL_CHUNKS)), args, updated)
-    pieces = [*first, *rest]
+    updated, pieces = [], []
+
+    def update(q, *done):
+        new, (piece,) = adam(after(where, *done), [q], args, updated)
+        updated[:] = new
+        pieces.append(piece)
+
     flip = (c ^ (z % 2)) != 0
-    crossed, tables = [], []
-    theirs, moved, acts = [], [], []
+    crossed, used, tables = [], [], []
+    theirs, pairs, moved, acts = [], [], [], []
     sends, backs, leaving, result = [], [], [], []
 
-    def to_plane(m):
-        send = other[m] if m == 0 else after(other[m], theirs[-1])
+    def to_plane(m, *done):
+        send = after(other[m], theirs[-1]) if m else other[m]
         theirs.append(permute(send, lambda z, x, y, c: (z, x, 1 - y, c)))
-        pair = swap_if(((z // 2) ^ y) != 0, own[m], theirs[m])
-        if m:
-            pair = after(pair, moved[-1], crossed[1])
-        got = [
-            permute(data, lambda z, x, y, c: (2 * ((z // 2) ^ a) + c, x, y, z % 2)) for a, data in enumerate(pair)
-        ]
-        moved.append(got)
+        pair = after(swap_if(((z // 2) ^ y) != 0, own[m], theirs[m]), *done)
+        pairs.append(pair)
+        moved.append(
+            [permute(data, lambda z, x, y, c: (2 * ((z // 2) ^ a) + c, x, y, z % 2)) for a, data in enumerate(pair)]
+        )
 
     def to_cores(m, *done):
         got = jnp.concatenate(after(moved[m], *done), axis=0)
-        moved[m] = got
         acts.append((got, permute(got, lambda z, x, y, c: (z, x, y, 1 - c))))
 
     def gather(q, *done):
@@ -161,6 +162,7 @@
         parts = after(parts, *done)
         here = jnp.stack([p[:, :half] for p in parts])
         there = jnp.stack([p[:, half:] for p in parts])
+        used.append(there)
         there = permute(there, lambda z, x, y, c: (z, x, y, 1 - c))
         tables.append(jnp.stack(swap_if(c != 0, here, there), axis=1).reshape(-1, half))
 
@@ -169,8 +171,7 @@
         half = table.shape[1] // 2
         totals = [jnp.dot(a, table, preferred_element_type=jnp.float32) for a in acts[m]]
         send = jnp.stack([total[:, half:].astype(jnp.bfloat16) for total in totals])
-        if len(backs) >= 2:
-            send = after(send, backs[-2])
+        send = after(send, *sends[-1:], *backs[-2:-1])
         sends.append(send)
         backs.append(permute(send, lambda z, x, y, c: (z, x, 1 - y, c)))
         return [total[:, :half] for total in totals], len(backs) - 1
@@ -179,23 +180,27 @@
         back = after(backs[j], leaving[-1]) if leaving else backs[j]
         near, far = swap_if(flip, *[total + b for total, b in zip(totals, back)])
         back = permute(far.astype(jnp.bfloat16), lambda z, x, y, c: (z ^ 1, x, y, c))
-        near = near + back
+        near = near + after(back, *sends[j + 3 : j + 4])
         send = near[part:].astype(jnp.bfloat16)
         leaving.append(send)
         back = permute(send, lambda z, x, y, c: (z ^ 2, x, y, c))
         result.append((near[:part] + back).astype(jnp.bfloat16))
 
+    update(0, own[0])
+    to_plane(0)
     gather(0)
+    update(1)
     gather(1)
-    to_plane(0)
-    to_plane(1)
-    to_cores(0)
+    update(2, pairs[0])
+    update(3, crossed[0])
+    to_cores(0, used[1])
+    to_plane(1, *moved[0])
+    gather(2)
     jobs = [multiply(0, 0), multiply(0, 1)]
-    gather(2, sends[0], sends[1])
-    gather(3, backs[0])
+    gather(3, backs[0], sends[1])
     jobs.append(multiply(0, 2))
-    to_cores(1, backs[1])
     jobs.append(multiply(0, 3))
+    to_cores(1, sends[3])
     jobs += [multiply(1, q) for q in range(COL_CHUNKS)]
     for job in jobs:
         reduce(*job)

time: 256 us -> 223 us (0.87)
  waiting for transfers between devices: 142 us -> 96.8 us
  local copies, waits for them, and re-layouts: 7.68 us -> 12.3 us
  other arithmetic: 6.82 us -> 10.2 us
    ppermute x40, waiting for transfers between devices: 142 us -> 96.8 us  [permute(): return lax.ppermute(value, AXES, pairs)]
    pallas_call x2 -> x4, Pallas kernels: 25.6 us -> 28 us  [adam(): pl.pallas_call(kernel, grid_spec=pltpu.PrefetchScalarGridSpec(num_scalar_...]
    another operation x6 -> x8, local copies, waits for them, and re-layouts: 2.89 us -> 5.12 us  [gather(): here = jnp.stack([p[:, :half] for p in parts])]
  transfers between devices with their start and end apart: 40 -> 40, of which waited for: 22 -> 21; matrix products, arithmetic and copies ran while one was open for 12% -> 17% of each run, Pallas kernels for 10% -> 13%
where the time goes in v5:
time: 223 us; the launch traced here: 221 us
  waiting for transfers between devices  96.8 us (43%)
  starting transfers between devices  52 us (23%)
  Pallas kernels  29.8 us (13%)
  matrix products  18.7 us (8%)
  local copies, waits for them, and re-layouts  12.3 us (6%)
  other arithmetic  10.2 us (5%)
    ppermute x40, waiting for transfers between devices, permute(): return lax.ppermute(value, AXES, pairs)  96.8 us
    ppermute x40, starting transfers between devices, permute(): return lax.ppermute(value, AXES, pairs)  52 us
    pallas_call x4, Pallas kernels, adam(): pl.pallas_call(kernel, grid_spec=pltpu.PrefetchScalarGridSpec(num_scalar_...  28 us
    dot_general x16, matrix products, multiply(): jnp.dot(a, table, preferred_element_type=jnp.float32)  18.7 us
    another operation x8, local copies, waits for them, and re-layouts, gather(): here = jnp.stack([p[:, :half] for p in parts])  5.12 us
    unnamed x11, local copies, waits for them, and re-layouts  4.67 us
  transfers between devices with their start and end apart: 40, of which 21 were waited for; matrix products, arithmetic and copies ran while one was open for 17% of the time, Pallas kernels for 13%

profile of v5, /device:TPU:0, one launch (start us, length us, event | category | flops | bytes accessed | tf_op | source)
XLA Modules:
  0.0 221.4 jit_solution(13490327283226715769)
XLA Ops:
  0.7 2.0 copy-done
  2.8 1.8 pack.1
  4.5 3.0 %collective-permute-start.1 = (bf16[256,1792]{1,0:T(8,128)(2,1)}, bf16[256,1792]{1,0:T(8,128)(2,1)}, u32[]{:S(2)}, u32[]{:S(2)}) collective-permute-start(bf16[256,1792]{1,0:T(8,128)(2,1)} %get-tuple-element.62), channel_id=1, source_target_pairs={{0,2},{1,3},{2,0},{3,1},{4,6},{5,7},{6,4},{7,5},{8,10},{9,11},{10,... | collective-permute-start | bytes 2752520 | tf_op jit(solution)/shard_map/ppermute | solution.py:125
  7.5 7.0 %adam.4 = (f32[448,4096]{1,0:T(8,128)}, f32[448,4096]{1,0:T(8,128)}, f32[448,4096]{1,0:T(8,128)}, bf16[448,1024]{1,0:T(8,128)(2,1)}) custom-call(s32[3]{0:T(128)} %copy-done.1, f32[448,4096]{1,0:T(8,128)} %master_ref.7, f32[448,4096]{1,0:T(8,128)} %one_ref.7, f32[448,4096]{1,0:T(8,128)} %two_ref.7, bf16[448,4096]{1,0:T(8,128)(2,1)} %grad_ref.7), custom_call_target="tpu_custom_call" | custom-call | flops 458752 | bytes 458752 | tf_op jit(solution)/shard_map/adam/pallas_call | solution.py:54
  16.0 7.0 %adam.5 = (f32[448,4096]{1,0:T(8,128)}, f32[448,4096]{1,0:T(8,128)}, f32[448,4096]{1,0:T(8,128)}, bf16[448,1024]{1,0:T(8,128)(2,1)}) custom-call(s32[3]{0:T(128)} %copy-done.1, f32[448,4096]{1,0:T(8,128)} %master_ref.7, f32[448,4096]{1,0:T(8,128)} %one_ref.7, f32[448,4096]{1,0:T(8,128)} %two_ref.7, ...), custom_call_target="tpu_custom_call", output_to_operand_aliasing={{0}: (5, {}), {1}: (6, {}), {2}: (7, {})} | custom-call | flops 458752 | bytes 458752 | tf_op jit(solution)/shard_map/adam/pallas_call | solution.py:54
  24.2 3.9 %collective-permute-done.1 = bf16[256,1792]{1,0:T(8,128)(2,1)} collective-permute-done((bf16[256,1792]{1,0:T(8,128)(2,1)}, bf16[256,1792]{1,0:T(8,128)(2,1)}, u32[]{:S(2)}, u32[]{:S(2)}) %collective-permute-start.1) | collective-permute-done | bytes 917536 | tf_op jit(solution)/shard_map/ppermute | solution.py:125
  28.2 1.7 collective-permute-start.17
  29.9 2.6 %broadcast_select_fusion.2 = (bf16[256,1792]{1,0:T(8,128)(2,1)}, bf16[256,1792]{1,0:T(8,128)(2,1)}) fusion(bf16[256,1792]{1,0:T(8,128)(2,1)S(1)} %get-tuple-element.58, bf16[256,1792]{1,0:T(8,128)(2,1)} %collective-permute-done.1, pred[]{:T(512)S(6)} %ne.49), kind=kLoop, calls=%fused_computation.23 | loop fusion | flops 917504 | bytes 3670017 | tf_op jit(solution)/shard_map/jit(_where)/select_n | solution.py:103
  32.5 2.6 %collective-permute-start.3 = (bf16[256,1792]{1,0:T(8,128)(2,1)}, bf16[256,1792]{1,0:T(8,128)(2,1)}, u32[]{:S(2)}, u32[]{:S(2)}) collective-permute-start(bf16[256,1792]{1,0:T(8,128)(2,1)} %get-tuple-element.130), channel_id=1, source_target_pairs={{0,16},{1,24},{2,18},{3,26},{4,20},{5,28},{6,22},{7,30},{8,17},{9,... | collective-permute-start | bytes 2752520 | tf_op jit(solution)/shard_map/ppermute | solution.py:125
  35.1 8.3 %collective-permute-start.2 = (bf16[256,1792]{1,0:T(8,128)(2,1)}, bf16[256,1792]{1,0:T(8,128)(2,1)}, u32[]{:S(2)}, u32[]{:S(2)}) collective-permute-start(bf16[256,1792]{1,0:T(8,128)(2,1)} %get-tuple-element.131), channel_id=1, source_target_pairs={{0,0},{1,8},{2,2},{3,10},{4,4},{5,12},{6,6},{7,14},{8,1},{9,9},{10... | collective-permute-start | bytes 2752520 | tf_op jit(solution)/shard_map/ppermute | solution.py:125
  46.3 7.0 %adam.6 = (f32[448,4096]{1,0:T(8,128)}, f32[448,4096]{1,0:T(8,128)}, f32[448,4096]{1,0:T(8,128)}, bf16[448,1024]{1,0:T(8,128)(2,1)}) custom-call(s32[3]{0:T(128)} %copy-done.1, f32[448,4096]{1,0:T(8,128)} %master_ref.7, f32[448,4096]{1,0:T(8,128)} %one_ref.7, f32[448,4096]{1,0:T(8,128)} %two_ref.7, ...), custom_call_target="tpu_custom_call", output_to_operand_aliasing={{0}: (5, {}), {1}: (6, {}), {2}: (7, {})} | custom-call | flops 458752 | bytes 458752 | tf_op jit(solution)/shard_map/adam/pallas_call | solution.py:54
  53.3 7.0 %adam.7 = (f32[448,4096]{1,0:T(8,128)}, f32[448,4096]{1,0:T(8,128)}, f32[448,4096]{1,0:T(8,128)}, bf16[448,1024]{1,0:T(8,128)(2,1)}) custom-call(s32[3]{0:T(128)} %copy-done.1, f32[448,4096]{1,0:T(8,128)} %master_ref.7, f32[448,4096]{1,0:T(8,128)} %one_ref.7, f32[448,4096]{1,0:T(8,128)} %two_ref.7, ...), custom_call_target="tpu_custom_call", output_to_operand_aliasing={{0}: (5, {}), {1}: (6, {}), {2}: (7, {})} | custom-call | flops 458752 | bytes 458752 | tf_op jit(solution)/shard_map/adam/pallas_call | solution.py:54
  62.9 12.4 %collective-permute-done.3 = bf16[256,1792]{1,0:T(8,128)(2,1)} collective-permute-done((bf16[256,1792]{1,0:T(8,128)(2,1)}, bf16[256,1792]{1,0:T(8,128)(2,1)}, u32[]{:S(2)}, u32[]{:S(2)}) %collective-permute-start.3) | collective-permute-done | bytes 917536 | tf_op jit(solution)/shard_map/ppermute | solution.py:125
  79.2 2.9 %collective-permute-start.11 = (bf16[2,448,512]{2,1,0:T(8,128)(2,1)S(1)}, bf16[2,448,512]{2,1,0:T(8,128)(2,1)S(1)}, u32[]{:S(2)}, u32[]{:S(2)}) collective-permute-start(bf16[2,448,512]{2,1,0:T(8,128)(2,1)S(1)} %pad_maximum_fusion.4), channel_id=1, source_target_pairs={{0,1},{1,0},{2,3},{3,2},{4,5},{5,4},{6,7},{7,6},{8,9},{9,8},{10,11... | collective-permute-start | bytes 2752520 | tf_op jit(solution)/shard_map/ppermute | solution.py:125
  84.7 12.7 %collective-permute-done.9 = bf16[448,1024]{1,0:T(8,128)(2,1)S(1)} collective-permute-done((bf16[448,1024]{1,0:T(8,128)(2,1)S(1)}, bf16[448,1024]{1,0:T(8,128)(2,1)S(1)}, u32[]{:S(2)}, u32[]{:S(2)}) %collective-permute-start.9) | collective-permute-done | bytes 917536 | tf_op jit(solution)/shard_map/ppermute | solution.py:125
  97.4 2.4 %collective-permute-start.5 = (bf16[512,1792]{1,0:T(8,128)(2,1)S(1)}, bf16[512,1792]{1,0:T(8,128)(2,1)S(1)}, u32[]{:S(2)}, u32[]{:S(2)}) collective-permute-start(bf16[512,1792]{1,0:T(8,128)(2,1)S(1)} %constant_dynamic-update-slice_fusion), channel_id=1, source_target_pairs={{0,1},{1,0},{2,3},{3,2},{4,5},{5,4},{6,7},{7,6},{8,9},{9,8},{10,11... | collective-permute-start | bytes 5505032 | tf_op jit(solution)/shard_map/ppermute | solution.py:125
  112.4 13.3 %collective-permute-done.10 = bf16[448,1024]{1,0:T(8,128)(2,1)S(1)} collective-permute-done((bf16[448,1024]{1,0:T(8,128)(2,1)S(1)}, bf16[448,1024]{1,0:T(8,128)(2,1)S(1)}, u32[]{:S(2)}, u32[]{:S(2)}) %collective-permute-start.10) | collective-permute-done | bytes 917536 | tf_op jit(solution)/shard_map/ppermute | solution.py:125
  136.4 2.2 collective-permute-start.15
  145.3 3.3 %collective-permute-done.16 = bf16[512,256]{0,1:T(8,128)(2,1)S(1)} collective-permute-done((bf16[512,256]{0,1:T(8,128)(2,1)S(1)}, bf16[512,256]{0,1:T(8,128)(2,1)S(1)}, u32[]{:S(2)}, u32[]{:S(2)}) %collective-permute-start.16) | collective-permute-done | bytes 262176 | tf_op jit(solution)/shard_map/ppermute | solution.py:125
  151.5 4.5 %collective-permute-done.24 = bf16[2,512,256]{1,2,0:T(8,128)(2,1)S(1)} collective-permute-done((bf16[2,512,256]{1,2,0:T(8,128)(2,1)S(1)}, bf16[2,512,256]{1,2,0:T(8,128)(2,1)S(1)}, u32[]{:S(2)}, u32[]{:S(2)}) %collective-permute-start.24) | collective-permute-done | bytes 524320 | tf_op jit(solution)/shard_map/ppermute | solution.py:125
  159.4 3.8 %collective-permute-done.23 = bf16[512,256]{0,1:T(8,128)(2,1)S(1)} collective-permute-done((bf16[512,256]{0,1:T(8,128)(2,1)S(1)}, bf16[512,256]{0,1:T(8,128)(2,1)S(1)}, u32[]{:S(2)}, u32[]{:S(2)}) %collective-permute-start.23) | collective-permute-done | bytes 262176 | tf_op jit(solution)/shard_map/ppermute | solution.py:125
  167.3 2.8 %collective-permute-done.26 = bf16[512,256]{0,1:T(8,128)(2,1)S(1)} collective-permute-done((bf16[512,256]{0,1:T(8,128)(2,1)S(1)}, bf16[512,256]{0,1:T(8,128)(2,1)S(1)}, u32[]{:S(2)}, u32[]{:S(2)}) %collective-permute-start.26) | collective-permute-done | bytes 262176 | tf_op jit(solution)/shard_map/ppermute | solution.py:125
  172.9 5.6 %collective-permute-done.30 = bf16[2,512,256]{1,2,0:T(8,128)(2,1)S(1)} collective-permute-done((bf16[2,512,256]{1,2,0:T(8,128)(2,1)S(1)}, bf16[2,512,256]{1,2,0:T(8,128)(2,1)S(1)}, u32[]{:S(2)}, u32[]{:S(2)}) %collective-permute-start.30) | collective-permute-done | bytes 524320 | tf_op jit(solution)/shard_map/ppermute | solution.py:125
  178.9 1.7 collective-permute-start.32
  181.7 2.0 collective-permute-start.28
  184.2 7.2 %collective-permute-done.32 = bf16[512,256]{0,1:T(8,128)(2,1)S(1)} collective-permute-done((bf16[512,256]{0,1:T(8,128)(2,1)S(1)}, bf16[512,256]{0,1:T(8,128)(2,1)S(1)}, u32[]{:S(2)}, u32[]{:S(2)}) %collective-permute-start.32) | collective-permute-done | bytes 262176 | tf_op jit(solution)/shard_map/ppermute | solution.py:125
  191.9 1.9 collective-permute-done.28
  194.0 2.9 %collective-permute-start.33 = (bf16[256,256]{0,1:T(8,128)(2,1)S(1)}, bf16[256,256]{0,1:T(8,128)(2,1)S(1)}, u32[]{:S(2)}, u32[]{:S(2)}) collective-permute-start(bf16[256,256]{0,1:T(8,128)(2,1)S(1)} %slice.512), channel_id=1, source_target_pairs={{0,16},{1,17},{2,18},{3,19},{4,20},{5,21},{6,22},{7,23},{8,24},{9,... | collective-permute-start | bytes 393224 | tf_op jit(solution)/shard_map/ppermute | solution.py:125
  196.9 5.1 %collective-permute-done.35 = bf16[512,256]{0,1:T(8,128)(2,1)S(1)} collective-permute-done((bf16[512,256]{0,1:T(8,128)(2,1)S(1)}, bf16[512,256]{0,1:T(8,128)(2,1)S(1)}, u32[]{:S(2)}, u32[]{:S(2)}) %collective-permute-start.35) | collective-permute-done | bytes 262176 | tf_op jit(solution)/shard_map/ppermute | solution.py:125
  202.5 4.6 %collective-permute-done.33 = bf16[256,256]{0,1:T(8,128)(2,1)S(1)} collective-permute-done((bf16[256,256]{0,1:T(8,128)(2,1)S(1)}, bf16[256,256]{0,1:T(8,128)(2,1)S(1)}, u32[]{:S(2)}, u32[]{:S(2)}) %collective-permute-start.33) | collective-permute-done | bytes 131104 | tf_op jit(solution)/shard_map/ppermute | solution.py:125
  207.2 3.9 %collective-permute-done.38 = bf16[512,256]{0,1:T(8,128)(2,1)S(1)} collective-permute-done((bf16[512,256]{0,1:T(8,128)(2,1)S(1)}, bf16[512,256]{0,1:T(8,128)(2,1)S(1)}, u32[]{:S(2)}, u32[]{:S(2)}) %collective-permute-start.38) | collective-permute-done | bytes 262176 | tf_op jit(solution)/shard_map/ppermute | solution.py:125
  212.3 6.0 %collective-permute-done.36 = bf16[256,256]{0,1:T(8,128)(2,1)S(1)} collective-permute-done((bf16[256,256]{0,1:T(8,128)(2,1)S(1)}, bf16[256,256]{0,1:T(8,128)(2,1)S(1)}, u32[]{:S(2)}, u32[]{:S(2)}) %collective-permute-start.36) | collective-permute-done | bytes 131104 | tf_op jit(solution)/shard_map/ppermute | solution.py:125
  (165 shorter events, 64.7 us)
Async XLA Ops:
  4.5 23.6 %collective-permute-start.1 = (bf16[256,1792]{1,0:T(8,128)(2,1)}, bf16[256,1792]{1,0:T(8,128)(2,1)}, u32[]{:S(2)}, u32[]{:S(2)}) collective-permute-start(bf16[256,1792]{1,0:T(8,128)(2,1)} %get-tuple-element.62), channel_id=1, source_target_pairs={{0,2},{1,3},{2,0},{3,1},{4,6},{5,7},{6,4},{7,5},{8,10},{9,11},{10,... | collective-permute-start | bytes 2752520 | tf_op jit(solution)/shard_map/ppermute | solution.py:125
  14.5 28.9 %collective-permute-start = (bf16[448,1024]{1,0:T(8,128)(2,1)}, bf16[448,1024]{1,0:T(8,128)(2,1)}, u32[]{:S(2)}, u32[]{:S(2)}) collective-permute-start(bf16[448,1024]{1,0:T(8,128)(2,1)} %get-tuple-element.60), channel_id=1, source_target_pairs={{0,4},{1,5},{2,6},{3,7},{4,0},{5,1},{6,2},{7,3},{8,12},{9,13},{10,... | collective-permute-start | bytes 2752520 | tf_op jit(solution)/shard_map/ppermute | solution.py:125
  28.2 33.3 %collective-permute-start.17 = (bf16[256,1792]{1,0:T(8,128)(2,1)S(1)}, bf16[256,1792]{1,0:T(8,128)(2,1)}, u32[]{:S(2)}, u32[]{:S(2)}) collective-permute-start(bf16[256,1792]{1,0:T(8,128)(2,1)S(1)} %get-tuple-element.92), channel_id=1, source_target_pairs={{0,2},{1,3},{2,0},{3,1},{4,6},{5,7},{6,4},{7,5},{8,10},{9,11},{10,... | collective-permute-start | bytes 2752520 | tf_op jit(solution)/shard_map/ppermute | solution.py:125
  32.5 42.9 %collective-permute-start.3 = (bf16[256,1792]{1,0:T(8,128)(2,1)}, bf16[256,1792]{1,0:T(8,128)(2,1)}, u32[]{:S(2)}, u32[]{:S(2)}) collective-permute-start(bf16[256,1792]{1,0:T(8,128)(2,1)} %get-tuple-element.130), channel_id=1, source_target_pairs={{0,16},{1,24},{2,18},{3,26},{4,20},{5,28},{6,22},{7,30},{8,17},{9,... | collective-permute-start | bytes 2752520 | tf_op jit(solution)/shard_map/ppermute | solution.py:125
  35.1 40.3 %collective-permute-start.2 = (bf16[256,1792]{1,0:T(8,128)(2,1)}, bf16[256,1792]{1,0:T(8,128)(2,1)}, u32[]{:S(2)}, u32[]{:S(2)}) collective-permute-start(bf16[256,1792]{1,0:T(8,128)(2,1)} %get-tuple-element.131), channel_id=1, source_target_pairs={{0,0},{1,8},{2,2},{3,10},{4,4},{5,12},{6,6},{7,14},{8,1},{9,9},{10... | collective-permute-start | bytes 2752520 | tf_op jit(solution)/shard_map/ppermute | solution.py:125
  43.4 32.9 %collective-permute-start.4 = (bf16[448,1024]{1,0:T(8,128)(2,1)}, bf16[448,1024]{1,0:T(8,128)(2,1)}, u32[]{:S(2)}, u32[]{:S(2)}) collective-permute-start(bf16[448,1024]{1,0:T(8,128)(2,1)} %get-tuple-element.77), channel_id=1, source_target_pairs={{0,4},{1,5},{2,6},{3,7},{4,0},{5,1},{6,2},{7,3},{8,12},{9,13},{10,... | collective-permute-start | bytes 2752520 | tf_op jit(solution)/shard_map/ppermute | solution.py:125
  46.2 53.7 %collective-permute-start.6 = (bf16[2,448,512]{2,1,0:T(8,128)(2,1)S(1)}, bf16[2,448,512]{2,1,0:T(8,128)(2,1)}, u32[]{:S(2)}, u32[]{:S(2)}) collective-permute-start(bf16[2,448,512]{2,1,0:T(8,128)(2,1)S(1)} %pad_maximum_fusion.5), channel_id=1, source_target_pairs={{0,1},{1,0},{2,3},{3,2},{4,5},{5,4},{6,7},{7,6},{8,9},{9,8},{10,11... | collective-permute-start | bytes 2752520 | tf_op jit(solution)/shard_map/ppermute | solution.py:125
  75.3 58.7 %collective-permute-start.18 = (bf16[256,1792]{1,0:T(8,128)(2,1)S(1)}, bf16[256,1792]{1,0:T(8,128)(2,1)S(1)}, u32[]{:S(2)}, u32[]{:S(2)}) collective-permute-start(bf16[256,1792]{1,0:T(8,128)(2,1)S(1)} %get-tuple-element.94), channel_id=1, source_target_pairs={{0,0},{1,8},{2,2},{3,10},{4,4},{5,12},{6,6},{7,14},{8,1},{9,9},{10... | collective-permute-start | bytes 2752520 | tf_op jit(solution)/shard_map/ppermute | solution.py:125
  76.2 57.8 %collective-permute-start.19 = (bf16[256,1792]{1,0:T(8,128)(2,1)S(1)}, bf16[256,1792]{1,0:T(8,128)(2,1)S(1)}, u32[]{:S(2)}, u32[]{:S(2)}) collective-permute-start(bf16[256,1792]{1,0:T(8,128)(2,1)S(1)} %get-tuple-element.95), channel_id=1, source_target_pairs={{0,16},{1,24},{2,18},{3,26},{4,20},{5,28},{6,22},{7,30},{8,17},{9,... | collective-permute-start | bytes 2752520 | tf_op jit(solution)/shard_map/ppermute | solution.py:125
  76.3 21.0 %collective-permute-start.9 = (bf16[448,1024]{1,0:T(8,128)(2,1)S(1)}, bf16[448,1024]{1,0:T(8,128)(2,1)S(1)}, u32[]{:S(2)}, u32[]{:S(2)}) collective-permute-start(bf16[448,1024]{1,0:T(8,128)(2,1)S(1)} %copy-done.3), channel_id=1, source_target_pairs={{0,4},{1,5},{2,6},{3,7},{4,0},{5,1},{6,2},{7,3},{8,12},{9,13},{10,... | collective-permute-start | bytes 2752520 | tf_op jit(solution)/shard_map/ppermute | solution.py:125
  79.2 23.6 %collective-permute-start.11 = (bf16[2,448,512]{2,1,0:T(8,128)(2,1)S(1)}, bf16[2,448,512]{2,1,0:T(8,128)(2,1)S(1)}, u32[]{:S(2)}, u32[]{:S(2)}) collective-permute-start(bf16[2,448,512]{2,1,0:T(8,128)(2,1)S(1)} %pad_maximum_fusion.4), channel_id=1, source_target_pairs={{0,1},{1,0},{2,3},{3,2},{4,5},{5,4},{6,7},{7,6},{8,9},{9,8},{10,11... | collective-permute-start | bytes 2752520 | tf_op jit(solution)/shard_map/ppermute | solution.py:125
  97.4 8.8 %collective-permute-start.5 = (bf16[512,1792]{1,0:T(8,128)(2,1)S(1)}, bf16[512,1792]{1,0:T(8,128)(2,1)S(1)}, u32[]{:S(2)}, u32[]{:S(2)}) collective-permute-start(bf16[512,1792]{1,0:T(8,128)(2,1)S(1)} %constant_dynamic-update-slice_fusion), channel_id=1, source_target_pairs={{0,1},{1,0},{2,3},{3,2},{4,5},{5,4},{6,7},{7,6},{8,9},{9,8},{10,11... | collective-permute-start | bytes 5505032 | tf_op jit(solution)/shard_map/ppermute | solution.py:125
  102.8 22.8 %collective-permute-start.10 = (bf16[448,1024]{1,0:T(8,128)(2,1)S(1)}, bf16[448,1024]{1,0:T(8,128)(2,1)S(1)}, u32[]{:S(2)}, u32[]{:S(2)}) collective-permute-start(bf16[448,1024]{1,0:T(8,128)(2,1)S(1)} %copy-done.2), channel_id=1, source_target_pairs={{0,4},{1,5},{2,6},{3,7},{4,0},{5,1},{6,2},{7,3},{8,12},{9,13},{10,... | collective-permute-start | bytes 2752520 | tf_op jit(solution)/shard_map/ppermute | solution.py:125
  107.5 18.2 %collective-permute-start.7 = (bf16[2,512,256]{1,2,0:T(8,128)(2,1)S(1)}, bf16[2,512,256]{1,2,0:T(8,128)(2,1)S(1)}, u32[]{:S(2)}, u32[]{:S(2)}) collective-permute-start(bf16[2,512,256]{1,2,0:T(8,128)(2,1)S(1)} %pad_maximum_fusion.12), channel_id=1, source_target_pairs={{0,2},{1,3},{2,0},{3,1},{4,6},{5,7},{6,4},{7,5},{8,10},{9,11},{10,... | collective-permute-start | bytes 1572872 | tf_op jit(solution)/shard_map/ppermute | solution.py:125
  109.7 23.9 %collective-permute-start.14 = (bf16[2,512,256]{1,2,0:T(8,128)(2,1)S(1)}, bf16[2,512,256]{1,2,0:T(8,128)(2,1)S(1)}, u32[]{:S(2)}, u32[]{:S(2)}) collective-permute-start(bf16[2,512,256]{1,2,0:T(8,128)(2,1)S(1)} %pad_maximum_fusion.13), channel_id=1, source_target_pairs={{0,2},{1,3},{2,0},{3,1},{4,6},{5,7},{6,4},{7,5},{8,10},{9,11},{10,... | collective-permute-start | bytes 1572872 | tf_op jit(solution)/shard_map/ppermute | solution.py:125
  127.5 8.8 %collective-permute-start.8 = (bf16[512,256]{0,1:T(8,128)(2,1)S(1)}, bf16[512,256]{0,1:T(8,128)(2,1)S(1)}, u32[]{:S(2)}, u32[]{:S(2)}) collective-permute-start(bf16[512,256]{0,1:T(8,128)(2,1)S(1)} %select_convert_fusion.7), channel_id=1, source_target_pairs={{0,8},{1,9},{2,10},{3,11},{4,12},{5,13},{6,14},{7,15},{8,0},{9,1},... | collective-permute-start | bytes 786440 | tf_op jit(solution)/shard_map/ppermute | solution.py:125
  128.7 16.1 %collective-permute-start.21 = (bf16[2,512,256]{1,2,0:T(8,128)(2,1)S(1)}, bf16[2,512,256]{1,2,0:T(8,128)(2,1)S(1)}, u32[]{:S(2)}, u32[]{:S(2)}) collective-permute-start(bf16[2,512,256]{1,2,0:T(8,128)(2,1)S(1)} %pad_maximum_fusion.15), channel_id=1, source_target_pairs={{0,2},{1,3},{2,0},{3,1},{4,6},{5,7},{6,4},{7,5},{8,10},{9,11},{10,... | collective-permute-start | bytes 1572872 | tf_op jit(solution)/shard_map/ppermute | solution.py:125
  133.6 22.5 %collective-permute-start.24 = (bf16[2,512,256]{1,2,0:T(8,128)(2,1)S(1)}, bf16[2,512,256]{1,2,0:T(8,128)(2,1)S(1)}, u32[]{:S(2)}, u32[]{:S(2)}) collective-permute-start(bf16[2,512,256]{1,2,0:T(8,128)(2,1)S(1)} %pad_maximum_fusion.14), channel_id=1, source_target_pairs={{0,2},{1,3},{2,0},{3,1},{4,6},{5,7},{6,4},{7,5},{8,10},{9,11},{10,... | collective-permute-start | bytes 1572872 | tf_op jit(solution)/shard_map/ppermute | solution.py:125
  136.4 44.1 %collective-permute-start.15 = (bf16[256,256]{0,1:T(8,128)(2,1)S(1)}, bf16[256,256]{0,1:T(8,128)(2,1)S(1)}, u32[]{:S(2)}, u32[]{:S(2)}) collective-permute-start(bf16[256,256]{0,1:T(8,128)(2,1)S(1)} %slice.517), channel_id=1, source_target_pairs={{0,16},{1,17},{2,18},{3,19},{4,20},{5,21},{6,22},{7,23},{8,24},{9,... | collective-permute-start | bytes 393224 | tf_op jit(solution)/shard_map/ppermute | solution.py:125
  138.8 9.8 %collective-permute-start.16 = (bf16[512,256]{0,1:T(8,128)(2,1)S(1)}, bf16[512,256]{0,1:T(8,128)(2,1)S(1)}, u32[]{:S(2)}, u32[]{:S(2)}) collective-permute-start(bf16[512,256]{0,1:T(8,128)(2,1)S(1)} %select_convert_fusion.6), channel_id=1, source_target_pairs={{0,8},{1,9},{2,10},{3,11},{4,12},{5,13},{6,14},{7,15},{8,0},{9,1},... | collective-permute-start | bytes 786440 | tf_op jit(solution)/shard_map/ppermute | solution.py:125
  144.8 22.5 %collective-permute-start.27 = (bf16[2,512,256]{1,2,0:T(8,128)(2,1)S(1)}, bf16[2,512,256]{1,2,0:T(8,128)(2,1)S(1)}, u32[]{:S(2)}, u32[]{:S(2)}) collective-permute-start(bf16[2,512,256]{1,2,0:T(8,128)(2,1)S(1)} %pad_maximum_fusion.16), channel_id=1, source_target_pairs={{0,2},{1,3},{2,0},{3,1},{4,6},{5,7},{6,4},{7,5},{8,10},{9,11},{10,... | collective-permute-start | bytes 1572872 | tf_op jit(solution)/shard_map/ppermute | solution.py:125
  148.8 31.8 %collective-permute-start.22 = (bf16[256,256]{0,1:T(8,128)(2,1)S(1)}, bf16[256,256]{0,1:T(8,128)(2,1)S(1)}, u32[]{:S(2)}, u32[]{:S(2)}) collective-permute-start(bf16[256,256]{0,1:T(8,128)(2,1)S(1)} %slice.516), channel_id=1, source_target_pairs={{0,16},{1,17},{2,18},{3,19},{4,20},{5,21},{6,22},{7,23},{8,24},{9,... | collective-permute-start | bytes 393224 | tf_op jit(solution)/shard_map/ppermute | solution.py:125
  157.7 20.8 %collective-permute-start.30 = (bf16[2,512,256]{1,2,0:T(8,128)(2,1)S(1)}, bf16[2,512,256]{1,2,0:T(8,128)(2,1)S(1)}, u32[]{:S(2)}, u32[]{:S(2)}) collective-permute-start(bf16[2,512,256]{1,2,0:T(8,128)(2,1)S(1)} %pad_maximum_fusion.17), channel_id=1, source_target_pairs={{0,2},{1,3},{2,0},{3,1},{4,6},{5,7},{6,4},{7,5},{8,10},{9,11},{10,... | collective-permute-start | bytes 1572872 | tf_op jit(solution)/shard_map/ppermute | solution.py:125
  171.7 19.9 %collective-permute-start.34 = (bf16[2,512,256]{1,2,0:T(8,128)(2,1)S(1)}, bf16[2,512,256]{1,2,0:T(8,128)(2,1)S(1)}, u32[]{:S(2)}, u32[]{:S(2)}) collective-permute-start(bf16[2,512,256]{1,2,0:T(8,128)(2,1)S(1)} %pad_maximum_fusion.18), channel_id=1, source_target_pairs={{0,2},{1,3},{2,0},{3,1},{4,6},{5,7},{6,4},{7,5},{8,10},{9,11},{10,... | collective-permute-start | bytes 1572872 | tf_op jit(solution)/shard_map/ppermute | solution.py:125
  178.9 12.6 %collective-permute-start.32 = (bf16[512,256]{0,1:T(8,128)(2,1)S(1)}, bf16[512,256]{0,1:T(8,128)(2,1)S(1)}, u32[]{:S(2)}, u32[]{:S(2)}) collective-permute-start(bf16[512,256]{0,1:T(8,128)(2,1)S(1)} %select_convert_fusion.2), channel_id=1, source_target_pairs={{0,8},{1,9},{2,10},{3,11},{4,12},{5,13},{6,14},{7,15},{8,0},{9,1},... | collective-permute-start | bytes 786440 | tf_op jit(solution)/shard_map/ppermute | solution.py:125
  180.7 11.2 %collective-permute-start.25 = (bf16[256,256]{0,1:T(8,128)(2,1)S(1)}, bf16[256,256]{0,1:T(8,128)(2,1)S(1)}, u32[]{:S(2)}, u32[]{:S(2)}) collective-permute-start(bf16[256,256]{0,1:T(8,128)(2,1)S(1)} %slice.515), channel_id=1, source_target_pairs={{0,16},{1,17},{2,18},{3,19},{4,20},{5,21},{6,22},{7,23},{8,24},{9,... | collective-permute-start | bytes 393224 | tf_op jit(solution)/shard_map/ppermute | solution.py:125
  181.7 12.1 %collective-permute-start.28 = (bf16[256,256]{0,1:T(8,128)(2,1)S(1)}, bf16[256,256]{0,1:T(8,128)(2,1)S(1)}, u32[]{:S(2)}, u32[]{:S(2)}) collective-permute-start(bf16[256,256]{0,1:T(8,128)(2,1)S(1)} %slice.514), channel_id=1, source_target_pairs={{0,16},{1,17},{2,18},{3,19},{4,20},{5,21},{6,22},{7,23},{8,24},{9,... | collective-permute-start | bytes 393224 | tf_op jit(solution)/shard_map/ppermute | solution.py:125
  183.7 18.5 %collective-permute-start.37 = (bf16[2,512,256]{1,2,0:T(8,128)(2,1)S(1)}, bf16[2,512,256]{1,2,0:T(8,128)(2,1)S(1)}, u32[]{:S(2)}, u32[]{:S(2)}) collective-permute-start(bf16[2,512,256]{1,2,0:T(8,128)(2,1)S(1)} %pad_maximum_fusion.19), channel_id=1, source_target_pairs={{0,2},{1,3},{2,0},{3,1},{4,6},{5,7},{6,4},{7,5},{8,10},{9,11},{10,... | collective-permute-start | bytes 1572872 | tf_op jit(solution)/shard_map/ppermute | solution.py:125
  191.8 10.2 %collective-permute-start.35 = (bf16[512,256]{0,1:T(8,128)(2,1)S(1)}, bf16[512,256]{0,1:T(8,128)(2,1)S(1)}, u32[]{:S(2)}, u32[]{:S(2)}) collective-permute-start(bf16[512,256]{0,1:T(8,128)(2,1)S(1)} %select_convert_fusion.1), channel_id=1, source_target_pairs={{0,8},{1,9},{2,10},{3,11},{4,12},{5,13},{6,14},{7,15},{8,0},{9,1},... | collective-permute-start | bytes 786440 | tf_op jit(solution)/shard_map/ppermute | solution.py:125
  194.0 13.1 %collective-permute-start.33 = (bf16[256,256]{0,1:T(8,128)(2,1)S(1)}, bf16[256,256]{0,1:T(8,128)(2,1)S(1)}, u32[]{:S(2)}, u32[]{:S(2)}) collective-permute-start(bf16[256,256]{0,1:T(8,128)(2,1)S(1)} %slice.512), channel_id=1, source_target_pairs={{0,16},{1,17},{2,18},{3,19},{4,20},{5,21},{6,22},{7,23},{8,24},{9,... | collective-permute-start | bytes 393224 | tf_op jit(solution)/shard_map/ppermute | solution.py:125
  202.3 8.8 %collective-permute-start.38 = (bf16[512,256]{0,1:T(8,128)(2,1)S(1)}, bf16[512,256]{0,1:T(8,128)(2,1)S(1)}, u32[]{:S(2)}, u32[]{:S(2)}) collective-permute-start(bf16[512,256]{0,1:T(8,128)(2,1)S(1)} %select_convert_fusion), channel_id=1, source_target_pairs={{0,8},{1,9},{2,10},{3,11},{4,12},{5,13},{6,14},{7,15},{8,0},{9,1},... | collective-permute-start | bytes 786440 | tf_op jit(solution)/shard_map/ppermute | solution.py:125
  207.1 11.2 %collective-permute-start.36 = (bf16[256,256]{0,1:T(8,128)(2,1)S(1)}, bf16[256,256]{0,1:T(8,128)(2,1)S(1)}, u32[]{:S(2)}, u32[]{:S(2)}) collective-permute-start(bf16[256,256]{0,1:T(8,128)(2,1)S(1)} %slice.511), channel_id=1, source_target_pairs={{0,16},{1,17},{2,18},{3,19},{4,20},{5,21},{6,22},{7,23},{8,24},{9,... | collective-permute-start | bytes 393224 | tf_op jit(solution)/shard_map/ppermute | solution.py:125
  (12 other events, 74.6 us)

commit v6 on v5

v6 whole, which is shorter than its diff:
```python
import jax
import jax.numpy as jnp
from jax import lax
from jax.experimental import pallas as pl
from jax.experimental.pallas import tpu as pltpu
from jax.sharding import PartitionSpec as P

AXES = ("fsdp", "tp")
ROW_CHUNKS = 2
CHUNKS = ((0, 1), (1, 1), (2, 2))


def adam(where, chunks, args, previous):
    rows, cols = args[0].shape
    widths = [cols // 16 * count for first, count in chunks]
    width = sum(widths)
    step = max(s for s in range(16, 449, 16) if rows % s == 0)
    tiles = rows // step
    spread = cols // 4 // width
    start = chunks[0][0] * (cols // 16) // width

    def kernel(where_ref, master_ref, one_ref, two_ref, grad_ref, *refs):
        outs = refs[-3 - len(chunks) :]
        grad = grad_ref[...].astype(jnp.float32)
        new_one = 0.9 * one_ref[...] + 0.1 * grad
        new_two = 0.95 * two_ref[...] + 0.05 * grad * grad
        new_master = master_ref[...] - 0.001 * new_one / (jnp.sqrt(new_two) + 1e-08)
        outs[0][...] = new_master
        outs[1][...] = new_one
        outs[2][...] = new_two
        at = 0
        for ref, size in zip(outs[3:], widths):
            ref[...] = new_master[:, at : at + size].astype(jnp.bfloat16)
            at += size

    def at(i, w):
        return i % tiles, i // tiles * spread + start

    def piece_at(i, w):
        j = i // tiles
        return i % tiles, 2 * ((j % 2) ^ w[1]) + ((j // 2) ^ w[0])

    block = pl.BlockSpec((step, width), at)
    full = jax.ShapeDtypeStruct((rows, cols), jnp.float32)
    size = 4 * rows * width
    out = pl.pallas_call(
        kernel,
        grid_spec=pltpu.PrefetchScalarGridSpec(
            num_scalar_prefetch=1,
            grid=(4 * tiles,),
            in_specs=[block] * 4 + [pl.BlockSpec(memory_space=pl.ANY)] * len(previous),
            out_specs=[block] * 3 + [pl.BlockSpec((step, size), piece_at) for size in widths],
        ),
        out_shape=[full] * 3 + [jax.ShapeDtypeStruct((rows, 4 * size), jnp.bfloat16) for size in widths],
        input_output_aliases={5 + i: i for i in range(len(previous))},
        compiler_params=pltpu.CompilerParams(vmem_limit_bytes=60 * 1024 * 1024),
        cost_estimate=pl.CostEstimate(flops=12 * size, bytes_accessed=28 * size, transcendentals=size),
        name="adam",
    )(where, *args, *previous)
    return out[:3], out[3:]


def pack(where, act, xs):
    rows, cols = act.shape
    run = cols // xs // 2
    part = rows // ROW_CHUNKS

    def kernel(where_ref, act_ref, *out_refs):
        for y in range(2):
            for x in range(xs):

                @pl.when((where_ref[0] == y) & (where_ref[2] == x))
                def _():
                    for m in range(ROW_CHUNKS):
                        for s in range(2):
                            for d in range(xs):
                                at = (2 * (x ^ d) + (y ^ s)) * run
                                out_refs[2 * m + s][:, d * run : (d + 1) * run] = act_ref[
                                    m * part : (m + 1) * part, at : at + run
                                ]

    out = pl.pallas_call(
        kernel,
        in_specs=[pl.BlockSpec(memory_space=pltpu.SMEM), pl.BlockSpec(memory_space=pltpu.VMEM)],
        out_specs=[pl.BlockSpec(memory_space=pltpu.VMEM)] * (2 * ROW_CHUNKS),
        out_shape=[jax.ShapeDtypeStruct((part, cols // 2), act.dtype)] * (2 * ROW_CHUNKS),
        compiler_params=pltpu.CompilerParams(vmem_limit_bytes=32 * 1024 * 1024),
        cost_estimate=pl.CostEstimate(flops=0, bytes_accessed=4 * rows * cols, transcendentals=0),
        name="pack",
    )(where, act)
    return out[0::2], out[1::2]


def swap_if(flag, low, high):
    return jnp.where(flag, high, low), jnp.where(flag, low, high)


def after(value, *done):
    return lax.optimization_barrier((value, *done))[0] if done else value


def local(master, moment_one, moment_two, gradient, hidden_act):
    fsdp, tp = lax.axis_size("fsdp"), lax.axis_size("tp")
    xs = fsdp // tp
    f, t = lax.axis_index("fsdp"), lax.axis_index("tp")
    z, x, y, c = f // xs, f % xs, t // 2, t % 2
    where = jnp.stack([y, c, x]).astype(jnp.int32)

    def permute(value, to):
        pairs = []
        for zi in range(tp):
            for xi in range(xs):
                for yi in range(2):
                    for ci in range(2):
                        zo, xo, yo, co = to(zi, xi, yi, ci)
                        pairs.append(((zi * xs + xi) * tp + 2 * yi + ci, (zo * xs + xo) * tp + 2 * yo + co))
        return lax.ppermute(value, AXES, pairs)

    rows = hidden_act.shape[0]
    part = rows // ROW_CHUNKS
    own, other = pack(where, hidden_act, xs)

    args = (master, moment_one, moment_two, gradient)
    updated, pieces = [], []

    def update(chunks, *done):
        new, weights = adam(after(where, *done), chunks, args, updated)
        updated[:] = new
        pieces.extend(weights)

    flip = (c ^ (z % 2)) != 0
    crossed, used, tables = [], [], []
    theirs, pairs, moved, acts = [], [], [], []
    sends, backs, leaving, result = [], [], [], []

    def cross(m):
        theirs.append(permute(other[m], lambda z, x, y, c: (z, x, 1 - y, c)))

    def to_plane(m, *done):
        pair = after(swap_if(((z // 2) ^ y) != 0, own[m], theirs[m]), *done)
        pairs.append(pair)
        moved.append(
            [permute(data, lambda z, x, y, c: (2 * ((z // 2) ^ a) + c, x, y, z % 2)) for a, data in enumerate(pair)]
        )

    def to_cores(m, *done):
        got = after(moved[m], *done)
        acts.append(got + [permute(data, lambda z, x, y, c: (z, x, y, 1 - c)) for data in got])

    def gather(q, *done):
        piece = after(pieces[q], *done)
        crossed.append([piece] + [permute(piece, lambda z, x, y, c: (z, x ^ d, y, c)) for d in range(1, xs)])

    def to_table(q, *done):
        parts = after(crossed[q], *done)
        half = parts[0].shape[1] // 2
        width = half // CHUNKS[q][1]
        near = jnp.stack([p[:, :half] for p in parts])
        far = []
        for at in range(half, 2 * half, width):
            there = jnp.stack([p[:, at : at + width] for p in parts])
            far.append(permute(there, lambda z, x, y, c: (z, x, y, 1 - c)))
        far = jnp.concatenate(far, axis=2)
        tables.append(jnp.stack(swap_if(c != 0, near, far), axis=1).reshape(-1, half))

    def multiply(m, q, *done):
        table = after(tables[q], *done)
        half = table.shape[1] // 2
        totals = [jnp.dot(a, table, preferred_element_type=jnp.float32) for a in acts[m]]
        width = half // CHUNKS[q][1]
        jobs = []
        for at in range(0, half, width):
            send = jnp.stack([total[:, half + at : half + at + width].astype(jnp.bfloat16) for total in totals])
            send = after(send, *sends[-1:], *backs[-2:-1])
            sends.append(send)
            backs.append(permute(send, lambda z, x, y, c: (z, x, 1 - y, c)))
            jobs.append(([total[:, at : at + width] for total in totals], len(backs) - 1))
        return jobs

    def reduce(totals, j):
        back = after(backs[j], leaving[-1]) if leaving else backs[j]
        totals = [total + b for total, b in zip(totals, back)]
        near, far = zip(*[swap_if(flip, own, sibling) for own, sibling in zip(totals[:2], totals[2:])])
        back = permute(jnp.stack(far).astype(jnp.bfloat16), lambda z, x, y, c: (z ^ 1, x, y, c))
        back = after(back, *sends[j + 3 : j + 4])
        send = (near[1] + back[1]).astype(jnp.bfloat16)
        leaving.append(send)
        back = near[0] + back[0] + permute(send, lambda z, x, y, c: (z ^ 2, x, y, c))
        result.append(back.astype(jnp.bfloat16))

    update(CHUNKS[:2], own[0])
    cross(0)
    cross(1)
    gather(0)
    gather(1)
    update(CHUNKS[2:])
    to_plane(0, pieces[2])
    gather(2, crossed[0][-1])
    to_table(0)
    to_table(1)
    to_cores(0)
    to_plane(1, *moved[0])
    jobs = multiply(0, 0) + multiply(0, 1)
    to_table(2, backs[0])
    jobs += multiply(0, 2)
    to_cores(1, backs[2])
    for q in range(len(CHUNKS)):
        jobs += multiply(1, q)
    for job in jobs:
        reduce(*job)
    count = len(result) // ROW_CHUNKS
    result = [jnp.concatenate(result[i : i + count], axis=1) for i in range(0, len(result), count)]
    decoded = jnp.concatenate(result, axis=0)
    return (*updated, decoded)


def solution(mesh):
    placed = (
        P(("fsdp", "tp"), None),
        P(("fsdp", "tp"), None),
        P(("fsdp", "tp"), None),
        P(("fsdp", "tp"), None),
        P("fsdp", "tp"),
    )
    return jax.shard_map(
        local,
        mesh=mesh,
        in_specs=placed,
        out_specs=(
            P(("fsdp", "tp"), None),
            P(("fsdp", "tp"), None),
            P(("fsdp", "tp"), None),
            P("fsdp", "tp"),
        ),
        check_vma=False,
    )
```

time: 223 us -> 223 us (level)
  waiting for transfers between devices: 96.8 us -> 127 us
  starting transfers between devices: 52 us -> 35.9 us
  Pallas kernels: 29.8 us -> 21.9 us
  local copies, waits for them, and re-layouts: 12.3 us -> 7.02 us
    ppermute x40 -> x41, waiting for transfers between devices: 96.8 us -> 127 us  [permute(): return lax.ppermute(value, AXES, pairs)]
    ppermute x40 -> x41, starting transfers between devices: 52 us -> 35.9 us  [permute(): return lax.ppermute(value, AXES, pairs)]
    pallas_call x4 -> x2, Pallas kernels: 28 us -> 20.2 us  [adam(): pl.pallas_call(kernel, grid_spec=pltpu.PrefetchScalarGridSpec(num_scalar_...]
    unnamed x11 -> x6, local copies, waits for them, and re-layouts: 4.67 us -> 2.05 us
    another operation x28 -> x33, local copies, waits for them, and re-layouts: 6.14 us -> 4.98 us  [the longest x5 4.14 us: to_table(): near = jnp.stack([p[:, :half] for p in parts])]
    dot_general x16 -> x24, matrix products: 18.7 us -> 19.2 us  [multiply(): jnp.dot(a, table, preferred_element_type=jnp.float32)]
  transfers between devices with their start and end apart: 40 -> 41, of which waited for: 21 -> 24; matrix products, arithmetic and copies ran while one was open for 17% -> 15% of each run, Pallas kernels for 13% -> 9%
where the time goes in v6:
time: 223 us
  waiting for transfers between devices  127 us (57%)
  starting transfers between devices  35.9 us (16%)
  Pallas kernels  21.9 us (10%)
  matrix products  19.2 us (9%)
  other arithmetic  9.92 us (4%)
  local copies, waits for them, and re-layouts  7.02 us (3%)
    ppermute x41, waiting for transfers between devices, permute(): return lax.ppermute(value, AXES, pairs)  127 us
    ppermute x41, starting transfers between devices, permute(): return lax.ppermute(value, AXES, pairs)  35.9 us
    pallas_call x2, Pallas kernels, adam(): pl.pallas_call(kernel, grid_spec=pltpu.PrefetchScalarGridSpec(num_scalar_...  20.2 us
    dot_general x24, matrix products, multiply(): jnp.dot(a, table, preferred_element_type=jnp.float32)  19.2 us
  transfers between devices with their start and end apart: 41, of which 24 were waited for; matrix products, arithmetic and copies ran while one was open for 15% of the time, Pallas kernels for 9%

profile of v6, /device:TPU:0, one launch (start us, length us, event | category | flops | bytes accessed | tf_op | source)
XLA Modules:
  0.0 222.7 jit_solution(14629495034565343740)
XLA Ops:
  0.7 2.0 copy-done
  2.8 1.8 pack.1
  4.6 3.0 %collective-permute-start = (bf16[256,1792]{1,0:T(8,128)(2,1)}, bf16[256,1792]{1,0:T(8,128)(2,1)}, u32[]{:S(2)}, u32[]{:S(2)}) collective-permute-start(bf16[256,1792]{1,0:T(8,128)(2,1)} %get-tuple-element.54), channel_id=1, source_target_pairs={{0,2},{1,3},{2,0},{3,1},{4,6},{5,7},{6,4},{7,5},{8,10},{9,11},{10,... | collective-permute-start | bytes 2752520 | tf_op jit(solution)/shard_map/ppermute | solution.py:117
  7.5 10.0 %adam.2 = (f32[448,4096]{1,0:T(8,128)}, f32[448,4096]{1,0:T(8,128)}, f32[448,4096]{1,0:T(8,128)}, bf16[448,1024]{1,0:T(8,128)(2,1)}, bf16[448,1024]{1,0:T(8,128)(2,1)}) custom-call(s32[3]{0:T(128)} %copy-done.1, f32[448,4096]{1,0:T(8,128)} %master_ref.3, f32[448,4096]{1,0:T(8,128)} %one_ref.3, f32[448,4096]{1,0:T(8,128)} %two_ref.3, bf16[448,4096]{1,0:T(8,128)(2,1)} %grad_ref.3), custom_call_target="tpu_custom_call" | custom-call | flops 11010048 | bytes 25690112 | tf_op jit(solution)/shard_map/adam/pallas_call | solution.py:46
  19.6 10.2 %adam.3 = (f32[448,4096]{1,0:T(8,128)}, f32[448,4096]{1,0:T(8,128)}, f32[448,4096]{1,0:T(8,128)}, bf16[448,2048]{1,0:T(8,128)(2,1)}) custom-call(s32[3]{0:T(128)} %copy-done.1, f32[448,4096]{1,0:T(8,128)} %master_ref.3, f32[448,4096]{1,0:T(8,128)} %one_ref.3, f32[448,4096]{1,0:T(8,128)} %two_ref.3, ...), custom_call_target="tpu_custom_call", output_to_operand_aliasing={{0}: (5, {}), {1}: (6, {}), {2}: (7, {})} | custom-call | flops 11010048 | bytes 25690112 | tf_op jit(solution)/shard_map/adam/pallas_call | solution.py:46
  33.5 3.1 %collective-permute-start.5 = (bf16[256,1792]{1,0:T(8,128)(2,1)S(1)}, bf16[256,1792]{1,0:T(8,128)(2,1)S(1)}, u32[]{:S(2)}, u32[]{:S(2)}) collective-permute-start(bf16[256,1792]{1,0:T(8,128)(2,1)S(1)} %get-tuple-element.58), channel_id=1, source_target_pairs={{0,16},{1,24},{2,18},{3,26},{4,20},{5,28},{6,22},{7,30},{8,17},{9,... | collective-permute-start | bytes 2752520 | tf_op jit(solution)/shard_map/ppermute | solution.py:117
  36.6 4.5 %collective-permute-done.3 = bf16[448,1024]{1,0:T(8,128)(2,1)} collective-permute-done((bf16[448,1024]{1,0:T(8,128)(2,1)}, bf16[448,1024]{1,0:T(8,128)(2,1)}, u32[]{:S(2)}, u32[]{:S(2)}) %collective-permute-start.3) | collective-permute-done | bytes 917536 | tf_op jit(solution)/shard_map/ppermute | solution.py:117
  43.9 16.9 %collective-permute-done.12 = bf16[448,1024]{1,0:T(8,128)(2,1)} collective-permute-done((bf16[448,1024]{1,0:T(8,128)(2,1)}, bf16[448,1024]{1,0:T(8,128)(2,1)}, u32[]{:S(2)}, u32[]{:S(2)}) %collective-permute-start.12) | collective-permute-done | bytes 917536 | tf_op jit(solution)/shard_map/ppermute | solution.py:117
  64.0 12.5 %collective-permute-done.5 = bf16[256,1792]{1,0:T(8,128)(2,1)S(1)} collective-permute-done((bf16[256,1792]{1,0:T(8,128)(2,1)S(1)}, bf16[256,1792]{1,0:T(8,128)(2,1)S(1)}, u32[]{:S(2)}, u32[]{:S(2)}) %collective-permute-start.5) | collective-permute-done | bytes 917536 | tf_op jit(solution)/shard_map/ppermute | solution.py:117
  79.0 4.3 %collective-permute-start.6 = (bf16[256,1792]{1,0:T(8,128)(2,1)S(1)}, bf16[256,1792]{1,0:T(8,128)(2,1)S(1)}, u32[]{:S(2)}, u32[]{:S(2)}) collective-permute-start(bf16[256,1792]{1,0:T(8,128)(2,1)S(1)} %collective-permute-done.5), channel_id=1, source_target_pairs={{0,1},{1,0},{2,3},{3,2},{4,5},{5,4},{6,7},{7,6},{8,9},{9,8},{10,11... | collective-permute-start | bytes 2752520 | tf_op jit(solution)/shard_map/ppermute | solution.py:117
  87.5 1.6 collective-permute-start.7
  91.1 7.5 %collective-permute-done.9 = bf16[448,2048]{1,0:T(8,128)(2,1)S(1)} collective-permute-done((bf16[448,2048]{1,0:T(8,128)(2,1)S(1)}, bf16[448,2048]{1,0:T(8,128)(2,1)S(1)}, u32[]{:S(2)}, u32[]{:S(2)}) %collective-permute-start.9) | collective-permute-done | bytes 1835040 | tf_op jit(solution)/shard_map/ppermute | solution.py:117
  98.5 3.8 %collective-permute-done.7 = bf16[4,256,256]{2,1,0:T(8,128)(2,1)S(1)} collective-permute-done((bf16[4,256,256]{2,1,0:T(8,128)(2,1)S(1)}, bf16[4,256,256]{2,1,0:T(8,128)(2,1)S(1)}, u32[]{:S(2)}, u32[]{:S(2)}) %collective-permute-start.7) | collective-permute-done | bytes 524320 | tf_op jit(solution)/shard_map/ppermute | solution.py:117
  112.4 1.6 collective-permute-start.20
  114.7 3.4 %collective-permute-done.8 = bf16[2,256,256]{2,1,0:T(8,128)(2,1)S(1)} collective-permute-done((bf16[2,256,256]{2,1,0:T(8,128)(2,1)S(1)}, bf16[2,256,256]{2,1,0:T(8,128)(2,1)S(1)}, u32[]{:S(2)}, u32[]{:S(2)}) %collective-permute-start.8) | collective-permute-done | bytes 262176 | tf_op jit(solution)/shard_map/ppermute | solution.py:117
  118.5 8.7 %collective-permute-done.20 = bf16[4,256,256]{2,1,0:T(8,128)(2,1)S(1)} collective-permute-done((bf16[4,256,256]{2,1,0:T(8,128)(2,1)S(1)}, bf16[4,256,256]{2,1,0:T(8,128)(2,1)S(1)}, u32[]{:S(2)}, u32[]{:S(2)}) %collective-permute-start.20) | collective-permute-done | bytes 524320 | tf_op jit(solution)/shard_map/ppermute | solution.py:117
  142.4 4.5 %collective-permute-done.24 = bf16[2,256,256]{2,1,0:T(8,128)(2,1)S(1)} collective-permute-done((bf16[2,256,256]{2,1,0:T(8,128)(2,1)S(1)}, bf16[2,256,256]{2,1,0:T(8,128)(2,1)S(1)}, u32[]{:S(2)}, u32[]{:S(2)}) %collective-permute-start.24) | collective-permute-done | bytes 262176 | tf_op jit(solution)/shard_map/ppermute | solution.py:117
  147.3 6.7 %collective-permute-done.26 = bf16[256,256]{1,0:T(8,128)(2,1)S(1)} collective-permute-done((bf16[256,256]{1,0:T(8,128)(2,1)S(1)}, bf16[256,256]{1,0:T(8,128)(2,1)S(1)}, u32[]{:S(2)}, u32[]{:S(2)}) %collective-permute-start.26) | collective-permute-done | bytes 131104 | tf_op jit(solution)/shard_map/ppermute | solution.py:117
  154.5 7.0 %collective-permute-done.27 = bf16[2,256,256]{2,1,0:T(8,128)(2,1)S(1)} collective-permute-done((bf16[2,256,256]{2,1,0:T(8,128)(2,1)S(1)}, bf16[2,256,256]{2,1,0:T(8,128)(2,1)S(1)}, u32[]{:S(2)}, u32[]{:S(2)}) %collective-permute-start.27) | collective-permute-done | bytes 262176 | tf_op jit(solution)/shard_map/ppermute | solution.py:117
  163.1 8.5 %collective-permute-done.30 = bf16[2,256,256]{2,1,0:T(8,128)(2,1)S(1)} collective-permute-done((bf16[2,256,256]{2,1,0:T(8,128)(2,1)S(1)}, bf16[2,256,256]{2,1,0:T(8,128)(2,1)S(1)}, u32[]{:S(2)}, u32[]{:S(2)}) %collective-permute-start.30) | collective-permute-done | bytes 262176 | tf_op jit(solution)/shard_map/ppermute | solution.py:117
  172.0 2.0 collective-permute-start.15
  174.0 9.7 %collective-permute-done.33 = bf16[2,256,256]{2,1,0:T(8,128)(2,1)S(1)} collective-permute-done((bf16[2,256,256]{2,1,0:T(8,128)(2,1)S(1)}, bf16[2,256,256]{2,1,0:T(8,128)(2,1)S(1)}, u32[]{:S(2)}, u32[]{:S(2)}) %collective-permute-start.33) | collective-permute-done | bytes 262176 | tf_op jit(solution)/shard_map/ppermute | solution.py:117
  185.4 2.1 collective-permute-start.23
  187.4 6.5 %collective-permute-done.36 = bf16[2,256,256]{2,1,0:T(8,128)(2,1)S(1)} collective-permute-done((bf16[2,256,256]{2,1,0:T(8,128)(2,1)S(1)}, bf16[2,256,256]{2,1,0:T(8,128)(2,1)S(1)}, u32[]{:S(2)}, u32[]{:S(2)}) %collective-permute-start.36) | collective-permute-done | bytes 262176 | tf_op jit(solution)/shard_map/ppermute | solution.py:117
  194.1 2.4 %collective-permute-done.23 = bf16[256,256]{1,0:T(8,128)(2,1)S(1)} collective-permute-done((bf16[256,256]{1,0:T(8,128)(2,1)S(1)}, bf16[256,256]{1,0:T(8,128)(2,1)S(1)}, u32[]{:S(2)}, u32[]{:S(2)}) %collective-permute-start.23) | collective-permute-done | bytes 131104 | tf_op jit(solution)/shard_map/ppermute | solution.py:117
  197.2 2.4 %collective-permute-start.32 = (bf16[256,256]{1,0:T(8,128)(2,1)S(1)}, bf16[256,256]{1,0:T(8,128)(2,1)S(1)}, u32[]{:S(2)}, u32[]{:S(2)}) collective-permute-start(bf16[256,256]{1,0:T(8,128)(2,1)S(1)} %fusion.9), channel_id=1, source_target_pairs={{0,16},{1,17},{2,18},{3,19},{4,20},{5,21},{6,22},{7,23},{8,24},{9,... | collective-permute-start | bytes 393224 | tf_op jit(solution)/shard_map/ppermute | solution.py:117
  199.6 6.5 %collective-permute-done.37 = bf16[256,256]{1,0:T(8,128)(2,1)S(1)} collective-permute-done((bf16[256,256]{1,0:T(8,128)(2,1)S(1)}, bf16[256,256]{1,0:T(8,128)(2,1)S(1)}, u32[]{:S(2)}, u32[]{:S(2)}) %collective-permute-start.37) | collective-permute-done | bytes 131104 | tf_op jit(solution)/shard_map/ppermute | solution.py:117
  206.4 2.4 %collective-permute-done.29 = bf16[256,256]{1,0:T(8,128)(2,1)S(1)} collective-permute-done((bf16[256,256]{1,0:T(8,128)(2,1)S(1)}, bf16[256,256]{1,0:T(8,128)(2,1)S(1)}, u32[]{:S(2)}, u32[]{:S(2)}) %collective-permute-start.29) | collective-permute-done | bytes 131104 | tf_op jit(solution)/shard_map/ppermute | solution.py:117
  208.9 2.7 %collective-permute-done.32 = bf16[256,256]{1,0:T(8,128)(2,1)S(1)} collective-permute-done((bf16[256,256]{1,0:T(8,128)(2,1)S(1)}, bf16[256,256]{1,0:T(8,128)(2,1)S(1)}, u32[]{:S(2)}, u32[]{:S(2)}) %collective-permute-start.32) | collective-permute-done | bytes 131104 | tf_op jit(solution)/shard_map/ppermute | solution.py:117
  211.9 2.5 %collective-permute-done.39 = bf16[2,256,256]{2,1,0:T(8,128)(2,1)S(1)} collective-permute-done((bf16[2,256,256]{2,1,0:T(8,128)(2,1)S(1)}, bf16[2,256,256]{2,1,0:T(8,128)(2,1)S(1)}, u32[]{:S(2)}, u32[]{:S(2)}) %collective-permute-start.39) | collective-permute-done | bytes 262176 | tf_op jit(solution)/shard_map/ppermute | solution.py:117
  215.0 3.4 %collective-permute-done.34 = bf16[256,256]{1,0:T(8,128)(2,1)S(1)} collective-permute-done((bf16[256,256]{1,0:T(8,128)(2,1)S(1)}, bf16[256,256]{1,0:T(8,128)(2,1)S(1)}, u32[]{:S(2)}, u32[]{:S(2)}) %collective-permute-start.34) | collective-permute-done | bytes 131104 | tf_op jit(solution)/shard_map/ppermute | solution.py:117
  218.5 3.0 %collective-permute-done.40 = bf16[256,256]{1,0:T(8,128)(2,1)S(1)} collective-permute-done((bf16[256,256]{1,0:T(8,128)(2,1)S(1)}, bf16[256,256]{1,0:T(8,128)(2,1)S(1)}, u32[]{:S(2)}, u32[]{:S(2)}) %collective-permute-start.40) | collective-permute-done | bytes 131104 | tf_op jit(solution)/shard_map/ppermute | solution.py:117
  (168 shorter events, 54.1 us)
Async XLA Ops:
  4.6 26.8 %collective-permute-start = (bf16[256,1792]{1,0:T(8,128)(2,1)}, bf16[256,1792]{1,0:T(8,128)(2,1)}, u32[]{:S(2)}, u32[]{:S(2)}) collective-permute-start(bf16[256,1792]{1,0:T(8,128)(2,1)} %get-tuple-element.54), channel_id=1, source_target_pairs={{0,2},{1,3},{2,0},{3,1},{4,6},{5,7},{6,4},{7,5},{8,10},{9,11},{10,... | collective-permute-start | bytes 2752520 | tf_op jit(solution)/shard_map/ppermute | solution.py:117
  17.5 23.6 %collective-permute-start.3 = (bf16[448,1024]{1,0:T(8,128)(2,1)}, bf16[448,1024]{1,0:T(8,128)(2,1)}, u32[]{:S(2)}, u32[]{:S(2)}) collective-permute-start(bf16[448,1024]{1,0:T(8,128)(2,1)} %get-tuple-element.57), channel_id=1, source_target_pairs={{0,4},{1,5},{2,6},{3,7},{4,0},{5,1},{6,2},{7,3},{8,12},{9,13},{10,... | collective-permute-start | bytes 2752520 | tf_op jit(solution)/shard_map/ppermute | solution.py:117
  19.0 43.1 %collective-permute-start.17 = (bf16[256,1792]{1,0:T(8,128)(2,1)S(1)}, bf16[256,1792]{1,0:T(8,128)(2,1)}, u32[]{:S(2)}, u32[]{:S(2)}) collective-permute-start(bf16[256,1792]{1,0:T(8,128)(2,1)S(1)} %get-tuple-element.68), channel_id=1, source_target_pairs={{0,2},{1,3},{2,0},{3,1},{4,6},{5,7},{6,4},{7,5},{8,10},{9,11},{10,... | collective-permute-start | bytes 2752520 | tf_op jit(solution)/shard_map/ppermute | solution.py:117
  19.5 41.3 %collective-permute-start.12 = (bf16[448,1024]{1,0:T(8,128)(2,1)}, bf16[448,1024]{1,0:T(8,128)(2,1)}, u32[]{:S(2)}, u32[]{:S(2)}) collective-permute-start(bf16[448,1024]{1,0:T(8,128)(2,1)} %get-tuple-element.62), channel_id=1, source_target_pairs={{0,4},{1,5},{2,6},{3,7},{4,0},{5,1},{6,2},{7,3},{8,12},{9,13},{10,... | collective-permute-start | bytes 2752520 | tf_op jit(solution)/shard_map/ppermute | solution.py:117
  32.8 31.2 %collective-permute-start.1 = (bf16[256,1792]{1,0:T(8,128)(2,1)S(1)}, bf16[256,1792]{1,0:T(8,128)(2,1)S(1)}, u32[]{:S(2)}, u32[]{:S(2)}) collective-permute-start(bf16[256,1792]{1,0:T(8,128)(2,1)S(1)} %get-tuple-element.56), channel_id=1, source_target_pairs={{0,0},{1,8},{2,2},{3,10},{4,4},{5,12},{6,6},{7,14},{8,1},{9,9},{10... | collective-permute-start | bytes 2752520 | tf_op jit(solution)/shard_map/ppermute | solution.py:117
  33.5 42.9 %collective-permute-start.5 = (bf16[256,1792]{1,0:T(8,128)(2,1)S(1)}, bf16[256,1792]{1,0:T(8,128)(2,1)S(1)}, u32[]{:S(2)}, u32[]{:S(2)}) collective-permute-start(bf16[256,1792]{1,0:T(8,128)(2,1)S(1)} %get-tuple-element.58), channel_id=1, source_target_pairs={{0,16},{1,24},{2,18},{3,26},{4,20},{5,28},{6,22},{7,30},{8,17},{9,... | collective-permute-start | bytes 2752520 | tf_op jit(solution)/shard_map/ppermute | solution.py:117
  41.1 57.4 %collective-permute-start.9 = (bf16[448,2048]{1,0:T(8,128)(2,1)S(1)}, bf16[448,2048]{1,0:T(8,128)(2,1)S(1)}, u32[]{:S(2)}, u32[]{:S(2)}) collective-permute-start(bf16[448,2048]{1,0:T(8,128)(2,1)S(1)} %copy-done.2), channel_id=1, source_target_pairs={{0,4},{1,5},{2,6},{3,7},{4,0},{5,1},{6,2},{7,3},{8,12},{9,13},{10,... | collective-permute-start | bytes 5505032 | tf_op jit(solution)/shard_map/ppermute | solution.py:117
  60.8 16.7 %collective-permute-start.4 = (bf16[2,448,512]{2,1,0:T(8,128)(2,1)S(1)}, bf16[2,448,512]{2,1,0:T(8,128)(2,1)S(1)}, u32[]{:S(2)}, u32[]{:S(2)}) collective-permute-start(bf16[2,448,512]{2,1,0:T(8,128)(2,1)S(1)} %pad_maximum_fusion.5), channel_id=1, source_target_pairs={{0,1},{1,0},{2,3},{3,2},{4,5},{5,4},{6,7},{7,6},{8,9},{9,8},{10,11... | collective-permute-start | bytes 2752520 | tf_op jit(solution)/shard_map/ppermute | solution.py:117
  62.1 16.4 %collective-permute-start.13 = (bf16[2,448,512]{2,1,0:T(8,128)(2,1)S(1)}, bf16[2,448,512]{2,1,0:T(8,128)(2,1)S(1)}, u32[]{:S(2)}, u32[]{:S(2)}) collective-permute-start(bf16[2,448,512]{2,1,0:T(8,128)(2,1)S(1)} %pad_maximum_fusion.9), channel_id=1, source_target_pairs={{0,1},{1,0},{2,3},{3,2},{4,5},{5,4},{6,7},{7,6},{8,9},{9,8},{10,11... | collective-permute-start | bytes 2752520 | tf_op jit(solution)/shard_map/ppermute | solution.py:117
  76.5 42.0 %collective-permute-start.18 = (bf16[256,1792]{1,0:T(8,128)(2,1)S(1)}, bf16[256,1792]{1,0:T(8,128)(2,1)S(1)}, u32[]{:S(2)}, u32[]{:S(2)}) collective-permute-start(bf16[256,1792]{1,0:T(8,128)(2,1)S(1)} %get-tuple-element.70), channel_id=1, source_target_pairs={{0,0},{1,8},{2,2},{3,10},{4,4},{5,12},{6,6},{7,14},{8,1},{9,9},{10... | collective-permute-start | bytes 2752520 | tf_op jit(solution)/shard_map/ppermute | solution.py:117
  77.4 41.1 %collective-permute-start.19 = (bf16[256,1792]{1,0:T(8,128)(2,1)S(1)}, bf16[256,1792]{1,0:T(8,128)(2,1)S(1)}, u32[]{:S(2)}, u32[]{:S(2)}) collective-permute-start(bf16[256,1792]{1,0:T(8,128)(2,1)S(1)} %get-tuple-element.71), channel_id=1, source_target_pairs={{0,16},{1,24},{2,18},{3,26},{4,20},{5,28},{6,22},{7,30},{8,17},{9,... | collective-permute-start | bytes 2752520 | tf_op jit(solution)/shard_map/ppermute | solution.py:117
  87.5 14.8 %collective-permute-start.7 = (bf16[4,256,256]{2,1,0:T(8,128)(2,1)S(1)}, bf16[4,256,256]{2,1,0:T(8,128)(2,1)S(1)}, u32[]{:S(2)}, u32[]{:S(2)}) collective-permute-start(bf16[4,256,256]{2,1,0:T(8,128)(2,1)S(1)} %pad_maximum_fusion.11), channel_id=1, source_target_pairs={{0,2},{1,3},{2,0},{3,1},{4,6},{5,7},{6,4},{7,5},{8,10},{9,11},{10,... | collective-permute-start | bytes 1572872 | tf_op jit(solution)/shard_map/ppermute | solution.py:117
  90.5 23.6 %collective-permute-start.14 = (bf16[4,256,256]{2,1,0:T(8,128)(2,1)S(1)}, bf16[4,256,256]{2,1,0:T(8,128)(2,1)S(1)}, u32[]{:S(2)}, u32[]{:S(2)}) collective-permute-start(bf16[4,256,256]{2,1,0:T(8,128)(2,1)S(1)} %pad_maximum_fusion.14), channel_id=1, source_target_pairs={{0,2},{1,3},{2,0},{3,1},{4,6},{5,7},{6,4},{7,5},{8,10},{9,11},{10,... | collective-permute-start | bytes 1572872 | tf_op jit(solution)/shard_map/ppermute | solution.py:117
  105.1 13.0 %collective-permute-start.8 = (bf16[2,256,256]{2,1,0:T(8,128)(2,1)S(1)}, bf16[2,256,256]{2,1,0:T(8,128)(2,1)S(1)}, u32[]{:S(2)}, u32[]{:S(2)}) collective-permute-start(bf16[2,256,256]{2,1,0:T(8,128)(2,1)S(1)} %pad_maximum_fusion.19), channel_id=1, source_target_pairs={{0,8},{1,9},{2,10},{3,11},{4,12},{5,13},{6,14},{7,15},{8,0},{9,1},... | collective-permute-start | bytes 786440 | tf_op jit(solution)/shard_map/ppermute | solution.py:117
  112.4 14.8 %collective-permute-start.20 = (bf16[4,256,256]{2,1,0:T(8,128)(2,1)S(1)}, bf16[4,256,256]{2,1,0:T(8,128)(2,1)S(1)}, u32[]{:S(2)}, u32[]{:S(2)}) collective-permute-start(bf16[4,256,256]{2,1,0:T(8,128)(2,1)S(1)} %pad_maximum_fusion.13), channel_id=1, source_target_pairs={{0,2},{1,3},{2,0},{3,1},{4,6},{5,7},{6,4},{7,5},{8,10},{9,11},{10,... | collective-permute-start | bytes 1572872 | tf_op jit(solution)/shard_map/ppermute | solution.py:117
  114.1 24.0 %collective-permute-start.25 = (bf16[4,256,256]{2,1,0:T(8,128)(2,1)S(1)}, bf16[4,256,256]{2,1,0:T(8,128)(2,1)S(1)}, u32[]{:S(2)}, u32[]{:S(2)}) collective-permute-start(bf16[4,256,256]{2,1,0:T(8,128)(2,1)S(1)} %pad_maximum_fusion.12), channel_id=1, source_target_pairs={{0,2},{1,3},{2,0},{3,1},{4,6},{5,7},{6,4},{7,5},{8,10},{9,11},{10,... | collective-permute-start | bytes 1572872 | tf_op jit(solution)/shard_map/ppermute | solution.py:117
  118.4 21.2 %collective-permute-start.16 = (bf16[2,256,256]{2,1,0:T(8,128)(2,1)S(1)}, bf16[2,256,256]{2,1,0:T(8,128)(2,1)S(1)}, u32[]{:S(2)}, u32[]{:S(2)}) collective-permute-start(bf16[2,256,256]{2,1,0:T(8,128)(2,1)S(1)} %pad_maximum_fusion.20), channel_id=1, source_target_pairs={{0,8},{1,9},{2,10},{3,11},{4,12},{5,13},{6,14},{7,15},{8,0},{9,1},... | collective-permute-start | bytes 786440 | tf_op jit(solution)/shard_map/ppermute | solution.py:117
  134.5 20.0 %collective-permute-start.28 = (bf16[4,256,256]{2,1,0:T(8,128)(2,1)S(1)}, bf16[4,256,256]{2,1,0:T(8,128)(2,1)S(1)}, u32[]{:S(2)}, u32[]{:S(2)}) collective-permute-start(bf16[4,256,256]{2,1,0:T(8,128)(2,1)S(1)} %pad_maximum_fusion.15), channel_id=1, source_target_pairs={{0,2},{1,3},{2,0},{3,1},{4,6},{5,7},{6,4},{7,5},{8,10},{9,11},{10,... | collective-permute-start | bytes 1572872 | tf_op jit(solution)/shard_map/ppermute | solution.py:117
  138.1 25.0 %collective-permute-start.31 = (bf16[4,256,256]{2,1,0:T(8,128)(2,1)S(1)}, bf16[4,256,256]{2,1,0:T(8,128)(2,1)S(1)}, u32[]{:S(2)}, u32[]{:S(2)}) collective-permute-start(bf16[4,256,256]{2,1,0:T(8,128)(2,1)S(1)} %pad_maximum_fusion.16), channel_id=1, source_target_pairs={{0,2},{1,3},{2,0},{3,1},{4,6},{5,7},{6,4},{7,5},{8,10},{9,11},{10,... | collective-permute-start | bytes 1572872 | tf_op jit(solution)/shard_map/ppermute | solution.py:117
  146.9 7.1 %collective-permute-start.26 = (bf16[256,256]{1,0:T(8,128)(2,1)S(1)}, bf16[256,256]{1,0:T(8,128)(2,1)S(1)}, u32[]{:S(2)}, u32[]{:S(2)}) collective-permute-start(bf16[256,256]{1,0:T(8,128)(2,1)S(1)} %fusion.15), channel_id=1, source_target_pairs={{0,16},{1,17},{2,18},{3,19},{4,20},{5,21},{6,22},{7,23},{8,24},{9,... | collective-permute-start | bytes 393224 | tf_op jit(solution)/shard_map/ppermute | solution.py:117
  154.3 7.2 %collective-permute-start.27 = (bf16[2,256,256]{2,1,0:T(8,128)(2,1)S(1)}, bf16[2,256,256]{2,1,0:T(8,128)(2,1)S(1)}, u32[]{:S(2)}, u32[]{:S(2)}) collective-permute-start(bf16[2,256,256]{2,1,0:T(8,128)(2,1)S(1)} %pad_maximum_fusion.22), channel_id=1, source_target_pairs={{0,8},{1,9},{2,10},{3,11},{4,12},{5,13},{6,14},{7,15},{8,0},{9,1},... | collective-permute-start | bytes 786440 | tf_op jit(solution)/shard_map/ppermute | solution.py:117
  161.8 9.8 %collective-permute-start.30 = (bf16[2,256,256]{2,1,0:T(8,128)(2,1)S(1)}, bf16[2,256,256]{2,1,0:T(8,128)(2,1)S(1)}, u32[]{:S(2)}, u32[]{:S(2)}) collective-permute-start(bf16[2,256,256]{2,1,0:T(8,128)(2,1)S(1)} %pad_maximum_fusion.23), channel_id=1, source_target_pairs={{0,8},{1,9},{2,10},{3,11},{4,12},{5,13},{6,14},{7,15},{8,0},{9,1},... | collective-permute-start | bytes 786440 | tf_op jit(solution)/shard_map/ppermute | solution.py:117
  162.0 21.8 %collective-permute-start.35 = (bf16[4,256,256]{2,1,0:T(8,128)(2,1)S(1)}, bf16[4,256,256]{2,1,0:T(8,128)(2,1)S(1)}, u32[]{:S(2)}, u32[]{:S(2)}) collective-permute-start(bf16[4,256,256]{2,1,0:T(8,128)(2,1)S(1)} %pad_maximum_fusion.17), channel_id=1, source_target_pairs={{0,2},{1,3},{2,0},{3,1},{4,6},{5,7},{6,4},{7,5},{8,10},{9,11},{10,... | collective-permute-start | bytes 1572872 | tf_op jit(solution)/shard_map/ppermute | solution.py:117
  171.9 11.8 %collective-permute-start.33 = (bf16[2,256,256]{2,1,0:T(8,128)(2,1)S(1)}, bf16[2,256,256]{2,1,0:T(8,128)(2,1)S(1)}, u32[]{:S(2)}, u32[]{:S(2)}) collective-permute-start(bf16[2,256,256]{2,1,0:T(8,128)(2,1)S(1)} %pad_maximum_fusion.24), channel_id=1, source_target_pairs={{0,8},{1,9},{2,10},{3,11},{4,12},{5,13},{6,14},{7,15},{8,0},{9,1},... | collective-permute-start | bytes 786440 | tf_op jit(solution)/shard_map/ppermute | solution.py:117
  172.0 13.3 %collective-permute-start.15 = (bf16[256,256]{1,0:T(8,128)(2,1)S(1)}, bf16[256,256]{1,0:T(8,128)(2,1)S(1)}, u32[]{:S(2)}, u32[]{:S(2)}) collective-permute-start(bf16[256,256]{1,0:T(8,128)(2,1)S(1)} %fusion.21), channel_id=1, source_target_pairs={{0,16},{1,17},{2,18},{3,19},{4,20},{5,21},{6,22},{7,23},{8,24},{9,... | collective-permute-start | bytes 393224 | tf_op jit(solution)/shard_map/ppermute | solution.py:117
  184.0 9.8 %collective-permute-start.36 = (bf16[2,256,256]{2,1,0:T(8,128)(2,1)S(1)}, bf16[2,256,256]{2,1,0:T(8,128)(2,1)S(1)}, u32[]{:S(2)}, u32[]{:S(2)}) collective-permute-start(bf16[2,256,256]{2,1,0:T(8,128)(2,1)S(1)} %pad_maximum_fusion.25), channel_id=1, source_target_pairs={{0,8},{1,9},{2,10},{3,11},{4,12},{5,13},{6,14},{7,15},{8,0},{9,1},... | collective-permute-start | bytes 786440 | tf_op jit(solution)/shard_map/ppermute | solution.py:117
  184.1 15.5 %collective-permute-start.38 = (bf16[4,256,256]{2,1,0:T(8,128)(2,1)S(1)}, bf16[4,256,256]{2,1,0:T(8,128)(2,1)S(1)}, u32[]{:S(2)}, u32[]{:S(2)}) collective-permute-start(bf16[4,256,256]{2,1,0:T(8,128)(2,1)S(1)} %pad_maximum_fusion.18), channel_id=1, source_target_pairs={{0,2},{1,3},{2,0},{3,1},{4,6},{5,7},{6,4},{7,5},{8,10},{9,11},{10,... | collective-permute-start | bytes 1572872 | tf_op jit(solution)/shard_map/ppermute | solution.py:117
  185.4 11.1 %collective-permute-start.23 = (bf16[256,256]{1,0:T(8,128)(2,1)S(1)}, bf16[256,256]{1,0:T(8,128)(2,1)S(1)}, u32[]{:S(2)}, u32[]{:S(2)}) collective-permute-start(bf16[256,256]{1,0:T(8,128)(2,1)S(1)} %fusion.18), channel_id=1, source_target_pairs={{0,16},{1,17},{2,18},{3,19},{4,20},{5,21},{6,22},{7,23},{8,24},{9,... | collective-permute-start | bytes 393224 | tf_op jit(solution)/shard_map/ppermute | solution.py:117
  194.0 12.0 %collective-permute-start.37 = (bf16[256,256]{1,0:T(8,128)(2,1)S(1)}, bf16[256,256]{1,0:T(8,128)(2,1)S(1)}, u32[]{:S(2)}, u32[]{:S(2)}) collective-permute-start(bf16[256,256]{1,0:T(8,128)(2,1)S(1)} %fusion.3), channel_id=1, source_target_pairs={{0,16},{1,17},{2,18},{3,19},{4,20},{5,21},{6,22},{7,23},{8,24},{9,... | collective-permute-start | bytes 393224 | tf_op jit(solution)/shard_map/ppermute | solution.py:117
  196.6 12.3 %collective-permute-start.29 = (bf16[256,256]{1,0:T(8,128)(2,1)S(1)}, bf16[256,256]{1,0:T(8,128)(2,1)S(1)}, u32[]{:S(2)}, u32[]{:S(2)}) collective-permute-start(bf16[256,256]{1,0:T(8,128)(2,1)S(1)} %fusion.12), channel_id=1, source_target_pairs={{0,16},{1,17},{2,18},{3,19},{4,20},{5,21},{6,22},{7,23},{8,24},{9,... | collective-permute-start | bytes 393224 | tf_op jit(solution)/shard_map/ppermute | solution.py:117
  197.2 14.5 %collective-permute-start.32 = (bf16[256,256]{1,0:T(8,128)(2,1)S(1)}, bf16[256,256]{1,0:T(8,128)(2,1)S(1)}, u32[]{:S(2)}, u32[]{:S(2)}) collective-permute-start(bf16[256,256]{1,0:T(8,128)(2,1)S(1)} %fusion.9), channel_id=1, source_target_pairs={{0,16},{1,17},{2,18},{3,19},{4,20},{5,21},{6,22},{7,23},{8,24},{9,... | collective-permute-start | bytes 393224 | tf_op jit(solution)/shard_map/ppermute | solution.py:117
  206.3 8.1 %collective-permute-start.39 = (bf16[2,256,256]{2,1,0:T(8,128)(2,1)S(1)}, bf16[2,256,256]{2,1,0:T(8,128)(2,1)S(1)}, u32[]{:S(2)}, u32[]{:S(2)}) collective-permute-start(bf16[2,256,256]{2,1,0:T(8,128)(2,1)S(1)} %pad_maximum_fusion.26), channel_id=1, source_target_pairs={{0,8},{1,9},{2,10},{3,11},{4,12},{5,13},{6,14},{7,15},{8,0},{9,1},... | collective-permute-start | bytes 786440 | tf_op jit(solution)/shard_map/ppermute | solution.py:117
  (12 other events, 60.0 us)

commit v7 on v6

--- a/solution.py
+++ b/solution.py
@@ -12,12 +12,13 @@
 
 def adam(where, chunks, args, previous):
     rows, cols = args[0].shape
-    widths = [cols // 16 * count for first, count in chunks]
-    width = sum(widths)
+    unit = cols // 16
+    counts = [count for first, count in chunks]
+    width = unit * sum(counts)
     step = max(s for s in range(16, 449, 16) if rows % s == 0)
     tiles = rows // step
     spread = cols // 4 // width
-    start = chunks[0][0] * (cols // 16) // width
+    start = chunks[0][0] * unit // width
 
     def kernel(where_ref, master_ref, one_ref, two_ref, grad_ref, *refs):
         outs = refs[-3 - len(chunks) :]
@@ -29,16 +30,17 @@
         outs[1][...] = new_one
         outs[2][...] = new_two
         at = 0
-        for ref, size in zip(outs[3:], widths):
-            ref[...] = new_master[:, at : at + size].astype(jnp.bfloat16)
-            at += size
+        for ref, count in zip(outs[3:], counts):
+            for k in range(count):
+                ref[k] = new_master[:, at : at + unit].astype(jnp.bfloat16)
+                at += unit
 
     def at(i, w):
         return i % tiles, i // tiles * spread + start
 
     def piece_at(i, w):
         j = i // tiles
-        return i % tiles, 2 * ((j % 2) ^ w[1]) + ((j // 2) ^ w[0])
+        return 0, i % tiles, 2 * ((j % 2) ^ w[1]) + ((j // 2) ^ w[0])
 
     block = pl.BlockSpec((step, width), at)
     full = jax.ShapeDtypeStruct((rows, cols), jnp.float32)
@@ -49,9 +51,9 @@
             num_scalar_prefetch=1,
             grid=(4 * tiles,),
             in_specs=[block] * 4 + [pl.BlockSpec(memory_space=pl.ANY)] * len(previous),
-            out_specs=[block] * 3 + [pl.BlockSpec((step, size), piece_at) for size in widths],
+            out_specs=[block] * 3 + [pl.BlockSpec((count, step, unit), piece_at) for count in counts],
         ),
-        out_shape=[full] * 3 + [jax.ShapeDtypeStruct((rows, 4 * size), jnp.bfloat16) for size in widths],
+        out_shape=[full] * 3 + [jax.ShapeDtypeStruct((count, rows, 4 * unit), jnp.bfloat16) for count in counts],
         input_output_aliases={5 + i: i for i in range(len(previous))},
         compiler_params=pltpu.CompilerParams(vmem_limit_bytes=60 * 1024 * 1024),
         cost_estimate=pl.CostEstimate(flops=12 * size, bytes_accessed=28 * size, transcendentals=size),
@@ -129,12 +131,13 @@
         pieces.extend(weights)
 
     flip = (c ^ (z % 2)) != 0
-    crossed, used, tables = [], [], []
+    crossed, tables = [], []
     theirs, pairs, moved, acts = [], [], [], []
-    sends, backs, leaving, result = [], [], [], []
-
-    def cross(m):
-        theirs.append(permute(other[m], lambda z, x, y, c: (z, x, 1 - y, c)))
+    jobs, sends, backs = [], [], []
+    nears, fars, halfway, leaving, result = [], [], [], [], []
+
+    def cross(m, *done):
+        theirs.append(permute(after(other[m], *done), lambda z, x, y, c: (z, x, 1 - y, c)))
 
     def to_plane(m, *done):
         pair = after(swap_if(((z // 2) ^ y) != 0, own[m], theirs[m]), *done)
@@ -151,42 +154,45 @@
         piece = after(pieces[q], *done)
         crossed.append([piece] + [permute(piece, lambda z, x, y, c: (z, x ^ d, y, c)) for d in range(1, xs)])
 
-    def to_table(q, *done):
+    def to_tables(q, *done):
         parts = after(crossed[q], *done)
-        half = parts[0].shape[1] // 2
-        width = half // CHUNKS[q][1]
-        near = jnp.stack([p[:, :half] for p in parts])
-        far = []
-        for at in range(half, 2 * half, width):
-            there = jnp.stack([p[:, at : at + width] for p in parts])
-            far.append(permute(there, lambda z, x, y, c: (z, x, y, 1 - c)))
-        far = jnp.concatenate(far, axis=2)
-        tables.append(jnp.stack(swap_if(c != 0, near, far), axis=1).reshape(-1, half))
-
-    def multiply(m, q, *done):
-        table = after(tables[q], *done)
-        half = table.shape[1] // 2
-        totals = [jnp.dot(a, table, preferred_element_type=jnp.float32) for a in acts[m]]
-        width = half // CHUNKS[q][1]
-        jobs = []
+        half = parts[0].shape[2] // 2
+        for k in range(parts[0].shape[0]):
+            near = jnp.stack([p[k, :, :half] for p in parts])
+            far = jnp.stack([p[k, :, half:] for p in parts])
+            far = permute(far, lambda z, x, y, c: (z, x, y, 1 - c))
+            tables.append(jnp.stack(swap_if(c != 0, near, far), axis=1).reshape(-1, half))
+
+    def multiply(m, q, pieces=1):
+        half = tables[q].shape[1] // 2
+        totals = [jnp.dot(a, tables[q], preferred_element_type=jnp.float32) for a in acts[m]]
+        width = half // pieces
         for at in range(0, half, width):
             send = jnp.stack([total[:, half + at : half + at + width].astype(jnp.bfloat16) for total in totals])
             send = after(send, *sends[-1:], *backs[-2:-1])
             sends.append(send)
             backs.append(permute(send, lambda z, x, y, c: (z, x, 1 - y, c)))
-            jobs.append(([total[:, at : at + width] for total in totals], len(backs) - 1))
-        return jobs
-
-    def reduce(totals, j):
-        back = after(backs[j], leaving[-1]) if leaving else backs[j]
-        totals = [total + b for total, b in zip(totals, back)]
-        near, far = zip(*[swap_if(flip, own, sibling) for own, sibling in zip(totals[:2], totals[2:])])
-        back = permute(jnp.stack(far).astype(jnp.bfloat16), lambda z, x, y, c: (z ^ 1, x, y, c))
-        back = after(back, *sends[j + 3 : j + 4])
-        send = (near[1] + back[1]).astype(jnp.bfloat16)
-        leaving.append(send)
-        back = near[0] + back[0] + permute(send, lambda z, x, y, c: (z ^ 2, x, y, c))
-        result.append(back.astype(jnp.bfloat16))
+            jobs.append([total[:, at : at + width] for total in totals])
+
+    def step_one(j):
+        back = after(backs[j], *leaving[j - 1 : j])
+        totals = [total + b for total, b in zip(jobs[j], back)]
+        count = len(totals) // 2
+        near, far = zip(*[swap_if(flip, own, sibling) for own, sibling in zip(totals[:count], totals[count:])])
+        near, far = [jnp.concatenate(v, axis=0) if count > 1 else v[0] for v in (near, far)]
+        nears.append(near)
+        fars.append(far.astype(jnp.bfloat16))
+        halfway.append(permute(fars[j], lambda z, x, y, c: (z ^ 1, x, y, c)))
+
+    def step_two(j):
+        back = after(halfway[j], *sends[j + 3 : j + 4])
+        total = nears[j] + back
+        leaving.append(total[part:].astype(jnp.bfloat16))
+        nears[j] = total[:part]
+        halfway[j] = permute(leaving[j], lambda z, x, y, c: (z ^ 2, x, y, c))
+
+    def step_three(j):
+        result.append((nears[j] + halfway[j]).astype(jnp.bfloat16))
 
     update(CHUNKS[:2], own[0])
     cross(0)
@@ -196,20 +202,27 @@
     update(CHUNKS[2:])
     to_plane(0, pieces[2])
     gather(2, crossed[0][-1])
-    to_table(0)
-    to_table(1)
+    to_tables(0)
+    to_tables(1)
     to_cores(0)
     to_plane(1, *moved[0])
-    jobs = multiply(0, 0) + multiply(0, 1)
-    to_table(2, backs[0])
-    jobs += multiply(0, 2)
+    multiply(0, 0)
+    multiply(0, 1)
+    to_tables(2, backs[0])
+    multiply(0, 2)
+    multiply(0, 3)
     to_cores(1, backs[2])
-    for q in range(len(CHUNKS)):
-        jobs += multiply(1, q)
-    for job in jobs:
-        reduce(*job)
-    count = len(result) // ROW_CHUNKS
-    result = [jnp.concatenate(result[i : i + count], axis=1) for i in range(0, len(result), count)]
+    for q in range(4):
+        multiply(1, q, 1 + q // 3)
+    count = len(jobs)
+    for j in range(count + 1):
+        if j >= 1:
+            step_two(j - 1)
+        if j < count:
+            step_one(j)
+        if j >= 1:
+            step_three(j - 1)
+    result = [jnp.concatenate(result[:4], axis=1), jnp.concatenate(result[4:], axis=1)]
     decoded = jnp.concatenate(result, axis=0)
     return (*updated, decoded)
 

time: 223 us -> 206 us (0.924)
  waiting for transfers between devices: 127 us -> 105 us
  starting transfers between devices: 35.9 us -> 41.4 us
    ppermute x41 -> x44, waiting for transfers between devices: 127 us -> 105 us  [permute(): return lax.ppermute(value, AXES, pairs)]
    ppermute x41 -> x44, starting transfers between devices: 35.9 us -> 41.4 us  [permute(): return lax.ppermute(value, AXES, pairs)]
    slice x0 -> x14, local copies, waits for them, and re-layouts: none -> 4.37 us  [the longest x5 4.24 us: to_tables(): near = jnp.stack([p[k, :, :half] for p in parts])]
    another operation x9 -> x4, local copies, waits for them, and re-layouts: 4.5 us -> 0.48 us  [to_tables(): jnp.stack(swap_if(c != 0, near, far), axis=1).reshape(-1, half)]
    dot_general x24 -> x32, matrix products: 19.2 us -> 20.4 us  [multiply(): jnp.dot(a, tables[q], preferred_element_type=jnp.float32)]
  transfers between devices with their start and end apart: 41 -> 44, of which waited for: 24 -> 23; matrix products, arithmetic and copies ran while one was open for 15% -> 16% of each run, Pallas kernels for 9% -> 10%
where the time goes in v7:
time: 206 us
  waiting for transfers between devices  105 us (51%)
  starting transfers between devices  41.4 us (20%)
  Pallas kernels  22 us (11%)
  matrix products  20.4 us (10%)
  other arithmetic  8.29 us (4%)
  local copies, waits for them, and re-layouts  7.5 us (4%)
    ppermute x44, waiting for transfers between devices, permute(): return lax.ppermute(value, AXES, pairs)  105 us
    ppermute x44, starting transfers between devices, permute(): return lax.ppermute(value, AXES, pairs)  41.4 us
    dot_general x32, matrix products, multiply(): jnp.dot(a, tables[q], preferred_element_type=jnp.float32)  20.4 us
    pallas_call x2, Pallas kernels, adam(): pl.pallas_call(kernel, grid_spec=pltpu.PrefetchScalarGridSpec(num_scalar_...  20.2 us
    slice x5, local copies, waits for them, and re-layouts, to_tables(): near = jnp.stack([p[k, :, :half] for p in parts])  4.24 us
  transfers between devices with their start and end apart: 44, of which 23 were waited for; matrix products, arithmetic and copies ran while one was open for 16% of the time, Pallas kernels for 10%

profile of v7, /device:TPU:0, one launch (start us, length us, event | category | flops | bytes accessed | tf_op | source)
XLA Modules:
  0.0 206.1 jit_solution(11170887259401217208)
XLA Ops:
  0.7 2.0 copy-done
  2.8 1.8 pack.1
  4.6 3.0 %collective-permute-start = (bf16[256,1792]{1,0:T(8,128)(2,1)}, bf16[256,1792]{1,0:T(8,128)(2,1)}, u32[]{:S(2)}, u32[]{:S(2)}) collective-permute-start(bf16[256,1792]{1,0:T(8,128)(2,1)} %get-tuple-element.57), channel_id=1, source_target_pairs={{0,2},{1,3},{2,0},{3,1},{4,6},{5,7},{6,4},{7,5},{8,10},{9,11},{10,... | collective-permute-start | bytes 2752520 | tf_op jit(solution)/shard_map/ppermute | solution.py:119
  7.5 10.0 %adam.2 = (f32[448,4096]{1,0:T(8,128)}, f32[448,4096]{1,0:T(8,128)}, f32[448,4096]{1,0:T(8,128)}, bf16[1,448,1024]{2,1,0:T(8,128)(2,1)}, bf16[1,448,1024]{2,1,0:T(8,128)(2,1)}) custom-call(s32[3]{0:T(128)} %copy-done.1, f32[448,4096]{1,0:T(8,128)} %master_ref.3, f32[448,4096]{1,0:T(8,128)} %one_ref.3, f32[448,4096]{1,0:T(8,128)} %two_ref.3, ...), custom_call_target="tpu_custom_call" | custom-call | flops 11010048 | bytes 25690112 | tf_op jit(solution)/shard_map/adam/pallas_call | solution.py:48
  19.6 10.2 %adam.3 = (f32[448,4096]{1,0:T(8,128)}, f32[448,4096]{1,0:T(8,128)}, f32[448,4096]{1,0:T(8,128)}, bf16[2,448,1024]{2,1,0:T(8,128)(2,1)}) custom-call(s32[3]{0:T(128)} %copy-done.1, f32[448,4096]{1,0:T(8,128)} %master_ref.3, f32[448,4096]{1,0:T(8,128)} %one_ref.3, f32[448,4096]{1,0:T(8,128)} %two_ref.3, ...), custom_call_target="tpu_custom_call", output_to_operand_aliasing={{0}: (5, {}), {1}: (6, {}), {2}: (7, {})} | custom-call | flops 11010048 | bytes 25690112 | tf_op jit(solution)/shard_map/adam/pallas_call | solution.py:48
  33.5 3.1 %collective-permute-start.5 = (bf16[256,1792]{1,0:T(8,128)(2,1)S(1)}, bf16[256,1792]{1,0:T(8,128)(2,1)S(1)}, u32[]{:S(2)}, u32[]{:S(2)}) collective-permute-start(bf16[256,1792]{1,0:T(8,128)(2,1)S(1)} %get-tuple-element.61), channel_id=1, source_target_pairs={{0,16},{1,24},{2,18},{3,26},{4,20},{5,28},{6,22},{7,30},{8,17},{9,... | collective-permute-start | bytes 2752520 | tf_op jit(solution)/shard_map/ppermute | solution.py:119
  36.7 4.5 %collective-permute-done.3 = bf16[1,448,1024]{2,1,0:T(8,128)(2,1)} collective-permute-done((bf16[1,448,1024]{2,1,0:T(8,128)(2,1)}, bf16[1,448,1024]{2,1,0:T(8,128)(2,1)}, u32[]{:S(2)}, u32[]{:S(2)}) %collective-permute-start.3) | collective-permute-done | bytes 917536 | tf_op jit(solution)/shard_map/ppermute | solution.py:119
  44.0 16.9 %collective-permute-done.12 = bf16[1,448,1024]{2,1,0:T(8,128)(2,1)} collective-permute-done((bf16[1,448,1024]{2,1,0:T(8,128)(2,1)}, bf16[1,448,1024]{2,1,0:T(8,128)(2,1)}, u32[]{:S(2)}, u32[]{:S(2)}) %collective-permute-start.12) | collective-permute-done | bytes 917536 | tf_op jit(solution)/shard_map/ppermute | solution.py:119
  64.0 12.5 %collective-permute-done.5 = bf16[256,1792]{1,0:T(8,128)(2,1)S(1)} collective-permute-done((bf16[256,1792]{1,0:T(8,128)(2,1)S(1)}, bf16[256,1792]{1,0:T(8,128)(2,1)S(1)}, u32[]{:S(2)}, u32[]{:S(2)}) %collective-permute-start.5) | collective-permute-done | bytes 917536 | tf_op jit(solution)/shard_map/ppermute | solution.py:119
  79.0 4.3 %collective-permute-start.6 = (bf16[256,1792]{1,0:T(8,128)(2,1)S(1)}, bf16[256,1792]{1,0:T(8,128)(2,1)S(1)}, u32[]{:S(2)}, u32[]{:S(2)}) collective-permute-start(bf16[256,1792]{1,0:T(8,128)(2,1)S(1)} %collective-permute-done.5), channel_id=1, source_target_pairs={{0,1},{1,0},{2,3},{3,2},{4,5},{5,4},{6,7},{7,6},{8,9},{9,8},{10,11... | collective-permute-start | bytes 2752520 | tf_op jit(solution)/shard_map/ppermute | solution.py:119
  87.5 1.6 collective-permute-start.7
  90.4 8.2 %collective-permute-done.9 = bf16[2,448,1024]{2,1,0:T(8,128)(2,1)S(1)} collective-permute-done((bf16[2,448,1024]{2,1,0:T(8,128)(2,1)S(1)}, bf16[2,448,1024]{2,1,0:T(8,128)(2,1)S(1)}, u32[]{:S(2)}, u32[]{:S(2)}) %collective-permute-start.9) | collective-permute-done | bytes 1835040 | tf_op jit(solution)/shard_map/ppermute | solution.py:119
  98.6 3.2 %collective-permute-done.7 = bf16[4,256,256]{2,1,0:T(8,128)(2,1)S(1)} collective-permute-done((bf16[4,256,256]{2,1,0:T(8,128)(2,1)S(1)}, bf16[4,256,256]{2,1,0:T(8,128)(2,1)S(1)}, u32[]{:S(2)}, u32[]{:S(2)}) %collective-permute-start.7) | collective-permute-done | bytes 524320 | tf_op jit(solution)/shard_map/ppermute | solution.py:119
  102.4 1.6 collective-permute-start.14
  112.6 4.5 %collective-permute-done.14 = bf16[4,256,256]{2,1,0:T(8,128)(2,1)S(1)} collective-permute-done((bf16[4,256,256]{2,1,0:T(8,128)(2,1)S(1)}, bf16[4,256,256]{2,1,0:T(8,128)(2,1)S(1)}, u32[]{:S(2)}, u32[]{:S(2)}) %collective-permute-start.14) | collective-permute-done | bytes 524320 | tf_op jit(solution)/shard_map/ppermute | solution.py:119
  119.0 8.0 %collective-permute-done.15 = bf16[256,256]{1,0:T(8,128)(2,1)S(1)} collective-permute-done((bf16[256,256]{1,0:T(8,128)(2,1)S(1)}, bf16[256,256]{1,0:T(8,128)(2,1)S(1)}, u32[]{:S(2)}, u32[]{:S(2)}) %collective-permute-start.15) | collective-permute-done | bytes 131104 | tf_op jit(solution)/shard_map/ppermute | solution.py:119
  135.9 1.6 collective-permute-start.28
  144.4 5.0 %collective-permute-done.24 = bf16[512,256]{1,0:T(8,128)(2,1)S(1)} collective-permute-done((bf16[512,256]{1,0:T(8,128)(2,1)S(1)}, bf16[512,256]{1,0:T(8,128)(2,1)S(1)}, u32[]{:S(2)}, u32[]{:S(2)}) %collective-permute-start.24) | collective-permute-done | bytes 262176 | tf_op jit(solution)/shard_map/ppermute | solution.py:119
  150.9 5.9 %collective-permute-done.27 = bf16[512,256]{1,0:T(8,128)(2,1)S(1)} collective-permute-done((bf16[512,256]{1,0:T(8,128)(2,1)S(1)}, bf16[512,256]{1,0:T(8,128)(2,1)S(1)}, u32[]{:S(2)}, u32[]{:S(2)}) %collective-permute-start.27) | collective-permute-done | bytes 262176 | tf_op jit(solution)/shard_map/ppermute | solution.py:119
  157.5 1.7 collective-permute-start.26
  159.7 2.4 %collective-permute-done.31 = bf16[4,256,256]{2,1,0:T(8,128)(2,1)S(1)} collective-permute-done((bf16[4,256,256]{2,1,0:T(8,128)(2,1)S(1)}, bf16[4,256,256]{2,1,0:T(8,128)(2,1)S(1)}, u32[]{:S(2)}, u32[]{:S(2)}) %collective-permute-start.31) | collective-permute-done | bytes 524320 | tf_op jit(solution)/shard_map/ppermute | solution.py:119
  162.1 3.9 %collective-permute-done.30 = bf16[512,256]{1,0:T(8,128)(2,1)S(1)} collective-permute-done((bf16[512,256]{1,0:T(8,128)(2,1)S(1)}, bf16[512,256]{1,0:T(8,128)(2,1)S(1)}, u32[]{:S(2)}, u32[]{:S(2)}) %collective-permute-start.30) | collective-permute-done | bytes 262176 | tf_op jit(solution)/shard_map/ppermute | solution.py:119
  167.0 2.1 %collective-permute-start.29 = (bf16[256,256]{1,0:T(8,128)(2,1)S(1)}, bf16[256,256]{1,0:T(8,128)(2,1)S(1)}, u32[]{:S(2)}, u32[]{:S(2)}) collective-permute-start(bf16[256,256]{1,0:T(8,128)(2,1)S(1)} %slice.884), channel_id=1, source_target_pairs={{0,16},{1,17},{2,18},{3,19},{4,20},{5,21},{6,22},{7,23},{8,24},{9,... | collective-permute-start | bytes 393224 | tf_op jit(solution)/shard_map/ppermute | solution.py:119
  170.0 4.1 %collective-permute-done.34 = bf16[4,256,256]{2,1,0:T(8,128)(2,1)S(1)} collective-permute-done((bf16[4,256,256]{2,1,0:T(8,128)(2,1)S(1)}, bf16[4,256,256]{2,1,0:T(8,128)(2,1)S(1)}, u32[]{:S(2)}, u32[]{:S(2)}) %collective-permute-start.34) | collective-permute-done | bytes 524320 | tf_op jit(solution)/shard_map/ppermute | solution.py:119
  174.0 3.9 %collective-permute-done.33 = bf16[512,256]{1,0:T(8,128)(2,1)S(1)} collective-permute-done((bf16[512,256]{1,0:T(8,128)(2,1)S(1)}, bf16[512,256]{1,0:T(8,128)(2,1)S(1)}, u32[]{:S(2)}, u32[]{:S(2)}) %collective-permute-start.33) | collective-permute-done | bytes 262176 | tf_op jit(solution)/shard_map/ppermute | solution.py:119
  180.1 2.2 %collective-permute-start.41 = (bf16[4,256,128]{2,1,0:T(8,128)(2,1)S(1)}, bf16[4,256,128]{2,1,0:T(8,128)(2,1)S(1)}, u32[]{:S(2)}, u32[]{:S(2)}) collective-permute-start(bf16[4,256,128]{2,1,0:T(8,128)(2,1)S(1)} %pad_maximum_fusion.27), channel_id=1, source_target_pairs={{0,2},{1,3},{2,0},{3,1},{4,6},{5,7},{6,4},{7,5},{8,10},{9,11},{10,... | collective-permute-start | bytes 786440 | tf_op jit(solution)/shard_map/ppermute | solution.py:119
  182.3 4.9 %collective-permute-done.36 = bf16[512,256]{1,0:T(8,128)(2,1)S(1)} collective-permute-done((bf16[512,256]{1,0:T(8,128)(2,1)S(1)}, bf16[512,256]{1,0:T(8,128)(2,1)S(1)}, u32[]{:S(2)}, u32[]{:S(2)}) %collective-permute-start.36) | collective-permute-done | bytes 262176 | tf_op jit(solution)/shard_map/ppermute | solution.py:119
  188.8 4.9 %collective-permute-done.39 = bf16[512,128]{1,0:T(8,128)(2,1)S(1)} collective-permute-done((bf16[512,128]{1,0:T(8,128)(2,1)S(1)}, bf16[512,128]{1,0:T(8,128)(2,1)S(1)}, u32[]{:S(2)}, u32[]{:S(2)}) %collective-permute-start.39) | collective-permute-done | bytes 131104 | tf_op jit(solution)/shard_map/ppermute | solution.py:119
  194.6 1.9 collective-permute-done.37
  196.6 3.1 %collective-permute-done.42 = bf16[512,128]{1,0:T(8,128)(2,1)S(1)} collective-permute-done((bf16[512,128]{1,0:T(8,128)(2,1)S(1)}, bf16[512,128]{1,0:T(8,128)(2,1)S(1)}, u32[]{:S(2)}, u32[]{:S(2)}) %collective-permute-start.42) | collective-permute-done | bytes 131104 | tf_op jit(solution)/shard_map/ppermute | solution.py:119
  199.8 2.3 %collective-permute-start.43 = (bf16[256,128]{1,0:T(8,128)(2,1)S(1)}, bf16[256,128]{1,0:T(8,128)(2,1)S(1)}, u32[]{:S(2)}, u32[]{:S(2)}) collective-permute-start(bf16[256,128]{1,0:T(8,128)(2,1)S(1)} %slice.888), channel_id=1, source_target_pairs={{0,16},{1,17},{2,18},{3,19},{4,20},{5,21},{6,22},{7,23},{8,24},{9,... | collective-permute-start | bytes 196616 | tf_op jit(solution)/shard_map/ppermute | solution.py:119
  202.0 3.0 %collective-permute-done.43 = bf16[256,128]{1,0:T(8,128)(2,1)S(1)} collective-permute-done((bf16[256,128]{1,0:T(8,128)(2,1)S(1)}, bf16[256,128]{1,0:T(8,128)(2,1)S(1)}, u32[]{:S(2)}, u32[]{:S(2)}) %collective-permute-start.43) | collective-permute-done | bytes 65568 | tf_op jit(solution)/shard_map/ppermute | solution.py:119
  (208 shorter events, 56.2 us)
Async XLA Ops:
  4.6 26.8 %collective-permute-start = (bf16[256,1792]{1,0:T(8,128)(2,1)}, bf16[256,1792]{1,0:T(8,128)(2,1)}, u32[]{:S(2)}, u32[]{:S(2)}) collective-permute-start(bf16[256,1792]{1,0:T(8,128)(2,1)} %get-tuple-element.57), channel_id=1, source_target_pairs={{0,2},{1,3},{2,0},{3,1},{4,6},{5,7},{6,4},{7,5},{8,10},{9,11},{10,... | collective-permute-start | bytes 2752520 | tf_op jit(solution)/shard_map/ppermute | solution.py:119
  17.5 23.6 %collective-permute-start.3 = (bf16[1,448,1024]{2,1,0:T(8,128)(2,1)}, bf16[1,448,1024]{2,1,0:T(8,128)(2,1)}, u32[]{:S(2)}, u32[]{:S(2)}) collective-permute-start(bf16[1,448,1024]{2,1,0:T(8,128)(2,1)} %get-tuple-element.60), channel_id=1, source_target_pairs={{0,4},{1,5},{2,6},{3,7},{4,0},{5,1},{6,2},{7,3},{8,12},{9,13},{10,... | collective-permute-start | bytes 2752520 | tf_op jit(solution)/shard_map/ppermute | solution.py:119
  19.0 43.1 %collective-permute-start.17 = (bf16[256,1792]{1,0:T(8,128)(2,1)S(1)}, bf16[256,1792]{1,0:T(8,128)(2,1)}, u32[]{:S(2)}, u32[]{:S(2)}) collective-permute-start(bf16[256,1792]{1,0:T(8,128)(2,1)S(1)} %get-tuple-element.71), channel_id=1, source_target_pairs={{0,2},{1,3},{2,0},{3,1},{4,6},{5,7},{6,4},{7,5},{8,10},{9,11},{10,... | collective-permute-start | bytes 2752520 | tf_op jit(solution)/shard_map/ppermute | solution.py:119
  19.6 41.3 %collective-permute-start.12 = (bf16[1,448,1024]{2,1,0:T(8,128)(2,1)}, bf16[1,448,1024]{2,1,0:T(8,128)(2,1)}, u32[]{:S(2)}, u32[]{:S(2)}) collective-permute-start(bf16[1,448,1024]{2,1,0:T(8,128)(2,1)} %get-tuple-element.65), channel_id=1, source_target_pairs={{0,4},{1,5},{2,6},{3,7},{4,0},{5,1},{6,2},{7,3},{8,12},{9,13},{10,... | collective-permute-start | bytes 2752520 | tf_op jit(solution)/shard_map/ppermute | solution.py:119
  32.8 31.2 %collective-permute-start.1 = (bf16[256,1792]{1,0:T(8,128)(2,1)S(1)}, bf16[256,1792]{1,0:T(8,128)(2,1)S(1)}, u32[]{:S(2)}, u32[]{:S(2)}) collective-permute-start(bf16[256,1792]{1,0:T(8,128)(2,1)S(1)} %get-tuple-element.59), channel_id=1, source_target_pairs={{0,0},{1,8},{2,2},{3,10},{4,4},{5,12},{6,6},{7,14},{8,1},{9,9},{10... | collective-permute-start | bytes 2752520 | tf_op jit(solution)/shard_map/ppermute | solution.py:119
  33.5 43.0 %collective-permute-start.5 = (bf16[256,1792]{1,0:T(8,128)(2,1)S(1)}, bf16[256,1792]{1,0:T(8,128)(2,1)S(1)}, u32[]{:S(2)}, u32[]{:S(2)}) collective-permute-start(bf16[256,1792]{1,0:T(8,128)(2,1)S(1)} %get-tuple-element.61), channel_id=1, source_target_pairs={{0,16},{1,24},{2,18},{3,26},{4,20},{5,28},{6,22},{7,30},{8,17},{9,... | collective-permute-start | bytes 2752520 | tf_op jit(solution)/shard_map/ppermute | solution.py:119
  41.1 57.4 %collective-permute-start.9 = (bf16[2,448,1024]{2,1,0:T(8,128)(2,1)S(1)}, bf16[2,448,1024]{2,1,0:T(8,128)(2,1)S(1)}, u32[]{:S(2)}, u32[]{:S(2)}) collective-permute-start(bf16[2,448,1024]{2,1,0:T(8,128)(2,1)S(1)} %copy-done.2), channel_id=1, source_target_pairs={{0,4},{1,5},{2,6},{3,7},{4,0},{5,1},{6,2},{7,3},{8,12},{9,13},{10,... | collective-permute-start | bytes 5505032 | tf_op jit(solution)/shard_map/ppermute | solution.py:119
  60.8 16.7 %collective-permute-start.4 = (bf16[2,448,512]{2,1,0:T(8,128)(2,1)S(1)}, bf16[2,448,512]{2,1,0:T(8,128)(2,1)S(1)}, u32[]{:S(2)}, u32[]{:S(2)}) collective-permute-start(bf16[2,448,512]{2,1,0:T(8,128)(2,1)S(1)} %pad_maximum_fusion.5), channel_id=1, source_target_pairs={{0,1},{1,0},{2,3},{3,2},{4,5},{5,4},{6,7},{7,6},{8,9},{9,8},{10,11... | collective-permute-start | bytes 2752520 | tf_op jit(solution)/shard_map/ppermute | solution.py:119
  62.1 16.5 %collective-permute-start.13 = (bf16[2,448,512]{2,1,0:T(8,128)(2,1)S(1)}, bf16[2,448,512]{2,1,0:T(8,128)(2,1)S(1)}, u32[]{:S(2)}, u32[]{:S(2)}) collective-permute-start(bf16[2,448,512]{2,1,0:T(8,128)(2,1)S(1)} %pad_maximum_fusion.11), channel_id=1, source_target_pairs={{0,1},{1,0},{2,3},{3,2},{4,5},{5,4},{6,7},{7,6},{8,9},{9,8},{10,11... | collective-permute-start | bytes 2752520 | tf_op jit(solution)/shard_map/ppermute | solution.py:119
  76.5 50.5 %collective-permute-start.18 = (bf16[256,1792]{1,0:T(8,128)(2,1)S(1)}, bf16[256,1792]{1,0:T(8,128)(2,1)S(1)}, u32[]{:S(2)}, u32[]{:S(2)}) collective-permute-start(bf16[256,1792]{1,0:T(8,128)(2,1)S(1)} %get-tuple-element.73), channel_id=1, source_target_pairs={{0,0},{1,8},{2,2},{3,10},{4,4},{5,12},{6,6},{7,14},{8,1},{9,9},{10... | collective-permute-start | bytes 2752520 | tf_op jit(solution)/shard_map/ppermute | solution.py:119
  77.4 49.6 %collective-permute-start.19 = (bf16[256,1792]{1,0:T(8,128)(2,1)S(1)}, bf16[256,1792]{1,0:T(8,128)(2,1)S(1)}, u32[]{:S(2)}, u32[]{:S(2)}) collective-permute-start(bf16[256,1792]{1,0:T(8,128)(2,1)S(1)} %get-tuple-element.74), channel_id=1, source_target_pairs={{0,16},{1,24},{2,18},{3,26},{4,20},{5,28},{6,22},{7,30},{8,17},{9,... | collective-permute-start | bytes 2752520 | tf_op jit(solution)/shard_map/ppermute | solution.py:119
  87.5 14.3 %collective-permute-start.7 = (bf16[4,256,256]{2,1,0:T(8,128)(2,1)S(1)}, bf16[4,256,256]{2,1,0:T(8,128)(2,1)S(1)}, u32[]{:S(2)}, u32[]{:S(2)}) collective-permute-start(bf16[4,256,256]{2,1,0:T(8,128)(2,1)S(1)} %pad_maximum_fusion.13), channel_id=1, source_target_pairs={{0,2},{1,3},{2,0},{3,1},{4,6},{5,7},{6,4},{7,5},{8,10},{9,11},{10,... | collective-permute-start | bytes 1572872 | tf_op jit(solution)/shard_map/ppermute | solution.py:119
  102.4 14.8 %collective-permute-start.14 = (bf16[4,256,256]{2,1,0:T(8,128)(2,1)S(1)}, bf16[4,256,256]{2,1,0:T(8,128)(2,1)S(1)}, u32[]{:S(2)}, u32[]{:S(2)}) collective-permute-start(bf16[4,256,256]{2,1,0:T(8,128)(2,1)S(1)} %pad_maximum_fusion.16), channel_id=1, source_target_pairs={{0,2},{1,3},{2,0},{3,1},{4,6},{5,7},{6,4},{7,5},{8,10},{9,11},{10,... | collective-permute-start | bytes 1572872 | tf_op jit(solution)/shard_map/ppermute | solution.py:119
  104.7 14.0 %collective-permute-start.8 = (bf16[512,256]{1,0:T(8,128)(2,1)S(1)}, bf16[512,256]{1,0:T(8,128)(2,1)S(1)}, u32[]{:S(2)}, u32[]{:S(2)}) collective-permute-start(bf16[512,256]{1,0:T(8,128)(2,1)S(1)} %pad_maximum_fusion.20), channel_id=1, source_target_pairs={{0,8},{1,9},{2,10},{3,11},{4,12},{5,13},{6,14},{7,15},{8,0},{9,1},... | collective-permute-start | bytes 786440 | tf_op jit(solution)/shard_map/ppermute | solution.py:119
  107.9 20.5 %collective-permute-start.20 = (bf16[4,256,256]{2,1,0:T(8,128)(2,1)S(1)}, bf16[4,256,256]{2,1,0:T(8,128)(2,1)S(1)}, u32[]{:S(2)}, u32[]{:S(2)}) collective-permute-start(bf16[4,256,256]{2,1,0:T(8,128)(2,1)S(1)} %pad_maximum_fusion.15), channel_id=1, source_target_pairs={{0,2},{1,3},{2,0},{3,1},{4,6},{5,7},{6,4},{7,5},{8,10},{9,11},{10,... | collective-permute-start | bytes 1572872 | tf_op jit(solution)/shard_map/ppermute | solution.py:119
  117.1 24.0 %collective-permute-start.25 = (bf16[4,256,256]{2,1,0:T(8,128)(2,1)S(1)}, bf16[4,256,256]{2,1,0:T(8,128)(2,1)S(1)}, u32[]{:S(2)}, u32[]{:S(2)}) collective-permute-start(bf16[4,256,256]{2,1,0:T(8,128)(2,1)S(1)} %pad_maximum_fusion.14), channel_id=1, source_target_pairs={{0,2},{1,3},{2,0},{3,1},{4,6},{5,7},{6,4},{7,5},{8,10},{9,11},{10,... | collective-permute-start | bytes 1572872 | tf_op jit(solution)/shard_map/ppermute | solution.py:119
  127.0 10.5 %collective-permute-start.16 = (bf16[512,256]{1,0:T(8,128)(2,1)S(1)}, bf16[512,256]{1,0:T(8,128)(2,1)S(1)}, u32[]{:S(2)}, u32[]{:S(2)}) collective-permute-start(bf16[512,256]{1,0:T(8,128)(2,1)S(1)} %pad_maximum_fusion.21), channel_id=1, source_target_pairs={{0,8},{1,9},{2,10},{3,11},{4,12},{5,13},{6,14},{7,15},{8,0},{9,1},... | collective-permute-start | bytes 786440 | tf_op jit(solution)/shard_map/ppermute | solution.py:119
  135.9 14.9 %collective-permute-start.28 = (bf16[4,256,256]{2,1,0:T(8,128)(2,1)S(1)}, bf16[4,256,256]{2,1,0:T(8,128)(2,1)S(1)}, u32[]{:S(2)}, u32[]{:S(2)}) collective-permute-start(bf16[4,256,256]{2,1,0:T(8,128)(2,1)S(1)} %pad_maximum_fusion.17), channel_id=1, source_target_pairs={{0,2},{1,3},{2,0},{3,1},{4,6},{5,7},{6,4},{7,5},{8,10},{9,11},{10,... | collective-permute-start | bytes 1572872 | tf_op jit(solution)/shard_map/ppermute | solution.py:119
  137.6 28.8 %collective-permute-start.23 = (bf16[256,256]{1,0:T(8,128)(2,1)S(1)}, bf16[256,256]{1,0:T(8,128)(2,1)S(1)}, u32[]{:S(2)}, u32[]{:S(2)}) collective-permute-start(bf16[256,256]{1,0:T(8,128)(2,1)S(1)} %slice.886), channel_id=1, source_target_pairs={{0,16},{1,17},{2,18},{3,19},{4,20},{5,21},{6,22},{7,23},{8,24},{9,... | collective-permute-start | bytes 393224 | tf_op jit(solution)/shard_map/ppermute | solution.py:119
  138.8 10.5 %collective-permute-start.24 = (bf16[512,256]{1,0:T(8,128)(2,1)S(1)}, bf16[512,256]{1,0:T(8,128)(2,1)S(1)}, u32[]{:S(2)}, u32[]{:S(2)}) collective-permute-start(bf16[512,256]{1,0:T(8,128)(2,1)S(1)} %pad_maximum_fusion.22), channel_id=1, source_target_pairs={{0,8},{1,9},{2,10},{3,11},{4,12},{5,13},{6,14},{7,15},{8,0},{9,1},... | collective-permute-start | bytes 786440 | tf_op jit(solution)/shard_map/ppermute | solution.py:119
  141.2 20.9 %collective-permute-start.31 = (bf16[4,256,256]{2,1,0:T(8,128)(2,1)S(1)}, bf16[4,256,256]{2,1,0:T(8,128)(2,1)S(1)}, u32[]{:S(2)}, u32[]{:S(2)}) collective-permute-start(bf16[4,256,256]{2,1,0:T(8,128)(2,1)S(1)} %pad_maximum_fusion.18), channel_id=1, source_target_pairs={{0,2},{1,3},{2,0},{3,1},{4,6},{5,7},{6,4},{7,5},{8,10},{9,11},{10,... | collective-permute-start | bytes 1572872 | tf_op jit(solution)/shard_map/ppermute | solution.py:119
  157.0 9.0 %collective-permute-start.30 = (bf16[512,256]{1,0:T(8,128)(2,1)S(1)}, bf16[512,256]{1,0:T(8,128)(2,1)S(1)}, u32[]{:S(2)}, u32[]{:S(2)}) collective-permute-start(bf16[512,256]{1,0:T(8,128)(2,1)S(1)} %pad_maximum_fusion.24), channel_id=1, source_target_pairs={{0,8},{1,9},{2,10},{3,11},{4,12},{5,13},{6,14},{7,15},{8,0},{9,1},... | collective-permute-start | bytes 786440 | tf_op jit(solution)/shard_map/ppermute | solution.py:119
  157.5 9.0 %collective-permute-start.26 = (bf16[256,256]{1,0:T(8,128)(2,1)S(1)}, bf16[256,256]{1,0:T(8,128)(2,1)S(1)}, u32[]{:S(2)}, u32[]{:S(2)}) collective-permute-start(bf16[256,256]{1,0:T(8,128)(2,1)S(1)} %slice.885), channel_id=1, source_target_pairs={{0,16},{1,17},{2,18},{3,19},{4,20},{5,21},{6,22},{7,23},{8,24},{9,... | collective-permute-start | bytes 393224 | tf_op jit(solution)/shard_map/ppermute | solution.py:119
  159.2 14.9 %collective-permute-start.34 = (bf16[4,256,256]{2,1,0:T(8,128)(2,1)S(1)}, bf16[4,256,256]{2,1,0:T(8,128)(2,1)S(1)}, u32[]{:S(2)}, u32[]{:S(2)}) collective-permute-start(bf16[4,256,256]{2,1,0:T(8,128)(2,1)S(1)} %pad_maximum_fusion.19), channel_id=1, source_target_pairs={{0,2},{1,3},{2,0},{3,1},{4,6},{5,7},{6,4},{7,5},{8,10},{9,11},{10,... | collective-permute-start | bytes 1572872 | tf_op jit(solution)/shard_map/ppermute | solution.py:119
  166.3 11.6 %collective-permute-start.33 = (bf16[512,256]{1,0:T(8,128)(2,1)S(1)}, bf16[512,256]{1,0:T(8,128)(2,1)S(1)}, u32[]{:S(2)}, u32[]{:S(2)}) collective-permute-start(bf16[512,256]{1,0:T(8,128)(2,1)S(1)} %pad_maximum_fusion.26), channel_id=1, source_target_pairs={{0,8},{1,9},{2,10},{3,11},{4,12},{5,13},{6,14},{7,15},{8,0},{9,1},... | collective-permute-start | bytes 786440 | tf_op jit(solution)/shard_map/ppermute | solution.py:119
  166.5 20.8 %collective-permute-start.38 = (bf16[4,256,128]{2,1,0:T(8,128)(2,1)S(1)}, bf16[4,256,128]{2,1,0:T(8,128)(2,1)S(1)}, u32[]{:S(2)}, u32[]{:S(2)}) collective-permute-start(bf16[4,256,128]{2,1,0:T(8,128)(2,1)S(1)} %pad_maximum_fusion.25), channel_id=1, source_target_pairs={{0,2},{1,3},{2,0},{3,1},{4,6},{5,7},{6,4},{7,5},{8,10},{9,11},{10,... | collective-permute-start | bytes 786440 | tf_op jit(solution)/shard_map/ppermute | solution.py:119
  167.0 11.2 %collective-permute-start.29 = (bf16[256,256]{1,0:T(8,128)(2,1)S(1)}, bf16[256,256]{1,0:T(8,128)(2,1)S(1)}, u32[]{:S(2)}, u32[]{:S(2)}) collective-permute-start(bf16[256,256]{1,0:T(8,128)(2,1)S(1)} %slice.884), channel_id=1, source_target_pairs={{0,16},{1,17},{2,18},{3,19},{4,20},{5,21},{6,22},{7,23},{8,24},{9,... | collective-permute-start | bytes 393224 | tf_op jit(solution)/shard_map/ppermute | solution.py:119
  169.2 10.1 %collective-permute-start.32 = (bf16[256,256]{1,0:T(8,128)(2,1)S(1)}, bf16[256,256]{1,0:T(8,128)(2,1)S(1)}, u32[]{:S(2)}, u32[]{:S(2)}) collective-permute-start(bf16[256,256]{1,0:T(8,128)(2,1)S(1)} %slice.883), channel_id=1, source_target_pairs={{0,16},{1,17},{2,18},{3,19},{4,20},{5,21},{6,22},{7,23},{8,24},{9,... | collective-permute-start | bytes 393224 | tf_op jit(solution)/shard_map/ppermute | solution.py:119
  178.2 9.0 %collective-permute-start.36 = (bf16[512,256]{1,0:T(8,128)(2,1)S(1)}, bf16[512,256]{1,0:T(8,128)(2,1)S(1)}, u32[]{:S(2)}, u32[]{:S(2)}) collective-permute-start(bf16[512,256]{1,0:T(8,128)(2,1)S(1)} %pad_maximum_fusion.28), channel_id=1, source_target_pairs={{0,8},{1,9},{2,10},{3,11},{4,12},{5,13},{6,14},{7,15},{8,0},{9,1},... | collective-permute-start | bytes 786440 | tf_op jit(solution)/shard_map/ppermute | solution.py:119
  180.1 13.7 %collective-permute-start.41 = (bf16[4,256,128]{2,1,0:T(8,128)(2,1)S(1)}, bf16[4,256,128]{2,1,0:T(8,128)(2,1)S(1)}, u32[]{:S(2)}, u32[]{:S(2)}) collective-permute-start(bf16[4,256,128]{2,1,0:T(8,128)(2,1)S(1)} %pad_maximum_fusion.27), channel_id=1, source_target_pairs={{0,2},{1,3},{2,0},{3,1},{4,6},{5,7},{6,4},{7,5},{8,10},{9,11},{10,... | collective-permute-start | bytes 786440 | tf_op jit(solution)/shard_map/ppermute | solution.py:119
  187.5 9.0 %collective-permute-start.37 = (bf16[256,256]{1,0:T(8,128)(2,1)S(1)}, bf16[256,256]{1,0:T(8,128)(2,1)S(1)}, u32[]{:S(2)}, u32[]{:S(2)}) collective-permute-start(bf16[256,256]{1,0:T(8,128)(2,1)S(1)} %slice.881), channel_id=1, source_target_pairs={{0,16},{1,17},{2,18},{3,19},{4,20},{5,21},{6,22},{7,23},{8,24},{9,... | collective-permute-start | bytes 393224 | tf_op jit(solution)/shard_map/ppermute | solution.py:119
  193.8 8.2 %collective-permute-start.40 = (bf16[256,128]{1,0:T(8,128)(2,1)S(1)}, bf16[256,128]{1,0:T(8,128)(2,1)S(1)}, u32[]{:S(2)}, u32[]{:S(2)}) collective-permute-start(bf16[256,128]{1,0:T(8,128)(2,1)S(1)} %slice.889), channel_id=1, source_target_pairs={{0,16},{1,17},{2,18},{3,19},{4,20},{5,21},{6,22},{7,23},{8,24},{9,... | collective-permute-start | bytes 196616 | tf_op jit(solution)/shard_map/ppermute | solution.py:119
  (15 other events, 82.9 us)

commit v8 on v7

--- a/solution.py
+++ b/solution.py
@@ -15,7 +15,7 @@
     unit = cols // 16
     counts = [count for first, count in chunks]
     width = unit * sum(counts)
-    step = max(s for s in range(16, 449, 16) if rows % s == 0)
+    step = max(s for s in range(16, 225, 16) if rows % s == 0)
     tiles = rows // step
     spread = cols // 4 // width
     start = chunks[0][0] * unit // width
@@ -163,6 +163,8 @@
             far = permute(far, lambda z, x, y, c: (z, x, y, 1 - c))
             tables.append(jnp.stack(swap_if(c != 0, near, far), axis=1).reshape(-1, half))
 
+    early = 5
+
     def multiply(m, q, pieces=1):
         half = tables[q].shape[1] // 2
         totals = [jnp.dot(a, tables[q], preferred_element_type=jnp.float32) for a in acts[m]]
@@ -175,7 +177,8 @@
             jobs.append([total[:, at : at + width] for total in totals])
 
     def step_one(j):
-        back = after(backs[j], *leaving[j - 1 : j])
+        done = leaving[j - 1 : j] if j <= early else leaving[j - 2 : j - 1]
+        back = after(backs[j], *done)
         totals = [total + b for total, b in zip(jobs[j], back)]
         count = len(totals) // 2
         near, far = zip(*[swap_if(flip, own, sibling) for own, sibling in zip(totals[:count], totals[count:])])
@@ -208,20 +211,22 @@
     to_plane(1, *moved[0])
     multiply(0, 0)
     multiply(0, 1)
-    to_tables(2, backs[0])
+    to_tables(2, backs[0], moved[1][0])
     multiply(0, 2)
     multiply(0, 3)
     to_cores(1, backs[2])
     for q in range(4):
         multiply(1, q, 1 + q // 3)
     count = len(jobs)
-    for j in range(count + 1):
-        if j >= 1:
+    for j in range(count + 2):
+        if j <= early and 1 <= j <= count:
             step_two(j - 1)
         if j < count:
             step_one(j)
-        if j >= 1:
-            step_three(j - 1)
+        if j > early and j <= count:
+            step_two(j - 1)
+        if j >= 2:
+            step_three(j - 2)
     result = [jnp.concatenate(result[:4], axis=1), jnp.concatenate(result[4:], axis=1)]
     decoded = jnp.concatenate(result, axis=0)
     return (*updated, decoded)

time: 206 us -> 209 us (1.015)
  waiting for transfers between devices: 105 us -> 96.2 us
  starting transfers between devices: 41.4 us -> 48 us
  Pallas kernels: 22 us -> 25.8 us
    ppermute x44, waiting for transfers between devices: 105 us -> 96.2 us  [permute(): return lax.ppermute(value, AXES, pairs)]
    ppermute x44, starting transfers between devices: 41.4 us -> 48 us  [permute(): return lax.ppermute(value, AXES, pairs)]
    pallas_call x2, Pallas kernels: 20.2 us -> 24 us  [adam(): pl.pallas_call(kernel, grid_spec=pltpu.PrefetchScalarGridSpec(num_scalar_...]
  transfers between devices with their start and end apart: 44 -> 44, of which waited for: 23 -> 22; matrix products, arithmetic and copies ran while one was open for 16% -> 16% of each run, Pallas kernels for 10% -> 12%
where the time goes in v8:
time: 209 us; the launch traced here: 208 us
  waiting for transfers between devices  96.2 us (46%)
  starting transfers between devices  48 us (23%)
  Pallas kernels  25.8 us (12%)
  matrix products  20.4 us (10%)
  other arithmetic  8.27 us (4%)
  local copies, waits for them, and re-layouts  7.49 us (4%)
    ppermute x44, waiting for transfers between devices, permute(): return lax.ppermute(value, AXES, pairs)  96.2 us
    ppermute x44, starting transfers between devices, permute(): return lax.ppermute(value, AXES, pairs)  48 us
    pallas_call x2, Pallas kernels, adam(): pl.pallas_call(kernel, grid_spec=pltpu.PrefetchScalarGridSpec(num_scalar_...  24 us
    dot_general x32, matrix products, multiply(): jnp.dot(a, tables[q], preferred_element_type=jnp.float32)  20.4 us
    slice x5, local copies, waits for them, and re-layouts, to_tables(): near = jnp.stack([p[k, :, :half] for p in parts])  4.23 us
  transfers between devices with their start and end apart: 44, of which 22 were waited for; matrix products, arithmetic and copies ran while one was open for 16% of the time, Pallas kernels for 12%

profile of v8, /device:TPU:0, one launch (start us, length us, event | category | flops | bytes accessed | tf_op | source)
XLA Modules:
  0.0 208.0 jit_solution(9949458717110753122)
XLA Ops:
  0.7 2.0 copy-done
  2.8 1.8 pack.1
  4.6 3.0 %collective-permute-start = (bf16[256,1792]{1,0:T(8,128)(2,1)}, bf16[256,1792]{1,0:T(8,128)(2,1)}, u32[]{:S(2)}, u32[]{:S(2)}) collective-permute-start(bf16[256,1792]{1,0:T(8,128)(2,1)} %get-tuple-element.57), channel_id=1, source_target_pairs={{0,2},{1,3},{2,0},{3,1},{4,6},{5,7},{6,4},{7,5},{8,10},{9,11},{10,... | collective-permute-start | bytes 2752520 | tf_op jit(solution)/shard_map/ppermute | solution.py:119
  7.5 12.0 %adam.2 = (f32[448,4096]{1,0:T(8,128)}, f32[448,4096]{1,0:T(8,128)}, f32[448,4096]{1,0:T(8,128)}, bf16[1,448,1024]{2,1,0:T(8,128)(2,1)}, bf16[1,448,1024]{2,1,0:T(8,128)(2,1)}) custom-call(s32[3]{0:T(128)} %copy-done.1, f32[448,4096]{1,0:T(8,128)} %master_ref.3, f32[448,4096]{1,0:T(8,128)} %one_ref.3, f32[448,4096]{1,0:T(8,128)} %two_ref.3, ...), custom_call_target="tpu_custom_call" | custom-call | flops 11010048 | bytes 25690112 | tf_op jit(solution)/shard_map/adam/pallas_call | solution.py:48
  21.7 12.0 %adam.3 = (f32[448,4096]{1,0:T(8,128)}, f32[448,4096]{1,0:T(8,128)}, f32[448,4096]{1,0:T(8,128)}, bf16[2,448,1024]{2,1,0:T(8,128)(2,1)}) custom-call(s32[3]{0:T(128)} %copy-done.1, f32[448,4096]{1,0:T(8,128)} %master_ref.3, f32[448,4096]{1,0:T(8,128)} %one_ref.3, f32[448,4096]{1,0:T(8,128)} %two_ref.3, ...), custom_call_target="tpu_custom_call", output_to_operand_aliasing={{0}: (5, {}), {1}: (6, {}), {2}: (7, {})} | custom-call | flops 11010048 | bytes 25690112 | tf_op jit(solution)/shard_map/adam/pallas_call | solution.py:48
  37.4 3.1 %collective-permute-start.5 = (bf16[256,1792]{1,0:T(8,128)(2,1)S(1)}, bf16[256,1792]{1,0:T(8,128)(2,1)S(1)}, u32[]{:S(2)}, u32[]{:S(2)}) collective-permute-start(bf16[256,1792]{1,0:T(8,128)(2,1)S(1)} %get-tuple-element.61), channel_id=1, source_target_pairs={{0,16},{1,24},{2,18},{3,26},{4,20},{5,28},{6,22},{7,30},{8,17},{9,... | collective-permute-start | bytes 2752520 | tf_op jit(solution)/shard_map/ppermute | solution.py:119
  40.6 2.7 %collective-permute-done.3 = bf16[1,448,1024]{2,1,0:T(8,128)(2,1)} collective-permute-done((bf16[1,448,1024]{2,1,0:T(8,128)(2,1)}, bf16[1,448,1024]{2,1,0:T(8,128)(2,1)}, u32[]{:S(2)}, u32[]{:S(2)}) %collective-permute-start.3) | collective-permute-done | bytes 917536 | tf_op jit(solution)/shard_map/ppermute | solution.py:119
  46.0 16.9 %collective-permute-done.14 = bf16[1,448,1024]{2,1,0:T(8,128)(2,1)} collective-permute-done((bf16[1,448,1024]{2,1,0:T(8,128)(2,1)}, bf16[1,448,1024]{2,1,0:T(8,128)(2,1)}, u32[]{:S(2)}, u32[]{:S(2)}) %collective-permute-start.14) | collective-permute-done | bytes 917536 | tf_op jit(solution)/shard_map/ppermute | solution.py:119
  66.1 14.3 %collective-permute-done.5 = bf16[256,1792]{1,0:T(8,128)(2,1)S(1)} collective-permute-done((bf16[256,1792]{1,0:T(8,128)(2,1)S(1)}, bf16[256,1792]{1,0:T(8,128)(2,1)S(1)}, u32[]{:S(2)}, u32[]{:S(2)}) %collective-permute-start.5) | collective-permute-done | bytes 917536 | tf_op jit(solution)/shard_map/ppermute | solution.py:119
  82.9 4.3 %collective-permute-start.6 = (bf16[256,1792]{1,0:T(8,128)(2,1)S(1)}, bf16[256,1792]{1,0:T(8,128)(2,1)S(1)}, u32[]{:S(2)}, u32[]{:S(2)}) collective-permute-start(bf16[256,1792]{1,0:T(8,128)(2,1)S(1)} %collective-permute-done.5), channel_id=1, source_target_pairs={{0,1},{1,0},{2,3},{3,2},{4,5},{5,4},{6,7},{7,6},{8,9},{9,8},{10,11... | collective-permute-start | bytes 2752520 | tf_op jit(solution)/shard_map/ppermute | solution.py:119
  91.4 1.6 collective-permute-start.7
  94.3 6.3 %collective-permute-done.9 = bf16[2,448,1024]{2,1,0:T(8,128)(2,1)S(1)} collective-permute-done((bf16[2,448,1024]{2,1,0:T(8,128)(2,1)S(1)}, bf16[2,448,1024]{2,1,0:T(8,128)(2,1)S(1)}, u32[]{:S(2)}, u32[]{:S(2)}) %collective-permute-start.9) | collective-permute-done | bytes 1835040 | tf_op jit(solution)/shard_map/ppermute | solution.py:119
  100.6 5.1 %collective-permute-done.7 = bf16[4,256,256]{2,1,0:T(8,128)(2,1)S(1)} collective-permute-done((bf16[4,256,256]{2,1,0:T(8,128)(2,1)S(1)}, bf16[4,256,256]{2,1,0:T(8,128)(2,1)S(1)}, u32[]{:S(2)}, u32[]{:S(2)}) %collective-permute-start.7) | collective-permute-done | bytes 524320 | tf_op jit(solution)/shard_map/ppermute | solution.py:119
  106.2 1.6 collective-permute-start.16
  116.5 4.5 %collective-permute-done.16 = bf16[4,256,256]{2,1,0:T(8,128)(2,1)S(1)} collective-permute-done((bf16[4,256,256]{2,1,0:T(8,128)(2,1)S(1)}, bf16[4,256,256]{2,1,0:T(8,128)(2,1)S(1)}, u32[]{:S(2)}, u32[]{:S(2)}) %collective-permute-start.16) | collective-permute-done | bytes 524320 | tf_op jit(solution)/shard_map/ppermute | solution.py:119
  122.9 2.3 %collective-permute-start.18 = (bf16[512,256]{1,0:T(8,128)(2,1)S(1)}, bf16[512,256]{1,0:T(8,128)(2,1)S(1)}, u32[]{:S(2)}, u32[]{:S(2)}) collective-permute-start(bf16[512,256]{1,0:T(8,128)(2,1)S(1)} %pad_maximum_fusion.21), channel_id=1, source_target_pairs={{0,8},{1,9},{2,10},{3,11},{4,12},{5,13},{6,14},{7,15},{8,0},{9,1},... | collective-permute-start | bytes 786440 | tf_op jit(solution)/shard_map/ppermute | solution.py:119
  125.2 5.8 %collective-permute-done.17 = bf16[256,256]{1,0:T(8,128)(2,1)S(1)} collective-permute-done((bf16[256,256]{1,0:T(8,128)(2,1)S(1)}, bf16[256,256]{1,0:T(8,128)(2,1)S(1)}, u32[]{:S(2)}, u32[]{:S(2)}) %collective-permute-start.17) | collective-permute-done | bytes 131104 | tf_op jit(solution)/shard_map/ppermute | solution.py:119
  139.8 1.6 collective-permute-start.28
  141.8 1.9 collective-permute-start.24
  148.4 4.2 %collective-permute-done.24 = bf16[512,256]{1,0:T(8,128)(2,1)S(1)} collective-permute-done((bf16[512,256]{1,0:T(8,128)(2,1)S(1)}, bf16[512,256]{1,0:T(8,128)(2,1)S(1)}, u32[]{:S(2)}, u32[]{:S(2)}) %collective-permute-start.24) | collective-permute-done | bytes 262176 | tf_op jit(solution)/shard_map/ppermute | solution.py:119
  153.1 2.9 %collective-permute-start.26 = (bf16[256,256]{1,0:T(8,128)(2,1)S(1)}, bf16[256,256]{1,0:T(8,128)(2,1)S(1)}, u32[]{:S(2)}, u32[]{:S(2)}) collective-permute-start(bf16[256,256]{1,0:T(8,128)(2,1)S(1)} %slice.885), channel_id=1, source_target_pairs={{0,16},{1,17},{2,18},{3,19},{4,20},{5,21},{6,22},{7,23},{8,24},{9,... | collective-permute-start | bytes 393224 | tf_op jit(solution)/shard_map/ppermute | solution.py:119
  156.0 6.9 %collective-permute-done.27 = bf16[512,256]{1,0:T(8,128)(2,1)S(1)} collective-permute-done((bf16[512,256]{1,0:T(8,128)(2,1)S(1)}, bf16[512,256]{1,0:T(8,128)(2,1)S(1)}, u32[]{:S(2)}, u32[]{:S(2)}) %collective-permute-start.27) | collective-permute-done | bytes 262176 | tf_op jit(solution)/shard_map/ppermute | solution.py:119
  163.6 2.5 %collective-permute-start.30 = (bf16[512,256]{1,0:T(8,128)(2,1)S(1)}, bf16[512,256]{1,0:T(8,128)(2,1)S(1)}, u32[]{:S(2)}, u32[]{:S(2)}) collective-permute-start(bf16[512,256]{1,0:T(8,128)(2,1)S(1)} %pad_maximum_fusion.24), channel_id=1, source_target_pairs={{0,8},{1,9},{2,10},{3,11},{4,12},{5,13},{6,14},{7,15},{8,0},{9,1},... | collective-permute-start | bytes 786440 | tf_op jit(solution)/shard_map/ppermute | solution.py:119
  168.3 2.4 %collective-permute-done.29 = bf16[256,256]{1,0:T(8,128)(2,1)S(1)} collective-permute-done((bf16[256,256]{1,0:T(8,128)(2,1)S(1)}, bf16[256,256]{1,0:T(8,128)(2,1)S(1)}, u32[]{:S(2)}, u32[]{:S(2)}) %collective-permute-start.29) | collective-permute-done | bytes 131104 | tf_op jit(solution)/shard_map/ppermute | solution.py:119
  170.8 3.3 %collective-permute-done.30 = bf16[512,256]{1,0:T(8,128)(2,1)S(1)} collective-permute-done((bf16[512,256]{1,0:T(8,128)(2,1)S(1)}, bf16[512,256]{1,0:T(8,128)(2,1)S(1)}, u32[]{:S(2)}, u32[]{:S(2)}) %collective-permute-start.30) | collective-permute-done | bytes 262176 | tf_op jit(solution)/shard_map/ppermute | solution.py:119
  174.8 1.8 collective-permute-start.33
  176.6 4.6 %collective-permute-done.34 = bf16[4,256,256]{2,1,0:T(8,128)(2,1)S(1)} collective-permute-done((bf16[4,256,256]{2,1,0:T(8,128)(2,1)S(1)}, bf16[4,256,256]{2,1,0:T(8,128)(2,1)S(1)}, u32[]{:S(2)}, u32[]{:S(2)}) %collective-permute-start.34) | collective-permute-done | bytes 524320 | tf_op jit(solution)/shard_map/ppermute | solution.py:119
  182.1 3.8 %collective-permute-done.33 = bf16[512,256]{1,0:T(8,128)(2,1)S(1)} collective-permute-done((bf16[512,256]{1,0:T(8,128)(2,1)S(1)}, bf16[512,256]{1,0:T(8,128)(2,1)S(1)}, u32[]{:S(2)}, u32[]{:S(2)}) %collective-permute-start.33) | collective-permute-done | bytes 262176 | tf_op jit(solution)/shard_map/ppermute | solution.py:119
  187.2 5.1 %collective-permute-done.36 = bf16[512,256]{1,0:T(8,128)(2,1)S(1)} collective-permute-done((bf16[512,256]{1,0:T(8,128)(2,1)S(1)}, bf16[512,256]{1,0:T(8,128)(2,1)S(1)}, u32[]{:S(2)}, u32[]{:S(2)}) %collective-permute-start.36) | collective-permute-done | bytes 262176 | tf_op jit(solution)/shard_map/ppermute | solution.py:119
  196.3 3.5 %collective-permute-done.39 = bf16[512,128]{1,0:T(8,128)(2,1)S(1)} collective-permute-done((bf16[512,128]{1,0:T(8,128)(2,1)S(1)}, bf16[512,128]{1,0:T(8,128)(2,1)S(1)}, u32[]{:S(2)}, u32[]{:S(2)}) %collective-permute-start.39) | collective-permute-done | bytes 131104 | tf_op jit(solution)/shard_map/ppermute | solution.py:119
  201.4 2.3 %collective-permute-start.43 = (bf16[256,128]{1,0:T(8,128)(2,1)S(1)}, bf16[256,128]{1,0:T(8,128)(2,1)S(1)}, u32[]{:S(2)}, u32[]{:S(2)}) collective-permute-start(bf16[256,128]{1,0:T(8,128)(2,1)S(1)} %slice.888), channel_id=1, source_target_pairs={{0,16},{1,17},{2,18},{3,19},{4,20},{5,21},{6,22},{7,23},{8,24},{9,... | collective-permute-start | bytes 196616 | tf_op jit(solution)/shard_map/ppermute | solution.py:119
  203.8 2.5 %collective-permute-done.40 = bf16[256,128]{1,0:T(8,128)(2,1)S(1)} collective-permute-done((bf16[256,128]{1,0:T(8,128)(2,1)S(1)}, bf16[256,128]{1,0:T(8,128)(2,1)S(1)}, u32[]{:S(2)}, u32[]{:S(2)}) %collective-permute-start.40) | collective-permute-done | bytes 65568 | tf_op jit(solution)/shard_map/ppermute | solution.py:119
  (208 shorter events, 57.8 us)
Async XLA Ops:
  4.6 30.7 %collective-permute-start = (bf16[256,1792]{1,0:T(8,128)(2,1)}, bf16[256,1792]{1,0:T(8,128)(2,1)}, u32[]{:S(2)}, u32[]{:S(2)}) collective-permute-start(bf16[256,1792]{1,0:T(8,128)(2,1)} %get-tuple-element.57), channel_id=1, source_target_pairs={{0,2},{1,3},{2,0},{3,1},{4,6},{5,7},{6,4},{7,5},{8,10},{9,11},{10,... | collective-permute-start | bytes 2752520 | tf_op jit(solution)/shard_map/ppermute | solution.py:119
  19.6 23.6 %collective-permute-start.3 = (bf16[1,448,1024]{2,1,0:T(8,128)(2,1)}, bf16[1,448,1024]{2,1,0:T(8,128)(2,1)}, u32[]{:S(2)}, u32[]{:S(2)}) collective-permute-start(bf16[1,448,1024]{2,1,0:T(8,128)(2,1)} %get-tuple-element.60), channel_id=1, source_target_pairs={{0,4},{1,5},{2,6},{3,7},{4,0},{5,1},{6,2},{7,3},{8,12},{9,13},{10,... | collective-permute-start | bytes 2752520 | tf_op jit(solution)/shard_map/ppermute | solution.py:119
  21.1 43.1 %collective-permute-start.10 = (bf16[256,1792]{1,0:T(8,128)(2,1)S(1)}, bf16[256,1792]{1,0:T(8,128)(2,1)}, u32[]{:S(2)}, u32[]{:S(2)}) collective-permute-start(bf16[256,1792]{1,0:T(8,128)(2,1)S(1)} %get-tuple-element.63), channel_id=1, source_target_pairs={{0,2},{1,3},{2,0},{3,1},{4,6},{5,7},{6,4},{7,5},{8,10},{9,11},{10,... | collective-permute-start | bytes 2752520 | tf_op jit(solution)/shard_map/ppermute | solution.py:119
  21.6 41.3 %collective-permute-start.14 = (bf16[1,448,1024]{2,1,0:T(8,128)(2,1)}, bf16[1,448,1024]{2,1,0:T(8,128)(2,1)}, u32[]{:S(2)}, u32[]{:S(2)}) collective-permute-start(bf16[1,448,1024]{2,1,0:T(8,128)(2,1)} %get-tuple-element.68), channel_id=1, source_target_pairs={{0,4},{1,5},{2,6},{3,7},{4,0},{5,1},{6,2},{7,3},{8,12},{9,13},{10,... | collective-permute-start | bytes 2752520 | tf_op jit(solution)/shard_map/ppermute | solution.py:119
  36.7 29.4 %collective-permute-start.1 = (bf16[256,1792]{1,0:T(8,128)(2,1)S(1)}, bf16[256,1792]{1,0:T(8,128)(2,1)S(1)}, u32[]{:S(2)}, u32[]{:S(2)}) collective-permute-start(bf16[256,1792]{1,0:T(8,128)(2,1)S(1)} %get-tuple-element.59), channel_id=1, source_target_pairs={{0,0},{1,8},{2,2},{3,10},{4,4},{5,12},{6,6},{7,14},{8,1},{9,9},{10... | collective-permute-start | bytes 2752520 | tf_op jit(solution)/shard_map/ppermute | solution.py:119
  37.4 43.0 %collective-permute-start.5 = (bf16[256,1792]{1,0:T(8,128)(2,1)S(1)}, bf16[256,1792]{1,0:T(8,128)(2,1)S(1)}, u32[]{:S(2)}, u32[]{:S(2)}) collective-permute-start(bf16[256,1792]{1,0:T(8,128)(2,1)S(1)} %get-tuple-element.61), channel_id=1, source_target_pairs={{0,16},{1,24},{2,18},{3,26},{4,20},{5,28},{6,22},{7,30},{8,17},{9,... | collective-permute-start | bytes 2752520 | tf_op jit(solution)/shard_map/ppermute | solution.py:119
  43.2 57.4 %collective-permute-start.9 = (bf16[2,448,1024]{2,1,0:T(8,128)(2,1)S(1)}, bf16[2,448,1024]{2,1,0:T(8,128)(2,1)S(1)}, u32[]{:S(2)}, u32[]{:S(2)}) collective-permute-start(bf16[2,448,1024]{2,1,0:T(8,128)(2,1)S(1)} %copy-done.2), channel_id=1, source_target_pairs={{0,4},{1,5},{2,6},{3,7},{4,0},{5,1},{6,2},{7,3},{8,12},{9,13},{10,... | collective-permute-start | bytes 5505032 | tf_op jit(solution)/shard_map/ppermute | solution.py:119
  62.9 18.5 %collective-permute-start.4 = (bf16[2,448,512]{2,1,0:T(8,128)(2,1)S(1)}, bf16[2,448,512]{2,1,0:T(8,128)(2,1)S(1)}, u32[]{:S(2)}, u32[]{:S(2)}) collective-permute-start(bf16[2,448,512]{2,1,0:T(8,128)(2,1)S(1)} %pad_maximum_fusion.5), channel_id=1, source_target_pairs={{0,1},{1,0},{2,3},{3,2},{4,5},{5,4},{6,7},{7,6},{8,9},{9,8},{10,11... | collective-permute-start | bytes 2752520 | tf_op jit(solution)/shard_map/ppermute | solution.py:119
  64.2 18.3 %collective-permute-start.15 = (bf16[2,448,512]{2,1,0:T(8,128)(2,1)S(1)}, bf16[2,448,512]{2,1,0:T(8,128)(2,1)S(1)}, u32[]{:S(2)}, u32[]{:S(2)}) collective-permute-start(bf16[2,448,512]{2,1,0:T(8,128)(2,1)S(1)} %pad_maximum_fusion.11), channel_id=1, source_target_pairs={{0,1},{1,0},{2,3},{3,2},{4,5},{5,4},{6,7},{7,6},{8,9},{9,8},{10,11... | collective-permute-start | bytes 2752520 | tf_op jit(solution)/shard_map/ppermute | solution.py:119
  80.4 13.9 %collective-permute-start.11 = (bf16[256,1792]{1,0:T(8,128)(2,1)S(1)}, bf16[256,1792]{1,0:T(8,128)(2,1)S(1)}, u32[]{:S(2)}, u32[]{:S(2)}) collective-permute-start(bf16[256,1792]{1,0:T(8,128)(2,1)S(1)} %get-tuple-element.65), channel_id=1, source_target_pairs={{0,0},{1,8},{2,2},{3,10},{4,4},{5,12},{6,6},{7,14},{8,1},{9,9},{10... | collective-permute-start | bytes 2752520 | tf_op jit(solution)/shard_map/ppermute | solution.py:119
  81.3 49.7 %collective-permute-start.19 = (bf16[256,1792]{1,0:T(8,128)(2,1)S(1)}, bf16[256,1792]{1,0:T(8,128)(2,1)S(1)}, u32[]{:S(2)}, u32[]{:S(2)}) collective-permute-start(bf16[256,1792]{1,0:T(8,128)(2,1)S(1)} %get-tuple-element.74), channel_id=1, source_target_pairs={{0,16},{1,24},{2,18},{3,26},{4,20},{5,28},{6,22},{7,30},{8,17},{9,... | collective-permute-start | bytes 2752520 | tf_op jit(solution)/shard_map/ppermute | solution.py:119
  91.4 14.3 %collective-permute-start.7 = (bf16[4,256,256]{2,1,0:T(8,128)(2,1)S(1)}, bf16[4,256,256]{2,1,0:T(8,128)(2,1)S(1)}, u32[]{:S(2)}, u32[]{:S(2)}) collective-permute-start(bf16[4,256,256]{2,1,0:T(8,128)(2,1)S(1)} %pad_maximum_fusion.13), channel_id=1, source_target_pairs={{0,2},{1,3},{2,0},{3,1},{4,6},{5,7},{6,4},{7,5},{8,10},{9,11},{10,... | collective-permute-start | bytes 1572872 | tf_op jit(solution)/shard_map/ppermute | solution.py:119
  106.2 14.8 %collective-permute-start.16 = (bf16[4,256,256]{2,1,0:T(8,128)(2,1)S(1)}, bf16[4,256,256]{2,1,0:T(8,128)(2,1)S(1)}, u32[]{:S(2)}, u32[]{:S(2)}) collective-permute-start(bf16[4,256,256]{2,1,0:T(8,128)(2,1)S(1)} %pad_maximum_fusion.16), channel_id=1, source_target_pairs={{0,2},{1,3},{2,0},{3,1},{4,6},{5,7},{6,4},{7,5},{8,10},{9,11},{10,... | collective-permute-start | bytes 1572872 | tf_op jit(solution)/shard_map/ppermute | solution.py:119
  108.4 14.2 %collective-permute-start.8 = (bf16[512,256]{1,0:T(8,128)(2,1)S(1)}, bf16[512,256]{1,0:T(8,128)(2,1)S(1)}, u32[]{:S(2)}, u32[]{:S(2)}) collective-permute-start(bf16[512,256]{1,0:T(8,128)(2,1)S(1)} %pad_maximum_fusion.20), channel_id=1, source_target_pairs={{0,8},{1,9},{2,10},{3,11},{4,12},{5,13},{6,14},{7,15},{8,0},{9,1},... | collective-permute-start | bytes 786440 | tf_op jit(solution)/shard_map/ppermute | solution.py:119
  111.8 20.5 %collective-permute-start.20 = (bf16[4,256,256]{2,1,0:T(8,128)(2,1)S(1)}, bf16[4,256,256]{2,1,0:T(8,128)(2,1)S(1)}, u32[]{:S(2)}, u32[]{:S(2)}) collective-permute-start(bf16[4,256,256]{2,1,0:T(8,128)(2,1)S(1)} %pad_maximum_fusion.15), channel_id=1, source_target_pairs={{0,2},{1,3},{2,0},{3,1},{4,6},{5,7},{6,4},{7,5},{8,10},{9,11},{10,... | collective-permute-start | bytes 1572872 | tf_op jit(solution)/shard_map/ppermute | solution.py:119
  121.0 26.7 %collective-permute-start.25 = (bf16[4,256,256]{2,1,0:T(8,128)(2,1)S(1)}, bf16[4,256,256]{2,1,0:T(8,128)(2,1)S(1)}, u32[]{:S(2)}, u32[]{:S(2)}) collective-permute-start(bf16[4,256,256]{2,1,0:T(8,128)(2,1)S(1)} %pad_maximum_fusion.14), channel_id=1, source_target_pairs={{0,2},{1,3},{2,0},{3,1},{4,6},{5,7},{6,4},{7,5},{8,10},{9,11},{10,... | collective-permute-start | bytes 1572872 | tf_op jit(solution)/shard_map/ppermute | solution.py:119
  122.7 8.4 %collective-permute-start.17 = (bf16[256,256]{1,0:T(8,128)(2,1)S(1)}, bf16[256,256]{1,0:T(8,128)(2,1)S(1)}, u32[]{:S(2)}, u32[]{:S(2)}) collective-permute-start(bf16[256,256]{1,0:T(8,128)(2,1)S(1)} %slice.887), channel_id=1, source_target_pairs={{0,16},{1,17},{2,18},{3,19},{4,20},{5,21},{6,22},{7,23},{8,24},{9,... | collective-permute-start | bytes 393224 | tf_op jit(solution)/shard_map/ppermute | solution.py:119
  122.9 18.5 %collective-permute-start.18 = (bf16[512,256]{1,0:T(8,128)(2,1)S(1)}, bf16[512,256]{1,0:T(8,128)(2,1)S(1)}, u32[]{:S(2)}, u32[]{:S(2)}) collective-permute-start(bf16[512,256]{1,0:T(8,128)(2,1)S(1)} %pad_maximum_fusion.21), channel_id=1, source_target_pairs={{0,8},{1,9},{2,10},{3,11},{4,12},{5,13},{6,14},{7,15},{8,0},{9,1},... | collective-permute-start | bytes 786440 | tf_op jit(solution)/shard_map/ppermute | solution.py:119
  139.8 16.2 %collective-permute-start.28 = (bf16[4,256,256]{2,1,0:T(8,128)(2,1)S(1)}, bf16[4,256,256]{2,1,0:T(8,128)(2,1)S(1)}, u32[]{:S(2)}, u32[]{:S(2)}) collective-permute-start(bf16[4,256,256]{2,1,0:T(8,128)(2,1)S(1)} %pad_maximum_fusion.17), channel_id=1, source_target_pairs={{0,2},{1,3},{2,0},{3,1},{4,6},{5,7},{6,4},{7,5},{8,10},{9,11},{10,... | collective-permute-start | bytes 1572872 | tf_op jit(solution)/shard_map/ppermute | solution.py:119
  141.5 11.6 %collective-permute-start.23 = (bf16[256,256]{1,0:T(8,128)(2,1)S(1)}, bf16[256,256]{1,0:T(8,128)(2,1)S(1)}, u32[]{:S(2)}, u32[]{:S(2)}) collective-permute-start(bf16[256,256]{1,0:T(8,128)(2,1)S(1)} %slice.886), channel_id=1, source_target_pairs={{0,16},{1,17},{2,18},{3,19},{4,20},{5,21},{6,22},{7,23},{8,24},{9,... | collective-permute-start | bytes 393224 | tf_op jit(solution)/shard_map/ppermute | solution.py:119
  141.8 10.8 %collective-permute-start.24 = (bf16[512,256]{1,0:T(8,128)(2,1)S(1)}, bf16[512,256]{1,0:T(8,128)(2,1)S(1)}, u32[]{:S(2)}, u32[]{:S(2)}) collective-permute-start(bf16[512,256]{1,0:T(8,128)(2,1)S(1)} %pad_maximum_fusion.22), channel_id=1, source_target_pairs={{0,8},{1,9},{2,10},{3,11},{4,12},{5,13},{6,14},{7,15},{8,0},{9,1},... | collective-permute-start | bytes 786440 | tf_op jit(solution)/shard_map/ppermute | solution.py:119
  147.7 19.1 %collective-permute-start.31 = (bf16[4,256,256]{2,1,0:T(8,128)(2,1)S(1)}, bf16[4,256,256]{2,1,0:T(8,128)(2,1)S(1)}, u32[]{:S(2)}, u32[]{:S(2)}) collective-permute-start(bf16[4,256,256]{2,1,0:T(8,128)(2,1)S(1)} %pad_maximum_fusion.18), channel_id=1, source_target_pairs={{0,2},{1,3},{2,0},{3,1},{4,6},{5,7},{6,4},{7,5},{8,10},{9,11},{10,... | collective-permute-start | bytes 1572872 | tf_op jit(solution)/shard_map/ppermute | solution.py:119
  152.9 10.0 %collective-permute-start.27 = (bf16[512,256]{1,0:T(8,128)(2,1)S(1)}, bf16[512,256]{1,0:T(8,128)(2,1)S(1)}, u32[]{:S(2)}, u32[]{:S(2)}) collective-permute-start(bf16[512,256]{1,0:T(8,128)(2,1)S(1)} %pad_maximum_fusion.23), channel_id=1, source_target_pairs={{0,8},{1,9},{2,10},{3,11},{4,12},{5,13},{6,14},{7,15},{8,0},{9,1},... | collective-permute-start | bytes 786440 | tf_op jit(solution)/shard_map/ppermute | solution.py:119
  153.1 13.1 %collective-permute-start.26 = (bf16[256,256]{1,0:T(8,128)(2,1)S(1)}, bf16[256,256]{1,0:T(8,128)(2,1)S(1)}, u32[]{:S(2)}, u32[]{:S(2)}) collective-permute-start(bf16[256,256]{1,0:T(8,128)(2,1)S(1)} %slice.885), channel_id=1, source_target_pairs={{0,16},{1,17},{2,18},{3,19},{4,20},{5,21},{6,22},{7,23},{8,24},{9,... | collective-permute-start | bytes 393224 | tf_op jit(solution)/shard_map/ppermute | solution.py:119
  163.6 10.4 %collective-permute-start.30 = (bf16[512,256]{1,0:T(8,128)(2,1)S(1)}, bf16[512,256]{1,0:T(8,128)(2,1)S(1)}, u32[]{:S(2)}, u32[]{:S(2)}) collective-permute-start(bf16[512,256]{1,0:T(8,128)(2,1)S(1)} %pad_maximum_fusion.24), channel_id=1, source_target_pairs={{0,8},{1,9},{2,10},{3,11},{4,12},{5,13},{6,14},{7,15},{8,0},{9,1},... | collective-permute-start | bytes 786440 | tf_op jit(solution)/shard_map/ppermute | solution.py:119
  166.2 14.9 %collective-permute-start.34 = (bf16[4,256,256]{2,1,0:T(8,128)(2,1)S(1)}, bf16[4,256,256]{2,1,0:T(8,128)(2,1)S(1)}, u32[]{:S(2)}, u32[]{:S(2)}) collective-permute-start(bf16[4,256,256]{2,1,0:T(8,128)(2,1)S(1)} %pad_maximum_fusion.19), channel_id=1, source_target_pairs={{0,2},{1,3},{2,0},{3,1},{4,6},{5,7},{6,4},{7,5},{8,10},{9,11},{10,... | collective-permute-start | bytes 1572872 | tf_op jit(solution)/shard_map/ppermute | solution.py:119
  166.8 20.4 %collective-permute-start.38 = (bf16[4,256,128]{2,1,0:T(8,128)(2,1)S(1)}, bf16[4,256,128]{2,1,0:T(8,128)(2,1)S(1)}, u32[]{:S(2)}, u32[]{:S(2)}) collective-permute-start(bf16[4,256,128]{2,1,0:T(8,128)(2,1)S(1)} %pad_maximum_fusion.25), channel_id=1, source_target_pairs={{0,2},{1,3},{2,0},{3,1},{4,6},{5,7},{6,4},{7,5},{8,10},{9,11},{10,... | collective-permute-start | bytes 786440 | tf_op jit(solution)/shard_map/ppermute | solution.py:119
  174.8 11.0 %collective-permute-start.33 = (bf16[512,256]{1,0:T(8,128)(2,1)S(1)}, bf16[512,256]{1,0:T(8,128)(2,1)S(1)}, u32[]{:S(2)}, u32[]{:S(2)}) collective-permute-start(bf16[512,256]{1,0:T(8,128)(2,1)S(1)} %pad_maximum_fusion.26), channel_id=1, source_target_pairs={{0,8},{1,9},{2,10},{3,11},{4,12},{5,13},{6,14},{7,15},{8,0},{9,1},... | collective-permute-start | bytes 786440 | tf_op jit(solution)/shard_map/ppermute | solution.py:119
  181.4 10.9 %collective-permute-start.36 = (bf16[512,256]{1,0:T(8,128)(2,1)S(1)}, bf16[512,256]{1,0:T(8,128)(2,1)S(1)}, u32[]{:S(2)}, u32[]{:S(2)}) collective-permute-start(bf16[512,256]{1,0:T(8,128)(2,1)S(1)} %pad_maximum_fusion.28), channel_id=1, source_target_pairs={{0,8},{1,9},{2,10},{3,11},{4,12},{5,13},{6,14},{7,15},{8,0},{9,1},... | collective-permute-start | bytes 786440 | tf_op jit(solution)/shard_map/ppermute | solution.py:119
  181.5 10.9 %collective-permute-start.41 = (bf16[4,256,128]{2,1,0:T(8,128)(2,1)S(1)}, bf16[4,256,128]{2,1,0:T(8,128)(2,1)S(1)}, u32[]{:S(2)}, u32[]{:S(2)}) collective-permute-start(bf16[4,256,128]{2,1,0:T(8,128)(2,1)S(1)} %pad_maximum_fusion.27), channel_id=1, source_target_pairs={{0,2},{1,3},{2,0},{3,1},{4,6},{5,7},{6,4},{7,5},{8,10},{9,11},{10,... | collective-permute-start | bytes 786440 | tf_op jit(solution)/shard_map/ppermute | solution.py:119
  186.0 8.1 %collective-permute-start.35 = (bf16[256,256]{1,0:T(8,128)(2,1)S(1)}, bf16[256,256]{1,0:T(8,128)(2,1)S(1)}, u32[]{:S(2)}, u32[]{:S(2)}) collective-permute-start(bf16[256,256]{1,0:T(8,128)(2,1)S(1)} %slice.882), channel_id=1, source_target_pairs={{0,16},{1,17},{2,18},{3,19},{4,20},{5,21},{6,22},{7,23},{8,24},{9,... | collective-permute-start | bytes 393224 | tf_op jit(solution)/shard_map/ppermute | solution.py:119
  194.1 9.6 %collective-permute-start.37 = (bf16[256,256]{1,0:T(8,128)(2,1)S(1)}, bf16[256,256]{1,0:T(8,128)(2,1)S(1)}, u32[]{:S(2)}, u32[]{:S(2)}) collective-permute-start(bf16[256,256]{1,0:T(8,128)(2,1)S(1)} %slice.881), channel_id=1, source_target_pairs={{0,16},{1,17},{2,18},{3,19},{4,20},{5,21},{6,22},{7,23},{8,24},{9,... | collective-permute-start | bytes 393224 | tf_op jit(solution)/shard_map/ppermute | solution.py:119
  (15 other events, 82.0 us)

commit v9 on v8

--- a/solution.py
+++ b/solution.py
@@ -15,7 +15,7 @@
     unit = cols // 16
     counts = [count for first, count in chunks]
     width = unit * sum(counts)
-    step = max(s for s in range(16, 225, 16) if rows % s == 0)
+    step = max(s for s in range(16, 449, 16) if rows % s == 0)
     tiles = rows // step
     spread = cols // 4 // width
     start = chunks[0][0] * unit // width
@@ -132,9 +132,10 @@
 
     flip = (c ^ (z % 2)) != 0
     crossed, tables = [], []
-    theirs, pairs, moved, acts = [], [], [], []
+    theirs, pairs, moved, acts = [], [], [], {}
     jobs, sends, backs = [], [], []
-    nears, fars, halfway, leaving, result = [], [], [], [], []
+    nears, fars, halfway, summed, done_sums = [], [], [], [], []
+    kept, result = [{}, {}], [{}, {}]
 
     def cross(m, *done):
         theirs.append(permute(after(other[m], *done), lambda z, x, y, c: (z, x, 1 - y, c)))
@@ -146,9 +147,9 @@
             [permute(data, lambda z, x, y, c: (2 * ((z // 2) ^ a) + c, x, y, z % 2)) for a, data in enumerate(pair)]
         )
 
-    def to_cores(m, *done):
-        got = after(moved[m], *done)
-        acts.append(got + [permute(data, lambda z, x, y, c: (z, x, y, 1 - c)) for data in got])
+    def to_cores(m, a, *done):
+        got = after(moved[m][a], *done)
+        acts[m, a] = (got, permute(got, lambda z, x, y, c: (z, x, y, 1 - c)))
 
     def gather(q, *done):
         piece = after(pieces[q], *done)
@@ -165,37 +166,42 @@
 
     early = 5
 
-    def multiply(m, q, pieces=1):
-        half = tables[q].shape[1] // 2
-        totals = [jnp.dot(a, tables[q], preferred_element_type=jnp.float32) for a in acts[m]]
-        width = half // pieces
-        for at in range(0, half, width):
-            send = jnp.stack([total[:, half + at : half + at + width].astype(jnp.bfloat16) for total in totals])
-            send = after(send, *sends[-1:], *backs[-2:-1])
-            sends.append(send)
-            backs.append(permute(send, lambda z, x, y, c: (z, x, 1 - y, c)))
-            jobs.append([total[:, at : at + width] for total in totals])
+    def multiply(m, a, *columns):
+        half = tables[0].shape[1] // 2
+        totals = [
+            [jnp.dot(act, tables[q], preferred_element_type=jnp.float32) for q in columns] for act in acts[m, a]
+        ]
+        send = jnp.stack(
+            [jnp.concatenate([v[:, half:].astype(jnp.bfloat16) for v in total], axis=1) for total in totals]
+        )
+        send = after(send, *sends[-1:], *backs[-3:-2])
+        sends.append(send)
+        backs.append(permute(send, lambda z, x, y, c: (z, x, 1 - y, c)))
+        jobs.append((m, a, columns, [jnp.concatenate([v[:, :half] for v in total], axis=1) for total in totals]))
 
     def step_one(j):
-        done = leaving[j - 1 : j] if j <= early else leaving[j - 2 : j - 1]
+        done = summed[j - 1 : j] if j <= early else summed[j - 2 : j - 1]
         back = after(backs[j], *done)
-        totals = [total + b for total, b in zip(jobs[j], back)]
-        count = len(totals) // 2
-        near, far = zip(*[swap_if(flip, own, sibling) for own, sibling in zip(totals[:count], totals[count:])])
-        near, far = [jnp.concatenate(v, axis=0) if count > 1 else v[0] for v in (near, far)]
+        near, far = swap_if(flip, *[total + b for total, b in zip(jobs[j][3], back)])
         nears.append(near)
         fars.append(far.astype(jnp.bfloat16))
         halfway.append(permute(fars[j], lambda z, x, y, c: (z ^ 1, x, y, c)))
 
     def step_two(j):
-        back = after(halfway[j], *sends[j + 3 : j + 4])
-        total = nears[j] + back
-        leaving.append(total[part:].astype(jnp.bfloat16))
-        nears[j] = total[:part]
-        halfway[j] = permute(leaving[j], lambda z, x, y, c: (z ^ 2, x, y, c))
+        m, a, columns, _ = jobs[j]
+        total = nears[j] + after(halfway[j], *sends[j + 3 : j + 4])
+        if a == 1:
+            total = total.astype(jnp.bfloat16)
+            halfway[j] = permute(total, lambda z, x, y, c: (z ^ 2, x, y, c))
+        summed.append(total)
 
     def step_three(j):
-        result.append((nears[j] + halfway[j]).astype(jnp.bfloat16))
+        m, a, columns, _ = jobs[j]
+        width = summed[j].shape[1] // len(columns)
+        for i, q in enumerate(columns):
+            kept[m][q, a] = (halfway[j] if a else summed[j])[:, i * width : (i + 1) * width]
+            if (q, 1 - a) in kept[m]:
+                result[m][q] = (kept[m][q, 0] + kept[m][q, 1]).astype(jnp.bfloat16)
 
     update(CHUNKS[:2], own[0])
     cross(0)
@@ -204,19 +210,23 @@
     gather(1)
     update(CHUNKS[2:])
     to_plane(0, pieces[2])
-    gather(2, crossed[0][-1])
+    gather(2, crossed[1][-1])
     to_tables(0)
     to_tables(1)
-    to_cores(0)
+    to_cores(0, 0, crossed[1][-1])
+    to_cores(0, 1)
     to_plane(1, *moved[0])
-    multiply(0, 0)
-    multiply(0, 1)
+    multiply(0, 0, 0, 1)
+    multiply(0, 1, 0, 1)
     to_tables(2, backs[0], moved[1][0])
-    multiply(0, 2)
-    multiply(0, 3)
-    to_cores(1, backs[2])
-    for q in range(4):
-        multiply(1, q, 1 + q // 3)
+    multiply(0, 1, 2, 3)
+    multiply(0, 0, 2, 3)
+    to_cores(1, 0, backs[-2])
+    to_cores(1, 1, sends[-1])
+    multiply(1, 1, 0, 1)
+    multiply(1, 1, 2, 3)
+    multiply(1, 0, 0, 1)
+    multiply(1, 0, 2, 3)
     count = len(jobs)
     for j in range(count + 2):
         if j <= early and 1 <= j <= count:
@@ -227,7 +237,7 @@
             step_two(j - 1)
         if j >= 2:
             step_three(j - 2)
-    result = [jnp.concatenate(result[:4], axis=1), jnp.concatenate(result[4:], axis=1)]
+    result = [jnp.concatenate([r[q] for q in sorted(r)], axis=1) for r in result]
     decoded = jnp.concatenate(result, axis=0)
     return (*updated, decoded)
 

time: 209 us -> 214 us (1.024)
  waiting for transfers between devices: 96.2 us -> 115 us
  starting transfers between devices: 48 us -> 37.9 us
  Pallas kernels: 25.8 us -> 22 us
    ppermute x44 -> x37, waiting for transfers between devices: 96.2 us -> 115 us  [permute(): return lax.ppermute(value, AXES, pairs)]
    ppermute x44 -> x37, starting transfers between devices: 48 us -> 37.9 us  [permute(): return lax.ppermute(value, AXES, pairs)]
    pallas_call x2, Pallas kernels: 24 us -> 20.2 us  [adam(): pl.pallas_call(kernel, grid_spec=pltpu.PrefetchScalarGridSpec(num_scalar_...]
  transfers between devices with their start and end apart: 44 -> 37, of which waited for: 22 -> 16; matrix products, arithmetic and copies ran while one was open for 16% -> 16% of each run, Pallas kernels for 12% -> 9%
where the time goes in v9:
time: 214 us
  waiting for transfers between devices  115 us (54%)
  starting transfers between devices  37.9 us (18%)
  Pallas kernels  22 us (10%)
  matrix products  20.2 us (9%)
  other arithmetic  8.62 us (4%)
  local copies, waits for them, and re-layouts  8.25 us (4%)
    ppermute x37, waiting for transfers between devices, permute(): return lax.ppermute(value, AXES, pairs)  115 us
    ppermute x37, starting transfers between devices, permute(): return lax.ppermute(value, AXES, pairs)  37.9 us
    pallas_call x2, Pallas kernels, adam(): pl.pallas_call(kernel, grid_spec=pltpu.PrefetchScalarGridSpec(num_scalar_...  20.2 us
    dot_general x32, matrix products, multiply(): jnp.dot(act, tables[q], preferred_element_type=jnp.float32)  20.2 us
  transfers between devices with their start and end apart: 37, of which 16 were waited for; matrix products, arithmetic and copies ran while one was open for 16% of the time, Pallas kernels for 9%

profile of v9, /device:TPU:0, one launch (start us, length us, event | category | flops | bytes accessed | tf_op | source)
XLA Modules:
  0.0 214.1 jit_solution(2519516065378193924)
XLA Ops:
  0.7 2.0 copy-done
  2.8 1.8 pack.1
  4.6 3.0 %collective-permute-start = (bf16[256,1792]{1,0:T(8,128)(2,1)}, bf16[256,1792]{1,0:T(8,128)(2,1)}, u32[]{:S(2)}, u32[]{:S(2)}) collective-permute-start(bf16[256,1792]{1,0:T(8,128)(2,1)} %get-tuple-element.55), channel_id=1, source_target_pairs={{0,2},{1,3},{2,0},{3,1},{4,6},{5,7},{6,4},{7,5},{8,10},{9,11},{10,... | collective-permute-start | bytes 2752520 | tf_op jit(solution)/shard_map/ppermute | solution.py:119
  7.5 10.0 %adam.2 = (f32[448,4096]{1,0:T(8,128)}, f32[448,4096]{1,0:T(8,128)}, f32[448,4096]{1,0:T(8,128)}, bf16[1,448,1024]{2,1,0:T(8,128)(2,1)}, bf16[1,448,1024]{2,1,0:T(8,128)(2,1)}) custom-call(s32[3]{0:T(128)} %copy-done.1, f32[448,4096]{1,0:T(8,128)} %master_ref.3, f32[448,4096]{1,0:T(8,128)} %one_ref.3, f32[448,4096]{1,0:T(8,128)} %two_ref.3, ...), custom_call_target="tpu_custom_call" | custom-call | flops 11010048 | bytes 25690112 | tf_op jit(solution)/shard_map/adam/pallas_call | solution.py:48
  19.6 10.2 %adam.3 = (f32[448,4096]{1,0:T(8,128)}, f32[448,4096]{1,0:T(8,128)}, f32[448,4096]{1,0:T(8,128)}, bf16[2,448,1024]{2,1,0:T(8,128)(2,1)}) custom-call(s32[3]{0:T(128)} %copy-done.1, f32[448,4096]{1,0:T(8,128)} %master_ref.3, f32[448,4096]{1,0:T(8,128)} %one_ref.3, f32[448,4096]{1,0:T(8,128)} %two_ref.3, ...), custom_call_target="tpu_custom_call", output_to_operand_aliasing={{0}: (5, {}), {1}: (6, {}), {2}: (7, {})} | custom-call | flops 11010048 | bytes 25690112 | tf_op jit(solution)/shard_map/adam/pallas_call | solution.py:48
  29.8 1.6 fusion.10
  33.5 3.1 %collective-permute-start.11 = (bf16[256,1792]{1,0:T(8,128)(2,1)S(1)}, bf16[256,1792]{1,0:T(8,128)(2,1)S(1)}, u32[]{:S(2)}, u32[]{:S(2)}) collective-permute-start(bf16[256,1792]{1,0:T(8,128)(2,1)S(1)} %get-tuple-element.64), channel_id=1, source_target_pairs={{0,16},{1,24},{2,18},{3,26},{4,20},{5,28},{6,22},{7,30},{8,17},{9,... | collective-permute-start | bytes 2752520 | tf_op jit(solution)/shard_map/ppermute | solution.py:119
  36.7 4.5 %collective-permute-done.2 = bf16[1,448,1024]{2,1,0:T(8,128)(2,1)} collective-permute-done((bf16[1,448,1024]{2,1,0:T(8,128)(2,1)}, bf16[1,448,1024]{2,1,0:T(8,128)(2,1)}, u32[]{:S(2)}, u32[]{:S(2)}) %collective-permute-start.2) | collective-permute-done | bytes 917536 | tf_op jit(solution)/shard_map/ppermute | solution.py:119
  41.1 1.5 collective-permute-start.9
  43.9 16.9 %collective-permute-done.4 = bf16[1,448,1024]{2,1,0:T(8,128)(2,1)} collective-permute-done((bf16[1,448,1024]{2,1,0:T(8,128)(2,1)}, bf16[1,448,1024]{2,1,0:T(8,128)(2,1)}, u32[]{:S(2)}, u32[]{:S(2)}) %collective-permute-start.4) | collective-permute-done | bytes 917536 | tf_op jit(solution)/shard_map/ppermute | solution.py:119
  64.0 12.5 %collective-permute-done.11 = bf16[256,1792]{1,0:T(8,128)(2,1)S(1)} collective-permute-done((bf16[256,1792]{1,0:T(8,128)(2,1)S(1)}, bf16[256,1792]{1,0:T(8,128)(2,1)S(1)}, u32[]{:S(2)}, u32[]{:S(2)}) %collective-permute-start.11) | collective-permute-done | bytes 917536 | tf_op jit(solution)/shard_map/ppermute | solution.py:119
  77.4 2.0 collective-permute-start.3
  83.8 1.6 collective-permute-start.7
  88.2 10.4 %collective-permute-done.9 = bf16[2,448,1024]{2,1,0:T(8,128)(2,1)S(1)} collective-permute-done((bf16[2,448,1024]{2,1,0:T(8,128)(2,1)S(1)}, bf16[2,448,1024]{2,1,0:T(8,128)(2,1)S(1)}, u32[]{:S(2)}, u32[]{:S(2)}) %collective-permute-start.9) | collective-permute-done | bytes 1835040 | tf_op jit(solution)/shard_map/ppermute | solution.py:119
  106.3 1.5 collective-permute-start.22
  110.6 17.8 %collective-permute-done.18 = bf16[256,1792]{1,0:T(8,128)(2,1)S(1)} collective-permute-done((bf16[256,1792]{1,0:T(8,128)(2,1)S(1)}, bf16[256,1792]{1,0:T(8,128)(2,1)S(1)}, u32[]{:S(2)}, u32[]{:S(2)}) %collective-permute-start.18) | collective-permute-done | bytes 917536 | tf_op jit(solution)/shard_map/ppermute | solution.py:119
  137.2 1.6 collective-permute-start.28
  138.8 2.0 collective-permute-done.17
  142.8 2.3 %collective-permute-start.20 = (bf16[256,512]{1,0:T(8,128)(2,1)S(1)}, bf16[256,512]{1,0:T(8,128)(2,1)S(1)}, u32[]{:S(2)}, u32[]{:S(2)}) collective-permute-start(bf16[256,512]{1,0:T(8,128)(2,1)S(1)} %add_convert_fusion.3), channel_id=1, source_target_pairs={{0,16},{1,17},{2,18},{3,19},{4,20},{5,21},{6,22},{7,23},{8,24},{9,... | collective-permute-start | bytes 786440 | tf_op jit(solution)/shard_map/ppermute | solution.py:119
  145.2 7.5 %collective-permute-done.23 = bf16[256,512]{1,0:T(8,128)(2,1)S(1)} collective-permute-done((bf16[256,512]{1,0:T(8,128)(2,1)S(1)}, bf16[256,512]{1,0:T(8,128)(2,1)S(1)}, u32[]{:S(2)}, u32[]{:S(2)}) %collective-permute-start.23) | collective-permute-done | bytes 262176 | tf_op jit(solution)/shard_map/ppermute | solution.py:119
  154.0 10.3 %collective-permute-done.20 = bf16[256,512]{1,0:T(8,128)(2,1)S(1)} collective-permute-done((bf16[256,512]{1,0:T(8,128)(2,1)S(1)}, bf16[256,512]{1,0:T(8,128)(2,1)S(1)}, u32[]{:S(2)}, u32[]{:S(2)}) %collective-permute-start.20) | collective-permute-done | bytes 262176 | tf_op jit(solution)/shard_map/ppermute | solution.py:119
  166.5 7.5 %collective-permute-done.24 = bf16[256,512]{1,0:T(8,128)(2,1)S(1)} collective-permute-done((bf16[256,512]{1,0:T(8,128)(2,1)S(1)}, bf16[256,512]{1,0:T(8,128)(2,1)S(1)}, u32[]{:S(2)}, u32[]{:S(2)}) %collective-permute-start.24) | collective-permute-done | bytes 262176 | tf_op jit(solution)/shard_map/ppermute | solution.py:119
  175.1 1.6 collective-permute-start.27
  177.4 5.2 %collective-permute-done.29 = bf16[256,512]{1,0:T(8,128)(2,1)S(1)} collective-permute-done((bf16[256,512]{1,0:T(8,128)(2,1)S(1)}, bf16[256,512]{1,0:T(8,128)(2,1)S(1)}, u32[]{:S(2)}, u32[]{:S(2)}) %collective-permute-start.29) | collective-permute-done | bytes 262176 | tf_op jit(solution)/shard_map/ppermute | solution.py:119
  183.3 2.8 %collective-permute-start.31 = (bf16[256,512]{1,0:T(8,128)(2,1)S(1)}, bf16[256,512]{1,0:T(8,128)(2,1)S(1)}, u32[]{:S(2)}, u32[]{:S(2)}) collective-permute-start(bf16[256,512]{1,0:T(8,128)(2,1)S(1)} %add_convert_fusion.1), channel_id=1, source_target_pairs={{0,16},{1,17},{2,18},{3,19},{4,20},{5,21},{6,22},{7,23},{8,24},{9,... | collective-permute-start | bytes 786440 | tf_op jit(solution)/shard_map/ppermute | solution.py:119
  186.0 4.0 %collective-permute-done.27 = bf16[2,256,512]{2,1,0:T(8,128)(2,1)S(1)} collective-permute-done((bf16[2,256,512]{2,1,0:T(8,128)(2,1)S(1)}, bf16[2,256,512]{2,1,0:T(8,128)(2,1)S(1)}, u32[]{:S(2)}, u32[]{:S(2)}) %collective-permute-start.27) | collective-permute-done | bytes 524320 | tf_op jit(solution)/shard_map/ppermute | solution.py:119
  190.1 2.1 collective-permute-start.30
  192.2 5.2 %collective-permute-done.34 = bf16[256,512]{1,0:T(8,128)(2,1)S(1)} collective-permute-done((bf16[256,512]{1,0:T(8,128)(2,1)S(1)}, bf16[256,512]{1,0:T(8,128)(2,1)S(1)}, u32[]{:S(2)}, u32[]{:S(2)}) %collective-permute-start.34) | collective-permute-done | bytes 262176 | tf_op jit(solution)/shard_map/ppermute | solution.py:119
  197.9 2.4 %collective-permute-done.32 = bf16[2,256,512]{2,1,0:T(8,128)(2,1)S(1)} collective-permute-done((bf16[2,256,512]{2,1,0:T(8,128)(2,1)S(1)}, bf16[2,256,512]{2,1,0:T(8,128)(2,1)S(1)}, u32[]{:S(2)}, u32[]{:S(2)}) %collective-permute-start.32) | collective-permute-done | bytes 524320 | tf_op jit(solution)/shard_map/ppermute | solution.py:119
  200.4 3.1 %collective-permute-start.35 = (bf16[256,512]{1,0:T(8,128)(2,1)S(1)}, bf16[256,512]{1,0:T(8,128)(2,1)S(1)}, u32[]{:S(2)}, u32[]{:S(2)}) collective-permute-start(bf16[256,512]{1,0:T(8,128)(2,1)S(1)} %select_convert_fusion), channel_id=1, source_target_pairs={{0,8},{1,9},{2,10},{3,11},{4,12},{5,13},{6,14},{7,15},{8,0},{9,1},... | collective-permute-start | bytes 786440 | tf_op jit(solution)/shard_map/ppermute | solution.py:119
  203.6 3.9 %collective-permute-done.30 = bf16[256,512]{1,0:T(8,128)(2,1)S(1)} collective-permute-done((bf16[256,512]{1,0:T(8,128)(2,1)S(1)}, bf16[256,512]{1,0:T(8,128)(2,1)S(1)}, u32[]{:S(2)}, u32[]{:S(2)}) %collective-permute-start.30) | collective-permute-done | bytes 262176 | tf_op jit(solution)/shard_map/ppermute | solution.py:119
  207.7 5.1 %collective-permute-done.35 = bf16[256,512]{1,0:T(8,128)(2,1)S(1)} collective-permute-done((bf16[256,512]{1,0:T(8,128)(2,1)S(1)}, bf16[256,512]{1,0:T(8,128)(2,1)S(1)}, u32[]{:S(2)}, u32[]{:S(2)}) %collective-permute-start.35) | collective-permute-done | bytes 262176 | tf_op jit(solution)/shard_map/ppermute | solution.py:119
  (216 shorter events, 45.3 us)
Async XLA Ops:
  4.6 26.8 %collective-permute-start = (bf16[256,1792]{1,0:T(8,128)(2,1)}, bf16[256,1792]{1,0:T(8,128)(2,1)}, u32[]{:S(2)}, u32[]{:S(2)}) collective-permute-start(bf16[256,1792]{1,0:T(8,128)(2,1)} %get-tuple-element.55), channel_id=1, source_target_pairs={{0,2},{1,3},{2,0},{3,1},{4,6},{5,7},{6,4},{7,5},{8,10},{9,11},{10,... | collective-permute-start | bytes 2752520 | tf_op jit(solution)/shard_map/ppermute | solution.py:119
  17.5 23.6 %collective-permute-start.2 = (bf16[1,448,1024]{2,1,0:T(8,128)(2,1)}, bf16[1,448,1024]{2,1,0:T(8,128)(2,1)}, u32[]{:S(2)}, u32[]{:S(2)}) collective-permute-start(bf16[1,448,1024]{2,1,0:T(8,128)(2,1)} %get-tuple-element.58), channel_id=1, source_target_pairs={{0,4},{1,5},{2,6},{3,7},{4,0},{5,1},{6,2},{7,3},{8,12},{9,13},{10,... | collective-permute-start | bytes 2752520 | tf_op jit(solution)/shard_map/ppermute | solution.py:119
  19.0 43.1 %collective-permute-start.10 = (bf16[256,1792]{1,0:T(8,128)(2,1)S(1)}, bf16[256,1792]{1,0:T(8,128)(2,1)}, u32[]{:S(2)}, u32[]{:S(2)}) collective-permute-start(bf16[256,1792]{1,0:T(8,128)(2,1)S(1)} %get-tuple-element.62), channel_id=1, source_target_pairs={{0,2},{1,3},{2,0},{3,1},{4,6},{5,7},{6,4},{7,5},{8,10},{9,11},{10,... | collective-permute-start | bytes 2752520 | tf_op jit(solution)/shard_map/ppermute | solution.py:119
  19.5 41.3 %collective-permute-start.4 = (bf16[1,448,1024]{2,1,0:T(8,128)(2,1)}, bf16[1,448,1024]{2,1,0:T(8,128)(2,1)}, u32[]{:S(2)}, u32[]{:S(2)}) collective-permute-start(bf16[1,448,1024]{2,1,0:T(8,128)(2,1)} %get-tuple-element.60), channel_id=1, source_target_pairs={{0,4},{1,5},{2,6},{3,7},{4,0},{5,1},{6,2},{7,3},{8,12},{9,13},{10,... | collective-permute-start | bytes 2752520 | tf_op jit(solution)/shard_map/ppermute | solution.py:119
  32.8 31.2 %collective-permute-start.1 = (bf16[256,1792]{1,0:T(8,128)(2,1)S(1)}, bf16[256,1792]{1,0:T(8,128)(2,1)S(1)}, u32[]{:S(2)}, u32[]{:S(2)}) collective-permute-start(bf16[256,1792]{1,0:T(8,128)(2,1)S(1)} %get-tuple-element.57), channel_id=1, source_target_pairs={{0,0},{1,8},{2,2},{3,10},{4,4},{5,12},{6,6},{7,14},{8,1},{9,9},{10... | collective-permute-start | bytes 2752520 | tf_op jit(solution)/shard_map/ppermute | solution.py:119
  33.5 43.0 %collective-permute-start.11 = (bf16[256,1792]{1,0:T(8,128)(2,1)S(1)}, bf16[256,1792]{1,0:T(8,128)(2,1)S(1)}, u32[]{:S(2)}, u32[]{:S(2)}) collective-permute-start(bf16[256,1792]{1,0:T(8,128)(2,1)S(1)} %get-tuple-element.64), channel_id=1, source_target_pairs={{0,16},{1,24},{2,18},{3,26},{4,20},{5,28},{6,22},{7,30},{8,17},{9,... | collective-permute-start | bytes 2752520 | tf_op jit(solution)/shard_map/ppermute | solution.py:119
  41.1 57.4 %collective-permute-start.9 = (bf16[2,448,1024]{2,1,0:T(8,128)(2,1)S(1)}, bf16[2,448,1024]{2,1,0:T(8,128)(2,1)S(1)}, u32[]{:S(2)}, u32[]{:S(2)}) collective-permute-start(bf16[2,448,1024]{2,1,0:T(8,128)(2,1)S(1)} %copy-done.2), channel_id=1, source_target_pairs={{0,4},{1,5},{2,6},{3,7},{4,0},{5,1},{6,2},{7,3},{8,12},{9,13},{10,... | collective-permute-start | bytes 5505032 | tf_op jit(solution)/shard_map/ppermute | solution.py:119
  60.8 18.6 %collective-permute-start.6 = (bf16[2,448,512]{2,1,0:T(8,128)(2,1)S(1)}, bf16[2,448,512]{2,1,0:T(8,128)(2,1)S(1)}, u32[]{:S(2)}, u32[]{:S(2)}) collective-permute-start(bf16[2,448,512]{2,1,0:T(8,128)(2,1)S(1)} %pad_maximum_fusion.6), channel_id=1, source_target_pairs={{0,1},{1,0},{2,3},{3,2},{4,5},{5,4},{6,7},{7,6},{8,9},{9,8},{10,11... | collective-permute-start | bytes 2752520 | tf_op jit(solution)/shard_map/ppermute | solution.py:119
  62.1 17.8 %collective-permute-start.5 = (bf16[2,448,512]{2,1,0:T(8,128)(2,1)S(1)}, bf16[2,448,512]{2,1,0:T(8,128)(2,1)S(1)}, u32[]{:S(2)}, u32[]{:S(2)}) collective-permute-start(bf16[2,448,512]{2,1,0:T(8,128)(2,1)S(1)} %pad_maximum_fusion.4), channel_id=1, source_target_pairs={{0,1},{1,0},{2,3},{3,2},{4,5},{5,4},{6,7},{7,6},{8,9},{9,8},{10,11... | collective-permute-start | bytes 2752520 | tf_op jit(solution)/shard_map/ppermute | solution.py:119
  76.5 11.6 %collective-permute-start.12 = (bf16[256,1792]{1,0:T(8,128)(2,1)S(1)}, bf16[256,1792]{1,0:T(8,128)(2,1)S(1)}, u32[]{:S(2)}, u32[]{:S(2)}) collective-permute-start(bf16[256,1792]{1,0:T(8,128)(2,1)S(1)} %get-tuple-element.65), channel_id=1, source_target_pairs={{0,0},{1,8},{2,2},{3,10},{4,4},{5,12},{6,6},{7,14},{8,1},{9,9},{10... | collective-permute-start | bytes 2752520 | tf_op jit(solution)/shard_map/ppermute | solution.py:119
  83.8 14.7 %collective-permute-start.7 = (bf16[2,256,512]{2,1,0:T(8,128)(2,1)S(1)}, bf16[2,256,512]{2,1,0:T(8,128)(2,1)S(1)}, u32[]{:S(2)}, u32[]{:S(2)}) collective-permute-start(bf16[2,256,512]{2,1,0:T(8,128)(2,1)S(1)} %pad_maximum_fusion.12), channel_id=1, source_target_pairs={{0,2},{1,3},{2,0},{3,1},{4,6},{5,7},{6,4},{7,5},{8,10},{9,11},{10,... | collective-permute-start | bytes 1572872 | tf_op jit(solution)/shard_map/ppermute | solution.py:119
  86.2 42.2 %collective-permute-start.18 = (bf16[256,1792]{1,0:T(8,128)(2,1)S(1)}, bf16[256,1792]{1,0:T(8,128)(2,1)S(1)}, u32[]{:S(2)}, u32[]{:S(2)}) collective-permute-start(bf16[256,1792]{1,0:T(8,128)(2,1)S(1)} %get-tuple-element.73), channel_id=1, source_target_pairs={{0,16},{1,24},{2,18},{3,26},{4,20},{5,28},{6,22},{7,30},{8,17},{9,... | collective-permute-start | bytes 2752520 | tf_op jit(solution)/shard_map/ppermute | solution.py:119
  99.8 32.3 %collective-permute-start.16 = (bf16[2,256,512]{2,1,0:T(8,128)(2,1)S(1)}, bf16[2,256,512]{2,1,0:T(8,128)(2,1)S(1)}, u32[]{:S(2)}, u32[]{:S(2)}) collective-permute-start(bf16[2,256,512]{2,1,0:T(8,128)(2,1)S(1)} %pad_maximum_fusion.15), channel_id=1, source_target_pairs={{0,2},{1,3},{2,0},{3,1},{4,6},{5,7},{6,4},{7,5},{8,10},{9,11},{10,... | collective-permute-start | bytes 1572872 | tf_op jit(solution)/shard_map/ppermute | solution.py:119
  101.6 29.3 %collective-permute-start.8 = (bf16[256,512]{1,0:T(8,128)(2,1)S(1)}, bf16[256,512]{1,0:T(8,128)(2,1)S(1)}, u32[]{:S(2)}, u32[]{:S(2)}) collective-permute-start(bf16[256,512]{1,0:T(8,128)(2,1)S(1)} %select_convert_fusion.7), channel_id=1, source_target_pairs={{0,8},{1,9},{2,10},{3,11},{4,12},{5,13},{6,14},{7,15},{8,0},{9,1},... | collective-permute-start | bytes 786440 | tf_op jit(solution)/shard_map/ppermute | solution.py:119
  106.3 26.1 %collective-permute-start.22 = (bf16[2,256,512]{2,1,0:T(8,128)(2,1)S(1)}, bf16[2,256,512]{2,1,0:T(8,128)(2,1)S(1)}, u32[]{:S(2)}, u32[]{:S(2)}) collective-permute-start(bf16[2,256,512]{2,1,0:T(8,128)(2,1)S(1)} %pad_maximum_fusion.14), channel_id=1, source_target_pairs={{0,2},{1,3},{2,0},{3,1},{4,6},{5,7},{6,4},{7,5},{8,10},{9,11},{10,... | collective-permute-start | bytes 1572872 | tf_op jit(solution)/shard_map/ppermute | solution.py:119
  129.7 23.7 %collective-permute-start.21 = (bf16[2,256,512]{2,1,0:T(8,128)(2,1)S(1)}, bf16[2,256,512]{2,1,0:T(8,128)(2,1)S(1)}, u32[]{:S(2)}, u32[]{:S(2)}) collective-permute-start(bf16[2,256,512]{2,1,0:T(8,128)(2,1)S(1)} %pad_maximum_fusion.13), channel_id=1, source_target_pairs={{0,2},{1,3},{2,0},{3,1},{4,6},{5,7},{6,4},{7,5},{8,10},{9,11},{10,... | collective-permute-start | bytes 1572872 | tf_op jit(solution)/shard_map/ppermute | solution.py:119
  132.3 8.5 %collective-permute-start.17 = (bf16[256,512]{1,0:T(8,128)(2,1)S(1)}, bf16[256,512]{1,0:T(8,128)(2,1)S(1)}, u32[]{:S(2)}, u32[]{:S(2)}) collective-permute-start(bf16[256,512]{1,0:T(8,128)(2,1)S(1)} %select_convert_fusion.6), channel_id=1, source_target_pairs={{0,8},{1,9},{2,10},{3,11},{4,12},{5,13},{6,14},{7,15},{8,0},{9,1},... | collective-permute-start | bytes 786440 | tf_op jit(solution)/shard_map/ppermute | solution.py:119
  133.7 30.7 %collective-permute-start.25 = (bf16[256,1792]{1,0:T(8,128)(2,1)S(1)}, bf16[256,1792]{1,0:T(8,128)(2,1)S(1)}, u32[]{:S(2)}, u32[]{:S(2)}) collective-permute-start(bf16[256,1792]{1,0:T(8,128)(2,1)S(1)} %collective-permute-done.12), channel_id=1, source_target_pairs={{0,1},{1,0},{2,3},{3,2},{4,5},{5,4},{6,7},{7,6},{8,9},{9,8},{10,11... | collective-permute-start | bytes 2752520 | tf_op jit(solution)/shard_map/ppermute | solution.py:119
  137.2 37.0 %collective-permute-start.28 = (bf16[2,256,512]{2,1,0:T(8,128)(2,1)S(1)}, bf16[2,256,512]{2,1,0:T(8,128)(2,1)S(1)}, u32[]{:S(2)}, u32[]{:S(2)}) collective-permute-start(bf16[2,256,512]{2,1,0:T(8,128)(2,1)S(1)} %pad_maximum_fusion.16), channel_id=1, source_target_pairs={{0,2},{1,3},{2,0},{3,1},{4,6},{5,7},{6,4},{7,5},{8,10},{9,11},{10,... | collective-permute-start | bytes 1572872 | tf_op jit(solution)/shard_map/ppermute | solution.py:119
  141.1 11.6 %collective-permute-start.23 = (bf16[256,512]{1,0:T(8,128)(2,1)S(1)}, bf16[256,512]{1,0:T(8,128)(2,1)S(1)}, u32[]{:S(2)}, u32[]{:S(2)}) collective-permute-start(bf16[256,512]{1,0:T(8,128)(2,1)S(1)} %select_convert_fusion.5), channel_id=1, source_target_pairs={{0,8},{1,9},{2,10},{3,11},{4,12},{5,13},{6,14},{7,15},{8,0},{9,1},... | collective-permute-start | bytes 786440 | tf_op jit(solution)/shard_map/ppermute | solution.py:119
  142.8 21.5 %collective-permute-start.20 = (bf16[256,512]{1,0:T(8,128)(2,1)S(1)}, bf16[256,512]{1,0:T(8,128)(2,1)S(1)}, u32[]{:S(2)}, u32[]{:S(2)}) collective-permute-start(bf16[256,512]{1,0:T(8,128)(2,1)S(1)} %add_convert_fusion.3), channel_id=1, source_target_pairs={{0,16},{1,17},{2,18},{3,19},{4,20},{5,21},{6,22},{7,23},{8,24},{9,... | collective-permute-start | bytes 786440 | tf_op jit(solution)/shard_map/ppermute | solution.py:119
  152.7 30.0 %collective-permute-start.33 = (bf16[2,256,512]{2,1,0:T(8,128)(2,1)S(1)}, bf16[2,256,512]{2,1,0:T(8,128)(2,1)S(1)}, u32[]{:S(2)}, u32[]{:S(2)}) collective-permute-start(bf16[2,256,512]{2,1,0:T(8,128)(2,1)S(1)} %pad_maximum_fusion.17), channel_id=1, source_target_pairs={{0,2},{1,3},{2,0},{3,1},{4,6},{5,7},{6,4},{7,5},{8,10},{9,11},{10,... | collective-permute-start | bytes 1572872 | tf_op jit(solution)/shard_map/ppermute | solution.py:119
  153.4 29.8 %collective-permute-start.26 = (bf16[256,512]{1,0:T(8,128)(2,1)S(1)}, bf16[256,512]{1,0:T(8,128)(2,1)S(1)}, u32[]{:S(2)}, u32[]{:S(2)}) collective-permute-start(bf16[256,512]{1,0:T(8,128)(2,1)S(1)} %add_convert_fusion.2), channel_id=1, source_target_pairs={{0,16},{1,17},{2,18},{3,19},{4,20},{5,21},{6,22},{7,23},{8,24},{9,... | collective-permute-start | bytes 786440 | tf_op jit(solution)/shard_map/ppermute | solution.py:119
  164.3 9.7 %collective-permute-start.24 = (bf16[256,512]{1,0:T(8,128)(2,1)S(1)}, bf16[256,512]{1,0:T(8,128)(2,1)S(1)}, u32[]{:S(2)}, u32[]{:S(2)}) collective-permute-start(bf16[256,512]{1,0:T(8,128)(2,1)S(1)} %select_convert_fusion.4), channel_id=1, source_target_pairs={{0,8},{1,9},{2,10},{3,11},{4,12},{5,13},{6,14},{7,15},{8,0},{9,1},... | collective-permute-start | bytes 786440 | tf_op jit(solution)/shard_map/ppermute | solution.py:119
  174.3 8.3 %collective-permute-start.29 = (bf16[256,512]{1,0:T(8,128)(2,1)S(1)}, bf16[256,512]{1,0:T(8,128)(2,1)S(1)}, u32[]{:S(2)}, u32[]{:S(2)}) collective-permute-start(bf16[256,512]{1,0:T(8,128)(2,1)S(1)} %select_convert_fusion.3), channel_id=1, source_target_pairs={{0,8},{1,9},{2,10},{3,11},{4,12},{5,13},{6,14},{7,15},{8,0},{9,1},... | collective-permute-start | bytes 786440 | tf_op jit(solution)/shard_map/ppermute | solution.py:119
  175.1 14.8 %collective-permute-start.27 = (bf16[2,256,512]{2,1,0:T(8,128)(2,1)S(1)}, bf16[2,256,512]{2,1,0:T(8,128)(2,1)S(1)}, u32[]{:S(2)}, u32[]{:S(2)}) collective-permute-start(bf16[2,256,512]{2,1,0:T(8,128)(2,1)S(1)} %pad_maximum_fusion.18), channel_id=1, source_target_pairs={{0,2},{1,3},{2,0},{3,1},{4,6},{5,7},{6,4},{7,5},{8,10},{9,11},{10,... | collective-permute-start | bytes 1572872 | tf_op jit(solution)/shard_map/ppermute | solution.py:119
  176.8 23.5 %collective-permute-start.32 = (bf16[2,256,512]{2,1,0:T(8,128)(2,1)S(1)}, bf16[2,256,512]{2,1,0:T(8,128)(2,1)S(1)}, u32[]{:S(2)}, u32[]{:S(2)}) collective-permute-start(bf16[2,256,512]{2,1,0:T(8,128)(2,1)S(1)} %pad_maximum_fusion.19), channel_id=1, source_target_pairs={{0,2},{1,3},{2,0},{3,1},{4,6},{5,7},{6,4},{7,5},{8,10},{9,11},{10,... | collective-permute-start | bytes 1572872 | tf_op jit(solution)/shard_map/ppermute | solution.py:119
  182.8 14.6 %collective-permute-start.34 = (bf16[256,512]{1,0:T(8,128)(2,1)S(1)}, bf16[256,512]{1,0:T(8,128)(2,1)S(1)}, u32[]{:S(2)}, u32[]{:S(2)}) collective-permute-start(bf16[256,512]{1,0:T(8,128)(2,1)S(1)} %select_convert_fusion.1), channel_id=1, source_target_pairs={{0,8},{1,9},{2,10},{3,11},{4,12},{5,13},{6,14},{7,15},{8,0},{9,1},... | collective-permute-start | bytes 786440 | tf_op jit(solution)/shard_map/ppermute | solution.py:119
  183.3 24.3 %collective-permute-start.31 = (bf16[256,512]{1,0:T(8,128)(2,1)S(1)}, bf16[256,512]{1,0:T(8,128)(2,1)S(1)}, u32[]{:S(2)}, u32[]{:S(2)}) collective-permute-start(bf16[256,512]{1,0:T(8,128)(2,1)S(1)} %add_convert_fusion.1), channel_id=1, source_target_pairs={{0,16},{1,17},{2,18},{3,19},{4,20},{5,21},{6,22},{7,23},{8,24},{9,... | collective-permute-start | bytes 786440 | tf_op jit(solution)/shard_map/ppermute | solution.py:119
  190.1 17.3 %collective-permute-start.30 = (bf16[256,512]{1,0:T(8,128)(2,1)S(1)}, bf16[256,512]{1,0:T(8,128)(2,1)S(1)}, u32[]{:S(2)}, u32[]{:S(2)}) collective-permute-start(bf16[256,512]{1,0:T(8,128)(2,1)S(1)} %select_convert_fusion.2), channel_id=1, source_target_pairs={{0,8},{1,9},{2,10},{3,11},{4,12},{5,13},{6,14},{7,15},{8,0},{9,1},... | collective-permute-start | bytes 786440 | tf_op jit(solution)/shard_map/ppermute | solution.py:119
  197.6 15.3 %collective-permute-start.36 = (bf16[256,512]{1,0:T(8,128)(2,1)S(1)}, bf16[256,512]{1,0:T(8,128)(2,1)S(1)}, u32[]{:S(2)}, u32[]{:S(2)}) collective-permute-start(bf16[256,512]{1,0:T(8,128)(2,1)S(1)} %add_convert_fusion), channel_id=1, source_target_pairs={{0,16},{1,17},{2,18},{3,19},{4,20},{5,21},{6,22},{7,23},{8,24},{9,... | collective-permute-start | bytes 786440 | tf_op jit(solution)/shard_map/ppermute | solution.py:119
  200.4 12.3 %collective-permute-start.35 = (bf16[256,512]{1,0:T(8,128)(2,1)S(1)}, bf16[256,512]{1,0:T(8,128)(2,1)S(1)}, u32[]{:S(2)}, u32[]{:S(2)}) collective-permute-start(bf16[256,512]{1,0:T(8,128)(2,1)S(1)} %select_convert_fusion), channel_id=1, source_target_pairs={{0,8},{1,9},{2,10},{3,11},{4,12},{5,13},{6,14},{7,15},{8,0},{9,1},... | collective-permute-start | bytes 786440 | tf_op jit(solution)/shard_map/ppermute | solution.py:119
  (8 other events, 37.9 us)

commit v10 on v8

--- a/solution.py
+++ b/solution.py
@@ -15,7 +15,7 @@
     unit = cols // 16
     counts = [count for first, count in chunks]
     width = unit * sum(counts)
-    step = max(s for s in range(16, 225, 16) if rows % s == 0)
+    step = max(s for s in range(16, 449, 16) if rows % s == 0)
     tiles = rows // step
     spread = cols // 4 // width
     start = chunks[0][0] * unit // width

time: 209 us -> 204 us (0.976)
  Pallas kernels: 25.8 us -> 22 us
    pallas_call x2, Pallas kernels: 24 us -> 20.2 us  [adam(): pl.pallas_call(kernel, grid_spec=pltpu.PrefetchScalarGridSpec(num_scalar_...]
  transfers between devices with their start and end apart: 44 -> 44, of which waited for: 22 -> 22; matrix products, arithmetic and copies ran while one was open for 16% -> 16% of each run, Pallas kernels for 12% -> 10%
where the time goes in v10:
time: 204 us
  waiting for transfers between devices  96.2 us (47%)
  starting transfers between devices  48 us (24%)
  Pallas kernels  22 us (11%)
  matrix products  20.4 us (10%)
  other arithmetic  8.27 us (4%)
  local copies, waits for them, and re-layouts  7.49 us (4%)
    ppermute x44, waiting for transfers between devices, permute(): return lax.ppermute(value, AXES, pairs)  96.2 us
    ppermute x44, starting transfers between devices, permute(): return lax.ppermute(value, AXES, pairs)  48 us
    dot_general x32, matrix products, multiply(): jnp.dot(a, tables[q], preferred_element_type=jnp.float32)  20.4 us
    pallas_call x2, Pallas kernels, adam(): pl.pallas_call(kernel, grid_spec=pltpu.PrefetchScalarGridSpec(num_scalar_...  20.2 us
    slice x5, local copies, waits for them, and re-layouts, to_tables(): near = jnp.stack([p[k, :, :half] for p in parts])  4.23 us
  transfers between devices with their start and end apart: 44, of which 22 were waited for; matrix products, arithmetic and copies ran while one was open for 16% of the time, Pallas kernels for 10%

profile of v10, /device:TPU:0, one launch (start us, length us, event | category | flops | bytes accessed | tf_op | source)
XLA Modules:
  0.0 204.1 jit_solution(8190472390181254401)
XLA Ops:
  0.7 2.0 copy-done
  2.8 1.8 pack.1
  4.6 3.0 %collective-permute-start = (bf16[256,1792]{1,0:T(8,128)(2,1)}, bf16[256,1792]{1,0:T(8,128)(2,1)}, u32[]{:S(2)}, u32[]{:S(2)}) collective-permute-start(bf16[256,1792]{1,0:T(8,128)(2,1)} %get-tuple-element.57), channel_id=1, source_target_pairs={{0,2},{1,3},{2,0},{3,1},{4,6},{5,7},{6,4},{7,5},{8,10},{9,11},{10,... | collective-permute-start | bytes 2752520 | tf_op jit(solution)/shard_map/ppermute | solution.py:119
  7.5 10.0 %adam.2 = (f32[448,4096]{1,0:T(8,128)}, f32[448,4096]{1,0:T(8,128)}, f32[448,4096]{1,0:T(8,128)}, bf16[1,448,1024]{2,1,0:T(8,128)(2,1)}, bf16[1,448,1024]{2,1,0:T(8,128)(2,1)}) custom-call(s32[3]{0:T(128)} %copy-done.1, f32[448,4096]{1,0:T(8,128)} %master_ref.3, f32[448,4096]{1,0:T(8,128)} %one_ref.3, f32[448,4096]{1,0:T(8,128)} %two_ref.3, ...), custom_call_target="tpu_custom_call" | custom-call | flops 11010048 | bytes 25690112 | tf_op jit(solution)/shard_map/adam/pallas_call | solution.py:48
  19.6 10.2 %adam.3 = (f32[448,4096]{1,0:T(8,128)}, f32[448,4096]{1,0:T(8,128)}, f32[448,4096]{1,0:T(8,128)}, bf16[2,448,1024]{2,1,0:T(8,128)(2,1)}) custom-call(s32[3]{0:T(128)} %copy-done.1, f32[448,4096]{1,0:T(8,128)} %master_ref.3, f32[448,4096]{1,0:T(8,128)} %one_ref.3, f32[448,4096]{1,0:T(8,128)} %two_ref.3, ...), custom_call_target="tpu_custom_call", output_to_operand_aliasing={{0}: (5, {}), {1}: (6, {}), {2}: (7, {})} | custom-call | flops 11010048 | bytes 25690112 | tf_op jit(solution)/shard_map/adam/pallas_call | solution.py:48
  33.5 3.1 %collective-permute-start.5 = (bf16[256,1792]{1,0:T(8,128)(2,1)S(1)}, bf16[256,1792]{1,0:T(8,128)(2,1)S(1)}, u32[]{:S(2)}, u32[]{:S(2)}) collective-permute-start(bf16[256,1792]{1,0:T(8,128)(2,1)S(1)} %get-tuple-element.61), channel_id=1, source_target_pairs={{0,16},{1,24},{2,18},{3,26},{4,20},{5,28},{6,22},{7,30},{8,17},{9,... | collective-permute-start | bytes 2752520 | tf_op jit(solution)/shard_map/ppermute | solution.py:119
  36.7 4.5 %collective-permute-done.3 = bf16[1,448,1024]{2,1,0:T(8,128)(2,1)} collective-permute-done((bf16[1,448,1024]{2,1,0:T(8,128)(2,1)}, bf16[1,448,1024]{2,1,0:T(8,128)(2,1)}, u32[]{:S(2)}, u32[]{:S(2)}) %collective-permute-start.3) | collective-permute-done | bytes 917536 | tf_op jit(solution)/shard_map/ppermute | solution.py:119
  44.0 16.9 %collective-permute-done.14 = bf16[1,448,1024]{2,1,0:T(8,128)(2,1)} collective-permute-done((bf16[1,448,1024]{2,1,0:T(8,128)(2,1)}, bf16[1,448,1024]{2,1,0:T(8,128)(2,1)}, u32[]{:S(2)}, u32[]{:S(2)}) %collective-permute-start.14) | collective-permute-done | bytes 917536 | tf_op jit(solution)/shard_map/ppermute | solution.py:119
  64.0 12.5 %collective-permute-done.5 = bf16[256,1792]{1,0:T(8,128)(2,1)S(1)} collective-permute-done((bf16[256,1792]{1,0:T(8,128)(2,1)S(1)}, bf16[256,1792]{1,0:T(8,128)(2,1)S(1)}, u32[]{:S(2)}, u32[]{:S(2)}) %collective-permute-start.5) | collective-permute-done | bytes 917536 | tf_op jit(solution)/shard_map/ppermute | solution.py:119
  79.0 4.3 %collective-permute-start.6 = (bf16[256,1792]{1,0:T(8,128)(2,1)S(1)}, bf16[256,1792]{1,0:T(8,128)(2,1)S(1)}, u32[]{:S(2)}, u32[]{:S(2)}) collective-permute-start(bf16[256,1792]{1,0:T(8,128)(2,1)S(1)} %collective-permute-done.5), channel_id=1, source_target_pairs={{0,1},{1,0},{2,3},{3,2},{4,5},{5,4},{6,7},{7,6},{8,9},{9,8},{10,11... | collective-permute-start | bytes 2752520 | tf_op jit(solution)/shard_map/ppermute | solution.py:119
  87.5 1.6 collective-permute-start.7
  90.4 8.2 %collective-permute-done.9 = bf16[2,448,1024]{2,1,0:T(8,128)(2,1)S(1)} collective-permute-done((bf16[2,448,1024]{2,1,0:T(8,128)(2,1)S(1)}, bf16[2,448,1024]{2,1,0:T(8,128)(2,1)S(1)}, u32[]{:S(2)}, u32[]{:S(2)}) %collective-permute-start.9) | collective-permute-done | bytes 1835040 | tf_op jit(solution)/shard_map/ppermute | solution.py:119
  98.6 3.2 %collective-permute-done.7 = bf16[4,256,256]{2,1,0:T(8,128)(2,1)S(1)} collective-permute-done((bf16[4,256,256]{2,1,0:T(8,128)(2,1)S(1)}, bf16[4,256,256]{2,1,0:T(8,128)(2,1)S(1)}, u32[]{:S(2)}, u32[]{:S(2)}) %collective-permute-start.7) | collective-permute-done | bytes 524320 | tf_op jit(solution)/shard_map/ppermute | solution.py:119
  102.3 1.6 collective-permute-start.16
  112.6 4.5 %collective-permute-done.16 = bf16[4,256,256]{2,1,0:T(8,128)(2,1)S(1)} collective-permute-done((bf16[4,256,256]{2,1,0:T(8,128)(2,1)S(1)}, bf16[4,256,256]{2,1,0:T(8,128)(2,1)S(1)}, u32[]{:S(2)}, u32[]{:S(2)}) %collective-permute-start.16) | collective-permute-done | bytes 524320 | tf_op jit(solution)/shard_map/ppermute | solution.py:119
  119.0 2.3 %collective-permute-start.18 = (bf16[512,256]{1,0:T(8,128)(2,1)S(1)}, bf16[512,256]{1,0:T(8,128)(2,1)S(1)}, u32[]{:S(2)}, u32[]{:S(2)}) collective-permute-start(bf16[512,256]{1,0:T(8,128)(2,1)S(1)} %pad_maximum_fusion.21), channel_id=1, source_target_pairs={{0,8},{1,9},{2,10},{3,11},{4,12},{5,13},{6,14},{7,15},{8,0},{9,1},... | collective-permute-start | bytes 786440 | tf_op jit(solution)/shard_map/ppermute | solution.py:119
  121.3 5.8 %collective-permute-done.17 = bf16[256,256]{1,0:T(8,128)(2,1)S(1)} collective-permute-done((bf16[256,256]{1,0:T(8,128)(2,1)S(1)}, bf16[256,256]{1,0:T(8,128)(2,1)S(1)}, u32[]{:S(2)}, u32[]{:S(2)}) %collective-permute-start.17) | collective-permute-done | bytes 131104 | tf_op jit(solution)/shard_map/ppermute | solution.py:119
  135.9 1.6 collective-permute-start.28
  137.9 1.9 collective-permute-start.24
  144.5 4.2 %collective-permute-done.24 = bf16[512,256]{1,0:T(8,128)(2,1)S(1)} collective-permute-done((bf16[512,256]{1,0:T(8,128)(2,1)S(1)}, bf16[512,256]{1,0:T(8,128)(2,1)S(1)}, u32[]{:S(2)}, u32[]{:S(2)}) %collective-permute-start.24) | collective-permute-done | bytes 262176 | tf_op jit(solution)/shard_map/ppermute | solution.py:119
  149.2 2.9 %collective-permute-start.26 = (bf16[256,256]{1,0:T(8,128)(2,1)S(1)}, bf16[256,256]{1,0:T(8,128)(2,1)S(1)}, u32[]{:S(2)}, u32[]{:S(2)}) collective-permute-start(bf16[256,256]{1,0:T(8,128)(2,1)S(1)} %slice.885), channel_id=1, source_target_pairs={{0,16},{1,17},{2,18},{3,19},{4,20},{5,21},{6,22},{7,23},{8,24},{9,... | collective-permute-start | bytes 393224 | tf_op jit(solution)/shard_map/ppermute | solution.py:119
  152.1 6.9 %collective-permute-done.27 = bf16[512,256]{1,0:T(8,128)(2,1)S(1)} collective-permute-done((bf16[512,256]{1,0:T(8,128)(2,1)S(1)}, bf16[512,256]{1,0:T(8,128)(2,1)S(1)}, u32[]{:S(2)}, u32[]{:S(2)}) %collective-permute-start.27) | collective-permute-done | bytes 262176 | tf_op jit(solution)/shard_map/ppermute | solution.py:119
  159.7 2.5 %collective-permute-start.30 = (bf16[512,256]{1,0:T(8,128)(2,1)S(1)}, bf16[512,256]{1,0:T(8,128)(2,1)S(1)}, u32[]{:S(2)}, u32[]{:S(2)}) collective-permute-start(bf16[512,256]{1,0:T(8,128)(2,1)S(1)} %pad_maximum_fusion.24), channel_id=1, source_target_pairs={{0,8},{1,9},{2,10},{3,11},{4,12},{5,13},{6,14},{7,15},{8,0},{9,1},... | collective-permute-start | bytes 786440 | tf_op jit(solution)/shard_map/ppermute | solution.py:119
  164.4 2.4 %collective-permute-done.29 = bf16[256,256]{1,0:T(8,128)(2,1)S(1)} collective-permute-done((bf16[256,256]{1,0:T(8,128)(2,1)S(1)}, bf16[256,256]{1,0:T(8,128)(2,1)S(1)}, u32[]{:S(2)}, u32[]{:S(2)}) %collective-permute-start.29) | collective-permute-done | bytes 131104 | tf_op jit(solution)/shard_map/ppermute | solution.py:119
  166.9 3.3 %collective-permute-done.30 = bf16[512,256]{1,0:T(8,128)(2,1)S(1)} collective-permute-done((bf16[512,256]{1,0:T(8,128)(2,1)S(1)}, bf16[512,256]{1,0:T(8,128)(2,1)S(1)}, u32[]{:S(2)}, u32[]{:S(2)}) %collective-permute-start.30) | collective-permute-done | bytes 262176 | tf_op jit(solution)/shard_map/ppermute | solution.py:119
  170.9 1.8 collective-permute-start.33
  172.7 4.6 %collective-permute-done.34 = bf16[4,256,256]{2,1,0:T(8,128)(2,1)S(1)} collective-permute-done((bf16[4,256,256]{2,1,0:T(8,128)(2,1)S(1)}, bf16[4,256,256]{2,1,0:T(8,128)(2,1)S(1)}, u32[]{:S(2)}, u32[]{:S(2)}) %collective-permute-start.34) | collective-permute-done | bytes 524320 | tf_op jit(solution)/shard_map/ppermute | solution.py:119
  178.2 3.8 %collective-permute-done.33 = bf16[512,256]{1,0:T(8,128)(2,1)S(1)} collective-permute-done((bf16[512,256]{1,0:T(8,128)(2,1)S(1)}, bf16[512,256]{1,0:T(8,128)(2,1)S(1)}, u32[]{:S(2)}, u32[]{:S(2)}) %collective-permute-start.33) | collective-permute-done | bytes 262176 | tf_op jit(solution)/shard_map/ppermute | solution.py:119
  183.3 5.1 %collective-permute-done.36 = bf16[512,256]{1,0:T(8,128)(2,1)S(1)} collective-permute-done((bf16[512,256]{1,0:T(8,128)(2,1)S(1)}, bf16[512,256]{1,0:T(8,128)(2,1)S(1)}, u32[]{:S(2)}, u32[]{:S(2)}) %collective-permute-start.36) | collective-permute-done | bytes 262176 | tf_op jit(solution)/shard_map/ppermute | solution.py:119
  192.4 3.5 %collective-permute-done.39 = bf16[512,128]{1,0:T(8,128)(2,1)S(1)} collective-permute-done((bf16[512,128]{1,0:T(8,128)(2,1)S(1)}, bf16[512,128]{1,0:T(8,128)(2,1)S(1)}, u32[]{:S(2)}, u32[]{:S(2)}) %collective-permute-start.39) | collective-permute-done | bytes 131104 | tf_op jit(solution)/shard_map/ppermute | solution.py:119
  197.5 2.3 %collective-permute-start.43 = (bf16[256,128]{1,0:T(8,128)(2,1)S(1)}, bf16[256,128]{1,0:T(8,128)(2,1)S(1)}, u32[]{:S(2)}, u32[]{:S(2)}) collective-permute-start(bf16[256,128]{1,0:T(8,128)(2,1)S(1)} %slice.888), channel_id=1, source_target_pairs={{0,16},{1,17},{2,18},{3,19},{4,20},{5,21},{6,22},{7,23},{8,24},{9,... | collective-permute-start | bytes 196616 | tf_op jit(solution)/shard_map/ppermute | solution.py:119
  199.9 2.5 %collective-permute-done.40 = bf16[256,128]{1,0:T(8,128)(2,1)S(1)} collective-permute-done((bf16[256,128]{1,0:T(8,128)(2,1)S(1)}, bf16[256,128]{1,0:T(8,128)(2,1)S(1)}, u32[]{:S(2)}, u32[]{:S(2)}) %collective-permute-start.40) | collective-permute-done | bytes 65568 | tf_op jit(solution)/shard_map/ppermute | solution.py:119
  (208 shorter events, 57.8 us)
Async XLA Ops:
  4.6 26.8 %collective-permute-start = (bf16[256,1792]{1,0:T(8,128)(2,1)}, bf16[256,1792]{1,0:T(8,128)(2,1)}, u32[]{:S(2)}, u32[]{:S(2)}) collective-permute-start(bf16[256,1792]{1,0:T(8,128)(2,1)} %get-tuple-element.57), channel_id=1, source_target_pairs={{0,2},{1,3},{2,0},{3,1},{4,6},{5,7},{6,4},{7,5},{8,10},{9,11},{10,... | collective-permute-start | bytes 2752520 | tf_op jit(solution)/shard_map/ppermute | solution.py:119
  17.5 23.6 %collective-permute-start.3 = (bf16[1,448,1024]{2,1,0:T(8,128)(2,1)}, bf16[1,448,1024]{2,1,0:T(8,128)(2,1)}, u32[]{:S(2)}, u32[]{:S(2)}) collective-permute-start(bf16[1,448,1024]{2,1,0:T(8,128)(2,1)} %get-tuple-element.60), channel_id=1, source_target_pairs={{0,4},{1,5},{2,6},{3,7},{4,0},{5,1},{6,2},{7,3},{8,12},{9,13},{10,... | collective-permute-start | bytes 2752520 | tf_op jit(solution)/shard_map/ppermute | solution.py:119
  19.0 43.1 %collective-permute-start.10 = (bf16[256,1792]{1,0:T(8,128)(2,1)S(1)}, bf16[256,1792]{1,0:T(8,128)(2,1)}, u32[]{:S(2)}, u32[]{:S(2)}) collective-permute-start(bf16[256,1792]{1,0:T(8,128)(2,1)S(1)} %get-tuple-element.63), channel_id=1, source_target_pairs={{0,2},{1,3},{2,0},{3,1},{4,6},{5,7},{6,4},{7,5},{8,10},{9,11},{10,... | collective-permute-start | bytes 2752520 | tf_op jit(solution)/shard_map/ppermute | solution.py:119
  19.6 41.3 %collective-permute-start.14 = (bf16[1,448,1024]{2,1,0:T(8,128)(2,1)}, bf16[1,448,1024]{2,1,0:T(8,128)(2,1)}, u32[]{:S(2)}, u32[]{:S(2)}) collective-permute-start(bf16[1,448,1024]{2,1,0:T(8,128)(2,1)} %get-tuple-element.68), channel_id=1, source_target_pairs={{0,4},{1,5},{2,6},{3,7},{4,0},{5,1},{6,2},{7,3},{8,12},{9,13},{10,... | collective-permute-start | bytes 2752520 | tf_op jit(solution)/shard_map/ppermute | solution.py:119
  32.8 31.2 %collective-permute-start.1 = (bf16[256,1792]{1,0:T(8,128)(2,1)S(1)}, bf16[256,1792]{1,0:T(8,128)(2,1)S(1)}, u32[]{:S(2)}, u32[]{:S(2)}) collective-permute-start(bf16[256,1792]{1,0:T(8,128)(2,1)S(1)} %get-tuple-element.59), channel_id=1, source_target_pairs={{0,0},{1,8},{2,2},{3,10},{4,4},{5,12},{6,6},{7,14},{8,1},{9,9},{10... | collective-permute-start | bytes 2752520 | tf_op jit(solution)/shard_map/ppermute | solution.py:119
  33.5 43.0 %collective-permute-start.5 = (bf16[256,1792]{1,0:T(8,128)(2,1)S(1)}, bf16[256,1792]{1,0:T(8,128)(2,1)S(1)}, u32[]{:S(2)}, u32[]{:S(2)}) collective-permute-start(bf16[256,1792]{1,0:T(8,128)(2,1)S(1)} %get-tuple-element.61), channel_id=1, source_target_pairs={{0,16},{1,24},{2,18},{3,26},{4,20},{5,28},{6,22},{7,30},{8,17},{9,... | collective-permute-start | bytes 2752520 | tf_op jit(solution)/shard_map/ppermute | solution.py:119
  41.1 57.4 %collective-permute-start.9 = (bf16[2,448,1024]{2,1,0:T(8,128)(2,1)S(1)}, bf16[2,448,1024]{2,1,0:T(8,128)(2,1)S(1)}, u32[]{:S(2)}, u32[]{:S(2)}) collective-permute-start(bf16[2,448,1024]{2,1,0:T(8,128)(2,1)S(1)} %copy-done.2), channel_id=1, source_target_pairs={{0,4},{1,5},{2,6},{3,7},{4,0},{5,1},{6,2},{7,3},{8,12},{9,13},{10,... | collective-permute-start | bytes 5505032 | tf_op jit(solution)/shard_map/ppermute | solution.py:119
  60.8 16.7 %collective-permute-start.4 = (bf16[2,448,512]{2,1,0:T(8,128)(2,1)S(1)}, bf16[2,448,512]{2,1,0:T(8,128)(2,1)S(1)}, u32[]{:S(2)}, u32[]{:S(2)}) collective-permute-start(bf16[2,448,512]{2,1,0:T(8,128)(2,1)S(1)} %pad_maximum_fusion.5), channel_id=1, source_target_pairs={{0,1},{1,0},{2,3},{3,2},{4,5},{5,4},{6,7},{7,6},{8,9},{9,8},{10,11... | collective-permute-start | bytes 2752520 | tf_op jit(solution)/shard_map/ppermute | solution.py:119
  62.1 16.5 %collective-permute-start.15 = (bf16[2,448,512]{2,1,0:T(8,128)(2,1)S(1)}, bf16[2,448,512]{2,1,0:T(8,128)(2,1)S(1)}, u32[]{:S(2)}, u32[]{:S(2)}) collective-permute-start(bf16[2,448,512]{2,1,0:T(8,128)(2,1)S(1)} %pad_maximum_fusion.11), channel_id=1, source_target_pairs={{0,1},{1,0},{2,3},{3,2},{4,5},{5,4},{6,7},{7,6},{8,9},{9,8},{10,11... | collective-permute-start | bytes 2752520 | tf_op jit(solution)/shard_map/ppermute | solution.py:119
  76.5 13.9 %collective-permute-start.11 = (bf16[256,1792]{1,0:T(8,128)(2,1)S(1)}, bf16[256,1792]{1,0:T(8,128)(2,1)S(1)}, u32[]{:S(2)}, u32[]{:S(2)}) collective-permute-start(bf16[256,1792]{1,0:T(8,128)(2,1)S(1)} %get-tuple-element.65), channel_id=1, source_target_pairs={{0,0},{1,8},{2,2},{3,10},{4,4},{5,12},{6,6},{7,14},{8,1},{9,9},{10... | collective-permute-start | bytes 2752520 | tf_op jit(solution)/shard_map/ppermute | solution.py:119
  77.4 49.7 %collective-permute-start.19 = (bf16[256,1792]{1,0:T(8,128)(2,1)S(1)}, bf16[256,1792]{1,0:T(8,128)(2,1)S(1)}, u32[]{:S(2)}, u32[]{:S(2)}) collective-permute-start(bf16[256,1792]{1,0:T(8,128)(2,1)S(1)} %get-tuple-element.74), channel_id=1, source_target_pairs={{0,16},{1,24},{2,18},{3,26},{4,20},{5,28},{6,22},{7,30},{8,17},{9,... | collective-permute-start | bytes 2752520 | tf_op jit(solution)/shard_map/ppermute | solution.py:119
  87.5 14.3 %collective-permute-start.7 = (bf16[4,256,256]{2,1,0:T(8,128)(2,1)S(1)}, bf16[4,256,256]{2,1,0:T(8,128)(2,1)S(1)}, u32[]{:S(2)}, u32[]{:S(2)}) collective-permute-start(bf16[4,256,256]{2,1,0:T(8,128)(2,1)S(1)} %pad_maximum_fusion.13), channel_id=1, source_target_pairs={{0,2},{1,3},{2,0},{3,1},{4,6},{5,7},{6,4},{7,5},{8,10},{9,11},{10,... | collective-permute-start | bytes 1572872 | tf_op jit(solution)/shard_map/ppermute | solution.py:119
  102.3 14.8 %collective-permute-start.16 = (bf16[4,256,256]{2,1,0:T(8,128)(2,1)S(1)}, bf16[4,256,256]{2,1,0:T(8,128)(2,1)S(1)}, u32[]{:S(2)}, u32[]{:S(2)}) collective-permute-start(bf16[4,256,256]{2,1,0:T(8,128)(2,1)S(1)} %pad_maximum_fusion.16), channel_id=1, source_target_pairs={{0,2},{1,3},{2,0},{3,1},{4,6},{5,7},{6,4},{7,5},{8,10},{9,11},{10,... | collective-permute-start | bytes 1572872 | tf_op jit(solution)/shard_map/ppermute | solution.py:119
  104.5 14.2 %collective-permute-start.8 = (bf16[512,256]{1,0:T(8,128)(2,1)S(1)}, bf16[512,256]{1,0:T(8,128)(2,1)S(1)}, u32[]{:S(2)}, u32[]{:S(2)}) collective-permute-start(bf16[512,256]{1,0:T(8,128)(2,1)S(1)} %pad_maximum_fusion.20), channel_id=1, source_target_pairs={{0,8},{1,9},{2,10},{3,11},{4,12},{5,13},{6,14},{7,15},{8,0},{9,1},... | collective-permute-start | bytes 786440 | tf_op jit(solution)/shard_map/ppermute | solution.py:119
  107.9 20.5 %collective-permute-start.20 = (bf16[4,256,256]{2,1,0:T(8,128)(2,1)S(1)}, bf16[4,256,256]{2,1,0:T(8,128)(2,1)S(1)}, u32[]{:S(2)}, u32[]{:S(2)}) collective-permute-start(bf16[4,256,256]{2,1,0:T(8,128)(2,1)S(1)} %pad_maximum_fusion.15), channel_id=1, source_target_pairs={{0,2},{1,3},{2,0},{3,1},{4,6},{5,7},{6,4},{7,5},{8,10},{9,11},{10,... | collective-permute-start | bytes 1572872 | tf_op jit(solution)/shard_map/ppermute | solution.py:119
  117.1 26.7 %collective-permute-start.25 = (bf16[4,256,256]{2,1,0:T(8,128)(2,1)S(1)}, bf16[4,256,256]{2,1,0:T(8,128)(2,1)S(1)}, u32[]{:S(2)}, u32[]{:S(2)}) collective-permute-start(bf16[4,256,256]{2,1,0:T(8,128)(2,1)S(1)} %pad_maximum_fusion.14), channel_id=1, source_target_pairs={{0,2},{1,3},{2,0},{3,1},{4,6},{5,7},{6,4},{7,5},{8,10},{9,11},{10,... | collective-permute-start | bytes 1572872 | tf_op jit(solution)/shard_map/ppermute | solution.py:119
  118.7 8.4 %collective-permute-start.17 = (bf16[256,256]{1,0:T(8,128)(2,1)S(1)}, bf16[256,256]{1,0:T(8,128)(2,1)S(1)}, u32[]{:S(2)}, u32[]{:S(2)}) collective-permute-start(bf16[256,256]{1,0:T(8,128)(2,1)S(1)} %slice.887), channel_id=1, source_target_pairs={{0,16},{1,17},{2,18},{3,19},{4,20},{5,21},{6,22},{7,23},{8,24},{9,... | collective-permute-start | bytes 393224 | tf_op jit(solution)/shard_map/ppermute | solution.py:119
  119.0 18.5 %collective-permute-start.18 = (bf16[512,256]{1,0:T(8,128)(2,1)S(1)}, bf16[512,256]{1,0:T(8,128)(2,1)S(1)}, u32[]{:S(2)}, u32[]{:S(2)}) collective-permute-start(bf16[512,256]{1,0:T(8,128)(2,1)S(1)} %pad_maximum_fusion.21), channel_id=1, source_target_pairs={{0,8},{1,9},{2,10},{3,11},{4,12},{5,13},{6,14},{7,15},{8,0},{9,1},... | collective-permute-start | bytes 786440 | tf_op jit(solution)/shard_map/ppermute | solution.py:119
  135.9 16.2 %collective-permute-start.28 = (bf16[4,256,256]{2,1,0:T(8,128)(2,1)S(1)}, bf16[4,256,256]{2,1,0:T(8,128)(2,1)S(1)}, u32[]{:S(2)}, u32[]{:S(2)}) collective-permute-start(bf16[4,256,256]{2,1,0:T(8,128)(2,1)S(1)} %pad_maximum_fusion.17), channel_id=1, source_target_pairs={{0,2},{1,3},{2,0},{3,1},{4,6},{5,7},{6,4},{7,5},{8,10},{9,11},{10,... | collective-permute-start | bytes 1572872 | tf_op jit(solution)/shard_map/ppermute | solution.py:119
  137.6 11.6 %collective-permute-start.23 = (bf16[256,256]{1,0:T(8,128)(2,1)S(1)}, bf16[256,256]{1,0:T(8,128)(2,1)S(1)}, u32[]{:S(2)}, u32[]{:S(2)}) collective-permute-start(bf16[256,256]{1,0:T(8,128)(2,1)S(1)} %slice.886), channel_id=1, source_target_pairs={{0,16},{1,17},{2,18},{3,19},{4,20},{5,21},{6,22},{7,23},{8,24},{9,... | collective-permute-start | bytes 393224 | tf_op jit(solution)/shard_map/ppermute | solution.py:119
  137.9 10.8 %collective-permute-start.24 = (bf16[512,256]{1,0:T(8,128)(2,1)S(1)}, bf16[512,256]{1,0:T(8,128)(2,1)S(1)}, u32[]{:S(2)}, u32[]{:S(2)}) collective-permute-start(bf16[512,256]{1,0:T(8,128)(2,1)S(1)} %pad_maximum_fusion.22), channel_id=1, source_target_pairs={{0,8},{1,9},{2,10},{3,11},{4,12},{5,13},{6,14},{7,15},{8,0},{9,1},... | collective-permute-start | bytes 786440 | tf_op jit(solution)/shard_map/ppermute | solution.py:119
  143.8 19.1 %collective-permute-start.31 = (bf16[4,256,256]{2,1,0:T(8,128)(2,1)S(1)}, bf16[4,256,256]{2,1,0:T(8,128)(2,1)S(1)}, u32[]{:S(2)}, u32[]{:S(2)}) collective-permute-start(bf16[4,256,256]{2,1,0:T(8,128)(2,1)S(1)} %pad_maximum_fusion.18), channel_id=1, source_target_pairs={{0,2},{1,3},{2,0},{3,1},{4,6},{5,7},{6,4},{7,5},{8,10},{9,11},{10,... | collective-permute-start | bytes 1572872 | tf_op jit(solution)/shard_map/ppermute | solution.py:119
  149.0 10.0 %collective-permute-start.27 = (bf16[512,256]{1,0:T(8,128)(2,1)S(1)}, bf16[512,256]{1,0:T(8,128)(2,1)S(1)}, u32[]{:S(2)}, u32[]{:S(2)}) collective-permute-start(bf16[512,256]{1,0:T(8,128)(2,1)S(1)} %pad_maximum_fusion.23), channel_id=1, source_target_pairs={{0,8},{1,9},{2,10},{3,11},{4,12},{5,13},{6,14},{7,15},{8,0},{9,1},... | collective-permute-start | bytes 786440 | tf_op jit(solution)/shard_map/ppermute | solution.py:119
  149.2 13.1 %collective-permute-start.26 = (bf16[256,256]{1,0:T(8,128)(2,1)S(1)}, bf16[256,256]{1,0:T(8,128)(2,1)S(1)}, u32[]{:S(2)}, u32[]{:S(2)}) collective-permute-start(bf16[256,256]{1,0:T(8,128)(2,1)S(1)} %slice.885), channel_id=1, source_target_pairs={{0,16},{1,17},{2,18},{3,19},{4,20},{5,21},{6,22},{7,23},{8,24},{9,... | collective-permute-start | bytes 393224 | tf_op jit(solution)/shard_map/ppermute | solution.py:119
  159.7 10.4 %collective-permute-start.30 = (bf16[512,256]{1,0:T(8,128)(2,1)S(1)}, bf16[512,256]{1,0:T(8,128)(2,1)S(1)}, u32[]{:S(2)}, u32[]{:S(2)}) collective-permute-start(bf16[512,256]{1,0:T(8,128)(2,1)S(1)} %pad_maximum_fusion.24), channel_id=1, source_target_pairs={{0,8},{1,9},{2,10},{3,11},{4,12},{5,13},{6,14},{7,15},{8,0},{9,1},... | collective-permute-start | bytes 786440 | tf_op jit(solution)/shard_map/ppermute | solution.py:119
  162.3 14.9 %collective-permute-start.34 = (bf16[4,256,256]{2,1,0:T(8,128)(2,1)S(1)}, bf16[4,256,256]{2,1,0:T(8,128)(2,1)S(1)}, u32[]{:S(2)}, u32[]{:S(2)}) collective-permute-start(bf16[4,256,256]{2,1,0:T(8,128)(2,1)S(1)} %pad_maximum_fusion.19), channel_id=1, source_target_pairs={{0,2},{1,3},{2,0},{3,1},{4,6},{5,7},{6,4},{7,5},{8,10},{9,11},{10,... | collective-permute-start | bytes 1572872 | tf_op jit(solution)/shard_map/ppermute | solution.py:119
  162.9 20.4 %collective-permute-start.38 = (bf16[4,256,128]{2,1,0:T(8,128)(2,1)S(1)}, bf16[4,256,128]{2,1,0:T(8,128)(2,1)S(1)}, u32[]{:S(2)}, u32[]{:S(2)}) collective-permute-start(bf16[4,256,128]{2,1,0:T(8,128)(2,1)S(1)} %pad_maximum_fusion.25), channel_id=1, source_target_pairs={{0,2},{1,3},{2,0},{3,1},{4,6},{5,7},{6,4},{7,5},{8,10},{9,11},{10,... | collective-permute-start | bytes 786440 | tf_op jit(solution)/shard_map/ppermute | solution.py:119
  170.9 11.0 %collective-permute-start.33 = (bf16[512,256]{1,0:T(8,128)(2,1)S(1)}, bf16[512,256]{1,0:T(8,128)(2,1)S(1)}, u32[]{:S(2)}, u32[]{:S(2)}) collective-permute-start(bf16[512,256]{1,0:T(8,128)(2,1)S(1)} %pad_maximum_fusion.26), channel_id=1, source_target_pairs={{0,8},{1,9},{2,10},{3,11},{4,12},{5,13},{6,14},{7,15},{8,0},{9,1},... | collective-permute-start | bytes 786440 | tf_op jit(solution)/shard_map/ppermute | solution.py:119
  177.5 10.9 %collective-permute-start.36 = (bf16[512,256]{1,0:T(8,128)(2,1)S(1)}, bf16[512,256]{1,0:T(8,128)(2,1)S(1)}, u32[]{:S(2)}, u32[]{:S(2)}) collective-permute-start(bf16[512,256]{1,0:T(8,128)(2,1)S(1)} %pad_maximum_fusion.28), channel_id=1, source_target_pairs={{0,8},{1,9},{2,10},{3,11},{4,12},{5,13},{6,14},{7,15},{8,0},{9,1},... | collective-permute-start | bytes 786440 | tf_op jit(solution)/shard_map/ppermute | solution.py:119
  177.6 10.9 %collective-permute-start.41 = (bf16[4,256,128]{2,1,0:T(8,128)(2,1)S(1)}, bf16[4,256,128]{2,1,0:T(8,128)(2,1)S(1)}, u32[]{:S(2)}, u32[]{:S(2)}) collective-permute-start(bf16[4,256,128]{2,1,0:T(8,128)(2,1)S(1)} %pad_maximum_fusion.27), channel_id=1, source_target_pairs={{0,2},{1,3},{2,0},{3,1},{4,6},{5,7},{6,4},{7,5},{8,10},{9,11},{10,... | collective-permute-start | bytes 786440 | tf_op jit(solution)/shard_map/ppermute | solution.py:119
  182.0 8.1 %collective-permute-start.35 = (bf16[256,256]{1,0:T(8,128)(2,1)S(1)}, bf16[256,256]{1,0:T(8,128)(2,1)S(1)}, u32[]{:S(2)}, u32[]{:S(2)}) collective-permute-start(bf16[256,256]{1,0:T(8,128)(2,1)S(1)} %slice.882), channel_id=1, source_target_pairs={{0,16},{1,17},{2,18},{3,19},{4,20},{5,21},{6,22},{7,23},{8,24},{9,... | collective-permute-start | bytes 393224 | tf_op jit(solution)/shard_map/ppermute | solution.py:119
  190.2 9.6 %collective-permute-start.37 = (bf16[256,256]{1,0:T(8,128)(2,1)S(1)}, bf16[256,256]{1,0:T(8,128)(2,1)S(1)}, u32[]{:S(2)}, u32[]{:S(2)}) collective-permute-start(bf16[256,256]{1,0:T(8,128)(2,1)S(1)} %slice.881), channel_id=1, source_target_pairs={{0,16},{1,17},{2,18},{3,19},{4,20},{5,21},{6,22},{7,23},{8,24},{9,... | collective-permute-start | bytes 393224 | tf_op jit(solution)/shard_map/ppermute | solution.py:119
  (15 other events, 83.8 us)

commit v11 on v10

--- a/solution.py
+++ b/solution.py
@@ -66,27 +66,31 @@
     rows, cols = act.shape
     run = cols // xs // 2
     part = rows // ROW_CHUNKS
+    step = part // 2
+    each = part // step
 
     def kernel(where_ref, act_ref, *out_refs):
         for y in range(2):
             for x in range(xs):
-
-                @pl.when((where_ref[0] == y) & (where_ref[2] == x))
-                def _():
-                    for m in range(ROW_CHUNKS):
+                for m in range(ROW_CHUNKS):
+
+                    @pl.when((where_ref[0] == y) & (where_ref[2] == x) & (pl.program_id(0) // each == m))
+                    def _():
                         for s in range(2):
                             for d in range(xs):
                                 at = (2 * (x ^ d) + (y ^ s)) * run
-                                out_refs[2 * m + s][:, d * run : (d + 1) * run] = act_ref[
-                                    m * part : (m + 1) * part, at : at + run
-                                ]
+                                out_refs[2 * m + s][:, d * run : (d + 1) * run] = act_ref[:, at : at + run]
+
+    def rows_of(m):
+        return lambda i: (jnp.clip(i - m * each, 0, each - 1), 0)
 
     out = pl.pallas_call(
         kernel,
-        in_specs=[pl.BlockSpec(memory_space=pltpu.SMEM), pl.BlockSpec(memory_space=pltpu.VMEM)],
-        out_specs=[pl.BlockSpec(memory_space=pltpu.VMEM)] * (2 * ROW_CHUNKS),
+        grid=(rows // step,),
+        in_specs=[pl.BlockSpec(memory_space=pltpu.SMEM), pl.BlockSpec((step, cols), lambda i: (i, 0))],
+        out_specs=[pl.BlockSpec((step, cols // 2), rows_of(m)) for m in range(ROW_CHUNKS) for s in range(2)],
         out_shape=[jax.ShapeDtypeStruct((part, cols // 2), act.dtype)] * (2 * ROW_CHUNKS),
-        compiler_params=pltpu.CompilerParams(vmem_limit_bytes=32 * 1024 * 1024),
+        compiler_params=pltpu.CompilerParams(vmem_limit_bytes=60 * 1024 * 1024),
         cost_estimate=pl.CostEstimate(flops=0, bytes_accessed=4 * rows * cols, transcendentals=0),
         name="pack",
     )(where, act)

time: 204 us -> 206 us (level)
  local copies, waits for them, and re-layouts: 7.49 us -> 2.75 us
  Pallas kernels: 22 us -> 25.2 us
  waiting for transfers between devices: 96.2 us -> 98.5 us
    slice x5, local copies, waits for them, and re-layouts: 4.23 us -> 0.5 us  [to_tables(): near = jnp.stack([p[k, :, :half] for p in parts])]
    pallas_call x1, Pallas kernels: 1.8 us -> 4.9 us  [pack(): pl.pallas_call(kernel, grid=(rows // step,), in_specs=[pl.BlockSpec(memor...]
    ppermute x44, waiting for transfers between devices: 96.2 us -> 98.5 us  [permute(): return lax.ppermute(value, AXES, pairs)]
  transfers between devices with their start and end apart: 44 -> 44, of which waited for: 22 -> 22; matrix products, arithmetic and copies ran while one was open for 16% -> 14% of each run, Pallas kernels for 10% -> 10%
where the time goes in v11:
time: 206 us; the launch traced here: 205 us
  waiting for transfers between devices  98.5 us (48%)
  starting transfers between devices  48 us (23%)
  Pallas kernels  25.2 us (12%)
  matrix products  20.4 us (10%)
  other arithmetic  8.71 us (4%)
  local copies, waits for them, and re-layouts  2.75 us (1%)
    ppermute x44, waiting for transfers between devices, permute(): return lax.ppermute(value, AXES, pairs)  98.5 us
    ppermute x44, starting transfers between devices, permute(): return lax.ppermute(value, AXES, pairs)  48 us
    dot_general x32, matrix products, multiply(): jnp.dot(a, tables[q], preferred_element_type=jnp.float32)  20.4 us
    pallas_call x2, Pallas kernels, adam(): pl.pallas_call(kernel, grid_spec=pltpu.PrefetchScalarGridSpec(num_scalar_...  20.3 us
    pallas_call x1, Pallas kernels, pack(): pl.pallas_call(kernel, grid=(rows // step,), in_specs=[pl.BlockSpec(memor...  4.9 us
  transfers between devices with their start and end apart: 44, of which 22 were waited for; matrix products, arithmetic and copies ran while one was open for 14% of the time, Pallas kernels for 10%

profile of v11, /device:TPU:0, one launch (start us, length us, event | category | flops | bytes accessed | tf_op | source)
XLA Modules:
  0.0 205.4 jit_solution(11199163822470716286)
XLA Ops:
  1.3 4.9 %pack.1 = (bf16[256,1792]{1,0:T(8,128)(2,1)}, bf16[256,1792]{1,0:T(8,128)(2,1)}, bf16[256,1792]{1,0:T(8,128)(2,1)}, bf16[256,1792]{1,0:T(8,128)(2,1)}) custom-call(s32[3]{0:T(128)} %pad_add_fusion.where_ref, bf16[512,3584]{1,0:T(8,128)(2,1)} %act_ref.1), custom_call_target="tpu_custom_call" | custom-call | bytes 7340032 | tf_op jit(solution)/shard_map/pack/pallas_call | solution.py:87
  6.2 3.0 %collective-permute-start = (bf16[256,1792]{1,0:T(8,128)(2,1)}, bf16[256,1792]{1,0:T(8,128)(2,1)}, u32[]{:S(2)}, u32[]{:S(2)}) collective-permute-start(bf16[256,1792]{1,0:T(8,128)(2,1)} %get-tuple-element.57), channel_id=1, source_target_pairs={{0,2},{1,3},{2,0},{3,1},{4,6},{5,7},{6,4},{7,5},{8,10},{9,11},{10,... | collective-permute-start | bytes 2752520 | tf_op jit(solution)/shard_map/ppermute | solution.py:123
  9.2 10.0 %adam.2 = (f32[448,4096]{1,0:T(8,128)}, f32[448,4096]{1,0:T(8,128)}, f32[448,4096]{1,0:T(8,128)}, bf16[1,448,1024]{2,1,0:T(8,128)(2,1)}, bf16[1,448,1024]{2,1,0:T(8,128)(2,1)}) custom-call(s32[3]{0:T(128)} %pad_add_fusion.where_ref, f32[448,4096]{1,0:T(8,128)} %master_ref.3, f32[448,4096]{1,0:T(8,128)} %one_ref.3, f32[448,4096]{1,0:T(8,128)} %two_ref.3, ...), custom_call_target="tpu_custom_call" | custom-call | flops 11010048 | bytes 25690112 | tf_op jit(solution)/shard_map/adam/pallas_call | solution.py:48
  21.3 10.3 %adam.3 = (f32[448,4096]{1,0:T(8,128)}, f32[448,4096]{1,0:T(8,128)}, f32[448,4096]{1,0:T(8,128)}, bf16[2,448,1024]{2,1,0:T(8,128)(2,1)}) custom-call(s32[3]{0:T(128)} %pad_add_fusion.where_ref, f32[448,4096]{1,0:T(8,128)} %master_ref.3, f32[448,4096]{1,0:T(8,128)} %one_ref.3, ...), custom_call_target="tpu_custom_call", output_to_operand_aliasing={{0}: (5, {}), {1}: (6, {}), {2}: (7, {})} | custom-call | flops 11010048 | bytes 25690112 | tf_op jit(solution)/shard_map/adam/pallas_call | solution.py:48
  34.8 3.1 %collective-permute-start.5 = (bf16[256,1792]{1,0:T(8,128)(2,1)S(1)}, bf16[256,1792]{1,0:T(8,128)(2,1)S(1)}, u32[]{:S(2)}, u32[]{:S(2)}) collective-permute-start(bf16[256,1792]{1,0:T(8,128)(2,1)S(1)} %get-tuple-element.61), channel_id=1, source_target_pairs={{0,16},{1,24},{2,18},{3,26},{4,20},{5,28},{6,22},{7,30},{8,17},{9,... | collective-permute-start | bytes 2752520 | tf_op jit(solution)/shard_map/ppermute | solution.py:123
  37.9 4.8 %collective-permute-done.3 = bf16[1,448,1024]{2,1,0:T(8,128)(2,1)S(1)} collective-permute-done((bf16[1,448,1024]{2,1,0:T(8,128)(2,1)}, bf16[1,448,1024]{2,1,0:T(8,128)(2,1)S(1)}, u32[]{:S(2)}, u32[]{:S(2)}) %collective-permute-start.3) | collective-permute-done | bytes 917536 | tf_op jit(solution)/shard_map/ppermute | solution.py:123
  44.4 18.0 %collective-permute-done.14 = bf16[1,448,1024]{2,1,0:T(8,128)(2,1)S(1)} collective-permute-done((bf16[1,448,1024]{2,1,0:T(8,128)(2,1)}, bf16[1,448,1024]{2,1,0:T(8,128)(2,1)S(1)}, u32[]{:S(2)}, u32[]{:S(2)}) %collective-permute-start.14) | collective-permute-done | bytes 917536 | tf_op jit(solution)/shard_map/ppermute | solution.py:123
  64.4 13.3 %collective-permute-done.5 = bf16[256,1792]{1,0:T(8,128)(2,1)S(1)} collective-permute-done((bf16[256,1792]{1,0:T(8,128)(2,1)S(1)}, bf16[256,1792]{1,0:T(8,128)(2,1)S(1)}, u32[]{:S(2)}, u32[]{:S(2)}) %collective-permute-start.5) | collective-permute-done | bytes 917536 | tf_op jit(solution)/shard_map/ppermute | solution.py:123
  80.3 4.3 %collective-permute-start.6 = (bf16[256,1792]{1,0:T(8,128)(2,1)S(1)}, bf16[256,1792]{1,0:T(8,128)(2,1)S(1)}, u32[]{:S(2)}, u32[]{:S(2)}) collective-permute-start(bf16[256,1792]{1,0:T(8,128)(2,1)S(1)} %collective-permute-done.5), channel_id=1, source_target_pairs={{0,1},{1,0},{2,3},{3,2},{4,5},{5,4},{6,7},{7,6},{8,9},{9,8},{10,11... | collective-permute-start | bytes 2752520 | tf_op jit(solution)/shard_map/ppermute | solution.py:123
  88.8 1.6 collective-permute-start.7
  91.7 8.5 %collective-permute-done.9 = bf16[2,448,1024]{2,1,0:T(8,128)(2,1)S(1)} collective-permute-done((bf16[2,448,1024]{2,1,0:T(8,128)(2,1)S(1)}, bf16[2,448,1024]{2,1,0:T(8,128)(2,1)S(1)}, u32[]{:S(2)}, u32[]{:S(2)}) %collective-permute-start.9) | collective-permute-done | bytes 1835040 | tf_op jit(solution)/shard_map/ppermute | solution.py:123
  100.2 2.8 %collective-permute-done.7 = bf16[4,256,256]{2,1,0:T(8,128)(2,1)S(1)} collective-permute-done((bf16[4,256,256]{2,1,0:T(8,128)(2,1)S(1)}, bf16[4,256,256]{2,1,0:T(8,128)(2,1)S(1)}, u32[]{:S(2)}, u32[]{:S(2)}) %collective-permute-start.7) | collective-permute-done | bytes 524320 | tf_op jit(solution)/shard_map/ppermute | solution.py:123
  103.6 1.6 collective-permute-start.16
  109.1 1.6 collective-permute-start.20
  113.9 4.5 %collective-permute-done.16 = bf16[4,256,256]{2,1,0:T(8,128)(2,1)S(1)} collective-permute-done((bf16[4,256,256]{2,1,0:T(8,128)(2,1)S(1)}, bf16[4,256,256]{2,1,0:T(8,128)(2,1)S(1)}, u32[]{:S(2)}, u32[]{:S(2)}) %collective-permute-start.16) | collective-permute-done | bytes 524320 | tf_op jit(solution)/shard_map/ppermute | solution.py:123
  120.3 2.3 %collective-permute-start.18 = (bf16[512,256]{1,0:T(8,128)(2,1)S(1)}, bf16[512,256]{1,0:T(8,128)(2,1)S(1)}, u32[]{:S(2)}, u32[]{:S(2)}) collective-permute-start(bf16[512,256]{1,0:T(8,128)(2,1)S(1)} %pad_maximum_fusion.21), channel_id=1, source_target_pairs={{0,8},{1,9},{2,10},{3,11},{4,12},{5,13},{6,14},{7,15},{8,0},{9,1},... | collective-permute-start | bytes 786440 | tf_op jit(solution)/shard_map/ppermute | solution.py:123
  122.6 5.8 %collective-permute-done.17 = bf16[256,256]{1,0:T(8,128)(2,1)S(1)} collective-permute-done((bf16[256,256]{1,0:T(8,128)(2,1)S(1)}, bf16[256,256]{1,0:T(8,128)(2,1)S(1)}, u32[]{:S(2)}, u32[]{:S(2)}) %collective-permute-start.17) | collective-permute-done | bytes 131104 | tf_op jit(solution)/shard_map/ppermute | solution.py:123
  137.2 1.6 collective-permute-start.28
  139.2 1.9 collective-permute-start.24
  145.8 4.2 %collective-permute-done.24 = bf16[512,256]{1,0:T(8,128)(2,1)S(1)} collective-permute-done((bf16[512,256]{1,0:T(8,128)(2,1)S(1)}, bf16[512,256]{1,0:T(8,128)(2,1)S(1)}, u32[]{:S(2)}, u32[]{:S(2)}) %collective-permute-start.24) | collective-permute-done | bytes 262176 | tf_op jit(solution)/shard_map/ppermute | solution.py:123
  150.5 2.9 %collective-permute-start.26 = (bf16[256,256]{1,0:T(8,128)(2,1)S(1)}, bf16[256,256]{1,0:T(8,128)(2,1)S(1)}, u32[]{:S(2)}, u32[]{:S(2)}) collective-permute-start(bf16[256,256]{1,0:T(8,128)(2,1)S(1)} %slice.885), channel_id=1, source_target_pairs={{0,16},{1,17},{2,18},{3,19},{4,20},{5,21},{6,22},{7,23},{8,24},{9,... | collective-permute-start | bytes 393224 | tf_op jit(solution)/shard_map/ppermute | solution.py:123
  153.4 6.9 %collective-permute-done.27 = bf16[512,256]{1,0:T(8,128)(2,1)S(1)} collective-permute-done((bf16[512,256]{1,0:T(8,128)(2,1)S(1)}, bf16[512,256]{1,0:T(8,128)(2,1)S(1)}, u32[]{:S(2)}, u32[]{:S(2)}) %collective-permute-start.27) | collective-permute-done | bytes 262176 | tf_op jit(solution)/shard_map/ppermute | solution.py:123
  161.0 2.5 %collective-permute-start.30 = (bf16[512,256]{1,0:T(8,128)(2,1)S(1)}, bf16[512,256]{1,0:T(8,128)(2,1)S(1)}, u32[]{:S(2)}, u32[]{:S(2)}) collective-permute-start(bf16[512,256]{1,0:T(8,128)(2,1)S(1)} %pad_maximum_fusion.24), channel_id=1, source_target_pairs={{0,8},{1,9},{2,10},{3,11},{4,12},{5,13},{6,14},{7,15},{8,0},{9,1},... | collective-permute-start | bytes 786440 | tf_op jit(solution)/shard_map/ppermute | solution.py:123
  165.7 2.4 %collective-permute-done.29 = bf16[256,256]{1,0:T(8,128)(2,1)S(1)} collective-permute-done((bf16[256,256]{1,0:T(8,128)(2,1)S(1)}, bf16[256,256]{1,0:T(8,128)(2,1)S(1)}, u32[]{:S(2)}, u32[]{:S(2)}) %collective-permute-start.29) | collective-permute-done | bytes 131104 | tf_op jit(solution)/shard_map/ppermute | solution.py:123
  168.2 3.3 %collective-permute-done.30 = bf16[512,256]{1,0:T(8,128)(2,1)S(1)} collective-permute-done((bf16[512,256]{1,0:T(8,128)(2,1)S(1)}, bf16[512,256]{1,0:T(8,128)(2,1)S(1)}, u32[]{:S(2)}, u32[]{:S(2)}) %collective-permute-start.30) | collective-permute-done | bytes 262176 | tf_op jit(solution)/shard_map/ppermute | solution.py:123
  172.2 1.8 collective-permute-start.33
  173.9 4.6 %collective-permute-done.34 = bf16[4,256,256]{2,1,0:T(8,128)(2,1)S(1)} collective-permute-done((bf16[4,256,256]{2,1,0:T(8,128)(2,1)S(1)}, bf16[4,256,256]{2,1,0:T(8,128)(2,1)S(1)}, u32[]{:S(2)}, u32[]{:S(2)}) %collective-permute-start.34) | collective-permute-done | bytes 524320 | tf_op jit(solution)/shard_map/ppermute | solution.py:123
  179.4 3.8 %collective-permute-done.33 = bf16[512,256]{1,0:T(8,128)(2,1)S(1)} collective-permute-done((bf16[512,256]{1,0:T(8,128)(2,1)S(1)}, bf16[512,256]{1,0:T(8,128)(2,1)S(1)}, u32[]{:S(2)}, u32[]{:S(2)}) %collective-permute-start.33) | collective-permute-done | bytes 262176 | tf_op jit(solution)/shard_map/ppermute | solution.py:123
  184.6 5.1 %collective-permute-done.36 = bf16[512,256]{1,0:T(8,128)(2,1)S(1)} collective-permute-done((bf16[512,256]{1,0:T(8,128)(2,1)S(1)}, bf16[512,256]{1,0:T(8,128)(2,1)S(1)}, u32[]{:S(2)}, u32[]{:S(2)}) %collective-permute-start.36) | collective-permute-done | bytes 262176 | tf_op jit(solution)/shard_map/ppermute | solution.py:123
  193.7 3.5 %collective-permute-done.39 = bf16[512,128]{1,0:T(8,128)(2,1)S(1)} collective-permute-done((bf16[512,128]{1,0:T(8,128)(2,1)S(1)}, bf16[512,128]{1,0:T(8,128)(2,1)S(1)}, u32[]{:S(2)}, u32[]{:S(2)}) %collective-permute-start.39) | collective-permute-done | bytes 131104 | tf_op jit(solution)/shard_map/ppermute | solution.py:123
  198.8 2.3 %collective-permute-start.43 = (bf16[256,128]{1,0:T(8,128)(2,1)S(1)}, bf16[256,128]{1,0:T(8,128)(2,1)S(1)}, u32[]{:S(2)}, u32[]{:S(2)}) collective-permute-start(bf16[256,128]{1,0:T(8,128)(2,1)S(1)} %slice.888), channel_id=1, source_target_pairs={{0,16},{1,17},{2,18},{3,19},{4,20},{5,21},{6,22},{7,23},{8,24},{9,... | collective-permute-start | bytes 196616 | tf_op jit(solution)/shard_map/ppermute | solution.py:123
  201.1 2.5 %collective-permute-done.40 = bf16[256,128]{1,0:T(8,128)(2,1)S(1)} collective-permute-done((bf16[256,128]{1,0:T(8,128)(2,1)S(1)}, bf16[256,128]{1,0:T(8,128)(2,1)S(1)}, u32[]{:S(2)}, u32[]{:S(2)}) %collective-permute-start.40) | collective-permute-done | bytes 65568 | tf_op jit(solution)/shard_map/ppermute | solution.py:123
  (212 shorter events, 53.9 us)
Async XLA Ops:
  6.2 25.5 %collective-permute-start = (bf16[256,1792]{1,0:T(8,128)(2,1)}, bf16[256,1792]{1,0:T(8,128)(2,1)}, u32[]{:S(2)}, u32[]{:S(2)}) collective-permute-start(bf16[256,1792]{1,0:T(8,128)(2,1)} %get-tuple-element.57), channel_id=1, source_target_pairs={{0,2},{1,3},{2,0},{3,1},{4,6},{5,7},{6,4},{7,5},{8,10},{9,11},{10,... | collective-permute-start | bytes 2752520 | tf_op jit(solution)/shard_map/ppermute | solution.py:123
  19.2 23.5 %collective-permute-start.3 = (bf16[1,448,1024]{2,1,0:T(8,128)(2,1)}, bf16[1,448,1024]{2,1,0:T(8,128)(2,1)S(1)}, u32[]{:S(2)}, u32[]{:S(2)}) collective-permute-start(bf16[1,448,1024]{2,1,0:T(8,128)(2,1)} %get-tuple-element.60), channel_id=1, source_target_pairs={{0,4},{1,5},{2,6},{3,7},{4,0},{5,1},{6,2},{7,3},{8,12},{9,13},{10,... | collective-permute-start | bytes 2752520 | tf_op jit(solution)/shard_map/ppermute | solution.py:123
  20.7 41.8 %collective-permute-start.10 = (bf16[256,1792]{1,0:T(8,128)(2,1)}, bf16[256,1792]{1,0:T(8,128)(2,1)}, u32[]{:S(2)}, u32[]{:S(2)}) collective-permute-start(bf16[256,1792]{1,0:T(8,128)(2,1)} %get-tuple-element.63), channel_id=1, source_target_pairs={{0,2},{1,3},{2,0},{3,1},{4,6},{5,7},{6,4},{7,5},{8,10},{9,11},{10,... | collective-permute-start | bytes 2752520 | tf_op jit(solution)/shard_map/ppermute | solution.py:123
  21.2 41.2 %collective-permute-start.14 = (bf16[1,448,1024]{2,1,0:T(8,128)(2,1)}, bf16[1,448,1024]{2,1,0:T(8,128)(2,1)S(1)}, u32[]{:S(2)}, u32[]{:S(2)}) collective-permute-start(bf16[1,448,1024]{2,1,0:T(8,128)(2,1)} %get-tuple-element.68), channel_id=1, source_target_pairs={{0,4},{1,5},{2,6},{3,7},{4,0},{5,1},{6,2},{7,3},{8,12},{9,13},{10,... | collective-permute-start | bytes 2752520 | tf_op jit(solution)/shard_map/ppermute | solution.py:123
  34.1 30.4 %collective-permute-start.1 = (bf16[256,1792]{1,0:T(8,128)(2,1)S(1)}, bf16[256,1792]{1,0:T(8,128)(2,1)S(1)}, u32[]{:S(2)}, u32[]{:S(2)}) collective-permute-start(bf16[256,1792]{1,0:T(8,128)(2,1)S(1)} %get-tuple-element.59), channel_id=1, source_target_pairs={{0,0},{1,8},{2,2},{3,10},{4,4},{5,12},{6,6},{7,14},{8,1},{9,9},{10... | collective-permute-start | bytes 2752520 | tf_op jit(solution)/shard_map/ppermute | solution.py:123
  34.8 43.0 %collective-permute-start.5 = (bf16[256,1792]{1,0:T(8,128)(2,1)S(1)}, bf16[256,1792]{1,0:T(8,128)(2,1)S(1)}, u32[]{:S(2)}, u32[]{:S(2)}) collective-permute-start(bf16[256,1792]{1,0:T(8,128)(2,1)S(1)} %get-tuple-element.61), channel_id=1, source_target_pairs={{0,16},{1,24},{2,18},{3,26},{4,20},{5,28},{6,22},{7,30},{8,17},{9,... | collective-permute-start | bytes 2752520 | tf_op jit(solution)/shard_map/ppermute | solution.py:123
  42.7 57.5 %collective-permute-start.9 = (bf16[2,448,1024]{2,1,0:T(8,128)(2,1)S(1)}, bf16[2,448,1024]{2,1,0:T(8,128)(2,1)S(1)}, u32[]{:S(2)}, u32[]{:S(2)}) collective-permute-start(bf16[2,448,1024]{2,1,0:T(8,128)(2,1)S(1)} %copy-done), channel_id=1, source_target_pairs={{0,4},{1,5},{2,6},{3,7},{4,0},{5,1},{6,2},{7,3},{8,12},{9,13},{10,... | collective-permute-start | bytes 5505032 | tf_op jit(solution)/shard_map/ppermute | solution.py:123
  62.4 16.4 %collective-permute-start.4 = (bf16[2,448,512]{2,1,0:T(8,128)(2,1)S(1)}, bf16[2,448,512]{2,1,0:T(8,128)(2,1)S(1)}, u32[]{:S(2)}, u32[]{:S(2)}) collective-permute-start(bf16[2,448,512]{2,1,0:T(8,128)(2,1)S(1)} %pad_maximum_fusion.5), channel_id=1, source_target_pairs={{0,1},{1,0},{2,3},{3,2},{4,5},{5,4},{6,7},{7,6},{8,9},{9,8},{10,11... | collective-permute-start | bytes 2752520 | tf_op jit(solution)/shard_map/ppermute | solution.py:123
  62.5 17.3 %collective-permute-start.15 = (bf16[2,448,512]{2,1,0:T(8,128)(2,1)S(1)}, bf16[2,448,512]{2,1,0:T(8,128)(2,1)S(1)}, u32[]{:S(2)}, u32[]{:S(2)}) collective-permute-start(bf16[2,448,512]{2,1,0:T(8,128)(2,1)S(1)} %pad_maximum_fusion.11), channel_id=1, source_target_pairs={{0,1},{1,0},{2,3},{3,2},{4,5},{5,4},{6,7},{7,6},{8,9},{9,8},{10,11... | collective-permute-start | bytes 2752520 | tf_op jit(solution)/shard_map/ppermute | solution.py:123
  77.8 13.9 %collective-permute-start.11 = (bf16[256,1792]{1,0:T(8,128)(2,1)S(1)}, bf16[256,1792]{1,0:T(8,128)(2,1)S(1)}, u32[]{:S(2)}, u32[]{:S(2)}) collective-permute-start(bf16[256,1792]{1,0:T(8,128)(2,1)S(1)} %get-tuple-element.65), channel_id=1, source_target_pairs={{0,0},{1,8},{2,2},{3,10},{4,4},{5,12},{6,6},{7,14},{8,1},{9,9},{10... | collective-permute-start | bytes 2752520 | tf_op jit(solution)/shard_map/ppermute | solution.py:123
  78.7 49.7 %collective-permute-start.19 = (bf16[256,1792]{1,0:T(8,128)(2,1)S(1)}, bf16[256,1792]{1,0:T(8,128)(2,1)S(1)}, u32[]{:S(2)}, u32[]{:S(2)}) collective-permute-start(bf16[256,1792]{1,0:T(8,128)(2,1)S(1)} %get-tuple-element.74), channel_id=1, source_target_pairs={{0,16},{1,24},{2,18},{3,26},{4,20},{5,28},{6,22},{7,30},{8,17},{9,... | collective-permute-start | bytes 2752520 | tf_op jit(solution)/shard_map/ppermute | solution.py:123
  88.8 14.3 %collective-permute-start.7 = (bf16[4,256,256]{2,1,0:T(8,128)(2,1)S(1)}, bf16[4,256,256]{2,1,0:T(8,128)(2,1)S(1)}, u32[]{:S(2)}, u32[]{:S(2)}) collective-permute-start(bf16[4,256,256]{2,1,0:T(8,128)(2,1)S(1)} %pad_maximum_fusion.13), channel_id=1, source_target_pairs={{0,2},{1,3},{2,0},{3,1},{4,6},{5,7},{6,4},{7,5},{8,10},{9,11},{10,... | collective-permute-start | bytes 1572872 | tf_op jit(solution)/shard_map/ppermute | solution.py:123
  103.6 14.8 %collective-permute-start.16 = (bf16[4,256,256]{2,1,0:T(8,128)(2,1)S(1)}, bf16[4,256,256]{2,1,0:T(8,128)(2,1)S(1)}, u32[]{:S(2)}, u32[]{:S(2)}) collective-permute-start(bf16[4,256,256]{2,1,0:T(8,128)(2,1)S(1)} %pad_maximum_fusion.16), channel_id=1, source_target_pairs={{0,2},{1,3},{2,0},{3,1},{4,6},{5,7},{6,4},{7,5},{8,10},{9,11},{10,... | collective-permute-start | bytes 1572872 | tf_op jit(solution)/shard_map/ppermute | solution.py:123
  105.8 14.2 %collective-permute-start.8 = (bf16[512,256]{1,0:T(8,128)(2,1)S(1)}, bf16[512,256]{1,0:T(8,128)(2,1)S(1)}, u32[]{:S(2)}, u32[]{:S(2)}) collective-permute-start(bf16[512,256]{1,0:T(8,128)(2,1)S(1)} %pad_maximum_fusion.20), channel_id=1, source_target_pairs={{0,8},{1,9},{2,10},{3,11},{4,12},{5,13},{6,14},{7,15},{8,0},{9,1},... | collective-permute-start | bytes 786440 | tf_op jit(solution)/shard_map/ppermute | solution.py:123
  109.1 20.5 %collective-permute-start.20 = (bf16[4,256,256]{2,1,0:T(8,128)(2,1)S(1)}, bf16[4,256,256]{2,1,0:T(8,128)(2,1)S(1)}, u32[]{:S(2)}, u32[]{:S(2)}) collective-permute-start(bf16[4,256,256]{2,1,0:T(8,128)(2,1)S(1)} %pad_maximum_fusion.15), channel_id=1, source_target_pairs={{0,2},{1,3},{2,0},{3,1},{4,6},{5,7},{6,4},{7,5},{8,10},{9,11},{10,... | collective-permute-start | bytes 1572872 | tf_op jit(solution)/shard_map/ppermute | solution.py:123
  118.4 26.7 %collective-permute-start.25 = (bf16[4,256,256]{2,1,0:T(8,128)(2,1)S(1)}, bf16[4,256,256]{2,1,0:T(8,128)(2,1)S(1)}, u32[]{:S(2)}, u32[]{:S(2)}) collective-permute-start(bf16[4,256,256]{2,1,0:T(8,128)(2,1)S(1)} %pad_maximum_fusion.14), channel_id=1, source_target_pairs={{0,2},{1,3},{2,0},{3,1},{4,6},{5,7},{6,4},{7,5},{8,10},{9,11},{10,... | collective-permute-start | bytes 1572872 | tf_op jit(solution)/shard_map/ppermute | solution.py:123
  120.0 8.3 %collective-permute-start.17 = (bf16[256,256]{1,0:T(8,128)(2,1)S(1)}, bf16[256,256]{1,0:T(8,128)(2,1)S(1)}, u32[]{:S(2)}, u32[]{:S(2)}) collective-permute-start(bf16[256,256]{1,0:T(8,128)(2,1)S(1)} %slice.887), channel_id=1, source_target_pairs={{0,16},{1,17},{2,18},{3,19},{4,20},{5,21},{6,22},{7,23},{8,24},{9,... | collective-permute-start | bytes 393224 | tf_op jit(solution)/shard_map/ppermute | solution.py:123
  120.3 18.5 %collective-permute-start.18 = (bf16[512,256]{1,0:T(8,128)(2,1)S(1)}, bf16[512,256]{1,0:T(8,128)(2,1)S(1)}, u32[]{:S(2)}, u32[]{:S(2)}) collective-permute-start(bf16[512,256]{1,0:T(8,128)(2,1)S(1)} %pad_maximum_fusion.21), channel_id=1, source_target_pairs={{0,8},{1,9},{2,10},{3,11},{4,12},{5,13},{6,14},{7,15},{8,0},{9,1},... | collective-permute-start | bytes 786440 | tf_op jit(solution)/shard_map/ppermute | solution.py:123
  137.2 16.2 %collective-permute-start.28 = (bf16[4,256,256]{2,1,0:T(8,128)(2,1)S(1)}, bf16[4,256,256]{2,1,0:T(8,128)(2,1)S(1)}, u32[]{:S(2)}, u32[]{:S(2)}) collective-permute-start(bf16[4,256,256]{2,1,0:T(8,128)(2,1)S(1)} %pad_maximum_fusion.17), channel_id=1, source_target_pairs={{0,2},{1,3},{2,0},{3,1},{4,6},{5,7},{6,4},{7,5},{8,10},{9,11},{10,... | collective-permute-start | bytes 1572872 | tf_op jit(solution)/shard_map/ppermute | solution.py:123
  138.9 11.5 %collective-permute-start.23 = (bf16[256,256]{1,0:T(8,128)(2,1)S(1)}, bf16[256,256]{1,0:T(8,128)(2,1)S(1)}, u32[]{:S(2)}, u32[]{:S(2)}) collective-permute-start(bf16[256,256]{1,0:T(8,128)(2,1)S(1)} %slice.886), channel_id=1, source_target_pairs={{0,16},{1,17},{2,18},{3,19},{4,20},{5,21},{6,22},{7,23},{8,24},{9,... | collective-permute-start | bytes 393224 | tf_op jit(solution)/shard_map/ppermute | solution.py:123
  139.2 10.8 %collective-permute-start.24 = (bf16[512,256]{1,0:T(8,128)(2,1)S(1)}, bf16[512,256]{1,0:T(8,128)(2,1)S(1)}, u32[]{:S(2)}, u32[]{:S(2)}) collective-permute-start(bf16[512,256]{1,0:T(8,128)(2,1)S(1)} %pad_maximum_fusion.22), channel_id=1, source_target_pairs={{0,8},{1,9},{2,10},{3,11},{4,12},{5,13},{6,14},{7,15},{8,0},{9,1},... | collective-permute-start | bytes 786440 | tf_op jit(solution)/shard_map/ppermute | solution.py:123
  145.1 19.0 %collective-permute-start.31 = (bf16[4,256,256]{2,1,0:T(8,128)(2,1)S(1)}, bf16[4,256,256]{2,1,0:T(8,128)(2,1)S(1)}, u32[]{:S(2)}, u32[]{:S(2)}) collective-permute-start(bf16[4,256,256]{2,1,0:T(8,128)(2,1)S(1)} %pad_maximum_fusion.18), channel_id=1, source_target_pairs={{0,2},{1,3},{2,0},{3,1},{4,6},{5,7},{6,4},{7,5},{8,10},{9,11},{10,... | collective-permute-start | bytes 1572872 | tf_op jit(solution)/shard_map/ppermute | solution.py:123
  150.3 10.0 %collective-permute-start.27 = (bf16[512,256]{1,0:T(8,128)(2,1)S(1)}, bf16[512,256]{1,0:T(8,128)(2,1)S(1)}, u32[]{:S(2)}, u32[]{:S(2)}) collective-permute-start(bf16[512,256]{1,0:T(8,128)(2,1)S(1)} %pad_maximum_fusion.23), channel_id=1, source_target_pairs={{0,8},{1,9},{2,10},{3,11},{4,12},{5,13},{6,14},{7,15},{8,0},{9,1},... | collective-permute-start | bytes 786440 | tf_op jit(solution)/shard_map/ppermute | solution.py:123
  150.5 13.1 %collective-permute-start.26 = (bf16[256,256]{1,0:T(8,128)(2,1)S(1)}, bf16[256,256]{1,0:T(8,128)(2,1)S(1)}, u32[]{:S(2)}, u32[]{:S(2)}) collective-permute-start(bf16[256,256]{1,0:T(8,128)(2,1)S(1)} %slice.885), channel_id=1, source_target_pairs={{0,16},{1,17},{2,18},{3,19},{4,20},{5,21},{6,22},{7,23},{8,24},{9,... | collective-permute-start | bytes 393224 | tf_op jit(solution)/shard_map/ppermute | solution.py:123
  161.0 10.4 %collective-permute-start.30 = (bf16[512,256]{1,0:T(8,128)(2,1)S(1)}, bf16[512,256]{1,0:T(8,128)(2,1)S(1)}, u32[]{:S(2)}, u32[]{:S(2)}) collective-permute-start(bf16[512,256]{1,0:T(8,128)(2,1)S(1)} %pad_maximum_fusion.24), channel_id=1, source_target_pairs={{0,8},{1,9},{2,10},{3,11},{4,12},{5,13},{6,14},{7,15},{8,0},{9,1},... | collective-permute-start | bytes 786440 | tf_op jit(solution)/shard_map/ppermute | solution.py:123
  163.6 14.9 %collective-permute-start.34 = (bf16[4,256,256]{2,1,0:T(8,128)(2,1)S(1)}, bf16[4,256,256]{2,1,0:T(8,128)(2,1)S(1)}, u32[]{:S(2)}, u32[]{:S(2)}) collective-permute-start(bf16[4,256,256]{2,1,0:T(8,128)(2,1)S(1)} %pad_maximum_fusion.19), channel_id=1, source_target_pairs={{0,2},{1,3},{2,0},{3,1},{4,6},{5,7},{6,4},{7,5},{8,10},{9,11},{10,... | collective-permute-start | bytes 1572872 | tf_op jit(solution)/shard_map/ppermute | solution.py:123
  164.2 20.4 %collective-permute-start.38 = (bf16[4,256,128]{2,1,0:T(8,128)(2,1)S(1)}, bf16[4,256,128]{2,1,0:T(8,128)(2,1)S(1)}, u32[]{:S(2)}, u32[]{:S(2)}) collective-permute-start(bf16[4,256,128]{2,1,0:T(8,128)(2,1)S(1)} %pad_maximum_fusion.25), channel_id=1, source_target_pairs={{0,2},{1,3},{2,0},{3,1},{4,6},{5,7},{6,4},{7,5},{8,10},{9,11},{10,... | collective-permute-start | bytes 786440 | tf_op jit(solution)/shard_map/ppermute | solution.py:123
  172.2 11.0 %collective-permute-start.33 = (bf16[512,256]{1,0:T(8,128)(2,1)S(1)}, bf16[512,256]{1,0:T(8,128)(2,1)S(1)}, u32[]{:S(2)}, u32[]{:S(2)}) collective-permute-start(bf16[512,256]{1,0:T(8,128)(2,1)S(1)} %pad_maximum_fusion.26), channel_id=1, source_target_pairs={{0,8},{1,9},{2,10},{3,11},{4,12},{5,13},{6,14},{7,15},{8,0},{9,1},... | collective-permute-start | bytes 786440 | tf_op jit(solution)/shard_map/ppermute | solution.py:123
  178.7 10.9 %collective-permute-start.36 = (bf16[512,256]{1,0:T(8,128)(2,1)S(1)}, bf16[512,256]{1,0:T(8,128)(2,1)S(1)}, u32[]{:S(2)}, u32[]{:S(2)}) collective-permute-start(bf16[512,256]{1,0:T(8,128)(2,1)S(1)} %pad_maximum_fusion.28), channel_id=1, source_target_pairs={{0,8},{1,9},{2,10},{3,11},{4,12},{5,13},{6,14},{7,15},{8,0},{9,1},... | collective-permute-start | bytes 786440 | tf_op jit(solution)/shard_map/ppermute | solution.py:123
  178.9 10.8 %collective-permute-start.41 = (bf16[4,256,128]{2,1,0:T(8,128)(2,1)S(1)}, bf16[4,256,128]{2,1,0:T(8,128)(2,1)S(1)}, u32[]{:S(2)}, u32[]{:S(2)}) collective-permute-start(bf16[4,256,128]{2,1,0:T(8,128)(2,1)S(1)} %pad_maximum_fusion.27), channel_id=1, source_target_pairs={{0,2},{1,3},{2,0},{3,1},{4,6},{5,7},{6,4},{7,5},{8,10},{9,11},{10,... | collective-permute-start | bytes 786440 | tf_op jit(solution)/shard_map/ppermute | solution.py:123
  183.3 8.1 %collective-permute-start.35 = (bf16[256,256]{1,0:T(8,128)(2,1)S(1)}, bf16[256,256]{1,0:T(8,128)(2,1)S(1)}, u32[]{:S(2)}, u32[]{:S(2)}) collective-permute-start(bf16[256,256]{1,0:T(8,128)(2,1)S(1)} %slice.882), channel_id=1, source_target_pairs={{0,16},{1,17},{2,18},{3,19},{4,20},{5,21},{6,22},{7,23},{8,24},{9,... | collective-permute-start | bytes 393224 | tf_op jit(solution)/shard_map/ppermute | solution.py:123
  191.5 9.6 %collective-permute-start.37 = (bf16[256,256]{1,0:T(8,128)(2,1)S(1)}, bf16[256,256]{1,0:T(8,128)(2,1)S(1)}, u32[]{:S(2)}, u32[]{:S(2)}) collective-permute-start(bf16[256,256]{1,0:T(8,128)(2,1)S(1)} %slice.881), channel_id=1, source_target_pairs={{0,16},{1,17},{2,18},{3,19},{4,20},{5,21},{6,22},{7,23},{8,24},{9,... | collective-permute-start | bytes 393224 | tf_op jit(solution)/shard_map/ppermute | solution.py:123
  (17 other events, 121.7 us)

commit v12 on v10

--- a/solution.py
+++ b/solution.py
@@ -62,7 +62,7 @@
     return out[:3], out[3:]
 
 
-def pack(where, act, xs):
+def pack(where, act, xs, m):
     rows, cols = act.shape
     run = cols // xs // 2
     part = rows // ROW_CHUNKS
@@ -73,24 +73,22 @@
 
                 @pl.when((where_ref[0] == y) & (where_ref[2] == x))
                 def _():
-                    for m in range(ROW_CHUNKS):
-                        for s in range(2):
-                            for d in range(xs):
-                                at = (2 * (x ^ d) + (y ^ s)) * run
-                                out_refs[2 * m + s][:, d * run : (d + 1) * run] = act_ref[
-                                    m * part : (m + 1) * part, at : at + run
-                                ]
-
-    out = pl.pallas_call(
+                    for s in range(2):
+                        for d in range(xs):
+                            at = (2 * (x ^ d) + (y ^ s)) * run
+                            out_refs[s][:, d * run : (d + 1) * run] = act_ref[:, at : at + run]
+
+    whole = pl.BlockSpec((part, cols // 2), lambda i: (0, 0))
+    return pl.pallas_call(
         kernel,
-        in_specs=[pl.BlockSpec(memory_space=pltpu.SMEM), pl.BlockSpec(memory_space=pltpu.VMEM)],
-        out_specs=[pl.BlockSpec(memory_space=pltpu.VMEM)] * (2 * ROW_CHUNKS),
-        out_shape=[jax.ShapeDtypeStruct((part, cols // 2), act.dtype)] * (2 * ROW_CHUNKS),
-        compiler_params=pltpu.CompilerParams(vmem_limit_bytes=32 * 1024 * 1024),
-        cost_estimate=pl.CostEstimate(flops=0, bytes_accessed=4 * rows * cols, transcendentals=0),
+        grid=(1,),
+        in_specs=[pl.BlockSpec(memory_space=pltpu.SMEM), pl.BlockSpec((part, cols), lambda i: (m, 0))],
+        out_specs=[whole] * 2,
+        out_shape=[jax.ShapeDtypeStruct((part, cols // 2), act.dtype)] * 2,
+        compiler_params=pltpu.CompilerParams(vmem_limit_bytes=60 * 1024 * 1024),
+        cost_estimate=pl.CostEstimate(flops=0, bytes_accessed=4 * part * cols, transcendentals=0),
         name="pack",
     )(where, act)
-    return out[0::2], out[1::2]
 
 
 def swap_if(flag, low, high):
@@ -120,7 +118,7 @@
 
     rows = hidden_act.shape[0]
     part = rows // ROW_CHUNKS
-    own, other = pack(where, hidden_act, xs)
+    own, other = [], []
 
     args = (master, moment_one, moment_two, gradient)
     updated, pieces = [], []
@@ -197,13 +195,19 @@
     def step_three(j):
         result.append((nears[j] + halfway[j]).astype(jnp.bfloat16))
 
+    def fill(m, *done):
+        for parts, value in zip((own, other), pack(after(where, *done), hidden_act, xs, m)):
+            parts.append(value)
+
+    fill(0)
     update(CHUNKS[:2], own[0])
     cross(0)
-    cross(1)
     gather(0)
     gather(1)
     update(CHUNKS[2:])
     to_plane(0, pieces[2])
+    fill(1, *pairs[0])
+    cross(1)
     gather(2, crossed[0][-1])
     to_tables(0)
     to_tables(1)

time: 204 us -> 209 us (1.025)
  Pallas kernels: 22 us -> 26.2 us
    pallas_call x1 -> x2, Pallas kernels: 1.8 us -> 5.92 us  [pack(): pl.pallas_call(kernel, grid=(1,), in_specs=[pl.BlockSpec(memory_space=plt...]
  transfers between devices with their start and end apart: 44 -> 44, of which waited for: 22 -> 21; matrix products, arithmetic and copies ran while one was open for 16% -> 16% of each run, Pallas kernels for 10% -> 11%
where the time goes in v12:
time: 209 us
  waiting for transfers between devices  96.3 us (46%)
  starting transfers between devices  48.9 us (23%)
  Pallas kernels  26.2 us (13%)
  matrix products  20.4 us (10%)
  other arithmetic  8.88 us (4%)
  local copies, waits for them, and re-layouts  6.46 us (3%)
    ppermute x44, waiting for transfers between devices, permute(): return lax.ppermute(value, AXES, pairs)  96.3 us
    ppermute x44, starting transfers between devices, permute(): return lax.ppermute(value, AXES, pairs)  48.9 us
    dot_general x32, matrix products, multiply(): jnp.dot(a, tables[q], preferred_element_type=jnp.float32)  20.4 us
    pallas_call x2, Pallas kernels, adam(): pl.pallas_call(kernel, grid_spec=pltpu.PrefetchScalarGridSpec(num_scalar_...  20.3 us
    pallas_call x2, Pallas kernels, pack(): pl.pallas_call(kernel, grid=(1,), in_specs=[pl.BlockSpec(memory_space=plt...  5.92 us
    slice x5, local copies, waits for them, and re-layouts, to_tables(): near = jnp.stack([p[k, :, :half] for p in parts])  5.24 us
  transfers between devices with their start and end apart: 44, of which 21 were waited for; matrix products, arithmetic and copies ran while one was open for 16% of the time, Pallas kernels for 11%

profile of v12, /device:TPU:0, one launch (start us, length us, event | category | flops | bytes accessed | tf_op | source)
XLA Modules:
  0.0 209.0 jit_solution(163724139206725528)
XLA Ops:
  1.3 2.9 %pack.2 = (bf16[256,1792]{1,0:T(8,128)(2,1)}, bf16[256,1792]{1,0:T(8,128)(2,1)}) custom-call(s32[3]{0:T(128)} %pad_add_fusion.where_ref, bf16[512,3584]{1,0:T(8,128)(2,1)} %act_ref.3), custom_call_target="tpu_custom_call" | custom-call | bytes 3670016 | tf_op jit(solution)/shard_map/pack/pallas_call | solution.py:82
  4.3 3.0 %collective-permute-start = (bf16[256,1792]{1,0:T(8,128)(2,1)}, bf16[256,1792]{1,0:T(8,128)(2,1)S(1)}, u32[]{:S(2)}, u32[]{:S(2)}) collective-permute-start(bf16[256,1792]{1,0:T(8,128)(2,1)} %get-tuple-element.58), channel_id=1, source_target_pairs={{0,2},{1,3},{2,0},{3,1},{4,6},{5,7},{6,4},{7,5},{8,10},{9,11},{10,... | collective-permute-start | bytes 2752520 | tf_op jit(solution)/shard_map/ppermute | solution.py:117
  7.2 10.0 %adam.2 = (f32[448,4096]{1,0:T(8,128)}, f32[448,4096]{1,0:T(8,128)}, f32[448,4096]{1,0:T(8,128)}, bf16[1,448,1024]{2,1,0:T(8,128)(2,1)}, bf16[1,448,1024]{2,1,0:T(8,128)(2,1)}) custom-call(s32[3]{0:T(128)} %pad_add_fusion.where_ref, f32[448,4096]{1,0:T(8,128)} %master_ref.3, f32[448,4096]{1,0:T(8,128)} %one_ref.3, f32[448,4096]{1,0:T(8,128)} %two_ref.3, ...), custom_call_target="tpu_custom_call" | custom-call | flops 11010048 | bytes 25690112 | tf_op jit(solution)/shard_map/adam/pallas_call | solution.py:48
  17.2 1.5 collective-permute-start.3
  19.3 10.3 %adam.3 = (f32[448,4096]{1,0:T(8,128)}, f32[448,4096]{1,0:T(8,128)}, f32[448,4096]{1,0:T(8,128)}, bf16[2,448,1024]{2,1,0:T(8,128)(2,1)}) custom-call(s32[3]{0:T(128)} %pad_add_fusion.where_ref, f32[448,4096]{1,0:T(8,128)} %master_ref.3, f32[448,4096]{1,0:T(8,128)} %one_ref.3, ...), custom_call_target="tpu_custom_call", output_to_operand_aliasing={{0}: (5, {}), {1}: (6, {}), {2}: (7, {})} | custom-call | flops 11010048 | bytes 25690112 | tf_op jit(solution)/shard_map/adam/pallas_call | solution.py:48
  31.0 3.0 %pack.3 = (bf16[256,1792]{1,0:T(8,128)(2,1)}, bf16[256,1792]{1,0:T(8,128)(2,1)}) custom-call(s32[3]{0:T(128)} %pad_add_fusion.where_ref, bf16[512,3584]{1,0:T(8,128)(2,1)} %act_ref.3), custom_call_target="tpu_custom_call" | custom-call | bytes 3670016 | tf_op jit(solution)/shard_map/pack/pallas_call | solution.py:82
  34.0 2.5 %fusion.62 = (bf16[1,448,512]{2,1,0:T(8,128)(2,1)S(1)}, bf16[1,448,512]{2,1,0:T(8,128)(2,1)S(1)}, bf16[1,448,512]{2,1,0:T(8,128)(2,1)S(1)}, bf16[1,448,512]{2,1,0:T(8,128)(2,1)}) fusion(bf16[1,448,1024]{2,1,0:T(8,128)(2,1)} %get-tuple-element.70, bf16[1,448,1024]{2,1,0:T(8,128)(2,1)} %get-tuple-element.61), kind=kLoop, calls=%fused_computation.227 | loop fusion | bytes 3670016 | tf_op jit(solution)/shard_map/slice | solution.py:159
  36.5 1.8 collective-permute-start.1
  38.3 3.0 %collective-permute-start.5 = (bf16[256,1792]{1,0:T(8,128)(2,1)}, bf16[256,1792]{1,0:T(8,128)(2,1)S(1)}, u32[]{:S(2)}, u32[]{:S(2)}) collective-permute-start(bf16[256,1792]{1,0:T(8,128)(2,1)} %get-tuple-element.62), channel_id=1, source_target_pairs={{0,16},{1,24},{2,18},{3,26},{4,20},{5,28},{6,22},{7,30},{8,17},{9,... | collective-permute-start | bytes 2752520 | tf_op jit(solution)/shard_map/ppermute | solution.py:117
  41.3 1.5 collective-permute-start.9
  44.1 16.4 %collective-permute-done.14 = bf16[1,448,1024]{2,1,0:T(8,128)(2,1)} collective-permute-done((bf16[1,448,1024]{2,1,0:T(8,128)(2,1)}, bf16[1,448,1024]{2,1,0:T(8,128)(2,1)}, u32[]{:S(2)}, u32[]{:S(2)}) %collective-permute-start.14) | collective-permute-done | bytes 917536 | tf_op jit(solution)/shard_map/ppermute | solution.py:117
  63.8 17.6 %collective-permute-done.5 = bf16[256,1792]{1,0:T(8,128)(2,1)S(1)} collective-permute-done((bf16[256,1792]{1,0:T(8,128)(2,1)}, bf16[256,1792]{1,0:T(8,128)(2,1)S(1)}, u32[]{:S(2)}, u32[]{:S(2)}) %collective-permute-start.5) | collective-permute-done | bytes 917536 | tf_op jit(solution)/shard_map/ppermute | solution.py:117
  84.0 4.3 %collective-permute-start.6 = (bf16[256,1792]{1,0:T(8,128)(2,1)S(1)}, bf16[256,1792]{1,0:T(8,128)(2,1)S(1)}, u32[]{:S(2)}, u32[]{:S(2)}) collective-permute-start(bf16[256,1792]{1,0:T(8,128)(2,1)S(1)} %collective-permute-done.5), channel_id=1, source_target_pairs={{0,1},{1,0},{2,3},{3,2},{4,5},{5,4},{6,7},{7,6},{8,9},{9,8},{10,11... | collective-permute-start | bytes 2752520 | tf_op jit(solution)/shard_map/ppermute | solution.py:117
  95.2 3.1 %collective-permute-done.9 = bf16[2,448,1024]{2,1,0:T(8,128)(2,1)S(1)} collective-permute-done((bf16[2,448,1024]{2,1,0:T(8,128)(2,1)S(1)}, bf16[2,448,1024]{2,1,0:T(8,128)(2,1)S(1)}, u32[]{:S(2)}, u32[]{:S(2)}) %collective-permute-start.9) | collective-permute-done | bytes 1835040 | tf_op jit(solution)/shard_map/ppermute | solution.py:117
  98.2 8.5 %collective-permute-done.7 = bf16[4,256,256]{2,1,0:T(8,128)(2,1)S(1)} collective-permute-done((bf16[4,256,256]{2,1,0:T(8,128)(2,1)S(1)}, bf16[4,256,256]{2,1,0:T(8,128)(2,1)S(1)}, u32[]{:S(2)}, u32[]{:S(2)}) %collective-permute-start.7) | collective-permute-done | bytes 524320 | tf_op jit(solution)/shard_map/ppermute | solution.py:117
  117.5 4.7 %collective-permute-done.16 = bf16[4,256,256]{2,1,0:T(8,128)(2,1)S(1)} collective-permute-done((bf16[4,256,256]{2,1,0:T(8,128)(2,1)S(1)}, bf16[4,256,256]{2,1,0:T(8,128)(2,1)S(1)}, u32[]{:S(2)}, u32[]{:S(2)}) %collective-permute-start.16) | collective-permute-done | bytes 524320 | tf_op jit(solution)/shard_map/ppermute | solution.py:117
  124.2 2.5 %collective-permute-start.18 = (bf16[512,256]{1,0:T(8,128)(2,1)S(1)}, bf16[512,256]{1,0:T(8,128)(2,1)S(1)}, u32[]{:S(2)}, u32[]{:S(2)}) collective-permute-start(bf16[512,256]{1,0:T(8,128)(2,1)S(1)} %pad_maximum_fusion.21), channel_id=1, source_target_pairs={{0,8},{1,9},{2,10},{3,11},{4,12},{5,13},{6,14},{7,15},{8,0},{9,1},... | collective-permute-start | bytes 786440 | tf_op jit(solution)/shard_map/ppermute | solution.py:117
  126.8 5.8 %collective-permute-done.17 = bf16[256,256]{1,0:T(8,128)(2,1)S(1)} collective-permute-done((bf16[256,256]{1,0:T(8,128)(2,1)S(1)}, bf16[256,256]{1,0:T(8,128)(2,1)S(1)}, u32[]{:S(2)}, u32[]{:S(2)}) %collective-permute-start.17) | collective-permute-done | bytes 131104 | tf_op jit(solution)/shard_map/ppermute | solution.py:117
  142.8 1.9 collective-permute-start.24
  149.5 4.1 %collective-permute-done.24 = bf16[512,256]{1,0:T(8,128)(2,1)S(1)} collective-permute-done((bf16[512,256]{1,0:T(8,128)(2,1)S(1)}, bf16[512,256]{1,0:T(8,128)(2,1)S(1)}, u32[]{:S(2)}, u32[]{:S(2)}) %collective-permute-start.24) | collective-permute-done | bytes 262176 | tf_op jit(solution)/shard_map/ppermute | solution.py:117
  154.1 2.9 %collective-permute-start.26 = (bf16[256,256]{1,0:T(8,128)(2,1)S(1)}, bf16[256,256]{1,0:T(8,128)(2,1)S(1)}, u32[]{:S(2)}, u32[]{:S(2)}) collective-permute-start(bf16[256,256]{1,0:T(8,128)(2,1)S(1)} %slice.885), channel_id=1, source_target_pairs={{0,16},{1,17},{2,18},{3,19},{4,20},{5,21},{6,22},{7,23},{8,24},{9,... | collective-permute-start | bytes 393224 | tf_op jit(solution)/shard_map/ppermute | solution.py:117
  157.0 6.9 %collective-permute-done.27 = bf16[512,256]{1,0:T(8,128)(2,1)S(1)} collective-permute-done((bf16[512,256]{1,0:T(8,128)(2,1)S(1)}, bf16[512,256]{1,0:T(8,128)(2,1)S(1)}, u32[]{:S(2)}, u32[]{:S(2)}) %collective-permute-start.27) | collective-permute-done | bytes 262176 | tf_op jit(solution)/shard_map/ppermute | solution.py:117
  164.6 2.5 %collective-permute-start.30 = (bf16[512,256]{1,0:T(8,128)(2,1)S(1)}, bf16[512,256]{1,0:T(8,128)(2,1)S(1)}, u32[]{:S(2)}, u32[]{:S(2)}) collective-permute-start(bf16[512,256]{1,0:T(8,128)(2,1)S(1)} %pad_maximum_fusion.24), channel_id=1, source_target_pairs={{0,8},{1,9},{2,10},{3,11},{4,12},{5,13},{6,14},{7,15},{8,0},{9,1},... | collective-permute-start | bytes 786440 | tf_op jit(solution)/shard_map/ppermute | solution.py:117
  169.3 2.4 %collective-permute-done.29 = bf16[256,256]{1,0:T(8,128)(2,1)S(1)} collective-permute-done((bf16[256,256]{1,0:T(8,128)(2,1)S(1)}, bf16[256,256]{1,0:T(8,128)(2,1)S(1)}, u32[]{:S(2)}, u32[]{:S(2)}) %collective-permute-start.29) | collective-permute-done | bytes 131104 | tf_op jit(solution)/shard_map/ppermute | solution.py:117
  171.8 3.3 %collective-permute-done.30 = bf16[512,256]{1,0:T(8,128)(2,1)S(1)} collective-permute-done((bf16[512,256]{1,0:T(8,128)(2,1)S(1)}, bf16[512,256]{1,0:T(8,128)(2,1)S(1)}, u32[]{:S(2)}, u32[]{:S(2)}) %collective-permute-start.30) | collective-permute-done | bytes 262176 | tf_op jit(solution)/shard_map/ppermute | solution.py:117
  175.8 1.8 collective-permute-start.33
  177.6 4.6 %collective-permute-done.34 = bf16[4,256,256]{2,1,0:T(8,128)(2,1)S(1)} collective-permute-done((bf16[4,256,256]{2,1,0:T(8,128)(2,1)S(1)}, bf16[4,256,256]{2,1,0:T(8,128)(2,1)S(1)}, u32[]{:S(2)}, u32[]{:S(2)}) %collective-permute-start.34) | collective-permute-done | bytes 524320 | tf_op jit(solution)/shard_map/ppermute | solution.py:117
  183.2 3.7 %collective-permute-done.33 = bf16[512,256]{1,0:T(8,128)(2,1)S(1)} collective-permute-done((bf16[512,256]{1,0:T(8,128)(2,1)S(1)}, bf16[512,256]{1,0:T(8,128)(2,1)S(1)}, u32[]{:S(2)}, u32[]{:S(2)}) %collective-permute-start.33) | collective-permute-done | bytes 262176 | tf_op jit(solution)/shard_map/ppermute | solution.py:117
  188.2 5.1 %collective-permute-done.36 = bf16[512,256]{1,0:T(8,128)(2,1)S(1)} collective-permute-done((bf16[512,256]{1,0:T(8,128)(2,1)S(1)}, bf16[512,256]{1,0:T(8,128)(2,1)S(1)}, u32[]{:S(2)}, u32[]{:S(2)}) %collective-permute-start.36) | collective-permute-done | bytes 262176 | tf_op jit(solution)/shard_map/ppermute | solution.py:117
  197.3 3.7 %collective-permute-done.39 = bf16[512,128]{1,0:T(8,128)(2,1)S(1)} collective-permute-done((bf16[512,128]{1,0:T(8,128)(2,1)S(1)}, bf16[512,128]{1,0:T(8,128)(2,1)S(1)}, u32[]{:S(2)}, u32[]{:S(2)}) %collective-permute-start.39) | collective-permute-done | bytes 131104 | tf_op jit(solution)/shard_map/ppermute | solution.py:117
  202.4 2.3 %collective-permute-start.43 = (bf16[256,128]{1,0:T(8,128)(2,1)S(1)}, bf16[256,128]{1,0:T(8,128)(2,1)S(1)}, u32[]{:S(2)}, u32[]{:S(2)}) collective-permute-start(bf16[256,128]{1,0:T(8,128)(2,1)S(1)} %slice.888), channel_id=1, source_target_pairs={{0,16},{1,17},{2,18},{3,19},{4,20},{5,21},{6,22},{7,23},{8,24},{9,... | collective-permute-start | bytes 196616 | tf_op jit(solution)/shard_map/ppermute | solution.py:117
  204.7 2.5 %collective-permute-done.40 = bf16[256,128]{1,0:T(8,128)(2,1)S(1)} collective-permute-done((bf16[256,128]{1,0:T(8,128)(2,1)S(1)}, bf16[256,128]{1,0:T(8,128)(2,1)S(1)}, u32[]{:S(2)}, u32[]{:S(2)}) %collective-permute-start.40) | collective-permute-done | bytes 65568 | tf_op jit(solution)/shard_map/ppermute | solution.py:117
  (211 shorter events, 57.5 us)
Async XLA Ops:
  4.3 25.3 %collective-permute-start = (bf16[256,1792]{1,0:T(8,128)(2,1)}, bf16[256,1792]{1,0:T(8,128)(2,1)S(1)}, u32[]{:S(2)}, u32[]{:S(2)}) collective-permute-start(bf16[256,1792]{1,0:T(8,128)(2,1)} %get-tuple-element.58), channel_id=1, source_target_pairs={{0,2},{1,3},{2,0},{3,1},{4,6},{5,7},{6,4},{7,5},{8,10},{9,11},{10,... | collective-permute-start | bytes 2752520 | tf_op jit(solution)/shard_map/ppermute | solution.py:117
  17.2 24.0 %collective-permute-start.3 = (bf16[1,448,1024]{2,1,0:T(8,128)(2,1)}, bf16[1,448,1024]{2,1,0:T(8,128)(2,1)}, u32[]{:S(2)}, u32[]{:S(2)}) collective-permute-start(bf16[1,448,1024]{2,1,0:T(8,128)(2,1)} %get-tuple-element.61), channel_id=1, source_target_pairs={{0,4},{1,5},{2,6},{3,7},{4,0},{5,1},{6,2},{7,3},{8,12},{9,13},{10,... | collective-permute-start | bytes 2752520 | tf_op jit(solution)/shard_map/ppermute | solution.py:117
  18.7 41.8 %collective-permute-start.14 = (bf16[1,448,1024]{2,1,0:T(8,128)(2,1)}, bf16[1,448,1024]{2,1,0:T(8,128)(2,1)}, u32[]{:S(2)}, u32[]{:S(2)}) collective-permute-start(bf16[1,448,1024]{2,1,0:T(8,128)(2,1)} %get-tuple-element.70), channel_id=1, source_target_pairs={{0,4},{1,5},{2,6},{3,7},{4,0},{5,1},{6,2},{7,3},{8,12},{9,13},{10,... | collective-permute-start | bytes 2752520 | tf_op jit(solution)/shard_map/ppermute | solution.py:117
  34.0 27.9 %collective-permute-start.10 = (bf16[256,1792]{1,0:T(8,128)(2,1)}, bf16[256,1792]{1,0:T(8,128)(2,1)}, u32[]{:S(2)}, u32[]{:S(2)}) collective-permute-start(bf16[256,1792]{1,0:T(8,128)(2,1)} %get-tuple-element.65), channel_id=1, source_target_pairs={{0,2},{1,3},{2,0},{3,1},{4,6},{5,7},{6,4},{7,5},{8,10},{9,11},{10,... | collective-permute-start | bytes 2752520 | tf_op jit(solution)/shard_map/ppermute | solution.py:117
  36.5 27.3 %collective-permute-start.1 = (bf16[256,1792]{1,0:T(8,128)(2,1)}, bf16[256,1792]{1,0:T(8,128)(2,1)S(1)}, u32[]{:S(2)}, u32[]{:S(2)}) collective-permute-start(bf16[256,1792]{1,0:T(8,128)(2,1)} %get-tuple-element.60), channel_id=1, source_target_pairs={{0,0},{1,8},{2,2},{3,10},{4,4},{5,12},{6,6},{7,14},{8,1},{9,9},{10... | collective-permute-start | bytes 2752520 | tf_op jit(solution)/shard_map/ppermute | solution.py:117
  38.3 43.1 %collective-permute-start.5 = (bf16[256,1792]{1,0:T(8,128)(2,1)}, bf16[256,1792]{1,0:T(8,128)(2,1)S(1)}, u32[]{:S(2)}, u32[]{:S(2)}) collective-permute-start(bf16[256,1792]{1,0:T(8,128)(2,1)} %get-tuple-element.62), channel_id=1, source_target_pairs={{0,16},{1,24},{2,18},{3,26},{4,20},{5,28},{6,22},{7,30},{8,17},{9,... | collective-permute-start | bytes 2752520 | tf_op jit(solution)/shard_map/ppermute | solution.py:117
  41.3 57.0 %collective-permute-start.9 = (bf16[2,448,1024]{2,1,0:T(8,128)(2,1)S(1)}, bf16[2,448,1024]{2,1,0:T(8,128)(2,1)S(1)}, u32[]{:S(2)}, u32[]{:S(2)}) collective-permute-start(bf16[2,448,1024]{2,1,0:T(8,128)(2,1)S(1)} %copy-done), channel_id=1, source_target_pairs={{0,4},{1,5},{2,6},{3,7},{4,0},{5,1},{6,2},{7,3},{8,12},{9,13},{10,... | collective-permute-start | bytes 5505032 | tf_op jit(solution)/shard_map/ppermute | solution.py:117
  60.5 21.9 %collective-permute-start.4 = (bf16[2,448,512]{2,1,0:T(8,128)(2,1)S(1)}, bf16[2,448,512]{2,1,0:T(8,128)(2,1)S(1)}, u32[]{:S(2)}, u32[]{:S(2)}) collective-permute-start(bf16[2,448,512]{2,1,0:T(8,128)(2,1)S(1)} %pad_maximum_fusion.5), channel_id=1, source_target_pairs={{0,1},{1,0},{2,3},{3,2},{4,5},{5,4},{6,7},{7,6},{8,9},{9,8},{10,11... | collective-permute-start | bytes 2752520 | tf_op jit(solution)/shard_map/ppermute | solution.py:117
  61.8 21.7 %collective-permute-start.15 = (bf16[2,448,512]{2,1,0:T(8,128)(2,1)S(1)}, bf16[2,448,512]{2,1,0:T(8,128)(2,1)S(1)}, u32[]{:S(2)}, u32[]{:S(2)}) collective-permute-start(bf16[2,448,512]{2,1,0:T(8,128)(2,1)S(1)} %pad_maximum_fusion.11), channel_id=1, source_target_pairs={{0,1},{1,0},{2,3},{3,2},{4,5},{5,4},{6,7},{7,6},{8,9},{9,8},{10,11... | collective-permute-start | bytes 2752520 | tf_op jit(solution)/shard_map/ppermute | solution.py:117
  81.4 13.8 %collective-permute-start.11 = (bf16[256,1792]{1,0:T(8,128)(2,1)S(1)}, bf16[256,1792]{1,0:T(8,128)(2,1)S(1)}, u32[]{:S(2)}, u32[]{:S(2)}) collective-permute-start(bf16[256,1792]{1,0:T(8,128)(2,1)S(1)} %get-tuple-element.67), channel_id=1, source_target_pairs={{0,0},{1,8},{2,2},{3,10},{4,4},{5,12},{6,6},{7,14},{8,1},{9,9},{10... | collective-permute-start | bytes 2752520 | tf_op jit(solution)/shard_map/ppermute | solution.py:117
  82.3 50.3 %collective-permute-start.19 = (bf16[256,1792]{1,0:T(8,128)(2,1)S(1)}, bf16[256,1792]{1,0:T(8,128)(2,1)S(1)}, u32[]{:S(2)}, u32[]{:S(2)}) collective-permute-start(bf16[256,1792]{1,0:T(8,128)(2,1)S(1)} %get-tuple-element.76), channel_id=1, source_target_pairs={{0,16},{1,24},{2,18},{3,26},{4,20},{5,28},{6,22},{7,30},{8,17},{9,... | collective-permute-start | bytes 2752520 | tf_op jit(solution)/shard_map/ppermute | solution.py:117
  92.4 14.3 %collective-permute-start.7 = (bf16[4,256,256]{2,1,0:T(8,128)(2,1)S(1)}, bf16[4,256,256]{2,1,0:T(8,128)(2,1)S(1)}, u32[]{:S(2)}, u32[]{:S(2)}) collective-permute-start(bf16[4,256,256]{2,1,0:T(8,128)(2,1)S(1)} %pad_maximum_fusion.13), channel_id=1, source_target_pairs={{0,2},{1,3},{2,0},{3,1},{4,6},{5,7},{6,4},{7,5},{8,10},{9,11},{10,... | collective-permute-start | bytes 1572872 | tf_op jit(solution)/shard_map/ppermute | solution.py:117
  107.4 14.8 %collective-permute-start.16 = (bf16[4,256,256]{2,1,0:T(8,128)(2,1)S(1)}, bf16[4,256,256]{2,1,0:T(8,128)(2,1)S(1)}, u32[]{:S(2)}, u32[]{:S(2)}) collective-permute-start(bf16[4,256,256]{2,1,0:T(8,128)(2,1)S(1)} %pad_maximum_fusion.16), channel_id=1, source_target_pairs={{0,2},{1,3},{2,0},{3,1},{4,6},{5,7},{6,4},{7,5},{8,10},{9,11},{10,... | collective-permute-start | bytes 1572872 | tf_op jit(solution)/shard_map/ppermute | solution.py:117
  109.4 14.1 %collective-permute-start.8 = (bf16[512,256]{1,0:T(8,128)(2,1)S(1)}, bf16[512,256]{1,0:T(8,128)(2,1)S(1)}, u32[]{:S(2)}, u32[]{:S(2)}) collective-permute-start(bf16[512,256]{1,0:T(8,128)(2,1)S(1)} %pad_maximum_fusion.20), channel_id=1, source_target_pairs={{0,8},{1,9},{2,10},{3,11},{4,12},{5,13},{6,14},{7,15},{8,0},{9,1},... | collective-permute-start | bytes 786440 | tf_op jit(solution)/shard_map/ppermute | solution.py:117
  112.9 20.5 %collective-permute-start.20 = (bf16[4,256,256]{2,1,0:T(8,128)(2,1)S(1)}, bf16[4,256,256]{2,1,0:T(8,128)(2,1)S(1)}, u32[]{:S(2)}, u32[]{:S(2)}) collective-permute-start(bf16[4,256,256]{2,1,0:T(8,128)(2,1)S(1)} %pad_maximum_fusion.15), channel_id=1, source_target_pairs={{0,2},{1,3},{2,0},{3,1},{4,6},{5,7},{6,4},{7,5},{8,10},{9,11},{10,... | collective-permute-start | bytes 1572872 | tf_op jit(solution)/shard_map/ppermute | solution.py:117
  122.1 26.6 %collective-permute-start.25 = (bf16[4,256,256]{2,1,0:T(8,128)(2,1)S(1)}, bf16[4,256,256]{2,1,0:T(8,128)(2,1)S(1)}, u32[]{:S(2)}, u32[]{:S(2)}) collective-permute-start(bf16[4,256,256]{2,1,0:T(8,128)(2,1)S(1)} %pad_maximum_fusion.14), channel_id=1, source_target_pairs={{0,2},{1,3},{2,0},{3,1},{4,6},{5,7},{6,4},{7,5},{8,10},{9,11},{10,... | collective-permute-start | bytes 1572872 | tf_op jit(solution)/shard_map/ppermute | solution.py:117
  123.6 9.0 %collective-permute-start.17 = (bf16[256,256]{1,0:T(8,128)(2,1)S(1)}, bf16[256,256]{1,0:T(8,128)(2,1)S(1)}, u32[]{:S(2)}, u32[]{:S(2)}) collective-permute-start(bf16[256,256]{1,0:T(8,128)(2,1)S(1)} %slice.887), channel_id=1, source_target_pairs={{0,16},{1,17},{2,18},{3,19},{4,20},{5,21},{6,22},{7,23},{8,24},{9,... | collective-permute-start | bytes 393224 | tf_op jit(solution)/shard_map/ppermute | solution.py:117
  124.2 18.1 %collective-permute-start.18 = (bf16[512,256]{1,0:T(8,128)(2,1)S(1)}, bf16[512,256]{1,0:T(8,128)(2,1)S(1)}, u32[]{:S(2)}, u32[]{:S(2)}) collective-permute-start(bf16[512,256]{1,0:T(8,128)(2,1)S(1)} %pad_maximum_fusion.21), channel_id=1, source_target_pairs={{0,8},{1,9},{2,10},{3,11},{4,12},{5,13},{6,14},{7,15},{8,0},{9,1},... | collective-permute-start | bytes 786440 | tf_op jit(solution)/shard_map/ppermute | solution.py:117
  140.9 16.0 %collective-permute-start.28 = (bf16[4,256,256]{2,1,0:T(8,128)(2,1)S(1)}, bf16[4,256,256]{2,1,0:T(8,128)(2,1)S(1)}, u32[]{:S(2)}, u32[]{:S(2)}) collective-permute-start(bf16[4,256,256]{2,1,0:T(8,128)(2,1)S(1)} %pad_maximum_fusion.17), channel_id=1, source_target_pairs={{0,2},{1,3},{2,0},{3,1},{4,6},{5,7},{6,4},{7,5},{8,10},{9,11},{10,... | collective-permute-start | bytes 1572872 | tf_op jit(solution)/shard_map/ppermute | solution.py:117
  142.5 11.6 %collective-permute-start.23 = (bf16[256,256]{1,0:T(8,128)(2,1)S(1)}, bf16[256,256]{1,0:T(8,128)(2,1)S(1)}, u32[]{:S(2)}, u32[]{:S(2)}) collective-permute-start(bf16[256,256]{1,0:T(8,128)(2,1)S(1)} %slice.886), channel_id=1, source_target_pairs={{0,16},{1,17},{2,18},{3,19},{4,20},{5,21},{6,22},{7,23},{8,24},{9,... | collective-permute-start | bytes 393224 | tf_op jit(solution)/shard_map/ppermute | solution.py:117
  142.8 10.8 %collective-permute-start.24 = (bf16[512,256]{1,0:T(8,128)(2,1)S(1)}, bf16[512,256]{1,0:T(8,128)(2,1)S(1)}, u32[]{:S(2)}, u32[]{:S(2)}) collective-permute-start(bf16[512,256]{1,0:T(8,128)(2,1)S(1)} %pad_maximum_fusion.22), channel_id=1, source_target_pairs={{0,8},{1,9},{2,10},{3,11},{4,12},{5,13},{6,14},{7,15},{8,0},{9,1},... | collective-permute-start | bytes 786440 | tf_op jit(solution)/shard_map/ppermute | solution.py:117
  148.7 19.2 %collective-permute-start.31 = (bf16[4,256,256]{2,1,0:T(8,128)(2,1)S(1)}, bf16[4,256,256]{2,1,0:T(8,128)(2,1)S(1)}, u32[]{:S(2)}, u32[]{:S(2)}) collective-permute-start(bf16[4,256,256]{2,1,0:T(8,128)(2,1)S(1)} %pad_maximum_fusion.18), channel_id=1, source_target_pairs={{0,2},{1,3},{2,0},{3,1},{4,6},{5,7},{6,4},{7,5},{8,10},{9,11},{10,... | collective-permute-start | bytes 1572872 | tf_op jit(solution)/shard_map/ppermute | solution.py:117
  153.9 10.0 %collective-permute-start.27 = (bf16[512,256]{1,0:T(8,128)(2,1)S(1)}, bf16[512,256]{1,0:T(8,128)(2,1)S(1)}, u32[]{:S(2)}, u32[]{:S(2)}) collective-permute-start(bf16[512,256]{1,0:T(8,128)(2,1)S(1)} %pad_maximum_fusion.23), channel_id=1, source_target_pairs={{0,8},{1,9},{2,10},{3,11},{4,12},{5,13},{6,14},{7,15},{8,0},{9,1},... | collective-permute-start | bytes 786440 | tf_op jit(solution)/shard_map/ppermute | solution.py:117
  154.1 13.1 %collective-permute-start.26 = (bf16[256,256]{1,0:T(8,128)(2,1)S(1)}, bf16[256,256]{1,0:T(8,128)(2,1)S(1)}, u32[]{:S(2)}, u32[]{:S(2)}) collective-permute-start(bf16[256,256]{1,0:T(8,128)(2,1)S(1)} %slice.885), channel_id=1, source_target_pairs={{0,16},{1,17},{2,18},{3,19},{4,20},{5,21},{6,22},{7,23},{8,24},{9,... | collective-permute-start | bytes 393224 | tf_op jit(solution)/shard_map/ppermute | solution.py:117
  164.6 10.4 %collective-permute-start.30 = (bf16[512,256]{1,0:T(8,128)(2,1)S(1)}, bf16[512,256]{1,0:T(8,128)(2,1)S(1)}, u32[]{:S(2)}, u32[]{:S(2)}) collective-permute-start(bf16[512,256]{1,0:T(8,128)(2,1)S(1)} %pad_maximum_fusion.24), channel_id=1, source_target_pairs={{0,8},{1,9},{2,10},{3,11},{4,12},{5,13},{6,14},{7,15},{8,0},{9,1},... | collective-permute-start | bytes 786440 | tf_op jit(solution)/shard_map/ppermute | solution.py:117
  167.2 14.9 %collective-permute-start.34 = (bf16[4,256,256]{2,1,0:T(8,128)(2,1)S(1)}, bf16[4,256,256]{2,1,0:T(8,128)(2,1)S(1)}, u32[]{:S(2)}, u32[]{:S(2)}) collective-permute-start(bf16[4,256,256]{2,1,0:T(8,128)(2,1)S(1)} %pad_maximum_fusion.19), channel_id=1, source_target_pairs={{0,2},{1,3},{2,0},{3,1},{4,6},{5,7},{6,4},{7,5},{8,10},{9,11},{10,... | collective-permute-start | bytes 1572872 | tf_op jit(solution)/shard_map/ppermute | solution.py:117
  167.9 20.3 %collective-permute-start.38 = (bf16[4,256,128]{2,1,0:T(8,128)(2,1)S(1)}, bf16[4,256,128]{2,1,0:T(8,128)(2,1)S(1)}, u32[]{:S(2)}, u32[]{:S(2)}) collective-permute-start(bf16[4,256,128]{2,1,0:T(8,128)(2,1)S(1)} %pad_maximum_fusion.25), channel_id=1, source_target_pairs={{0,2},{1,3},{2,0},{3,1},{4,6},{5,7},{6,4},{7,5},{8,10},{9,11},{10,... | collective-permute-start | bytes 786440 | tf_op jit(solution)/shard_map/ppermute | solution.py:117
  175.8 11.0 %collective-permute-start.33 = (bf16[512,256]{1,0:T(8,128)(2,1)S(1)}, bf16[512,256]{1,0:T(8,128)(2,1)S(1)}, u32[]{:S(2)}, u32[]{:S(2)}) collective-permute-start(bf16[512,256]{1,0:T(8,128)(2,1)S(1)} %pad_maximum_fusion.26), channel_id=1, source_target_pairs={{0,8},{1,9},{2,10},{3,11},{4,12},{5,13},{6,14},{7,15},{8,0},{9,1},... | collective-permute-start | bytes 786440 | tf_op jit(solution)/shard_map/ppermute | solution.py:117
  182.3 10.9 %collective-permute-start.36 = (bf16[512,256]{1,0:T(8,128)(2,1)S(1)}, bf16[512,256]{1,0:T(8,128)(2,1)S(1)}, u32[]{:S(2)}, u32[]{:S(2)}) collective-permute-start(bf16[512,256]{1,0:T(8,128)(2,1)S(1)} %pad_maximum_fusion.28), channel_id=1, source_target_pairs={{0,8},{1,9},{2,10},{3,11},{4,12},{5,13},{6,14},{7,15},{8,0},{9,1},... | collective-permute-start | bytes 786440 | tf_op jit(solution)/shard_map/ppermute | solution.py:117
  182.5 10.9 %collective-permute-start.41 = (bf16[4,256,128]{2,1,0:T(8,128)(2,1)S(1)}, bf16[4,256,128]{2,1,0:T(8,128)(2,1)S(1)}, u32[]{:S(2)}, u32[]{:S(2)}) collective-permute-start(bf16[4,256,128]{2,1,0:T(8,128)(2,1)S(1)} %pad_maximum_fusion.27), channel_id=1, source_target_pairs={{0,2},{1,3},{2,0},{3,1},{4,6},{5,7},{6,4},{7,5},{8,10},{9,11},{10,... | collective-permute-start | bytes 786440 | tf_op jit(solution)/shard_map/ppermute | solution.py:117
  186.9 8.1 %collective-permute-start.35 = (bf16[256,256]{1,0:T(8,128)(2,1)S(1)}, bf16[256,256]{1,0:T(8,128)(2,1)S(1)}, u32[]{:S(2)}, u32[]{:S(2)}) collective-permute-start(bf16[256,256]{1,0:T(8,128)(2,1)S(1)} %slice.882), channel_id=1, source_target_pairs={{0,16},{1,17},{2,18},{3,19},{4,20},{5,21},{6,22},{7,23},{8,24},{9,... | collective-permute-start | bytes 393224 | tf_op jit(solution)/shard_map/ppermute | solution.py:117
  195.1 9.6 %collective-permute-start.37 = (bf16[256,256]{1,0:T(8,128)(2,1)S(1)}, bf16[256,256]{1,0:T(8,128)(2,1)S(1)}, u32[]{:S(2)}, u32[]{:S(2)}) collective-permute-start(bf16[256,256]{1,0:T(8,128)(2,1)S(1)} %slice.881), channel_id=1, source_target_pairs={{0,16},{1,17},{2,18},{3,19},{4,20},{5,21},{6,22},{7,23},{8,24},{9,... | collective-permute-start | bytes 393224 | tf_op jit(solution)/shard_map/ppermute | solution.py:117
  (16 other events, 126.2 us)
